TPU v7x, 32 devices: a whole 2x2x4 slice. The times are simulated.
32 devices in a mesh: groups: 2 (over x), tm: 8 (over z, y), space: 2 (over core).
Axes of the slice: x: 2, y: 2, z: 4, core: 2. Of those that a mesh axis runs over, the one named last changes fastest.
Arguments:
- grad_out: bfloat16 [112, 128, 1024], P(('groups', 'tm'), 'space'), parts along dimension 0, may hold values from -6 to 6
- time_q: bfloat16 [112, 128, 1024], P(('groups', 'tm'), 'space'), parts along dimension 0, may hold values from -7 to 7
- time_k: bfloat16 [112, 128, 1024], P(('groups', 'tm'), 'space'), parts along dimension 0, may hold values from -7 to 7
- time_v: bfloat16 [112, 128, 1024], P(('groups', 'tm'), 'space'), parts along dimension 0, may hold values from -6 to 6
- space_q: bfloat16 [112, 128, 1024], P(('groups', 'tm'), 'space'), parts along dimension 0, may hold values from -7 to 7
- space_k: bfloat16 [112, 128, 1024], P(('groups', 'tm'), 'space'), parts along dimension 0, may hold values from -7 to 7
- space_v: bfloat16 [112, 128, 1024], P(('groups', 'tm'), 'space'), parts along dimension 0, may hold values from -6 to 6
- time_wo: bfloat16 [1024, 1024], P(('tm', 'space')), may hold values from -0.1875 to 0.1875
- space_wo: bfloat16 [1024, 1024], P(('tm', 'space')), may hold values from -0.1875 to 0.1875
Outputs:
- time_dq: bfloat16 [112, 128, 1024], P(('groups', 'tm'), 'space'), parts along dimension 0
- time_dk: bfloat16 [112, 128, 1024], P(('groups', 'tm'), 'space'), parts along dimension 0
- time_dv: bfloat16 [112, 128, 1024], P(('groups', 'tm'), 'space'), parts along dimension 0
- space_dq: bfloat16 [112, 128, 1024], P(('groups', 'tm'), 'space'), parts along dimension 0
- space_dk: bfloat16 [112, 128, 1024], P(('groups', 'tm'), 'space'), parts along dimension 0
- space_dv: bfloat16 [112, 128, 1024], P(('groups', 'tm'), 'space'), parts along dimension 0
There are 2 independent parts, one for each index of `groups`. A program takes and returns all parts, laid end to end along the dimension named above; an argument that names none is the same for every part. Nothing has to cross between parts.
All inputs are finite; a program needn't handle non-finite values.
Results may differ from a plain program's by a relative error of at most 0.011.
Values may be sent and summed in bfloat16 or wider, within the bound.
No kernel may reach another device: no remote copies, remote signals or barrier semaphores. Data moves between devices by JAX's collectives and lax.ppermute only.
A program may use at most 128 MiB of HBM per device.

v0:
```python
import math

import jax
import jax.numpy as jnp
from jax import lax
from jax.sharding import PartitionSpec as P

HEAD_DIM = 64


def attend_back(query, keys, values, out_grad, layout):
    key_layout = layout.replace("s", "t")
    batch_letters = "".join([letter for letter in layout if letter not in "se"])
    score_layout = batch_letters + "st"
    score_scale = 1.0 / math.sqrt(query.shape[-1])
    scores = (
        jnp.einsum(
            layout + "," + key_layout + "->" + score_layout,
            query,
            keys,
            preferred_element_type=jnp.float32,
        )
        * score_scale
    )
    row_max = jnp.max(scores, axis=-1, keepdims=True)
    expo = jnp.exp(scores - row_max)
    probs = expo / jnp.sum(expo, axis=-1, keepdims=True)
    probs_low = probs.astype(jnp.bfloat16)
    grad_values = jnp.einsum(
        score_layout + "," + layout + "->" + key_layout,
        probs_low,
        out_grad,
        preferred_element_type=jnp.float32,
    )
    dprob = jnp.einsum(
        layout + "," + key_layout + "->" + score_layout,
        out_grad,
        values,
        preferred_element_type=jnp.float32,
    )
    delta = jnp.sum(probs * dprob, axis=-1, keepdims=True)
    dscore = (probs * (dprob - delta)).astype(jnp.bfloat16)
    grad_query = score_scale * jnp.einsum(
        score_layout + "," + key_layout + "->" + layout,
        dscore,
        keys,
        preferred_element_type=jnp.float32,
    )
    grad_keys = score_scale * jnp.einsum(
        score_layout + "," + layout + "->" + key_layout,
        dscore,
        query,
        preferred_element_type=jnp.float32,
    )
    return (grad_query, grad_keys, grad_values)


def per_device(grad_out, time_q, time_k, time_v, space_q, space_k, space_v, time_wo, space_wo):
    frames_here, patches_here, model_width = grad_out.shape
    tok_rows = grad_out.reshape(frames_here * patches_here, model_width)
    both_wo = jnp.concatenate([time_wo, space_wo], axis=1)
    block_rows = lax.all_gather(both_wo, ("tm", "space"), axis=0, tiled=True)
    time_part = jnp.einsum(
        "td,cd->tc", tok_rows, block_rows[:, :model_width], preferred_element_type=jnp.float32
    )
    space_part = jnp.einsum(
        "td,cd->tc", tok_rows, block_rows[:, model_width:], preferred_element_type=jnp.float32
    )
    projected = jnp.stack([time_part, space_part])
    time_grad = projected[0].astype(jnp.bfloat16).reshape(frames_here, patches_here, model_width)
    space_grad = projected[1].astype(jnp.bfloat16).reshape(frames_here, patches_here, model_width)
    head_pairs = model_width // (2 * HEAD_DIM)

    def paired(tensor):
        return tensor.reshape(frames_here, patches_here, head_pairs, 2 * HEAD_DIM)

    time_in = (paired(time_q), paired(time_k), paired(time_v), paired(time_grad))
    query = lax.all_to_all(time_in[0], "tm", split_axis=1, concat_axis=0, tiled=True)
    keys = lax.all_to_all(time_in[1], "tm", split_axis=1, concat_axis=0, tiled=True)
    values = lax.all_to_all(time_in[2], "tm", split_axis=1, concat_axis=0, tiled=True)
    out_grad = lax.all_to_all(time_in[3], "tm", split_axis=1, concat_axis=0, tiled=True)
    all_frames, patch_count, pair_count, pair_width = query.shape

    def to_heads(tensor):
        return tensor.reshape(all_frames, patch_count * pair_count * 2, pair_width // 2)

    def to_pairs(tensor):
        return tensor.astype(jnp.bfloat16).reshape(all_frames, patch_count, pair_count, pair_width)

    results = attend_back(
        to_heads(query), to_heads(keys), to_heads(values), to_heads(out_grad), "sbe"
    )
    time_dq = lax.all_to_all(to_pairs(results[0]), "tm", split_axis=0, concat_axis=1, tiled=True)
    time_dk = lax.all_to_all(to_pairs(results[1]), "tm", split_axis=0, concat_axis=1, tiled=True)
    time_dv = lax.all_to_all(to_pairs(results[2]), "tm", split_axis=0, concat_axis=1, tiled=True)
    space_in = (paired(space_q), paired(space_k), paired(space_v), paired(space_grad))
    query = lax.all_to_all(space_in[0], "space", split_axis=2, concat_axis=1, tiled=True)
    keys = lax.all_to_all(space_in[1], "space", split_axis=2, concat_axis=1, tiled=True)
    values = lax.all_to_all(space_in[2], "space", split_axis=2, concat_axis=1, tiled=True)
    out_grad = lax.all_to_all(space_in[3], "space", split_axis=2, concat_axis=1, tiled=True)
    frame_count, all_patches, space_pair_count, space_pair_width = query.shape

    def to_heads(tensor):
        return tensor.reshape(frame_count, all_patches, space_pair_count * 2, space_pair_width // 2)

    def to_pairs(tensor):
        return tensor.astype(jnp.bfloat16).reshape(
            frame_count, all_patches, space_pair_count, space_pair_width
        )

    results = attend_back(
        to_heads(query), to_heads(keys), to_heads(values), to_heads(out_grad), "asbe"
    )
    space_dq = lax.all_to_all(
        to_pairs(results[0]), "space", split_axis=1, concat_axis=2, tiled=True
    )
    space_dk = lax.all_to_all(
        to_pairs(results[1]), "space", split_axis=1, concat_axis=2, tiled=True
    )
    space_dv = lax.all_to_all(
        to_pairs(results[2]), "space", split_axis=1, concat_axis=2, tiled=True
    )

    def flat_out(tensor):
        return tensor.reshape(frames_here, patches_here, model_width)

    return (
        flat_out(time_dq),
        flat_out(time_dk),
        flat_out(time_dv),
        flat_out(space_dq),
        flat_out(space_dk),
        flat_out(space_dv),
    )


def solution(mesh):
    in_specs = (
        P(("groups", "tm"), "space", None),
        P(("groups", "tm"), "space", None),
        P(("groups", "tm"), "space", None),
        P(("groups", "tm"), "space", None),
        P(("groups", "tm"), "space", None),
        P(("groups", "tm"), "space", None),
        P(("groups", "tm"), "space", None),
        P(("tm", "space"), None),
        P(("tm", "space"), None),
    )
    out_specs = (
        P(("groups", "tm"), "space", None),
        P(("groups", "tm"), "space", None),
        P(("groups", "tm"), "space", None),
        P(("groups", "tm"), "space", None),
        P(("groups", "tm"), "space", None),
        P(("groups", "tm"), "space", None),
    )
    return jax.shard_map(
        per_device, mesh=mesh, in_specs=in_specs, out_specs=out_specs, check_vma=False
    )
```

profile of v0, /device:TPU:0, one launch (start us, length us, event | category | flops | bytes accessed | tf_op | source)
XLA Modules:
  0.0 319.9 jit_solution(16564373491233327781)
XLA Ops:
  7.2 1.8 pad_maximum_fusion
  9.0 2.4 copy_bitcast_fusion.2
  11.5 4.4 %all-to-all-start.8 = ((bf16[7,64,8,128]{3,1,0,2:T(8,128)(2,1)}), bf16[7,64,8,128]{3,1,0,2:T(8,128)(2,1)}, u32[]{:S(2)}, u32[]{:S(2)}) async-start(bf16[7,64,8,128]{3,1,0,2:T(8,128)(2,1)} %copy_bitcast_fusion.2), calls=%async_computation.8 | async-start | bytes 1835008 | tf_op jit(solution)/shard_map/all_to_all | solution.py:98
  18.0 5.2 %all_to_all.210 = bf16[7,64,8,128]{3,1,0,2:T(8,128)(2,1)} all-to-all(bf16[7,64,8,128]{3,1,0,2:T(8,128)(2,1)S(1)} %copy_bitcast_fusion.1), channel_id=1, replica_groups=mesh['groups'=2,'tm'=8,'space'=2] {'space'}, dimensions={2} | all-to-all | bytes 1835008 | tf_op jit(solution)/shard_map/all_to_all | solution.py:97
  23.3 5.4 %all_to_all.211 = bf16[7,64,8,128]{3,1,0,2:T(8,128)(2,1)} all-to-all(bf16[7,64,8,128]{3,1,0,2:T(8,128)(2,1)S(1)} %copy_bitcast_fusion), channel_id=1, replica_groups=mesh['groups'=2,'tm'=8,'space'=2] {'space'}, dimensions={2} | all-to-all | bytes 1835008 | tf_op jit(solution)/shard_map/all_to_all | solution.py:99
  28.6 7.3 %all-to-all-start.1 = ((bf16[7,64,8,128]{3,2,0,1:T(8,128)(2,1)}), bf16[7,64,8,128]{3,2,0,1:T(8,128)(2,1)S(1)}, u32[]{:S(2)}, u32[]{:S(2)}) async-start(bf16[7,64,8,128]{3,2,0,1:T(8,128)(2,1)} %copy.152), calls=%async_computation.1 | async-start | bytes 1835008 | tf_op jit(solution)/shard_map/all_to_all | solution.py:79
  37.2 38.5 %all-to-all-done.1 = bf16[7,64,8,128]{3,2,0,1:T(8,128)(2,1)S(1)} async-done(((bf16[7,64,8,128]{3,2,0,1:T(8,128)(2,1)}), bf16[7,64,8,128]{3,2,0,1:T(8,128)(2,1)S(1)}, u32[]{:S(2)}, u32[]{:S(2)}) %all-to-all-start.1) | async-done | bytes 917536 | tf_op jit(solution)/shard_map/all_to_all | solution.py:79
  75.7 3.9 %all-to-all-start = ((bf16[7,64,8,128]{3,2,0,1:T(8,128)(2,1)}), bf16[7,64,8,128]{3,2,0,1:T(8,128)(2,1)S(1)}, u32[]{:S(2)}, u32[]{:S(2)}) async-start(bf16[7,64,8,128]{3,2,0,1:T(8,128)(2,1)} %copy.149), calls=%async_computation | async-start | bytes 1835008 | tf_op jit(solution)/shard_map/all_to_all | solution.py:78
  79.6 1.4 copy.232
  82.1 20.6 %all-to-all-done = bf16[7,64,8,128]{3,2,0,1:T(8,128)(2,1)S(1)} async-done(((bf16[7,64,8,128]{3,2,0,1:T(8,128)(2,1)}), bf16[7,64,8,128]{3,2,0,1:T(8,128)(2,1)S(1)}, u32[]{:S(2)}, u32[]{:S(2)}) %all-to-all-start) | async-done | bytes 917536 | tf_op jit(solution)/shard_map/all_to_all | solution.py:78
  102.7 4.8 %all-to-all-start.3 = ((bf16[7,64,8,128]{3,2,0,1:T(8,128)(2,1)}), bf16[7,64,8,128]{3,2,0,1:T(8,128)(2,1)}, u32[]{:S(2)}, u32[]{:S(2)}) async-start(bf16[7,64,8,128]{3,2,0,1:T(8,128)(2,1)} %copy.160), calls=%async_computation.3 | async-start | bytes 1835008 | tf_op jit(solution)/shard_map/all_to_all | solution.py:80
  107.5 4.4 %copy.220 = bf16[7,2,64,4,128]{2,1,4,3,0:T(2,128)(2,1)S(1)} copy(bf16[7,2,64,4,128]{4,2,0,3,1:T(8,128)(2,1)} %bitcast.28) | data formatting | bytes 1835008 | tf_op jit(solution)/shard_map/reshape | solution.py:104
  111.9 1.6 reshape.142
  113.5 4.3 %copy.219 = bf16[7,2,64,4,128]{2,1,4,3,0:T(2,128)(2,1)S(1)} copy(bf16[7,2,64,4,128]{4,2,0,3,1:T(8,128)(2,1)} %bitcast.148) | data formatting | bytes 1835008 | tf_op jit(solution)/shard_map/reshape | solution.py:104
  117.8 1.6 reshape.141
  119.4 4.3 %copy.218 = bf16[7,2,64,4,128]{2,1,4,3,0:T(2,128)(2,1)S(1)} copy(bf16[7,2,64,4,128]{4,2,0,3,1:T(8,128)(2,1)} %bitcast.147) | data formatting | bytes 1835008 | tf_op jit(solution)/shard_map/reshape | solution.py:104
  123.8 1.6 reshape.140
  125.4 4.9 %fusion.55 = (f32[7,8,128]{2,1,0:T(8,128)S(1)}, f32[7,8,128,128]{2,3,1,0:T(8,128)}) fusion(bf16[7,128,8,64]{1,3,2,0:T(8,128)(2,1)} %reshape.141, bf16[7,128,8,64]{1,3,2,0:T(8,128)(2,1)} %reshape.142), kind=kOutput, calls=%fused_computation.53 | convolution fusion | flops 120193152 | bytes 5533696 | tf_op jit(solution)/shard_map/sub | solution.py:26
  130.5 1.8 reshape.116
  132.3 1.2 copy.151
  133.5 2.6 reshape.114
  136.1 2.3 copy.162
  138.5 3.6 %reshape.120 = bf16[56,128,64]{2,1,0:T(8,128)(2,1)} reshape(bf16[8,7,8,8,128]{4,3,2,1,0:T(8,128)(2,1)} %copy.162) | data formatting | bytes 1835008 | tf_op jit(solution)/shard_map/reshape | solution.py:85
  142.1 3.9 %fusion.25 = f32[128,56,56]{1,2,0:T(8,128)S(1)} fusion(bf16[56,128,64]{2,1,0:T(8,128)(2,1)} %reshape.116, bf16[56,128,64]{2,1,0:T(8,128)(2,1)S(1)} %reshape.114), kind=kOutput, calls=%fused_computation.34 | convolution fusion | flops 51380224 | bytes 3440640 | tf_op jit(solution)/shard_map/sbe,tbe->bst/dot_general | solution.py:17
  146.0 2.9 fusion.54
  148.9 2.9 fusion.47
  153.1 1.2 fusion.44
  154.7 4.5 %all_to_all.212 = bf16[7,64,8,128]{3,1,0,2:T(8,128)(2,1)S(1)} all-to-all(bf16[7,64,8,128]{3,1,0,2:T(8,128)(2,1)S(1)} %copy.183), channel_id=1, replica_groups=mesh['groups'=2,'tm'=8,'space'=2] {'space'}, dimensions={2} | all-to-all | bytes 1835008 | tf_op jit(solution)/shard_map/all_to_all | solution.py:100
  159.2 6.2 %all-to-all-start.2 = ((bf16[7,64,8,128]{3,2,0,1:T(8,128)(2,1)}), bf16[7,64,8,128]{3,2,0,1:T(8,128)(2,1)}, u32[]{:S(2)}, u32[]{:S(2)}) async-start(bf16[7,64,8,128]{3,2,0,1:T(8,128)(2,1)} %copy.157), calls=%async_computation.2 | async-start | bytes 1835008 | tf_op jit(solution)/shard_map/all_to_all | solution.py:81
  165.4 3.6 %copy.221 = bf16[7,2,64,4,128]{2,1,4,3,0:T(2,128)(2,1)} copy(bf16[7,2,64,4,128]{4,2,0,3,1:T(8,128)(2,1)S(1)} %bitcast.149) | data formatting | bytes 1835008 | tf_op jit(solution)/shard_map/reshape | solution.py:104
  169.0 4.4 %reshape.143 = bf16[7,128,8,64]{1,3,2,0:T(8,128)(2,1)} reshape(bf16[7,2,64,4,128]{2,1,4,3,0:T(2,128)(2,1)} %copy.221) | data formatting | bytes 1835008 | tf_op jit(solution)/shard_map/reshape | solution.py:104
  173.4 3.4 %multiply_reduce_fusion = (f32[7,8,128]{2,1,0:T(8,128)S(1)}, f32[7,8,128,128]{2,3,1,0:T(8,128)S(1)}) fusion(f32[7,8,128,128]{2,3,1,0:T(8,128)} %get-tuple-element.11, f32[7,8,128]{2,1,0:T(8,128)S(1)} %get-tuple-element.10, bf16[7,128,8,64]{1,3,2,0:T(8,128)(2,1)} %reshape.143, bf16[7,128,8,64]{1,3,2,0:T(8,128)(2,1)S(1)} %copy-done.19), kind=kOutput, calls=%fused_computation.3 | convolution fusion | flops 120185856 | bytes 9232384 | tf_op jit(solution)/shard_map/asbe,atbe->abst/dot_general | solution.py:35
  179.3 1.8 copy.193
  181.0 3.1 multiply_convert_fusion.4
  184.1 1.8 copy.198
  185.9 3.7 %fusion.35 = bf16[7,8,64,128]{3,2,1,0:T(8,128)(2,1)S(1)} fusion(bf16[7,128,8,64]{1,3,2,0:T(8,128)(2,1)} %reshape.143, f32[7,8,128,128]{2,3,1,0:T(8,128)} %get-tuple-element.11, f32[7,8,128]{2,1,0:T(8,128)S(1)} %get-tuple-element.10), kind=kOutput, calls=%fused_computation.40 | convolution fusion | flops 119734272 | bytes 5533696 | tf_op jit(solution)/shard_map/abst,asbe->atbe/dot_general | solution.py:29
  189.6 1.8 copy.203
  191.4 3.8 %all-to-all-start.11 = ((bf16[7,128,4,128]{3,2,0,1:T(4,128)(2,1)}), bf16[7,128,4,128]{3,2,0,1:T(4,128)(2,1)S(1)}, u32[]{:S(2)}, u32[]{:S(2)}) async-start(bf16[7,128,4,128]{3,2,0,1:T(4,128)(2,1)} %copy.193), calls=%async_computation.11 | async-start | bytes 1835008 | tf_op jit(solution)/shard_map/all_to_all | solution.py:114
  195.1 2.3 copy.159
  197.5 3.6 %reshape.118 = bf16[56,128,64]{2,1,0:T(8,128)(2,1)} reshape(bf16[8,7,8,8,128]{4,3,2,1,0:T(8,128)(2,1)} %copy.159) | data formatting | bytes 1835008 | tf_op jit(solution)/shard_map/reshape | solution.py:85
  201.1 6.0 %multiply_reduce_fusion.1 = (f32[128,56]{1,0:T(8,128)S(1)}, f32[128,56,56]{1,2,0:T(8,128)S(1)}) fusion(f32[128,56,56]{1,2,0:T(8,128)} %get-tuple-element.7, f32[128,56]{1,0:T(8,128)S(1)} %get-tuple-element.6, bf16[56,128,64]{2,1,0:T(8,128)(2,1)} %reshape.120, bf16[56,128,64]{2,1,0:T(8,128)(2,1)} %reshape.118), kind=kOutput, calls=%fused_computation.8 | convolution fusion | flops 52577280 | bytes 5103616 | tf_op jit(solution)/shard_map/sbe,tbe->bst/dot_general | solution.py:35
  208.6 2.3 fusion.29
  211.0 1.7 copy.167
  212.6 3.6 %reshape.121 = bf16[56,8,8,128]{3,2,1,0:T(8,128)(2,1)} reshape(bf16[56,128,64]{2,1,0:T(8,128)(2,1)} %copy.167) | data formatting | bytes 1835008 | tf_op jit(solution)/shard_map/reshape | solution.py:88
  216.3 6.6 %all_to_all.213 = bf16[7,128,4,128]{3,2,0,1:T(4,128)(2,1)} all-to-all(bf16[7,128,4,128]{3,2,0,1:T(4,128)(2,1)} %copy.198), channel_id=1, replica_groups=mesh['groups'=2,'tm'=8,'space'=2] {'space'}, dimensions={1} | all-to-all | bytes 1835008 | tf_op jit(solution)/shard_map/all_to_all | solution.py:117
  222.9 5.2 %all_to_all.214 = bf16[7,128,4,128]{3,2,0,1:T(4,128)(2,1)} all-to-all(bf16[7,128,4,128]{3,2,0,1:T(4,128)(2,1)S(1)} %copy-done.10), channel_id=1, replica_groups=mesh['groups'=2,'tm'=8,'space'=2] {'space'}, dimensions={1} | all-to-all | bytes 1835008 | tf_op jit(solution)/shard_map/all_to_all | solution.py:120
  228.1 6.0 %all-to-all-start.4 = ((bf16[56,8,8,128]{3,2,1,0:T(8,128)(2,1)}), bf16[56,8,8,128]{3,2,1,0:T(8,128)(2,1)}, u32[]{:S(2)}, u32[]{:S(2)}) async-start(bf16[56,8,8,128]{3,2,1,0:T(8,128)(2,1)} %reshape.121), calls=%async_computation.4 | async-start | bytes 1835008 | tf_op jit(solution)/shard_map/all_to_all | solution.py:93
  234.1 3.8 %fusion.32 = bf16[56,128,64]{2,0,1:T(8,128)(2,1)S(1)} fusion(bf16[128,56,56]{1,2,0:T(8,128)(2,1)} %copy-done.4, bf16[56,128,64]{2,1,0:T(8,128)(2,1)S(1)} %reshape.114), kind=kOutput, calls=%fused_computation.39 | convolution fusion | flops 52297728 | bytes 2637824 | tf_op jit(solution)/shard_map/bst,sbe->tbe/dot_general | solution.py:49
  238.3 1.6 reshape.123
  239.9 17.5 %all-to-all-done.4 = bf16[56,8,8,128]{3,2,1,0:T(8,128)(2,1)} async-done(((bf16[56,8,8,128]{3,2,1,0:T(8,128)(2,1)}), bf16[56,8,8,128]{3,2,1,0:T(8,128)(2,1)}, u32[]{:S(2)}, u32[]{:S(2)}) %all-to-all-start.4) | async-done | bytes 917536 | tf_op jit(solution)/shard_map/all_to_all | solution.py:93
  257.5 4.5 %all-to-all-start.5 = ((bf16[56,8,8,128]{3,2,1,0:T(8,128)(2,1)}), bf16[56,8,8,128]{3,2,1,0:T(8,128)(2,1)}, u32[]{:S(2)}, u32[]{:S(2)}) async-start(bf16[56,8,8,128]{3,2,1,0:T(8,128)(2,1)} %reshape.123), calls=%async_computation.5 | async-start | bytes 1835008 | tf_op jit(solution)/shard_map/all_to_all | solution.py:94
  262.0 4.3 %convert_bitcast_fusion = bf16[56,128,64]{2,0,1:T(8,128)(2,1)S(1)} fusion(bf16[56,128,64]{2,1,0:T(8,128)(2,1)} %reshape.118, f32[128,56,56]{1,2,0:T(8,128)} %get-tuple-element.7, f32[128,56]{1,0:T(8,128)S(1)} %get-tuple-element.6), kind=kOutput, calls=%fused_computation.26 | convolution fusion | flops 52641792 | bytes 3469312 | tf_op jit(solution)/shard_map/bst,sbe->tbe/dot_general | solution.py:29
  266.7 1.6 reshape.125
  268.3 16.5 %all-to-all-done.5 = bf16[56,8,8,128]{3,2,1,0:T(8,128)(2,1)} async-done(((bf16[56,8,8,128]{3,2,1,0:T(8,128)(2,1)}), bf16[56,8,8,128]{3,2,1,0:T(8,128)(2,1)}, u32[]{:S(2)}, u32[]{:S(2)}) %all-to-all-start.5) | async-done | bytes 917536 | tf_op jit(solution)/shard_map/all_to_all | solution.py:94
  284.8 3.6 %all-to-all-start.6 = ((bf16[56,8,8,128]{3,2,1,0:T(8,128)(2,1)}), bf16[56,8,8,128]{3,2,1,0:T(8,128)(2,1)S(1)}, u32[]{:S(2)}, u32[]{:S(2)}) async-start(bf16[56,8,8,128]{3,2,1,0:T(8,128)(2,1)} %reshape.125), calls=%async_computation.6 | async-start | bytes 1835008 | tf_op jit(solution)/shard_map/all_to_all | solution.py:95
  289.3 1.6 reshape.135
  291.9 1.6 reshape.137
  294.4 1.6 reshape.139
  295.9 1.2 copy.168
  297.2 1.3 reshape.122
  298.5 1.2 copy.171
  299.8 1.3 reshape.124
  301.1 10.3 %all-to-all-done.6 = bf16[56,8,8,128]{3,2,1,0:T(8,128)(2,1)S(1)} async-done(((bf16[56,8,8,128]{3,2,1,0:T(8,128)(2,1)}), bf16[56,8,8,128]{3,2,1,0:T(8,128)(2,1)S(1)}, u32[]{:S(2)}, u32[]{:S(2)}) %all-to-all-start.6) | async-done | bytes 917536 | tf_op jit(solution)/shard_map/all_to_all | solution.py:95
  311.5 1.3 reshape.126
  (73 shorter events, 14.3 us)
Async XLA Ops:
  7.2 141.7 %copy-start = (bf16[7,64,1024]{2,1,0:T(8,128)(2,1)S(1)}, bf16[7,64,1024]{2,1,0:T(8,128)(2,1)}, u32[]{:S(2)}) copy-start(bf16[7,64,1024]{2,1,0:T(8,128)(2,1)} %param.9) | copy-start | bytes 2752516
  7.2 141.7 %all-gather.2.cloned.1.call-start = ((), (), s32[]{:S(2)}) async-start(), calls=%async_computation.14 | async-start | bytes 4456448 | tf_op jit(solution)/shard_map/all_gather | solution.py:62
  9.0 6.8 %copy-start.15 = (bf16[7,64,1024]{2,1,0:T(8,128)(2,1)S(1)}, bf16[7,64,1024]{2,1,0:T(8,128)(2,1)}, u32[]{:S(2)}) copy-start(bf16[7,64,1024]{2,1,0:T(8,128)(2,1)} %param.11) | copy-start | bytes 2752516
  11.5 6.5 %all-to-all-start.8 = ((bf16[7,64,8,128]{3,1,0,2:T(8,128)(2,1)}), bf16[7,64,8,128]{3,1,0,2:T(8,128)(2,1)}, u32[]{:S(2)}, u32[]{:S(2)}) async-start(bf16[7,64,8,128]{3,1,0,2:T(8,128)(2,1)} %copy_bitcast_fusion.2), calls=%async_computation.8 | async-start | bytes 1835008 | tf_op jit(solution)/shard_map/all_to_all | solution.py:98
  15.9 1.3 copy-start.16
  16.1 1.6 copy-start.17
  23.2 12.6 %copy-start.18 = (bf16[7,64,1024]{2,1,0:T(8,128)(2,1)S(1)}, bf16[7,64,1024]{2,1,0:T(8,128)(2,1)}, u32[]{:S(2)}) copy-start(bf16[7,64,1024]{2,1,0:T(8,128)(2,1)} %param.10) | copy-start | bytes 2752516
  28.6 47.1 %all-to-all-start.1 = ((bf16[7,64,8,128]{3,2,0,1:T(8,128)(2,1)}), bf16[7,64,8,128]{3,2,0,1:T(8,128)(2,1)S(1)}, u32[]{:S(2)}, u32[]{:S(2)}) async-start(bf16[7,64,8,128]{3,2,0,1:T(8,128)(2,1)} %copy.152), calls=%async_computation.1 | async-start | bytes 1835008 | tf_op jit(solution)/shard_map/all_to_all | solution.py:79
  75.7 5.3 %copy-start.8 = (bf16[7,64,8,128]{3,2,0,1:T(8,128)(2,1)}, bf16[7,64,8,128]{3,2,0,1:T(8,128)(2,1)S(1)}, u32[]{:S(2)}) copy-start(bf16[7,64,8,128]{3,2,0,1:T(8,128)(2,1)S(1)} %all-to-all-done.1) | copy-start | bytes 2752516
  75.7 27.1 %all-to-all-start = ((bf16[7,64,8,128]{3,2,0,1:T(8,128)(2,1)}), bf16[7,64,8,128]{3,2,0,1:T(8,128)(2,1)S(1)}, u32[]{:S(2)}, u32[]{:S(2)}) async-start(bf16[7,64,8,128]{3,2,0,1:T(8,128)(2,1)} %copy.149), calls=%async_computation | async-start | bytes 1835008 | tf_op jit(solution)/shard_map/all_to_all | solution.py:78
  102.7 4.8 %copy-start.11 = (bf16[7,64,8,128]{3,2,0,1:T(8,128)(2,1)}, bf16[7,64,8,128]{3,2,0,1:T(8,128)(2,1)S(1)}, u32[]{:S(2)}) copy-start(bf16[7,64,8,128]{3,2,0,1:T(8,128)(2,1)S(1)} %all-to-all-done) | copy-start | bytes 2752516
  102.7 33.4 %all-to-all-start.3 = ((bf16[7,64,8,128]{3,2,0,1:T(8,128)(2,1)}), bf16[7,64,8,128]{3,2,0,1:T(8,128)(2,1)}, u32[]{:S(2)}, u32[]{:S(2)}) async-start(bf16[7,64,8,128]{3,2,0,1:T(8,128)(2,1)} %copy.160), calls=%async_computation.3 | async-start | bytes 1835008 | tf_op jit(solution)/shard_map/all_to_all | solution.py:80
  125.4 4.9 %copy-start.9 = (bf16[7,64,8,128]{3,2,0,1:T(8,128)(2,1)S(1)}, bf16[7,64,8,128]{3,2,0,1:T(8,128)(2,1)}, u32[]{:S(2)}) copy-start(bf16[7,64,8,128]{3,2,0,1:T(8,128)(2,1)} %copy-done.8) | copy-start | bytes 2752516
  130.5 1.8 copy-start.12
  148.9 4.2 %copy-start.20 = (bf16[1024,2048]{1,0:T(8,128)(2,1)S(1)}, bf16[1024,2048]{1,0:T(8,128)(2,1)}, u32[]{:S(2)}) copy-start(bf16[1024,2048]{1,0:T(8,128)(2,1)} %all-gather.2.cloned.1.call-done) | copy-start | bytes 12582916
  159.2 32.1 %all-to-all-start.2 = ((bf16[7,64,8,128]{3,2,0,1:T(8,128)(2,1)}), bf16[7,64,8,128]{3,2,0,1:T(8,128)(2,1)}, u32[]{:S(2)}, u32[]{:S(2)}) async-start(bf16[7,64,8,128]{3,2,0,1:T(8,128)(2,1)} %copy.157), calls=%async_computation.2 | async-start | bytes 1835008 | tf_op jit(solution)/shard_map/all_to_all | solution.py:81
  169.0 4.4 %copy-start.19 = (bf16[7,128,8,64]{1,3,2,0:T(8,128)(2,1)S(1)}, bf16[7,128,8,64]{1,3,2,0:T(8,128)(2,1)}, u32[]{:S(2)}) copy-start(bf16[7,128,8,64]{1,3,2,0:T(8,128)(2,1)} %reshape.140) | copy-start | bytes 2752516
  173.4 3.4 %copy-start.13 = (f32[7,8,128,128]{2,3,1,0:T(8,128)S(1)}, f32[7,8,128,128]{2,3,1,0:T(8,128)}, u32[]{:S(2)}) copy-start(f32[7,8,128,128]{2,3,1,0:T(8,128)} %get-tuple-element.11) | copy-start | bytes 11010052
  176.8 1.2 copy-start.14
  178.0 1.3 copy-start.3
  191.4 24.9 %all-to-all-start.11 = ((bf16[7,128,4,128]{3,2,0,1:T(4,128)(2,1)}), bf16[7,128,4,128]{3,2,0,1:T(4,128)(2,1)S(1)}, u32[]{:S(2)}, u32[]{:S(2)}) async-start(bf16[7,128,4,128]{3,2,0,1:T(4,128)(2,1)} %copy.193), calls=%async_computation.11 | async-start | bytes 1835008 | tf_op jit(solution)/shard_map/all_to_all | solution.py:114
  201.1 6.0 %copy-start.5 = (f32[128,56,56]{1,2,0:T(8,128)S(1)}, f32[128,56,56]{1,2,0:T(8,128)}, u32[]{:S(2)}) copy-start(f32[128,56,56]{1,2,0:T(8,128)} %get-tuple-element.7) | copy-start | bytes 4816900
  207.1 1.5 copy-start.2
  208.6 2.3 copy-start.4
  216.3 6.6 %copy-start.10 = (bf16[7,128,4,128]{3,2,0,1:T(4,128)(2,1)S(1)}, bf16[7,128,4,128]{3,2,0,1:T(4,128)(2,1)}, u32[]{:S(2)}) copy-start(bf16[7,128,4,128]{3,2,0,1:T(4,128)(2,1)} %copy.203) | copy-start | bytes 2752516
  228.1 29.4 %all-to-all-start.4 = ((bf16[56,8,8,128]{3,2,1,0:T(8,128)(2,1)}), bf16[56,8,8,128]{3,2,1,0:T(8,128)(2,1)}, u32[]{:S(2)}, u32[]{:S(2)}) async-start(bf16[56,8,8,128]{3,2,1,0:T(8,128)(2,1)} %reshape.121), calls=%async_computation.4 | async-start | bytes 1835008 | tf_op jit(solution)/shard_map/all_to_all | solution.py:93
  257.5 27.3 %all-to-all-start.5 = ((bf16[56,8,8,128]{3,2,1,0:T(8,128)(2,1)}), bf16[56,8,8,128]{3,2,1,0:T(8,128)(2,1)}, u32[]{:S(2)}, u32[]{:S(2)}) async-start(bf16[56,8,8,128]{3,2,1,0:T(8,128)(2,1)} %reshape.123), calls=%async_computation.5 | async-start | bytes 1835008 | tf_op jit(solution)/shard_map/all_to_all | solution.py:94
  284.8 26.6 %all-to-all-start.6 = ((bf16[56,8,8,128]{3,2,1,0:T(8,128)(2,1)}), bf16[56,8,8,128]{3,2,1,0:T(8,128)(2,1)S(1)}, u32[]{:S(2)}, u32[]{:S(2)}) async-start(bf16[56,8,8,128]{3,2,1,0:T(8,128)(2,1)} %reshape.125), calls=%async_computation.6 | async-start | bytes 1835008 | tf_op jit(solution)/shard_map/all_to_all | solution.py:95
  288.6 2.3 copy-start.7
  291.1 2.3 copy-start.6
  311.4 1.4 copy-start.1
Sparse Core Ops, SparseCore 0:
  10.2 67.5 all-gather.1
where the time goes:
time: 324 us; the launch traced here: 320 us
  waiting for transfers between devices  104 us (32%)
  local copies, waits for them, and re-layouts  83.8 us (26%)
  starting transfers between devices  44.4 us (14%)
  matrix products  39.9 us (12%)
  blocking collectives  26.9 us (8%)
  between operations  14.7 us (5%)
  other arithmetic  6.58 us (2%)
    all_to_all x1, waiting for transfers between devices, per_device(): lax.all_to_all(time_in[1], 'tm', split_axis=1, concat_axis=0, tiled=True)  38.5 us
    reshape x8, local copies, waits for them, and re-layouts, to_heads(): tensor.reshape(frame_count, all_patches, space_pair_count * 2, space_pair...  25.8 us
    all_to_all x1, waiting for transfers between devices, per_device(): lax.all_to_all(time_in[0], 'tm', split_axis=1, concat_axis=0, tiled=True)  20.6 us
    all_to_all x1, waiting for transfers between devices, per_device(): lax.all_to_all(to_pairs(results[0]), 'tm', split_axis=0, concat_axis=1, t...  17.5 us
    all_to_all x1, waiting for transfers between devices, per_device(): lax.all_to_all(to_pairs(results[1]), 'tm', split_axis=0, concat_axis=1, t...  16.5 us
    reshape x6, local copies, waits for them, and re-layouts, to_pairs(): tensor.astype(jnp.bfloat16)  12.1 us
    reshape x4, local copies, waits for them, and re-layouts, to_heads(): tensor.reshape(all_frames, patch_count * pair_count * 2, pair_width // 2)  11.7 us
    all_to_all x1, waiting for transfers between devices, per_device(): lax.all_to_all(to_pairs(results[2]), 'tm', split_axis=0, concat_axis=1, t...  10.3 us
  transfers between devices with their start and end apart: 10, of which 5 were waited for; matrix products, arithmetic and copies ran while one was open for 37% of the time, Pallas kernels for 0%

commit v1 on v0

v1 whole, which is shorter than its diff:
```python
import functools
import math

import jax
import jax.numpy as jnp
from jax import lax
from jax.experimental import pallas as pl
from jax.experimental.pallas import tpu as pltpu
from jax.sharding import PartitionSpec as P

HEAD_DIM = 64
PAIR = 2 * HEAD_DIM
F32 = jnp.float32
BF16 = jnp.bfloat16
SCALE = 1.0 / math.sqrt(HEAD_DIM)


def dot(left, right, contract):
    return lax.dot_general(left, right, (contract, ((), ())), preferred_element_type=F32)


def pair_back(query, keys, values, out_grad):
    rows = query.shape[0]
    lane = lax.broadcasted_iota(jnp.int32, (rows, PAIR), 1)
    first = lane < HEAD_DIM

    def stacked(tensor):
        zero = jnp.zeros_like(tensor)
        both = [jnp.where(first, tensor, zero), jnp.where(first, zero, tensor)]
        return jnp.concatenate(both, axis=0).astype(BF16)

    query2 = stacked(query)
    grad2 = stacked(out_grad)
    keys = keys.astype(BF16)
    values = values.astype(BF16)
    scores = dot(keys, query2, ((1,), (1,))) * SCALE
    expo = jnp.exp(scores - jnp.max(scores, axis=0, keepdims=True))
    probs = expo * (1.0 / jnp.sum(expo, axis=0, keepdims=True))
    dprob = dot(values, grad2, ((1,), (1,)))
    delta = jnp.sum(probs * dprob, axis=0, keepdims=True)
    dscore = (probs * (dprob - delta)).astype(BF16)
    grad_values = dot(probs.astype(BF16), grad2, ((1,), (0,)))
    grad_keys = dot(dscore, query2, ((1,), (0,))) * SCALE
    both = dot(dscore, keys, ((0,), (0,))) * SCALE
    grad_query = jnp.where(first, both[:rows], both[rows:])
    return grad_query, grad_keys, grad_values


def time_kernel(qkv_ref, grad_ref, out_ref, *scratch):
    sources, frames, patches, lanes = grad_ref.shape
    total = sources * frames
    held, results = scratch[:4], scratch[4:]
    for pair in range(lanes // PAIR):
        columns = slice(pair * PAIR, (pair + 1) * PAIR)
        for index in range(4):
            part = qkv_ref[:, index, :, :, columns] if index < 3 else grad_ref[:, :, :, columns]
            held[index][pair] = part.astype(F32).reshape(total * patches, PAIR)
        for patch in range(patches):
            rows = pl.ds(patch, total, stride=patches)
            done = pair_back(*[ref[pair, rows, :] for ref in held])
            for ref, value in zip(results, done):
                ref[pair, rows, :] = value
        for index in range(3):
            value = results[index][pair].reshape(sources, frames, patches, PAIR)
            out_ref[:, index, :, :, columns] = value.astype(BF16)


def time_kernel_wide(qkv_ref, grad_ref, out_ref):
    done = pair_back(*[qkv_ref[index, 0].astype(F32) for index in range(3)], grad_ref[0].astype(F32))
    for index in range(3):
        out_ref[index, 0] = done[index].astype(BF16)


def time_attention(qkv, grad):
    sources, _, frames, patches, width = qkv.shape
    total = sources * frames
    if patches % 8 == 0:
        lanes = 2 * PAIR
        return pl.pallas_call(
            time_kernel,
            grid=(width // lanes,),
            in_specs=[
                pl.BlockSpec((sources, 3, frames, patches, lanes), lambda i: (0, 0, 0, 0, i)),
                pl.BlockSpec((sources, frames, patches, lanes), lambda i: (0, 0, 0, i)),
            ],
            out_specs=pl.BlockSpec((sources, 3, frames, patches, lanes), lambda i: (0, 0, 0, 0, i)),
            out_shape=jax.ShapeDtypeStruct(qkv.shape, BF16),
            scratch_shapes=[pltpu.VMEM((lanes // PAIR, total * patches, PAIR), F32)] * 7,
            compiler_params=pltpu.CompilerParams(vmem_limit_bytes=40 * 2**20),
            name="time_attention",
        )(qkv, grad)
    qkv = qkv.transpose(1, 3, 0, 2, 4).reshape(3, patches, total, width)
    grad = grad.transpose(2, 0, 1, 3).reshape(patches, total, width)
    done = pl.pallas_call(
        time_kernel_wide,
        grid=(patches, width // PAIR),
        in_specs=[
            pl.BlockSpec((3, 1, total, PAIR), lambda p, i: (0, p, 0, i)),
            pl.BlockSpec((1, total, PAIR), lambda p, i: (p, 0, i)),
        ],
        out_specs=pl.BlockSpec((3, 1, total, PAIR), lambda p, i: (0, p, 0, i)),
        out_shape=jax.ShapeDtypeStruct(qkv.shape, BF16),
        compiler_params=pltpu.CompilerParams(vmem_limit_bytes=40 * 2**20),
        name="time_attention_wide",
    )(qkv, grad)
    done = done.reshape(3, patches, sources, frames, width)
    return done.transpose(2, 0, 3, 1, 4)


def space_kernel(core_ref, q_ref, k_ref, v_ref, g_ref, qkv_ref, grad_ref, *outs):
    own_outs, send_ref = outs[:3], outs[3]
    rows, lanes = q_ref.shape[1:]
    own = (q_ref, k_ref, v_ref, g_ref)
    for pair in range(lanes // PAIR):
        columns = slice(pair * PAIR, (pair + 1) * PAIR)
        operands = []
        for index in range(4):
            near = own[index][0, :, columns].astype(F32)
            far = (qkv_ref[index, 0] if index < 3 else grad_ref[0])[:, columns].astype(F32)
            operands.append(jnp.concatenate([near, far], axis=0))
        done = pair_back(*operands)
        for index in range(3):
            value = done[index].astype(BF16)
            own_outs[index][0, :, columns] = value[:rows]
            send_ref[index, 0, :, columns] = value[rows:]


def space_attention(core, query, keys, values, grad, far_qkv, far_grad):
    frames, rows, width = query.shape
    half = width // 2
    mine = pl.BlockSpec((1, rows, half), lambda f, core_ref: (f, 0, core_ref[0]))
    far = pl.BlockSpec((1, rows, half), lambda f, core_ref: (f, 0, 0))
    far3 = pl.BlockSpec((3, 1, rows, half), lambda f, core_ref: (0, f, 0, 0))
    own_shape = jax.ShapeDtypeStruct((frames, rows, half), BF16)
    return pl.pallas_call(
        space_kernel,
        grid_spec=pltpu.PrefetchScalarGridSpec(
            num_scalar_prefetch=1,
            grid=(frames,),
            in_specs=[mine] * 4 + [far3, far],
            out_specs=[far] * 3 + [far3],
        ),
        out_shape=[own_shape] * 3 + [jax.ShapeDtypeStruct((3, frames, rows, half), BF16)],
        compiler_params=pltpu.CompilerParams(vmem_limit_bytes=40 * 2**20),
        name="space_attention",
    )(core.reshape(1), query, keys, values, grad, far_qkv, far_grad)


def per_device(sizes, grad_out, time_q, time_k, time_v, space_q, space_k, space_v, time_wo, space_wo):
    frames, rows, width = grad_out.shape
    groups, tm, space = sizes
    patches = rows // tm
    half = width // 2
    core = lax.axis_index("space")
    swap = [(0, 1), (1, 0)]

    def to_patches(tensor):
        split = tensor.reshape(tensor.shape[:-2] + (tm, patches, width))
        return jnp.moveaxis(split, -3, 0)

    def exchanged(tensor):
        return lax.all_to_all(tensor, "tm", split_axis=0, concat_axis=0, tiled=True)

    time_qkv = exchanged(to_patches(jnp.stack([time_q, time_k, time_v])))

    both_wo = jnp.concatenate([time_wo, space_wo], axis=1)
    share = both_wo.shape[0] // groups
    if share * groups == both_wo.shape[0]:
        piece = lax.dynamic_slice_in_dim(both_wo, lax.axis_index("groups") * share, share, 0)
        whole = lax.all_gather(piece, ("tm", "space", "groups"), axis=0, tiled=True)
    else:
        whole = lax.all_gather(both_wo, ("tm", "space"), axis=0, tiled=True)

    def other_half(tensor):
        return lax.dynamic_slice_in_dim(tensor, (1 - core) * half, half, tensor.ndim - 1)

    far_qkv = lax.ppermute(jnp.stack([other_half(t) for t in (space_q, space_k, space_v)]), "space", swap)

    tokens = grad_out.reshape(frames * rows, width)
    time_grad = jnp.einsum("td,cd->tc", tokens, whole[:, :width], preferred_element_type=F32)
    time_grad = exchanged(to_patches(time_grad.astype(BF16).reshape(frames, rows, width)))
    space_grad = jnp.einsum("td,cd->tc", tokens, whole[:, width:], preferred_element_type=F32)
    space_grad = space_grad.astype(BF16).reshape(frames, rows, width)
    far_grad = lax.ppermute(other_half(space_grad), "space", swap)

    *own, send = space_attention(core, space_q, space_k, space_v, space_grad, far_qkv, far_grad)
    far = lax.ppermute(send, "space", swap)
    space_out = [
        jnp.where(
            core == 0,
            jnp.concatenate([own[index], far[index]], axis=-1),
            jnp.concatenate([far[index], own[index]], axis=-1),
        )
        for index in range(3)
    ]

    back = exchanged(time_attention(time_qkv, time_grad))
    time_out = [jnp.moveaxis(back[:, index], 0, 1).reshape(frames, rows, width) for index in range(3)]
    return (*time_out, *space_out)


def solution(mesh):
    tokens = P(("groups", "tm"), "space", None)
    weights = P(("tm", "space"), None)
    sizes = tuple(mesh.shape[name] for name in ("groups", "tm", "space"))
    return jax.shard_map(
        functools.partial(per_device, sizes),
        mesh=mesh,
        in_specs=(tokens,) * 7 + (weights,) * 2,
        out_specs=(tokens,) * 6,
        check_vma=False,
    )
```

time: 324 us -> 240 us (0.74); the launches traced: 320 us -> 239 us
  local copies, waits for them, and re-layouts: 83.8 us -> 11.1 us
  matrix products: 39.9 us -> 3.89 us
  starting transfers between devices: 44.4 us -> 12.1 us
  waiting for transfers between devices: 104 us -> 134 us
  Pallas kernels: 0 us -> 27 us
    all_gather x1, waiting for transfers between devices: 0.01 us -> 93.6 us  [per_device(): whole = lax.all_gather(piece, ('tm', 'space', 'groups'), axis=0, tiled=True)]
    all_to_all x9 -> x2, waiting for transfers between devices: 104 us -> 35.7 us  [exchanged(): return lax.all_to_all(tensor, 'tm', split_axis=0, concat_axis=0, tiled=True)]
    reshape x30 -> x1, local copies, waits for them, and re-layouts: 64.5 us -> 1.4 us  [per_device(): jnp.moveaxis(back[:, index], 0, 1).reshape(frames, rows, width)]
    all_to_all x9 -> x2, starting transfers between devices: 44.3 us -> 11.8 us  [exchanged(): return lax.all_to_all(tensor, 'tm', split_axis=0, concat_axis=0, tiled=True)]
    dot_general x11 -> x2, matrix products: 35.1 us -> 3.89 us  [the longest x1 2.74 us: per_device(): jnp.einsum('td,cd->tc', tokens, whole[:, :width], preferred_element_type=...]
    pallas_call x0 -> x2, Pallas kernels: none -> 27 us  [the longest x1 16.7 us: time_attention(): pl.pallas_call(time_kernel, grid=(width // lanes,), in_specs=[pl.BlockSpe...]
    all_to_all x13 -> x0, local copies, waits for them, and re-layouts: 11.4 us -> none  [the longest x1 2.35 us: per_device(): lax.all_to_all(time_in[2], 'tm', split_axis=1, concat_axis=0, tiled=True)]
    ppermute x0 -> x3, waiting for transfers between devices: none -> 5.13 us  [the longest x1 3.33 us: per_device(): far = lax.ppermute(send, 'space', swap)]
  transfers between devices with their start and end apart: 10 -> 6, of which waited for: 5 -> 5; matrix products, arithmetic and copies ran while one was open for 37% -> 6% of each run, Pallas kernels for 0% -> 4%
where the time goes in v1:
time: 240 us; the launch traced here: 239 us
  waiting for transfers between devices  134 us (56%)
  blocking collectives  27.6 us (12%)
  Pallas kernels  27 us (11%)
  between operations  14.2 us (6%)
  starting transfers between devices  12.1 us (5%)
  local copies, waits for them, and re-layouts  11.1 us (5%)
  other arithmetic  8.93 us (4%)
  matrix products  3.89 us (2%)
    all_gather x1, waiting for transfers between devices, per_device(): whole = lax.all_gather(piece, ('tm', 'space', 'groups'), axis=0, tiled=True)  93.6 us
    all_to_all x2, waiting for transfers between devices, exchanged(): return lax.all_to_all(tensor, 'tm', split_axis=0, concat_axis=0, tiled=True)  35.7 us
    all_to_all x1, blocking collectives, exchanged(): return lax.all_to_all(tensor, 'tm', split_axis=0, concat_axis=0, tiled=True)  27.6 us
    pallas_call x1, Pallas kernels, time_attention(): pl.pallas_call(time_kernel, grid=(width // lanes,), in_specs=[pl.BlockSpe...  16.7 us
    all_to_all x2, starting transfers between devices, exchanged(): return lax.all_to_all(tensor, 'tm', split_axis=0, concat_axis=0, tiled=True)  11.8 us
    pallas_call x1, Pallas kernels, space_attention(): pl.pallas_call(space_kernel, grid_spec=pltpu.PrefetchScalarGridSpec(num_s...  10.3 us
  transfers between devices with their start and end apart: 6, of which 5 were waited for; matrix products, arithmetic and copies ran while one was open for 6% of the time, Pallas kernels for 4%

profile of v1, /device:TPU:0, one launch (start us, length us, event | category | flops | bytes accessed | tf_op | source)
XLA Modules:
  0.0 239.3 jit_solution(6835652386088413032)
XLA Ops:
  7.2 0.0 copy-start
  7.2 0.0 all-gather.2.cloned.1.call-start
  7.2 1.6 fusion.10
  8.8 0.0 all-gather.2.cloned.1.call-update
  8.9 3.6 %copy_bitcast_fusion = bf16[8,3,7,8,1024]{4,3,2,1,0:T(8,128)(2,1)} fusion(bf16[1,7,8,8,1024]{4,3,2,1,0:T(8,128)(2,1)} %bitcast.56, bf16[1,7,8,8,1024]{4,3,2,1,0:T(8,128)(2,1)} %bitcast.57, bf16[1,7,8,8,1024]{4,3,2,1,0:T(8,128)(2,1)} %bitcast.58), kind=kLoop, calls=%fused_computation.1 | loop fusion | flops 2752512 | bytes 5505024 | tf_op jit(solution)/shard_map/transpose | solution.py:159
  12.5 7.3 %all-to-all-start = ((bf16[8,3,7,8,1024]{4,3,2,1,0:T(8,128)(2,1)}), bf16[8,3,7,8,1024]{4,3,2,1,0:T(8,128)(2,1)}, u32[]{:S(2)}, u32[]{:S(2)}) async-start(bf16[8,3,7,8,1024]{4,3,2,1,0:T(8,128)(2,1)} %copy_bitcast_fusion), calls=%async_computation | async-start | bytes 5505024 | tf_op jit(solution)/shard_map/all_to_all | solution.py:162
  19.8 93.6 %all-gather.2.cloned.1.call-done = bf16[1024,2048]{1,0:T(8,128)(2,1)} async-done(((bf16[32,2048]{1,0:T(8,128)(2,1)}), bf16[1024,2048]{1,0:T(8,128)(2,1)}) %all-gather.2.cloned.1.call-update) | async-done | bytes 4194320 | tf_op jit(solution)/shard_map/all_gather | solution.py:170
  113.3 0.0 copy-done
  113.3 2.7 %fusion.4 = bf16[1024,448]{0,1:T(8,128)(2,1)S(1)} fusion(bf16[448,1024]{1,0:T(8,128)(2,1)S(1)} %bitcast.49, bf16[1024,2048]{1,0:T(8,128)(2,1)} %all-gather.2.cloned.1.call-done), kind=kOutput, calls=%fused_computation.6 | convolution fusion | flops 939982848 | bytes 3932160 | tf_op jit(solution)/shard_map/td,cd->tc/dot_general | solution.py:180
  116.1 0.1 copy.29
  116.2 0.0 all-to-all-done.qkv_ref
  116.2 27.6 %all_to_all.15.grad_ref = bf16[8,7,8,1024]{3,2,1,0:T(8,128)(2,1)S(1)} all-to-all(bf16[8,7,8,1024]{3,2,1,0:T(8,128)(2,1)S(1)} %bitcast.53), channel_id=1, replica_groups=mesh['groups'=2,'tm'=8,'space'=2] {'tm'}, dimensions={0} | all-to-all | bytes 1835008 | tf_op jit(solution)/shard_map/all_to_all | solution.py:162
  143.7 16.7 %time_attention.1 = bf16[8,3,7,8,1024]{4,3,2,1,0:T(8,128)(2,1)S(1)} custom-call(bf16[8,3,7,8,1024]{4,3,2,1,0:T(8,128)(2,1)} %all-to-all-done.qkv_ref, bf16[8,7,8,1024]{3,2,1,0:T(8,128)(2,1)S(1)} %all_to_all.15.grad_ref), custom_call_target="tpu_custom_call" | custom-call | tf_op jit(solution)/shard_map/time_attention/pallas_call | solution.py:79
  160.5 0.0 copy-start.1
  160.5 1.6 copy-done.1
  162.0 0.0 copy-start.2
  162.0 0.0 copy-start.3
  162.0 4.5 %all-to-all-start.2 = ((bf16[8,3,7,8,1024]{4,3,2,1,0:T(8,128)(2,1)}), bf16[8,3,7,8,1024]{4,3,2,1,0:T(8,128)(2,1)}, u32[]{:S(2)}, u32[]{:S(2)}) async-start(bf16[8,3,7,8,1024]{4,3,2,1,0:T(8,128)(2,1)} %copy-done.1), calls=%async_computation.2 | async-start | bytes 5505024 | tf_op jit(solution)/shard_map/all_to_all | solution.py:162
  166.6 0.0 copy-done.2
  166.6 0.0 copy-done.3
  166.7 0.0 copy-start.9
  166.7 1.3 dynamic-slice_bitcast_fusion
  167.9 0.2 pad_maximum_fusion.1
  168.1 0.0 copy-start.4
  168.1 0.1 collective-permute-start
  168.2 0.8 copy-done.9
  169.0 1.1 fusion.7
  170.2 0.1 collective-permute-start.1
  170.3 1.0 collective-permute-done.qkv_ref
  171.3 0.8 collective-permute-done.1.grad_ref
  172.1 0.0 copy-done.4
  172.1 10.3 %space_attention.1 = (bf16[7,64,512]{2,1,0:T(8,128)(2,1)S(1)}, bf16[7,64,512]{2,1,0:T(8,128)(2,1)S(1)}, bf16[7,64,512]{2,1,0:T(8,128)(2,1)S(1)}, bf16[3,7,64,512]{3,2,1,0:T(8,128)(2,1)}) custom-call(s32[1]{0:T(128)} %bitcast.17.core_ref, bf16[7,64,1024]{2,1,0:T(8,128)(2,1)S(1)} %copy-done.2, bf16[7,64,1024]{2,1,0:T(8,128)(2,1)S(1)} %copy-done.3, ...), custom_call_target="tpu_custom_call" | custom-call | tf_op jit(solution)/shard_map/space_attention/pallas_call | solution.py:135
  182.4 0.0 copy-start.5
  182.4 0.8 copy-done.5
  183.2 0.0 copy-start.7
  183.2 0.8 copy-done.7
  183.9 0.0 copy-start.8
  183.9 0.1 collective-permute-start.2
  184.1 0.0 copy-start.6
  184.1 3.3 %collective-permute-done.2 = bf16[3,7,64,512]{3,2,1,0:T(8,128)(2,1)} collective-permute-done((bf16[3,7,64,512]{3,2,1,0:T(8,128)(2,1)}, bf16[3,7,64,512]{3,2,1,0:T(8,128)(2,1)}, u32[]{:S(2)}, u32[]{:S(2)}) %collective-permute-start.2) | collective-permute-done | bytes 1376288 | tf_op jit(solution)/shard_map/ppermute | solution.py:187
  187.4 1.4 slice_bitcast_fusion.3
  188.8 0.0 copy-done.8
  188.8 1.2 maximum_select_fusion.2
  190.0 0.0 copy-done.6
  190.0 1.2 maximum_select_fusion.1
  191.2 1.2 maximum_select_fusion
  192.4 35.7 %all-to-all-done.2 = bf16[8,3,7,8,1024]{4,3,2,1,0:T(8,128)(2,1)} async-done(((bf16[8,3,7,8,1024]{4,3,2,1,0:T(8,128)(2,1)}), bf16[8,3,7,8,1024]{4,3,2,1,0:T(8,128)(2,1)}, u32[]{:S(2)}, u32[]{:S(2)}) %all-to-all-start.2) | async-done | bytes 2752544 | tf_op jit(solution)/shard_map/all_to_all | solution.py:162
  228.1 2.0 slice_bitcast_fusion
  230.1 1.0 copy.28
  231.1 1.4 copy_bitcast_fusion.1
  (2 shorter events, 0.1 us)
Async XLA Ops:
  7.2 106.2 %copy-start = (bf16[7,64,1024]{2,1,0:T(8,128)(2,1)S(1)}, bf16[7,64,1024]{2,1,0:T(8,128)(2,1)}, u32[]{:S(2)}) copy-start(bf16[7,64,1024]{2,1,0:T(8,128)(2,1)} %param.9) | copy-start | bytes 2752516
  7.2 106.2 %all-gather.2.cloned.1.call-start = ((), (), s32[]{:S(2)}) async-start(), calls=%async_computation.3 | async-start | bytes 4325376 | tf_op jit(solution)/shard_map/all_gather | solution.py:170
  12.5 103.7 %all-to-all-start = ((bf16[8,3,7,8,1024]{4,3,2,1,0:T(8,128)(2,1)}), bf16[8,3,7,8,1024]{4,3,2,1,0:T(8,128)(2,1)}, u32[]{:S(2)}, u32[]{:S(2)}) async-start(bf16[8,3,7,8,1024]{4,3,2,1,0:T(8,128)(2,1)} %copy_bitcast_fusion), calls=%async_computation | async-start | bytes 5505024 | tf_op jit(solution)/shard_map/all_to_all | solution.py:162
  160.5 1.6 copy-start.1
  162.0 4.6 %copy-start.2 = (bf16[7,64,1024]{2,1,0:T(8,128)(2,1)S(1)}, bf16[7,64,1024]{2,1,0:T(8,128)(2,1)}, u32[]{:S(2)}) copy-start(bf16[7,64,1024]{2,1,0:T(8,128)(2,1)} %q_ref.1) | copy-start | bytes 2752516
  162.0 4.6 %copy-start.3 = (bf16[7,64,1024]{2,1,0:T(8,128)(2,1)S(1)}, bf16[7,64,1024]{2,1,0:T(8,128)(2,1)}, u32[]{:S(2)}) copy-start(bf16[7,64,1024]{2,1,0:T(8,128)(2,1)} %k_ref.1) | copy-start | bytes 2752516
  162.0 66.0 %all-to-all-start.2 = ((bf16[8,3,7,8,1024]{4,3,2,1,0:T(8,128)(2,1)}), bf16[8,3,7,8,1024]{4,3,2,1,0:T(8,128)(2,1)}, u32[]{:S(2)}, u32[]{:S(2)}) async-start(bf16[8,3,7,8,1024]{4,3,2,1,0:T(8,128)(2,1)} %copy-done.1), calls=%async_computation.2 | async-start | bytes 5505024 | tf_op jit(solution)/shard_map/all_to_all | solution.py:162
  166.7 2.3 copy-start.9
  168.1 4.0 %copy-start.4 = (bf16[7,64,1024]{2,1,0:T(8,128)(2,1)S(1)}, bf16[7,64,1024]{2,1,0:T(8,128)(2,1)}, u32[]{:S(2)}) copy-start(bf16[7,64,1024]{2,1,0:T(8,128)(2,1)} %v_ref.1) | copy-start | bytes 2752516
  168.1 3.2 %collective-permute-start = (bf16[3,7,64,512]{3,2,1,0:T(8,128)(2,1)S(1)}, bf16[3,7,64,512]{3,2,1,0:T(8,128)(2,1)S(1)}, u32[]{:S(2)}, u32[]{:S(2)}) collective-permute-start(bf16[3,7,64,512]{3,2,1,0:T(8,128)(2,1)S(1)} %pad_maximum_fusion.1), channel_id=1, source_target_pairs={{0,1},{1,0},{2,3},{3,2},{4,5},{5,4},{6,7},{7,6},{8,9},{9,8},{10,11... | collective-permute-start | bytes 4128776 | tf_op jit(solution)/shard_map/ppermute | solution.py:177
  170.2 1.9 collective-permute-start.1
  182.4 0.8 copy-start.5
  183.2 0.8 copy-start.7
  183.9 4.9 %copy-start.8 = (bf16[7,64,512]{2,1,0:T(8,128)(2,1)S(1)}, bf16[7,64,512]{2,1,0:T(8,128)(2,1)}, u32[]{:S(2)}) copy-start(bf16[7,64,512]{2,1,0:T(8,128)(2,1)} %copy-done.7) | copy-start | bytes 1376260
  183.9 3.5 %collective-permute-start.2 = (bf16[3,7,64,512]{3,2,1,0:T(8,128)(2,1)}, bf16[3,7,64,512]{3,2,1,0:T(8,128)(2,1)}, u32[]{:S(2)}, u32[]{:S(2)}) collective-permute-start(bf16[3,7,64,512]{3,2,1,0:T(8,128)(2,1)} %get-tuple-element.11), channel_id=1, source_target_pairs={{0,1},{1,0},{2,3},{3,2},{4,5},{5,4},{6,7},{7,6},{8,9},{9,8},{10,11... | collective-permute-start | bytes 4128776 | tf_op jit(solution)/shard_map/ppermute | solution.py:187
  184.1 6.0 %copy-start.6 = (bf16[7,64,512]{2,1,0:T(8,128)(2,1)S(1)}, bf16[7,64,512]{2,1,0:T(8,128)(2,1)}, u32[]{:S(2)}) copy-start(bf16[7,64,512]{2,1,0:T(8,128)(2,1)} %copy-done.5) | copy-start | bytes 1376260
Sparse Core Ops, SparseCore 0:
  11.6 101.7 all-gather.1

commit v2 on v1

--- a/solution.py
+++ b/solution.py
@@ -137,7 +137,7 @@
         grid_spec=pltpu.PrefetchScalarGridSpec(
             num_scalar_prefetch=1,
             grid=(frames,),
-            in_specs=[mine] * 4 + [far3, far],
+            in_specs=[mine] * 3 + [far, far3, far],
             out_specs=[far] * 3 + [far3],
         ),
         out_shape=[own_shape] * 3 + [jax.ShapeDtypeStruct((3, frames, rows, half), BF16)],
@@ -146,44 +146,270 @@
     )(core.reshape(1), query, keys, values, grad, far_qkv, far_grad)
 
 
+HBM = pl.BlockSpec(memory_space=pl.ANY)
+SCALARS = pl.BlockSpec(memory_space=pltpu.SMEM)
+WHOLE = pl.BlockSpec(memory_space=pltpu.VMEM)
+BIG = pltpu.CompilerParams(vmem_limit_bytes=48 * 2**20)
+
+
+def run_copies(sem, pairs):
+    copies = [pltpu.make_async_copy(src, dst, sem) for src, dst in pairs]
+    for copy in copies:
+        copy.start()
+    for copy in copies:
+        copy.wait()
+
+
+def packed(spots, parts, shape, place, name, after=()):
+    def kernel(spots_ref, *refs):
+        run_copies(refs[-1], place(spots_ref, refs[: len(parts)], refs[-2]))
+
+    return pl.pallas_call(
+        kernel,
+        in_specs=[SCALARS] + [HBM] * (len(parts) + len(after)),
+        out_specs=HBM,
+        out_shape=jax.ShapeDtypeStruct(shape, BF16),
+        scratch_shapes=[pltpu.SemaphoreType.DMA],
+        name=name,
+    )(spots, *parts, *after)
+
+
+def load_weights(spots_ref, near_ref, far_ref, weights, sem, base):
+    near_count = near_ref.shape[0]
+    pairs = []
+    for index in range(near_count):
+        pairs.append((near_ref.at[index], weights.at[spots_ref[base + index]]))
+        pairs.append((far_ref.at[index], weights.at[spots_ref[base + near_count + index]]))
+    run_copies(sem, pairs)
+
+
+def attend_pair(held, results, patches, total):
+    for patch in range(patches):
+        rows = pl.ds(patch, total, stride=patches)
+        done = pair_back(*[ref[rows, :] for ref in held])
+        for ref, value in zip(results, done):
+            ref[rows, :] = value
+
+
+def time_chunk(spots, base, blocks, near, far, late_grad, name):
+    count = len(blocks)
+    kinds, frames, patches, lanes = blocks[0].shape
+    total, part = count * frames, frames * patches
+    rows = total * patches
+    first = late_grad is None
+    width = 2 * lanes
+
+    def kernel(spots_ref, *refs):
+        refs = list(refs)
+        block_refs = [refs.pop(0) for _ in range(count)]
+        extra = [refs.pop(0) for _ in range(2 if first else 1)]
+        out_refs = [refs.pop(0) for _ in range(count)]
+        later_ref = refs.pop(0) if first else None
+        held = [refs.pop(0) for _ in range(4)]
+        results = [refs.pop(0) for _ in range(3)]
+        if first:
+            tokens, weights, sem = refs
+            load_weights(spots_ref, extra[0], extra[1], weights, sem, base)
+            for index, ref in enumerate(block_refs):
+                at = slice(index * part, (index + 1) * part)
+                for side in range(2):
+                    value = ref[3 + side].astype(F32).reshape(part, lanes)
+                    tokens[at, side * lanes : (side + 1) * lanes] = value.astype(BF16)
+            features = weights.shape[0] * weights.shape[1]
+            later = weights[weights.shape[0] // 2 :].reshape(features // 2, width)
+            later_ref[...] = dot(tokens[...], later, ((1,), (1,))).astype(BF16)
+
+        def one_pair(pair, carry):
+            columns = pl.ds(pl.multiple_of(pair * PAIR, PAIR), PAIR)
+            for index, ref in enumerate(block_refs):
+                at = slice(index * part, (index + 1) * part)
+                for kind in range(3):
+                    held[kind][at, :] = ref[kind, :, :, columns].astype(F32).reshape(part, PAIR)
+            if first:
+                share = weights.shape[1]
+                pieces = weights[pl.ds(pair * (PAIR // share), PAIR // share)].reshape(PAIR, width)
+                held[3][...] = dot(tokens[...], pieces, ((1,), (1,))).astype(BF16).astype(F32)
+            else:
+                held[3][...] = extra[0][:, columns].astype(F32)
+            attend_pair(held, results, patches, total)
+            for index, ref in enumerate(out_refs):
+                at = slice(index * part, (index + 1) * part)
+                for kind in range(3):
+                    value = results[kind][at, :].reshape(frames, patches, PAIR)
+                    ref[kind, :, :, columns] = value.astype(BF16)
+            return carry
+
+        lax.fori_loop(0, lanes // PAIR, one_pair, 0)
+
+    out_shapes = [jax.ShapeDtypeStruct((3, frames, patches, lanes), BF16)] * count
+    scratch = [pltpu.VMEM((rows, PAIR), F32)] * 7
+    if first:
+        operands, specs = (near, far), [HBM, HBM]
+        out_shapes = out_shapes + [jax.ShapeDtypeStruct((rows, lanes), BF16)]
+        pieces = (2 * near.shape[0],) + near.shape[1:]
+        scratch = scratch + [pltpu.VMEM((rows, width), BF16), pltpu.VMEM(pieces, BF16), pltpu.SemaphoreType.DMA]
+    else:
+        operands, specs = (late_grad,), [WHOLE]
+    return pl.pallas_call(
+        kernel,
+        in_specs=[SCALARS] + [WHOLE] * count + specs,
+        out_specs=[WHOLE] * len(out_shapes),
+        out_shape=out_shapes,
+        scratch_shapes=scratch,
+        compiler_params=BIG,
+        name=name,
+    )(spots, *blocks, *operands)
+
+
+def space_project(spots, base, core_at, tokens, near, far, after):
+    frames, rows, width = tokens.shape
+    half = width // 2
+
+    def kernel(spots_ref, token_ref, near_ref, far_ref, after_ref, own_ref, send_ref, weights, sem):
+        load_weights(spots_ref, near_ref, far_ref, weights, sem, base)
+        flat = token_ref[...].reshape(frames * rows, width)
+        pieces = weights.shape[0] // 2
+        core = spots_ref[core_at]
+        for ref, side in ((send_ref, 1 - core), (own_ref, core)):
+            part = weights[pl.ds(side * pieces, pieces)].reshape(half, width)
+            ref[...] = dot(flat, part, ((1,), (1,))).astype(BF16).reshape(frames, rows, half)
+
+    pieces = (2 * near.shape[0],) + near.shape[1:]
+    return pl.pallas_call(
+        kernel,
+        in_specs=[SCALARS, WHOLE, HBM, HBM, HBM],
+        out_specs=[WHOLE, WHOLE],
+        out_shape=[jax.ShapeDtypeStruct((frames, rows, half), BF16)] * 2,
+        scratch_shapes=[pltpu.VMEM(pieces, BF16), pltpu.SemaphoreType.DMA],
+        compiler_params=BIG,
+        name="space_project",
+    )(spots, tokens, near, far, after)
+
+
+def placed(spots, blocks, outs, chunk, shape, name):
+    count = len(blocks)
+    lanes = blocks[0].shape[-1]
+    kept = outs is not None
+
+    def kernel(spots_ref, *refs):
+        block_refs, sem, out_refs = refs[:count], refs[-1], refs[-4:-1]
+        columns = pl.ds(chunk * lanes, lanes)
+        pairs = []
+        for index, ref in enumerate(block_refs):
+            for kind in range(3):
+                pairs.append((ref.at[kind], out_refs[kind].at[:, spots_ref[index], :, columns]))
+        run_copies(sem, pairs)
+
+    return pl.pallas_call(
+        kernel,
+        in_specs=[SCALARS] + [HBM] * (count + (3 if kept else 0)),
+        out_specs=[HBM] * 3,
+        out_shape=[jax.ShapeDtypeStruct(shape, BF16)] * 3,
+        scratch_shapes=[pltpu.SemaphoreType.DMA],
+        input_output_aliases={1 + count + kind: kind for kind in range(3)} if kept else {},
+        name=name,
+    )(spots, *blocks, *(outs or ()))
+
+
 def per_device(sizes, grad_out, time_q, time_k, time_v, space_q, space_k, space_v, time_wo, space_wo):
     frames, rows, width = grad_out.shape
     groups, tm, space = sizes
-    patches = rows // tm
-    half = width // 2
-    core = lax.axis_index("space")
+    patches, half = rows // tm, width // 2
+    group, me, core = (lax.axis_index(name) for name in ("groups", "tm", "space"))
+    steps = tm // 2
+    share = time_wo.shape[0] // groups
     swap = [(0, 1), (1, 0)]
 
-    def to_patches(tensor):
-        split = tensor.reshape(tensor.shape[:-2] + (tm, patches, width))
-        return jnp.moveaxis(split, -3, 0)
-
-    def exchanged(tensor):
-        return lax.all_to_all(tensor, "tm", split_axis=0, concat_axis=0, tiled=True)
-
-    time_qkv = exchanged(to_patches(jnp.stack([time_q, time_k, time_v])))
-
-    both_wo = jnp.concatenate([time_wo, space_wo], axis=1)
-    share = both_wo.shape[0] // groups
-    if share * groups == both_wo.shape[0]:
-        piece = lax.dynamic_slice_in_dim(both_wo, lax.axis_index("groups") * share, share, 0)
-        whole = lax.all_gather(piece, ("tm", "space", "groups"), axis=0, tiled=True)
-    else:
-        whole = lax.all_gather(both_wo, ("tm", "space"), axis=0, tiled=True)
-
-    def other_half(tensor):
-        return lax.dynamic_slice_in_dim(tensor, (1 - core) * half, half, tensor.ndim - 1)
-
-    far_qkv = lax.ppermute(jnp.stack([other_half(t) for t in (space_q, space_k, space_v)]), "space", swap)
-
-    tokens = grad_out.reshape(frames * rows, width)
-    time_grad = jnp.einsum("td,cd->tc", tokens, whole[:, :width], preferred_element_type=F32)
-    time_grad = exchanged(to_patches(time_grad.astype(BF16).reshape(frames, rows, width)))
-    space_grad = jnp.einsum("td,cd->tc", tokens, whole[:, width:], preferred_element_type=F32)
-    space_grad = space_grad.astype(BF16).reshape(frames, rows, width)
-    far_grad = lax.ppermute(other_half(space_grad), "space", swap)
-
-    *own, send = space_attention(core, space_q, space_k, space_v, space_grad, far_qkv, far_grad)
+    near_places = []
+    for far_core in range(2):
+        for hop in range(4):
+            for step in range(steps):
+                owner = (me ^ (2 * step) ^ (hop & 1)) * 2 + (core ^ far_core)
+                near_places.append(owner * 2 + (group ^ (hop >> 1)))
+    spots = jnp.stack([me ^ k for k in range(tm)] + near_places + [core, group]).astype(jnp.int32)
+    base, core_at = tm, tm + len(near_places)
+    group_at = core_at + 1
+
+    def to_partner(tensor, k):
+        return lax.ppermute(tensor, "tm", [(i, i ^ k) for i in range(tm)])
+
+    def to_hop(tensor, hop):
+        pairs = [
+            (g * tm + t, (g ^ (hop >> 1)) * tm + (t ^ (hop & 1))) for g in range(groups) for t in range(tm)
+        ]
+        return lax.ppermute(tensor, ("groups", "tm"), pairs)
+
+    piece = packed(
+        spots,
+        [tensor.reshape(groups, share, width) for tensor in (time_wo, space_wo)],
+        (2, share, width),
+        lambda at, parts, out: [(part.at[at[group_at]], out.at[i]) for i, part in enumerate(parts)],
+        "own_piece",
+    )
+    stage1 = [piece] + [to_partner(piece, 2 * step) for step in range(1, steps)]
+
+    split = [t.reshape(frames, tm, patches, width) for t in (time_q, time_k, time_v, grad_out)]
+    order = sorted(range(tm), reverse=True)
+
+    def payload(k, chunk, after=()):
+        def place(at, parts, out):
+            columns = pl.ds(chunk * half, half)
+            pairs = [(part.at[:, at[k], :, columns], out.at[i]) for i, part in enumerate(parts[:3])]
+            if chunk == 0:
+                for side in range(2):
+                    pairs.append((parts[3].at[:, at[k], :, pl.ds(side * half, half)], out.at[3 + side]))
+            return pairs
+
+        kinds = 5 if chunk == 0 else 3
+        return packed(spots, split, (kinds, frames, patches, half), place, "payload", after)
+
+    early, late = [None] * tm, [None] * tm
+    for k in order:
+        sent = payload(k, 0)
+        early[k] = to_partner(sent, k) if k else sent
+
+    def other_half(parts, shape, name):
+        def place(at, refs, out):
+            columns = pl.ds(pl.multiple_of((1 - at[core_at]) * half, half), half)
+            return [(ref.at[:, :, columns], out.at[i]) for i, ref in enumerate(refs)]
+
+        return packed(spots, parts, shape, place, name)
+
+    far_qkv = lax.ppermute(
+        other_half([space_q, space_k, space_v], (3, frames, rows, half), "space_payload"), "space", swap
+    )
+
+    def gathered(which):
+        mine = packed(
+            spots,
+            stage1,
+            (steps, share, width),
+            lambda at, parts, out: [(part.at[which], out.at[i]) for i, part in enumerate(parts)],
+            "stage_two",
+        )
+        quarters = [mine] + [to_hop(mine, hop) for hop in range(1, 4)]
+        near = packed(
+            spots,
+            quarters,
+            (4 * steps, share, width),
+            lambda at, parts, out: [(part, out.at[pl.ds(i * steps, steps)]) for i, part in enumerate(parts)],
+            "stage_three",
+        )
+        return near, lax.ppermute(near, "space", swap)
+
+    time_near, time_far = gathered(0)
+    space_near, space_far = gathered(1)
+
+    for k in order:
+        sent = payload(k, 1, (early[k],))
+        late[k] = to_partner(sent, k) if k else sent
+
+    *done, late_grad = time_chunk(spots, base, early, time_near, time_far, None, "time_first")
+    back = [to_partner(done[k], k) if k else done[k] for k in range(tm)]
+
+    own_grad, send_grad = space_project(spots, base, core_at, grad_out, space_near, space_far, done[0])
+    far_grad = lax.ppermute(send_grad, "space", swap)
+    *own, send = space_attention(core, space_q, space_k, space_v, own_grad, far_qkv, far_grad)
     far = lax.ppermute(send, "space", swap)
     space_out = [
         jnp.where(
@@ -194,6 +420,64 @@
         for index in range(3)
     ]
 
+    done = time_chunk(spots, base, late, None, None, late_grad, "time_second")
+    back2 = [to_partner(done[k], k) if k else done[k] for k in range(tm)]
+    shape = (frames, tm, patches, width)
+    outs = placed(spots, back, None, 0, shape, "place_first")
+    outs = placed(spots, back2, outs, 1, shape, "place_second")
+    time_out = [out.reshape(frames, rows, width) for out in outs]
+    return (*time_out, *space_out)
+
+
+def per_device_plain(sizes, grad_out, time_q, time_k, time_v, space_q, space_k, space_v, time_wo, space_wo):
+    frames, rows, width = grad_out.shape
+    groups, tm, space = sizes
+    patches = rows // tm
+    half = width // 2
+    core = lax.axis_index("space")
+    swap = [(0, 1), (1, 0)]
+
+    def to_patches(tensor):
+        split = tensor.reshape(tensor.shape[:-2] + (tm, patches, width))
+        return jnp.moveaxis(split, -3, 0)
+
+    def exchanged(tensor):
+        return lax.all_to_all(tensor, "tm", split_axis=0, concat_axis=0, tiled=True)
+
+    time_qkv = exchanged(to_patches(jnp.stack([time_q, time_k, time_v])))
+
+    both_wo = jnp.concatenate([time_wo, space_wo], axis=1)
+    share = both_wo.shape[0] // groups
+    if share * groups == both_wo.shape[0]:
+        piece = lax.dynamic_slice_in_dim(both_wo, lax.axis_index("groups") * share, share, 0)
+        whole = lax.all_gather(piece, ("tm", "space", "groups"), axis=0, tiled=True)
+    else:
+        whole = lax.all_gather(both_wo, ("tm", "space"), axis=0, tiled=True)
+
+    def other_half(tensor):
+        return lax.dynamic_slice_in_dim(tensor, (1 - core) * half, half, tensor.ndim - 1)
+
+    far_qkv = lax.ppermute(jnp.stack([other_half(t) for t in (space_q, space_k, space_v)]), "space", swap)
+
+    tokens = grad_out.reshape(frames * rows, width)
+    time_grad = jnp.einsum("td,cd->tc", tokens, whole[:, :width], preferred_element_type=F32)
+    time_grad = exchanged(to_patches(time_grad.astype(BF16).reshape(frames, rows, width)))
+    space_grad = jnp.einsum("td,cd->tc", tokens, whole[:, width:], preferred_element_type=F32)
+    space_grad = space_grad.astype(BF16).reshape(frames, rows, width)
+    far_grad = lax.ppermute(other_half(space_grad), "space", swap)
+
+    own_grad = lax.dynamic_slice_in_dim(space_grad, core * half, half, 2)
+    *own, send = space_attention(core, space_q, space_k, space_v, own_grad, far_qkv, far_grad)
+    far = lax.ppermute(send, "space", swap)
+    space_out = [
+        jnp.where(
+            core == 0,
+            jnp.concatenate([own[index], far[index]], axis=-1),
+            jnp.concatenate([far[index], own[index]], axis=-1),
+        )
+        for index in range(3)
+    ]
+
     back = exchanged(time_attention(time_qkv, time_grad))
     time_out = [jnp.moveaxis(back[:, index], 0, 1).reshape(frames, rows, width) for index in range(3)]
     return (*time_out, *space_out)
@@ -203,8 +487,16 @@
     tokens = P(("groups", "tm"), "space", None)
     weights = P(("tm", "space"), None)
     sizes = tuple(mesh.shape[name] for name in ("groups", "tm", "space"))
+    groups, tm, space = sizes
+    paired = groups == 2 and space == 2 and tm % 2 == 0 and tm & (tm - 1) == 0
+
+    def body(*tensors):
+        patches, rows = tensors[0].shape[1] // tm, tensors[-1].shape[0]
+        fits = paired and patches % 8 == 0 and rows % (16 * groups) == 0
+        return (per_device if fits else per_device_plain)(sizes, *tensors)
+
     return jax.shard_map(
-        functools.partial(per_device, sizes),
+        body,
         mesh=mesh,
         in_specs=(tokens,) * 7 + (weights,) * 2,
         out_specs=(tokens,) * 6,

time: 240 us -> 555 us (2.31); the launches traced: 239 us -> 547 us
  Pallas kernels: 27 us -> 402 us
  waiting for transfers between devices: 134 us -> 60.9 us
  starting transfers between devices: 12.1 us -> 64 us
  blocking collectives: 27.6 us -> 0 us
  between operations: 14.2 us -> 1.44 us
  other arithmetic: 8.93 us -> 3.04 us
    pallas_call x1 -> x27, Pallas kernels: 16.7 us -> 391 us  [the longest x22 275 us: packed(): pl.pallas_call(kernel, in_specs=[SCALARS] + [HBM] * (len(parts) + len(aft...]
    all_gather x1 -> x0, waiting for transfers between devices: 93.6 us -> none  [per_device(): whole = lax.all_gather(piece, ('tm', 'space', 'groups'), axis=0, tiled=True)]
    ppermute x2 -> x41, starting transfers between devices: 0.14 us -> 63.8 us  [the longest x31 56 us: to_partner(): return lax.ppermute(tensor, 'tm', [(i, i ^ k) for i in range(tm)])]
    ppermute x2 -> x41, waiting for transfers between devices: 1.8 us -> 60.9 us  [the longest x31 59.1 us: to_partner(): return lax.ppermute(tensor, 'tm', [(i, i ^ k) for i in range(tm)])]
    all_to_all x2 -> x0, waiting for transfers between devices: 35.7 us -> none  [exchanged(): return lax.all_to_all(tensor, 'tm', split_axis=0, concat_axis=0, tiled=True)]
    all_to_all x1 -> x0, blocking collectives: 27.6 us -> none  [exchanged(): return lax.all_to_all(tensor, 'tm', split_axis=0, concat_axis=0, tiled=True)]
    all_to_all x2 -> x0, starting transfers between devices: 11.8 us -> none  [exchanged(): return lax.all_to_all(tensor, 'tm', split_axis=0, concat_axis=0, tiled=True)]
    unnamed x20 -> x108, local copies, waits for them, and re-layouts: 3.94 us -> 13.8 us
  transfers between devices with their start and end apart: 6 -> 42, of which waited for: 5 -> 10; matrix products, arithmetic and copies ran while one was open for 6% -> 0% of each run, Pallas kernels for 4% -> 69%
where the time goes in v2:
time: 555 us; the launch traced here: 547 us
  Pallas kernels  402 us (72%)
  starting transfers between devices  64 us (12%)
  waiting for transfers between devices  60.9 us (11%)
  local copies, waits for them, and re-layouts  15.9 us (3%)
    pallas_call x22, Pallas kernels, packed(): pl.pallas_call(kernel, in_specs=[SCALARS] + [HBM] * (len(parts) + len(aft...  275 us
    pallas_call x2, Pallas kernels, placed(): pl.pallas_call(kernel, in_specs=[SCALARS] + [HBM] * (count + (3 if kept e...  86.9 us
    ppermute x31, waiting for transfers between devices, to_partner(): return lax.ppermute(tensor, 'tm', [(i, i ^ k) for i in range(tm)])  59.1 us
    ppermute x31, starting transfers between devices, to_partner(): return lax.ppermute(tensor, 'tm', [(i, i ^ k) for i in range(tm)])  56 us
    pallas_call x2, Pallas kernels, time_chunk(): pl.pallas_call(kernel, in_specs=[SCALARS] + [WHOLE] * count + specs, out_...  24.9 us
    unnamed x108, local copies, waits for them, and re-layouts  13.8 us
  transfers between devices with their start and end apart: 42, of which 10 were waited for; matrix products, arithmetic and copies ran while one was open for 0% of the time, Pallas kernels for 69%

profile of v2, /device:TPU:0, one launch (start us, length us, event | category | flops | bytes accessed | tf_op | source)
XLA Modules:
  0.0 546.7 jit_solution(18168022292505898378)
XLA Ops:
  1.3 5.7 %own_piece.1.refs_0_ = bf16[2,32,1024]{2,1,0:T(8,128)(2,1)} custom-call(s32[42]{0:T(128)} %stack.171.spots_ref, bf16[2,32,1024]{2,1,0:T(8,128)(2,1)} %bitcast.124, bf16[2,32,1024]{2,1,0:T(8,128)(2,1)} %bitcast.125), custom_call_target="tpu_custom_call" | custom-call | tf_op jit(solution)/shard_map/own_piece/pallas_call | solution.py:167
  7.1 3.1 collective-permute-start.14
  10.2 2.6 collective-permute-start.15
  12.7 2.6 collective-permute-done.14.refs_1_
  15.4 7.9 %collective-permute-done.15.refs_2_ = bf16[2,32,1024]{2,1,0:T(8,128)(2,1)S(1)} collective-permute-done((bf16[2,32,1024]{2,1,0:T(8,128)(2,1)}, bf16[2,32,1024]{2,1,0:T(8,128)(2,1)S(1)}, u32[]{:S(2)}, u32[]{:S(2)}) %collective-permute-start.15) | collective-permute-done | bytes 131104 | tf_op jit(solution)/shard_map/ppermute | solution.py:334
  24.6 9.7 %stage_two.2.refs_0_ = bf16[4,32,1024]{2,1,0:T(8,128)(2,1)} custom-call(s32[42]{0:T(128)} %stack.171.spots_ref, bf16[2,32,1024]{2,1,0:T(8,128)(2,1)} %own_piece.1.refs_0_, bf16[2,32,1024]{2,1,0:T(8,128)(2,1)} %copy-done.31, bf16[2,32,1024]{2,1,0:T(8,128)(2,1)} %copy-done.32, bf16[2,32,1024]{2,1,0:T(8,128)(2,1)} %copy-done.33), custom_call_target="tpu_custom_call" | custom-call | tf_op jit(solution)/shard_map/stage_two/pallas_call | solution.py:167
  34.3 1.6 collective-permute-start.17
  35.9 1.5 collective-permute-start.18
  37.9 9.7 %stage_two.3.refs_0_ = bf16[4,32,1024]{2,1,0:T(8,128)(2,1)} custom-call(s32[42]{0:T(128)} %stack.171.spots_ref, bf16[2,32,1024]{2,1,0:T(8,128)(2,1)} %own_piece.1.refs_0_, bf16[2,32,1024]{2,1,0:T(8,128)(2,1)} %copy-done.31, bf16[2,32,1024]{2,1,0:T(8,128)(2,1)} %copy-done.32, bf16[2,32,1024]{2,1,0:T(8,128)(2,1)} %copy-done.33), custom_call_target="tpu_custom_call" | custom-call | tf_op jit(solution)/shard_map/stage_two/pallas_call | solution.py:167
  47.6 1.6 collective-permute-start.35
  49.2 1.5 collective-permute-start.36
  51.2 10.5 %payload.18 = bf16[5,7,8,512]{3,2,1,0:T(8,128)(2,1)} custom-call(s32[42]{0:T(128)} %stack.171.spots_ref, bf16[7,8,8,1024]{3,2,1,0:T(8,128)(2,1)} %bitcast.73, bf16[7,8,8,1024]{3,2,1,0:T(8,128)(2,1)} %bitcast.89, bf16[7,8,8,1024]{3,2,1,0:T(8,128)(2,1)} %bitcast.105, bf16[7,8,8,1024]{3,2,1,0:T(8,128)(2,1)} %bitcast.57), custom_call_target="tpu_custom_call" | custom-call | tf_op jit(solution)/shard_map/payload/pallas_call | solution.py:167
  61.7 1.6 collective-permute-start
  64.0 33.5 %stage_three.2.refs_8_ = bf16[16,32,1024]{2,1,0:T(8,128)(2,1)} custom-call(s32[42]{0:T(128)} %stack.171.spots_ref, bf16[4,32,1024]{2,1,0:T(8,128)(2,1)} %stage_two.2.refs_0_, bf16[4,32,1024]{2,1,0:T(8,128)(2,1)} %copy-done.35, bf16[4,32,1024]{2,1,0:T(8,128)(2,1)} %copy-done.37, bf16[4,32,1024]{2,1,0:T(8,128)(2,1)} %copy-done.38), custom_call_target="tpu_custom_call" | custom-call | tf_op jit(solution)/shard_map/stage_three/pallas_call | solution.py:167
  99.1 33.5 %stage_three.3.near_ref = bf16[16,32,1024]{2,1,0:T(8,128)(2,1)} custom-call(s32[42]{0:T(128)} %stack.171.spots_ref, bf16[4,32,1024]{2,1,0:T(8,128)(2,1)} %stage_two.3.refs_0_, bf16[4,32,1024]{2,1,0:T(8,128)(2,1)} %copy-done.34, bf16[4,32,1024]{2,1,0:T(8,128)(2,1)} %copy-done.36, bf16[4,32,1024]{2,1,0:T(8,128)(2,1)} %copy-done.39), custom_call_target="tpu_custom_call" | custom-call | tf_op jit(solution)/shard_map/stage_three/pallas_call | solution.py:167
  133.2 43.5 %space_payload.1 = bf16[3,7,64,512]{3,2,1,0:T(8,128)(2,1)} custom-call(s32[42]{0:T(128)} %stack.171.spots_ref, bf16[7,64,1024]{2,1,0:T(8,128)(2,1)} %q_ref.1, bf16[7,64,1024]{2,1,0:T(8,128)(2,1)} %k_ref.1, bf16[7,64,1024]{2,1,0:T(8,128)(2,1)} %v_ref.1), custom_call_target="tpu_custom_call" | custom-call | tf_op jit(solution)/shard_map/space_payload/pallas_call | solution.py:167
  176.8 10.5 %payload.20 = bf16[5,7,8,512]{3,2,1,0:T(8,128)(2,1)} custom-call(s32[42]{0:T(128)} %stack.171.spots_ref, bf16[7,8,8,1024]{3,2,1,0:T(8,128)(2,1)} %bitcast.74, bf16[7,8,8,1024]{3,2,1,0:T(8,128)(2,1)} %bitcast.90, bf16[7,8,8,1024]{3,2,1,0:T(8,128)(2,1)} %bitcast.106, bf16[7,8,8,1024]{3,2,1,0:T(8,128)(2,1)} %bitcast.58), custom_call_target="tpu_custom_call" | custom-call | tf_op jit(solution)/shard_map/payload/pallas_call | solution.py:167
  187.2 1.4 collective-permute-start.2
  188.6 10.5 %payload.22 = bf16[5,7,8,512]{3,2,1,0:T(8,128)(2,1)} custom-call(s32[42]{0:T(128)} %stack.171.spots_ref, bf16[7,8,8,1024]{3,2,1,0:T(8,128)(2,1)} %bitcast.75, bf16[7,8,8,1024]{3,2,1,0:T(8,128)(2,1)} %bitcast.91, bf16[7,8,8,1024]{3,2,1,0:T(8,128)(2,1)} %bitcast.107, bf16[7,8,8,1024]{3,2,1,0:T(8,128)(2,1)} %bitcast.59), custom_call_target="tpu_custom_call" | custom-call | tf_op jit(solution)/shard_map/payload/pallas_call | solution.py:167
  199.9 10.5 %payload.24 = bf16[5,7,8,512]{3,2,1,0:T(8,128)(2,1)} custom-call(s32[42]{0:T(128)} %stack.171.spots_ref, bf16[7,8,8,1024]{3,2,1,0:T(8,128)(2,1)} %bitcast.76, bf16[7,8,8,1024]{3,2,1,0:T(8,128)(2,1)} %bitcast.92, bf16[7,8,8,1024]{3,2,1,0:T(8,128)(2,1)} %bitcast.108, bf16[7,8,8,1024]{3,2,1,0:T(8,128)(2,1)} %bitcast.60), custom_call_target="tpu_custom_call" | custom-call | tf_op jit(solution)/shard_map/payload/pallas_call | solution.py:167
  210.4 10.5 %payload.26 = bf16[5,7,8,512]{3,2,1,0:T(8,128)(2,1)} custom-call(s32[42]{0:T(128)} %stack.171.spots_ref, bf16[7,8,8,1024]{3,2,1,0:T(8,128)(2,1)} %bitcast.77, bf16[7,8,8,1024]{3,2,1,0:T(8,128)(2,1)} %bitcast.93, bf16[7,8,8,1024]{3,2,1,0:T(8,128)(2,1)} %bitcast.109, bf16[7,8,8,1024]{3,2,1,0:T(8,128)(2,1)} %bitcast.61), custom_call_target="tpu_custom_call" | custom-call | tf_op jit(solution)/shard_map/payload/pallas_call | solution.py:167
  220.9 2.4 collective-permute-start.6
  223.3 1.5 collective-permute-start.8
  224.7 10.5 %payload.28 = bf16[5,7,8,512]{3,2,1,0:T(8,128)(2,1)} custom-call(s32[42]{0:T(128)} %stack.171.spots_ref, bf16[7,8,8,1024]{3,2,1,0:T(8,128)(2,1)} %bitcast.78, bf16[7,8,8,1024]{3,2,1,0:T(8,128)(2,1)} %bitcast.94, bf16[7,8,8,1024]{3,2,1,0:T(8,128)(2,1)} %bitcast.110, bf16[7,8,8,1024]{3,2,1,0:T(8,128)(2,1)} %bitcast.62), custom_call_target="tpu_custom_call" | custom-call | tf_op jit(solution)/shard_map/payload/pallas_call | solution.py:167
  235.2 10.5 %payload.30 = bf16[5,7,8,512]{3,2,1,0:T(8,128)(2,1)} custom-call(s32[42]{0:T(128)} %stack.171.spots_ref, bf16[7,8,8,1024]{3,2,1,0:T(8,128)(2,1)} %bitcast.79, bf16[7,8,8,1024]{3,2,1,0:T(8,128)(2,1)} %bitcast.95, bf16[7,8,8,1024]{3,2,1,0:T(8,128)(2,1)} %bitcast.111, bf16[7,8,8,1024]{3,2,1,0:T(8,128)(2,1)} %bitcast.63), custom_call_target="tpu_custom_call" | custom-call | tf_op jit(solution)/shard_map/payload/pallas_call | solution.py:167
  245.7 2.3 collective-permute-start.10
  248.0 12.1 %collective-permute-done.8.refs_4_.refs_5_ = bf16[5,7,8,512]{3,2,1,0:T(8,128)(2,1)} collective-permute-done((bf16[5,7,8,512]{3,2,1,0:T(8,128)(2,1)}, bf16[5,7,8,512]{3,2,1,0:T(8,128)(2,1)}, u32[]{:S(2)}, u32[]{:S(2)}) %collective-permute-start.8) | collective-permute-done | bytes 286752 | tf_op jit(solution)/shard_map/ppermute | solution.py:334
  260.2 10.5 %payload.16.refs_4_.refs_0_ = bf16[5,7,8,512]{3,2,1,0:T(8,128)(2,1)} custom-call(s32[42]{0:T(128)} %stack.171.spots_ref, bf16[7,8,8,1024]{3,2,1,0:T(8,128)(2,1)} %bitcast.80, bf16[7,8,8,1024]{3,2,1,0:T(8,128)(2,1)} %bitcast.96, bf16[7,8,8,1024]{3,2,1,0:T(8,128)(2,1)} %bitcast.112, bf16[7,8,8,1024]{3,2,1,0:T(8,128)(2,1)} %bitcast.64), custom_call_target="tpu_custom_call" | custom-call | tf_op jit(solution)/shard_map/payload/pallas_call | solution.py:167
  271.8 15.3 %time_first.1 = (bf16[3,7,8,512]{3,2,1,0:T(8,128)(2,1)S(1)}, bf16[3,7,8,512]{3,2,1,0:T(8,128)(2,1)S(1)}, bf16[3,7,8,512]{3,2,1,0:T(8,128)(2,1)S(1)}, bf16[3,7,8,...) custom-call(s32[42]{0:T(128)S(1)} %copy-done.14, ...), custom_call_target="tpu_custom_call" | custom-call | tf_op jit(solution)/shard_map/time_first/pallas_call | solution.py:253
  291.4 4.0 space_project.1
  295.5 1.8 collective-permute-done.40.grad_ref
  297.3 10.3 %space_attention.1 = (bf16[7,64,512]{2,1,0:T(8,128)(2,1)S(1)}, bf16[7,64,512]{2,1,0:T(8,128)(2,1)S(1)}, bf16[7,64,512]{2,1,0:T(8,128)(2,1)S(1)}, bf16[3,7,64,512]{3,2,1,0:T(8,128)(2,1)}) custom-call(s32[1]{0:T(128)} %bitcast.40.core_ref, bf16[7,64,1024]{2,1,0:T(8,128)(2,1)S(1)} %copy-done.3, bf16[7,64,1024]{2,1,0:T(8,128)(2,1)S(1)} %copy-done.4, ...), custom_call_target="tpu_custom_call" | custom-call | tf_op jit(solution)/shard_map/space_attention/pallas_call | solution.py:135
  307.7 7.0 %payload.19 = bf16[3,7,8,512]{3,2,1,0:T(8,128)(2,1)} custom-call(s32[42]{0:T(128)} %stack.171.spots_ref, bf16[7,8,8,1024]{3,2,1,0:T(8,128)(2,1)} %bitcast.81, bf16[7,8,8,1024]{3,2,1,0:T(8,128)(2,1)} %bitcast.97, bf16[7,8,8,1024]{3,2,1,0:T(8,128)(2,1)} %bitcast.113, bf16[7,8,8,1024]{3,2,1,0:T(8,128)(2,1)} %bitcast.65, bf16[5,7,8,512]{3,2,1,0:T(8,128)(2,1)} %copy-done.7), custom_call_target="tpu_custom_call" | custom-call | tf_op jit(solution)/shard_map/payload/pallas_call | solution.py:167
  314.7 4.0 collective-permute-start.1
  318.7 7.0 %payload.21 = bf16[3,7,8,512]{3,2,1,0:T(8,128)(2,1)} custom-call(s32[42]{0:T(128)} %stack.171.spots_ref, bf16[7,8,8,1024]{3,2,1,0:T(8,128)(2,1)} %bitcast.82, bf16[7,8,8,1024]{3,2,1,0:T(8,128)(2,1)} %bitcast.98, bf16[7,8,8,1024]{3,2,1,0:T(8,128)(2,1)} %bitcast.114, bf16[7,8,8,1024]{3,2,1,0:T(8,128)(2,1)} %bitcast.66, bf16[5,7,8,512]{3,2,1,0:T(8,128)(2,1)} %copy-done.8), custom_call_target="tpu_custom_call" | custom-call | tf_op jit(solution)/shard_map/payload/pallas_call | solution.py:167
  325.7 1.2 collective-permute-start.3
  326.9 7.0 %payload.23 = bf16[3,7,8,512]{3,2,1,0:T(8,128)(2,1)} custom-call(s32[42]{0:T(128)} %stack.171.spots_ref, bf16[7,8,8,1024]{3,2,1,0:T(8,128)(2,1)} %bitcast.83, bf16[7,8,8,1024]{3,2,1,0:T(8,128)(2,1)} %bitcast.99, bf16[7,8,8,1024]{3,2,1,0:T(8,128)(2,1)} %bitcast.115, bf16[7,8,8,1024]{3,2,1,0:T(8,128)(2,1)} %bitcast.67, bf16[5,7,8,512]{3,2,1,0:T(8,128)(2,1)} %copy-done.9), custom_call_target="tpu_custom_call" | custom-call | tf_op jit(solution)/shard_map/payload/pallas_call | solution.py:167
  334.8 7.0 %payload.25 = bf16[3,7,8,512]{3,2,1,0:T(8,128)(2,1)} custom-call(s32[42]{0:T(128)} %stack.171.spots_ref, bf16[7,8,8,1024]{3,2,1,0:T(8,128)(2,1)} %bitcast.84, bf16[7,8,8,1024]{3,2,1,0:T(8,128)(2,1)} %bitcast.100, bf16[7,8,8,1024]{3,2,1,0:T(8,128)(2,1)} %bitcast.116, bf16[7,8,8,1024]{3,2,1,0:T(8,128)(2,1)} %bitcast.68, ...), custom_call_target="tpu_custom_call" | custom-call | tf_op jit(solution)/shard_map/payload/pallas_call | solution.py:167
  341.8 2.9 collective-permute-start.7
  344.7 7.0 %payload.27 = bf16[3,7,8,512]{3,2,1,0:T(8,128)(2,1)} custom-call(s32[42]{0:T(128)} %stack.171.spots_ref, bf16[7,8,8,1024]{3,2,1,0:T(8,128)(2,1)} %bitcast.85, bf16[7,8,8,1024]{3,2,1,0:T(8,128)(2,1)} %bitcast.101, bf16[7,8,8,1024]{3,2,1,0:T(8,128)(2,1)} %bitcast.117, bf16[7,8,8,1024]{3,2,1,0:T(8,128)(2,1)} %bitcast.69, ...), custom_call_target="tpu_custom_call" | custom-call | tf_op jit(solution)/shard_map/payload/pallas_call | solution.py:167
  351.7 7.0 %payload.29 = bf16[3,7,8,512]{3,2,1,0:T(8,128)(2,1)} custom-call(s32[42]{0:T(128)} %stack.171.spots_ref, bf16[7,8,8,1024]{3,2,1,0:T(8,128)(2,1)} %bitcast.86, bf16[7,8,8,1024]{3,2,1,0:T(8,128)(2,1)} %bitcast.102, bf16[7,8,8,1024]{3,2,1,0:T(8,128)(2,1)} %bitcast.118, bf16[7,8,8,1024]{3,2,1,0:T(8,128)(2,1)} %bitcast.70, ...), custom_call_target="tpu_custom_call" | custom-call | tf_op jit(solution)/shard_map/payload/pallas_call | solution.py:167
  358.7 7.0 %payload.31 = bf16[3,7,8,512]{3,2,1,0:T(8,128)(2,1)} custom-call(s32[42]{0:T(128)} %stack.171.spots_ref, bf16[7,8,8,1024]{3,2,1,0:T(8,128)(2,1)} %bitcast.87, bf16[7,8,8,1024]{3,2,1,0:T(8,128)(2,1)} %bitcast.103, bf16[7,8,8,1024]{3,2,1,0:T(8,128)(2,1)} %bitcast.119, bf16[7,8,8,1024]{3,2,1,0:T(8,128)(2,1)} %bitcast.71, ...), custom_call_target="tpu_custom_call" | custom-call | tf_op jit(solution)/shard_map/payload/pallas_call | solution.py:167
  366.8 1.4 collective-permute-start.11
  368.2 2.4 collective-permute-start.13
  370.6 7.1 %payload.17.refs_0_ = bf16[3,7,8,512]{3,2,1,0:T(8,128)(2,1)} custom-call(s32[42]{0:T(128)} %stack.171.spots_ref, bf16[7,8,8,1024]{3,2,1,0:T(8,128)(2,1)} %bitcast.88, bf16[7,8,8,1024]{3,2,1,0:T(8,128)(2,1)} %bitcast.104, bf16[7,8,8,1024]{3,2,1,0:T(8,128)(2,1)} %bitcast.120, bf16[7,8,8,1024]{3,2,1,0:T(8,128)(2,1)} %bitcast.72, ...), custom_call_target="tpu_custom_call" | custom-call | tf_op jit(solution)/shard_map/payload/pallas_call | solution.py:167
  377.8 6.4 %collective-permute-done.9.refs_5_ = bf16[3,7,8,512]{3,2,1,0:T(8,128)(2,1)S(1)} collective-permute-done((bf16[3,7,8,512]{3,2,1,0:T(8,128)(2,1)}, bf16[3,7,8,512]{3,2,1,0:T(8,128)(2,1)S(1)}, u32[]{:S(2)}, u32[]{:S(2)}) %collective-permute-start.9) | collective-permute-done | bytes 172064 | tf_op jit(solution)/shard_map/ppermute | solution.py:334
  385.2 9.6 %time_second.1 = (bf16[3,7,8,512]{3,2,1,0:T(8,128)(2,1)S(1)}, bf16[3,7,8,512]{3,2,1,0:T(8,128)(2,1)S(1)}, bf16[3,7,8,512]{3,2,1,0:T(8,128)(2,1)S(1)}, bf16[3,7,8...) custom-call(s32[42]{0:T(128)S(1)} %copy-done.15, ...), custom_call_target="tpu_custom_call" | custom-call | tf_op jit(solution)/shard_map/time_second/pallas_call | solution.py:253
  396.0 7.8 %collective-permute-start.22 = (bf16[3,7,8,512]{3,2,1,0:T(8,128)(2,1)S(1)}, bf16[3,7,8,512]{3,2,1,0:T(8,128)(2,1)S(1)}, u32[]{:S(2)}, u32[]{:S(2)}) collective-permute-start(bf16[3,7,8,512]{3,2,1,0:T(8,128)(2,1)S(1)} %get-tuple-element.38), channel_id=1, source_target_pairs={{0,4},{2,6},{4,0},{6,2},{8,12},{10,14},{12,8},{14,10},{1,5},{3,7},... | collective-permute-start | bytes 516104 | tf_op jit(solution)/shard_map/ppermute | solution.py:334
  405.3 6.2 %collective-permute-start.29 = (bf16[3,7,8,512]{3,2,1,0:T(8,128)(2,1)S(1)}, bf16[3,7,8,512]{3,2,1,0:T(8,128)(2,1)S(1)}, u32[]{:S(2)}, u32[]{:S(2)}) collective-permute-start(bf16[3,7,8,512]{3,2,1,0:T(8,128)(2,1)S(1)} %copy-done.28), channel_id=1, source_target_pairs={{0,4},{2,6},{4,0},{6,2},{8,12},{10,14},{12,8},{14,10},{1,5},{3,7},... | collective-permute-start | bytes 516104 | tf_op jit(solution)/shard_map/ppermute | solution.py:334
  412.0 1.7 collective-permute-done.23.refs_3_
  413.6 2.2 collective-permute-start.31
  415.8 1.6 collective-permute-start.32
  417.4 3.9 collective-permute-done.29.refs_2_
  421.4 1.7 collective-permute-start.33
  423.1 2.4 collective-permute-done.30.refs_3_
  425.4 1.4 collective-permute-start.34
  426.9 17.1 %collective-permute-done.31.refs_4_ = bf16[3,7,8,512]{3,2,1,0:T(8,128)(2,1)S(1)} collective-permute-done((bf16[3,7,8,512]{3,2,1,0:T(8,128)(2,1)S(1)}, bf16[3,7,8,512]{3,2,1,0:T(8,128)(2,1)S(1)}, u32[]{:S(2)}, u32[]{:S(2)}) %collective-permute-start.31) | collective-permute-done | bytes 172064 | tf_op jit(solution)/shard_map/ppermute | solution.py:334
  444.7 4.8 collective-permute-done.32.refs_5_
  451.5 2.9 collective-permute-start.27
  454.4 43.5 %place_first.1 = (bf16[7,8,8,1024]{3,2,1,0:T(8,128)(2,1)}, bf16[7,8,8,1024]{3,2,1,0:T(8,128)(2,1)}, bf16[7,8,8,1024]{3,2,1,0:T(8,128)(2,1)}) custom-call(s32[42]{0:T(128)} %stack.171.spots_ref, bf16[3,7,8,512]{3,2,1,0:T(8,128)(2,1)} %copy-done.11, bf16[3,7,8,512]{3,2,1,0:T(8,128)(2,1)} %copy-done.47, bf16[3,7,8,512]{3,2,1,0:T(8,128)(2,1)} %copy-done.48, ...), custom_call_target="tpu_custom_call" | custom-call | tf_op jit(solution)/shard_map/place_first/pallas_call | solution.py:303
  498.7 43.5 %place_second.1 = (bf16[7,8,8,1024]{3,2,1,0:T(8,128)(2,1)}, bf16[7,8,8,1024]{3,2,1,0:T(8,128)(2,1)}, bf16[7,8,8,1024]{3,2,1,0:T(8,128)(2,1)}) custom-call(s32[42]{0:T(128)} %stack.171.spots_ref, bf16[3,7,8,512]{3,2,1,0:T(8,128)(2,1)} %copy-done.16, bf16[3,7,8,512]{3,2,1,0:T(8,128)(2,1)} %copy-done.40, ...), custom_call_target="tpu_custom_call", output_to_operand_aliasing={{0}: (9, {}), {1}: (10, {}), {2}: (11, {})} | custom-call | tf_op jit(solution)/shard_map/place_second/pallas_call | solution.py:303
  542.2 1.4 slice_bitcast_fusion
  543.6 1.2 maximum_select_fusion.2
  544.9 1.8 maximum_select_fusion
  (160 shorter events, 21.8 us)
Async XLA Ops:
  7.1 8.3 %collective-permute-start.14 = (bf16[2,32,1024]{2,1,0:T(8,128)(2,1)}, bf16[2,32,1024]{2,1,0:T(8,128)(2,1)S(1)}, u32[]{:S(2)}, u32[]{:S(2)}) collective-permute-start(bf16[2,32,1024]{2,1,0:T(8,128)(2,1)} %own_piece.1.refs_0_), channel_id=1, source_target_pairs={{0,4},{2,6},{4,0},{6,2},{8,12},{10,14},{12,8},{14,10},{1,5},{3,7},... | collective-permute-start | bytes 393224 | tf_op jit(solution)/shard_map/ppermute | solution.py:334
  10.2 13.2 %collective-permute-start.15 = (bf16[2,32,1024]{2,1,0:T(8,128)(2,1)}, bf16[2,32,1024]{2,1,0:T(8,128)(2,1)S(1)}, u32[]{:S(2)}, u32[]{:S(2)}) collective-permute-start(bf16[2,32,1024]{2,1,0:T(8,128)(2,1)} %own_piece.1.refs_0_), channel_id=1, source_target_pairs={{0,8},{2,10},{4,12},{6,14},{8,0},{10,2},{12,4},{14,6},{1,9},{3,11}... | collective-permute-start | bytes 393224 | tf_op jit(solution)/shard_map/ppermute | solution.py:334
  12.7 10.6 %collective-permute-start.16 = (bf16[2,32,1024]{2,1,0:T(8,128)(2,1)}, bf16[2,32,1024]{2,1,0:T(8,128)(2,1)S(1)}, u32[]{:S(2)}, u32[]{:S(2)}) collective-permute-start(bf16[2,32,1024]{2,1,0:T(8,128)(2,1)} %own_piece.1.refs_0_), channel_id=1, source_target_pairs={{0,12},{2,14},{4,8},{6,10},{8,4},{10,6},{12,0},{14,2},{1,13},{3,15... | collective-permute-start | bytes 393224 | tf_op jit(solution)/shard_map/ppermute | solution.py:334
  34.3 16.4 %collective-permute-start.17 = (bf16[4,32,1024]{2,1,0:T(8,128)(2,1)}, bf16[4,32,1024]{2,1,0:T(8,128)(2,1)S(1)}, u32[]{:S(2)}, u32[]{:S(2)}) collective-permute-start(bf16[4,32,1024]{2,1,0:T(8,128)(2,1)} %stage_two.2.refs_0_), channel_id=1, source_target_pairs={{0,2},{2,0},{4,6},{6,4},{8,10},{10,8},{12,14},{14,12},{16,18},{18,... | collective-permute-start | bytes 786440 | tf_op jit(solution)/shard_map/ppermute | solution.py:340
  35.9 25.7 %collective-permute-start.18 = (bf16[4,32,1024]{2,1,0:T(8,128)(2,1)}, bf16[4,32,1024]{2,1,0:T(8,128)(2,1)S(1)}, u32[]{:S(2)}, u32[]{:S(2)}) collective-permute-start(bf16[4,32,1024]{2,1,0:T(8,128)(2,1)} %stage_two.2.refs_0_), channel_id=1, source_target_pairs={{0,16},{2,18},{4,20},{6,22},{8,24},{10,26},{12,28},{14,30},{16,0},... | collective-permute-start | bytes 786440 | tf_op jit(solution)/shard_map/ppermute | solution.py:340
  37.4 25.8 %collective-permute-start.19 = (bf16[4,32,1024]{2,1,0:T(8,128)(2,1)}, bf16[4,32,1024]{2,1,0:T(8,128)(2,1)S(1)}, u32[]{:S(2)}, u32[]{:S(2)}) collective-permute-start(bf16[4,32,1024]{2,1,0:T(8,128)(2,1)} %stage_two.2.refs_0_), channel_id=1, source_target_pairs={{0,18},{2,16},{4,22},{6,20},{8,26},{10,24},{12,30},{14,28},{16,2},... | collective-permute-start | bytes 786440 | tf_op jit(solution)/shard_map/ppermute | solution.py:340
  47.6 50.0 %collective-permute-start.35 = (bf16[4,32,1024]{2,1,0:T(8,128)(2,1)}, bf16[4,32,1024]{2,1,0:T(8,128)(2,1)S(1)}, u32[]{:S(2)}, u32[]{:S(2)}) collective-permute-start(bf16[4,32,1024]{2,1,0:T(8,128)(2,1)} %stage_two.3.refs_0_), channel_id=1, source_target_pairs={{0,2},{2,0},{4,6},{6,4},{8,10},{10,8},{12,14},{14,12},{16,18},{18,... | collective-permute-start | bytes 786440 | tf_op jit(solution)/shard_map/ppermute | solution.py:340
  49.2 48.4 %collective-permute-start.36 = (bf16[4,32,1024]{2,1,0:T(8,128)(2,1)}, bf16[4,32,1024]{2,1,0:T(8,128)(2,1)S(1)}, u32[]{:S(2)}, u32[]{:S(2)}) collective-permute-start(bf16[4,32,1024]{2,1,0:T(8,128)(2,1)} %stage_two.3.refs_0_), channel_id=1, source_target_pairs={{0,16},{2,18},{4,20},{6,22},{8,24},{10,26},{12,28},{14,30},{16,0},... | collective-permute-start | bytes 786440 | tf_op jit(solution)/shard_map/ppermute | solution.py:340
  50.7 46.9 %collective-permute-start.37 = (bf16[4,32,1024]{2,1,0:T(8,128)(2,1)}, bf16[4,32,1024]{2,1,0:T(8,128)(2,1)S(1)}, u32[]{:S(2)}, u32[]{:S(2)}) collective-permute-start(bf16[4,32,1024]{2,1,0:T(8,128)(2,1)} %stage_two.3.refs_0_), channel_id=1, source_target_pairs={{0,18},{2,16},{4,22},{6,20},{8,26},{10,24},{12,30},{14,28},{16,2},... | collective-permute-start | bytes 786440 | tf_op jit(solution)/shard_map/ppermute | solution.py:340
  61.7 137.4 %collective-permute-start = (bf16[5,7,8,512]{3,2,1,0:T(8,128)(2,1)}, bf16[5,7,8,512]{3,2,1,0:T(8,128)(2,1)S(1)}, u32[]{:S(2)}, u32[]{:S(2)}) collective-permute-start(bf16[5,7,8,512]{3,2,1,0:T(8,128)(2,1)} %payload.18), channel_id=1, source_target_pairs={{0,2},{2,0},{4,6},{6,4},{8,10},{10,8},{12,14},{14,12},{1,3},{3,1},... | collective-permute-start | bytes 860168 | tf_op jit(solution)/shard_map/ppermute | solution.py:334
  97.5 173.2 %collective-permute-start.20 = (bf16[16,32,1024]{2,1,0:T(8,128)(2,1)}, bf16[16,32,1024]{2,1,0:T(8,128)(2,1)}, u32[]{:S(2)}, u32[]{:S(2)}) collective-permute-start(bf16[16,32,1024]{2,1,0:T(8,128)(2,1)} %stage_three.2.refs_8_), channel_id=1, source_target_pairs={{0,1},{1,0},{2,3},{3,2},{4,5},{5,4},{6,7},{7,6},{8,9},{9,8},{10,11... | collective-permute-start | bytes 3145736 | tf_op jit(solution)/shard_map/ppermute | solution.py:398
  132.6 158.7 %collective-permute-start.38 = (bf16[16,32,1024]{2,1,0:T(8,128)(2,1)}, bf16[16,32,1024]{2,1,0:T(8,128)(2,1)}, u32[]{:S(2)}, u32[]{:S(2)}) collective-permute-start(bf16[16,32,1024]{2,1,0:T(8,128)(2,1)} %stage_three.3.near_ref), channel_id=1, source_target_pairs={{0,1},{1,0},{2,3},{3,2},{4,5},{5,4},{6,7},{7,6},{8,9},{9,8},{10,11... | collective-permute-start | bytes 3145736 | tf_op jit(solution)/shard_map/ppermute | solution.py:398
  176.7 118.9 %collective-permute-start.39 = (bf16[3,7,64,512]{3,2,1,0:T(8,128)(2,1)}, bf16[3,7,64,512]{3,2,1,0:T(8,128)(2,1)S(1)}, u32[]{:S(2)}, u32[]{:S(2)}) collective-permute-start(bf16[3,7,64,512]{3,2,1,0:T(8,128)(2,1)} %space_payload.1), channel_id=1, source_target_pairs={{0,1},{1,0},{2,3},{3,2},{4,5},{5,4},{6,7},{7,6},{8,9},{9,8},{10,11... | collective-permute-start | bytes 4128776 | tf_op jit(solution)/shard_map/ppermute | solution.py:378
  187.2 33.6 %collective-permute-start.2 = (bf16[5,7,8,512]{3,2,1,0:T(8,128)(2,1)}, bf16[5,7,8,512]{3,2,1,0:T(8,128)(2,1)S(1)}, u32[]{:S(2)}, u32[]{:S(2)}) collective-permute-start(bf16[5,7,8,512]{3,2,1,0:T(8,128)(2,1)} %payload.20), channel_id=1, source_target_pairs={{0,4},{2,6},{4,0},{6,2},{8,12},{10,14},{12,8},{14,10},{1,5},{3,7},... | collective-permute-start | bytes 860168 | tf_op jit(solution)/shard_map/ppermute | solution.py:334
  199.1 71.6 %copy-start.7 = (bf16[5,7,8,512]{3,2,1,0:T(8,128)(2,1)}, bf16[5,7,8,512]{3,2,1,0:T(8,128)(2,1)S(1)}, u32[]{:S(2)}) copy-start(bf16[5,7,8,512]{3,2,1,0:T(8,128)(2,1)S(1)} %collective-permute-done.refs_4_.refs_1_) | copy-start | bytes 860164
  199.1 24.2 %collective-permute-start.4 = (bf16[5,7,8,512]{3,2,1,0:T(8,128)(2,1)}, bf16[5,7,8,512]{3,2,1,0:T(8,128)(2,1)S(1)}, u32[]{:S(2)}, u32[]{:S(2)}) collective-permute-start(bf16[5,7,8,512]{3,2,1,0:T(8,128)(2,1)} %payload.22), channel_id=1, source_target_pairs={{0,6},{2,4},{4,2},{6,0},{8,14},{10,12},{12,10},{14,8},{1,7},{3,5},... | collective-permute-start | bytes 860168 | tf_op jit(solution)/shard_map/ppermute | solution.py:334
  220.9 49.8 %copy-start.8 = (bf16[5,7,8,512]{3,2,1,0:T(8,128)(2,1)}, bf16[5,7,8,512]{3,2,1,0:T(8,128)(2,1)S(1)}, u32[]{:S(2)}) copy-start(bf16[5,7,8,512]{3,2,1,0:T(8,128)(2,1)S(1)} %collective-permute-done.2.refs_4_.refs_2_) | copy-start | bytes 860164
  220.9 24.8 %collective-permute-start.6 = (bf16[5,7,8,512]{3,2,1,0:T(8,128)(2,1)}, bf16[5,7,8,512]{3,2,1,0:T(8,128)(2,1)}, u32[]{:S(2)}, u32[]{:S(2)}) collective-permute-start(bf16[5,7,8,512]{3,2,1,0:T(8,128)(2,1)} %payload.24), channel_id=1, source_target_pairs={{0,8},{2,10},{4,12},{6,14},{8,0},{10,2},{12,4},{14,6},{1,9},{3,11}... | collective-permute-start | bytes 860168 | tf_op jit(solution)/shard_map/ppermute | solution.py:334
  223.3 47.5 %copy-start.9 = (bf16[5,7,8,512]{3,2,1,0:T(8,128)(2,1)}, bf16[5,7,8,512]{3,2,1,0:T(8,128)(2,1)S(1)}, u32[]{:S(2)}) copy-start(bf16[5,7,8,512]{3,2,1,0:T(8,128)(2,1)S(1)} %collective-permute-done.4.refs_4_.refs_3_) | copy-start | bytes 860164
  223.3 36.9 %collective-permute-start.8 = (bf16[5,7,8,512]{3,2,1,0:T(8,128)(2,1)}, bf16[5,7,8,512]{3,2,1,0:T(8,128)(2,1)}, u32[]{:S(2)}, u32[]{:S(2)}) collective-permute-start(bf16[5,7,8,512]{3,2,1,0:T(8,128)(2,1)} %payload.26), channel_id=1, source_target_pairs={{0,10},{2,8},{4,14},{6,12},{8,2},{10,0},{12,6},{14,4},{1,11},{3,9}... | collective-permute-start | bytes 860168 | tf_op jit(solution)/shard_map/ppermute | solution.py:334
  245.7 25.1 %copy-start.1 = (bf16[16,32,1024]{2,1,0:T(8,128)(2,1)S(1)}, bf16[16,32,1024]{2,1,0:T(8,128)(2,1)}, u32[]{:S(2)}) copy-start(bf16[16,32,1024]{2,1,0:T(8,128)(2,1)} %stage_three.2.refs_8_) | copy-start | bytes 3145732
  245.7 25.1 %copy-start.14 = (s32[42]{0:T(128)S(1)}, s32[42]{0:T(128)}, u32[]{:S(2)}) copy-start(s32[42]{0:T(128)} %stack.171.spots_ref) | copy-start | bytes 508
  245.7 25.0 %collective-permute-start.10 = (bf16[5,7,8,512]{3,2,1,0:T(8,128)(2,1)}, bf16[5,7,8,512]{3,2,1,0:T(8,128)(2,1)}, u32[]{:S(2)}, u32[]{:S(2)}) collective-permute-start(bf16[5,7,8,512]{3,2,1,0:T(8,128)(2,1)} %payload.28), channel_id=1, source_target_pairs={{0,12},{2,14},{4,8},{6,10},{8,4},{10,6},{12,0},{14,2},{1,13},{3,15... | collective-permute-start | bytes 860168 | tf_op jit(solution)/shard_map/ppermute | solution.py:334
  260.2 10.5 %collective-permute-start.12 = (bf16[5,7,8,512]{3,2,1,0:T(8,128)(2,1)}, bf16[5,7,8,512]{3,2,1,0:T(8,128)(2,1)}, u32[]{:S(2)}, u32[]{:S(2)}) collective-permute-start(bf16[5,7,8,512]{3,2,1,0:T(8,128)(2,1)} %payload.30), channel_id=1, source_target_pairs={{0,14},{2,12},{4,10},{6,8},{8,6},{10,4},{12,2},{14,0},{1,15},{3,13... | collective-permute-start | bytes 860168 | tf_op jit(solution)/shard_map/ppermute | solution.py:334
  270.7 20.7 %copy-start = (bf16[7,64,1024]{2,1,0:T(8,128)(2,1)S(1)}, bf16[7,64,1024]{2,1,0:T(8,128)(2,1)}, u32[]{:S(2)}) copy-start(bf16[7,64,1024]{2,1,0:T(8,128)(2,1)} %token_ref.1) | copy-start | bytes 2752516
  270.7 20.7 %copy-start.2 = (bf16[16,32,1024]{2,1,0:T(8,128)(2,1)S(1)}, bf16[16,32,1024]{2,1,0:T(8,128)(2,1)}, u32[]{:S(2)}) copy-start(bf16[16,32,1024]{2,1,0:T(8,128)(2,1)} %stage_three.3.near_ref) | copy-start | bytes 3145732
  295.4 1.9 collective-permute-start.40
  307.6 234.6 %collective-permute-start.41 = (bf16[3,7,64,512]{3,2,1,0:T(8,128)(2,1)}, bf16[3,7,64,512]{3,2,1,0:T(8,128)(2,1)}, u32[]{:S(2)}, u32[]{:S(2)}) collective-permute-start(bf16[3,7,64,512]{3,2,1,0:T(8,128)(2,1)} %get-tuple-element.61), channel_id=1, source_target_pairs={{0,1},{1,0},{2,3},{3,2},{4,5},{5,4},{6,7},{7,6},{8,9},{9,8},{10,11... | collective-permute-start | bytes 4128776 | tf_op jit(solution)/shard_map/ppermute | solution.py:413
  314.7 51.0 %collective-permute-start.1 = (bf16[3,7,8,512]{3,2,1,0:T(8,128)(2,1)}, bf16[3,7,8,512]{3,2,1,0:T(8,128)(2,1)S(1)}, u32[]{:S(2)}, u32[]{:S(2)}) collective-permute-start(bf16[3,7,8,512]{3,2,1,0:T(8,128)(2,1)} %payload.19), channel_id=1, source_target_pairs={{0,2},{2,0},{4,6},{6,4},{8,10},{10,8},{12,14},{14,12},{1,3},{3,1},... | collective-permute-start | bytes 516104 | tf_op jit(solution)/shard_map/ppermute | solution.py:334
  325.7 41.1 %collective-permute-start.3 = (bf16[3,7,8,512]{3,2,1,0:T(8,128)(2,1)}, bf16[3,7,8,512]{3,2,1,0:T(8,128)(2,1)S(1)}, u32[]{:S(2)}, u32[]{:S(2)}) collective-permute-start(bf16[3,7,8,512]{3,2,1,0:T(8,128)(2,1)} %payload.21), channel_id=1, source_target_pairs={{0,4},{2,6},{4,0},{6,2},{8,12},{10,14},{12,8},{14,10},{1,5},{3,7},... | collective-permute-start | bytes 516104 | tf_op jit(solution)/shard_map/ppermute | solution.py:334
  333.9 34.3 %collective-permute-start.5 = (bf16[3,7,8,512]{3,2,1,0:T(8,128)(2,1)}, bf16[3,7,8,512]{3,2,1,0:T(8,128)(2,1)S(1)}, u32[]{:S(2)}, u32[]{:S(2)}) collective-permute-start(bf16[3,7,8,512]{3,2,1,0:T(8,128)(2,1)} %payload.23), channel_id=1, source_target_pairs={{0,6},{2,4},{4,2},{6,0},{8,14},{10,12},{12,10},{14,8},{1,7},{3,5},... | collective-permute-start | bytes 516104 | tf_op jit(solution)/shard_map/ppermute | solution.py:334
  341.8 35.9 %collective-permute-start.7 = (bf16[3,7,8,512]{3,2,1,0:T(8,128)(2,1)}, bf16[3,7,8,512]{3,2,1,0:T(8,128)(2,1)S(1)}, u32[]{:S(2)}, u32[]{:S(2)}) collective-permute-start(bf16[3,7,8,512]{3,2,1,0:T(8,128)(2,1)} %payload.25), channel_id=1, source_target_pairs={{0,8},{2,10},{4,12},{6,14},{8,0},{10,2},{12,4},{14,6},{1,9},{3,11}... | collective-permute-start | bytes 516104 | tf_op jit(solution)/shard_map/ppermute | solution.py:334
  365.7 18.5 %copy-start.13 = (bf16[448,512]{1,0:T(8,128)(2,1)S(1)}, bf16[448,512]{1,0:T(8,128)(2,1)}, u32[]{:S(2)}) copy-start(bf16[448,512]{1,0:T(8,128)(2,1)} %copy-done.12) | copy-start | bytes 1376260
  365.7 18.5 %copy-start.15 = (s32[42]{0:T(128)S(1)}, s32[42]{0:T(128)}, u32[]{:S(2)}) copy-start(s32[42]{0:T(128)} %stack.171.spots_ref) | copy-start | bytes 508
  365.7 18.5 %collective-permute-start.9 = (bf16[3,7,8,512]{3,2,1,0:T(8,128)(2,1)}, bf16[3,7,8,512]{3,2,1,0:T(8,128)(2,1)S(1)}, u32[]{:S(2)}, u32[]{:S(2)}) collective-permute-start(bf16[3,7,8,512]{3,2,1,0:T(8,128)(2,1)} %payload.27), channel_id=1, source_target_pairs={{0,10},{2,8},{4,14},{6,12},{8,2},{10,0},{12,6},{14,4},{1,11},{3,9}... | collective-permute-start | bytes 516104 | tf_op jit(solution)/shard_map/ppermute | solution.py:334
  366.8 17.4 %collective-permute-start.11 = (bf16[3,7,8,512]{3,2,1,0:T(8,128)(2,1)}, bf16[3,7,8,512]{3,2,1,0:T(8,128)(2,1)S(1)}, u32[]{:S(2)}, u32[]{:S(2)}) collective-permute-start(bf16[3,7,8,512]{3,2,1,0:T(8,128)(2,1)} %payload.29), channel_id=1, source_target_pairs={{0,12},{2,14},{4,8},{6,10},{8,4},{10,6},{12,0},{14,2},{1,13},{3,15... | collective-permute-start | bytes 516104 | tf_op jit(solution)/shard_map/ppermute | solution.py:334
  368.2 16.0 %collective-permute-start.13 = (bf16[3,7,8,512]{3,2,1,0:T(8,128)(2,1)}, bf16[3,7,8,512]{3,2,1,0:T(8,128)(2,1)S(1)}, u32[]{:S(2)}, u32[]{:S(2)}) collective-permute-start(bf16[3,7,8,512]{3,2,1,0:T(8,128)(2,1)} %payload.31), channel_id=1, source_target_pairs={{0,14},{2,12},{4,10},{6,8},{8,6},{10,4},{12,2},{14,0},{1,15},{3,13... | collective-permute-start | bytes 516104 | tf_op jit(solution)/shard_map/ppermute | solution.py:334
  370.6 50.7 %copy-start.20 = (bf16[3,7,8,512]{3,2,1,0:T(8,128)(2,1)S(1)}, bf16[3,7,8,512]{3,2,1,0:T(8,128)(2,1)}, u32[]{:S(2)}) copy-start(bf16[3,7,8,512]{3,2,1,0:T(8,128)(2,1)} %copy-done.19) | copy-start | bytes 516100
  370.6 54.8 %copy-start.18 = (bf16[3,7,8,512]{3,2,1,0:T(8,128)(2,1)S(1)}, bf16[3,7,8,512]{3,2,1,0:T(8,128)(2,1)}, u32[]{:S(2)}) copy-start(bf16[3,7,8,512]{3,2,1,0:T(8,128)(2,1)} %copy-done.17) | copy-start | bytes 516100
  385.1 19.5 %copy-start.30 = (bf16[3,7,8,512]{3,2,1,0:T(8,128)(2,1)S(1)}, bf16[3,7,8,512]{3,2,1,0:T(8,128)(2,1)}, u32[]{:S(2)}) copy-start(bf16[3,7,8,512]{3,2,1,0:T(8,128)(2,1)} %copy-done.29) | copy-start | bytes 516100
  385.2 20.2 %copy-start.28 = (bf16[3,7,8,512]{3,2,1,0:T(8,128)(2,1)S(1)}, bf16[3,7,8,512]{3,2,1,0:T(8,128)(2,1)}, u32[]{:S(2)}) copy-start(bf16[3,7,8,512]{3,2,1,0:T(8,128)(2,1)} %copy-done.27) | copy-start | bytes 516100
  385.2 26.4 %copy-start.26 = (bf16[3,7,8,512]{3,2,1,0:T(8,128)(2,1)S(1)}, bf16[3,7,8,512]{3,2,1,0:T(8,128)(2,1)}, u32[]{:S(2)}) copy-start(bf16[3,7,8,512]{3,2,1,0:T(8,128)(2,1)} %copy-done.25) | copy-start | bytes 516100
  385.2 28.5 %copy-start.24 = (bf16[3,7,8,512]{3,2,1,0:T(8,128)(2,1)S(1)}, bf16[3,7,8,512]{3,2,1,0:T(8,128)(2,1)}, u32[]{:S(2)}) copy-start(bf16[3,7,8,512]{3,2,1,0:T(8,128)(2,1)} %copy-done.23) | copy-start | bytes 516100
  385.2 30.6 %copy-start.22 = (bf16[3,7,8,512]{3,2,1,0:T(8,128)(2,1)S(1)}, bf16[3,7,8,512]{3,2,1,0:T(8,128)(2,1)}, u32[]{:S(2)}) copy-start(bf16[3,7,8,512]{3,2,1,0:T(8,128)(2,1)} %copy-done.21) | copy-start | bytes 516100
  395.4 9.9 %collective-permute-start.21 = (bf16[3,7,8,512]{3,2,1,0:T(8,128)(2,1)S(1)}, bf16[3,7,8,512]{3,2,1,0:T(8,128)(2,1)S(1)}, u32[]{:S(2)}, u32[]{:S(2)}) collective-permute-start(bf16[3,7,8,512]{3,2,1,0:T(8,128)(2,1)S(1)} %get-tuple-element.37), channel_id=1, source_target_pairs={{0,2},{2,0},{4,6},{6,4},{8,10},{10,8},{12,14},{14,12},{1,3},{3,1},... | collective-permute-start | bytes 516104 | tf_op jit(solution)/shard_map/ppermute | solution.py:334
  396.0 15.5 %collective-permute-start.22 = (bf16[3,7,8,512]{3,2,1,0:T(8,128)(2,1)S(1)}, bf16[3,7,8,512]{3,2,1,0:T(8,128)(2,1)S(1)}, u32[]{:S(2)}, u32[]{:S(2)}) collective-permute-start(bf16[3,7,8,512]{3,2,1,0:T(8,128)(2,1)S(1)} %get-tuple-element.38), channel_id=1, source_target_pairs={{0,4},{2,6},{4,0},{6,2},{8,12},{10,14},{12,8},{14,10},{1,5},{3,7},... | collective-permute-start | bytes 516104 | tf_op jit(solution)/shard_map/ppermute | solution.py:334
  403.9 9.8 %collective-permute-start.23 = (bf16[3,7,8,512]{3,2,1,0:T(8,128)(2,1)S(1)}, bf16[3,7,8,512]{3,2,1,0:T(8,128)(2,1)S(1)}, u32[]{:S(2)}, u32[]{:S(2)}) collective-permute-start(bf16[3,7,8,512]{3,2,1,0:T(8,128)(2,1)S(1)} %get-tuple-element.39), channel_id=1, source_target_pairs={{0,6},{2,4},{4,2},{6,0},{8,14},{10,12},{12,10},{14,8},{1,7},{3,5},... | collective-permute-start | bytes 516104 | tf_op jit(solution)/shard_map/ppermute | solution.py:334
  404.7 11.1 %collective-permute-start.28 = (bf16[3,7,8,512]{3,2,1,0:T(8,128)(2,1)S(1)}, bf16[3,7,8,512]{3,2,1,0:T(8,128)(2,1)S(1)}, u32[]{:S(2)}, u32[]{:S(2)}) collective-permute-start(bf16[3,7,8,512]{3,2,1,0:T(8,128)(2,1)S(1)} %copy-done.30), channel_id=1, source_target_pairs={{0,2},{2,0},{4,6},{6,4},{8,10},{10,8},{12,14},{14,12},{1,3},{3,1},... | collective-permute-start | bytes 516104 | tf_op jit(solution)/shard_map/ppermute | solution.py:334
  405.3 92.7 %copy-start.40 = (bf16[3,7,8,512]{3,2,1,0:T(8,128)(2,1)}, bf16[3,7,8,512]{3,2,1,0:T(8,128)(2,1)S(1)}, u32[]{:S(2)}) copy-start(bf16[3,7,8,512]{3,2,1,0:T(8,128)(2,1)S(1)} %collective-permute-done.21.refs_1_) | copy-start | bytes 516100
  405.3 16.0 %collective-permute-start.29 = (bf16[3,7,8,512]{3,2,1,0:T(8,128)(2,1)S(1)}, bf16[3,7,8,512]{3,2,1,0:T(8,128)(2,1)S(1)}, u32[]{:S(2)}, u32[]{:S(2)}) collective-permute-start(bf16[3,7,8,512]{3,2,1,0:T(8,128)(2,1)S(1)} %copy-done.28), channel_id=1, source_target_pairs={{0,4},{2,6},{4,0},{6,2},{8,12},{10,14},{12,8},{14,10},{1,5},{3,7},... | collective-permute-start | bytes 516104 | tf_op jit(solution)/shard_map/ppermute | solution.py:334
  411.5 86.5 %copy-start.41 = (bf16[3,7,8,512]{3,2,1,0:T(8,128)(2,1)}, bf16[3,7,8,512]{3,2,1,0:T(8,128)(2,1)S(1)}, u32[]{:S(2)}) copy-start(bf16[3,7,8,512]{3,2,1,0:T(8,128)(2,1)S(1)} %collective-permute-done.22.refs_2_) | copy-start | bytes 516100
  411.5 13.9 %collective-permute-start.30 = (bf16[3,7,8,512]{3,2,1,0:T(8,128)(2,1)S(1)}, bf16[3,7,8,512]{3,2,1,0:T(8,128)(2,1)S(1)}, u32[]{:S(2)}, u32[]{:S(2)}) collective-permute-start(bf16[3,7,8,512]{3,2,1,0:T(8,128)(2,1)S(1)} %copy-done.26), channel_id=1, source_target_pairs={{0,6},{2,4},{4,2},{6,0},{8,14},{10,12},{12,10},{14,8},{1,7},{3,5},... | collective-permute-start | bytes 516104 | tf_op jit(solution)/shard_map/ppermute | solution.py:334
  413.6 84.4 %copy-start.42 = (bf16[3,7,8,512]{3,2,1,0:T(8,128)(2,1)}, bf16[3,7,8,512]{3,2,1,0:T(8,128)(2,1)S(1)}, u32[]{:S(2)}) copy-start(bf16[3,7,8,512]{3,2,1,0:T(8,128)(2,1)S(1)} %collective-permute-done.23.refs_3_) | copy-start | bytes 516100
  413.6 30.3 %collective-permute-start.31 = (bf16[3,7,8,512]{3,2,1,0:T(8,128)(2,1)S(1)}, bf16[3,7,8,512]{3,2,1,0:T(8,128)(2,1)S(1)}, u32[]{:S(2)}, u32[]{:S(2)}) collective-permute-start(bf16[3,7,8,512]{3,2,1,0:T(8,128)(2,1)S(1)} %copy-done.24), channel_id=1, source_target_pairs={{0,8},{2,10},{4,12},{6,14},{8,0},{10,2},{12,4},{14,6},{1,9},{3,11}... | collective-permute-start | bytes 516104 | tf_op jit(solution)/shard_map/ppermute | solution.py:334
  415.8 38.6 %copy-start.47 = (bf16[3,7,8,512]{3,2,1,0:T(8,128)(2,1)}, bf16[3,7,8,512]{3,2,1,0:T(8,128)(2,1)S(1)}, u32[]{:S(2)}) copy-start(bf16[3,7,8,512]{3,2,1,0:T(8,128)(2,1)S(1)} %collective-permute-done.28.refs_1_) | copy-start | bytes 516100
  415.8 33.6 %collective-permute-start.32 = (bf16[3,7,8,512]{3,2,1,0:T(8,128)(2,1)S(1)}, bf16[3,7,8,512]{3,2,1,0:T(8,128)(2,1)S(1)}, u32[]{:S(2)}, u32[]{:S(2)}) collective-permute-start(bf16[3,7,8,512]{3,2,1,0:T(8,128)(2,1)S(1)} %copy-done.22), channel_id=1, source_target_pairs={{0,10},{2,8},{4,14},{6,12},{8,2},{10,0},{12,6},{14,4},{1,11},{3,9}... | collective-permute-start | bytes 516104 | tf_op jit(solution)/shard_map/ppermute | solution.py:334
  421.3 33.1 %copy-start.48 = (bf16[3,7,8,512]{3,2,1,0:T(8,128)(2,1)}, bf16[3,7,8,512]{3,2,1,0:T(8,128)(2,1)S(1)}, u32[]{:S(2)}) copy-start(bf16[3,7,8,512]{3,2,1,0:T(8,128)(2,1)S(1)} %collective-permute-done.29.refs_2_) | copy-start | bytes 516100
  421.4 28.8 %collective-permute-start.33 = (bf16[3,7,8,512]{3,2,1,0:T(8,128)(2,1)S(1)}, bf16[3,7,8,512]{3,2,1,0:T(8,128)(2,1)S(1)}, u32[]{:S(2)}, u32[]{:S(2)}) collective-permute-start(bf16[3,7,8,512]{3,2,1,0:T(8,128)(2,1)S(1)} %copy-done.20), channel_id=1, source_target_pairs={{0,12},{2,14},{4,8},{6,10},{8,4},{10,6},{12,0},{14,2},{1,13},{3,15... | collective-permute-start | bytes 516104 | tf_op jit(solution)/shard_map/ppermute | solution.py:334
  425.4 25.4 %copy-start.49 = (bf16[3,7,8,512]{3,2,1,0:T(8,128)(2,1)}, bf16[3,7,8,512]{3,2,1,0:T(8,128)(2,1)S(1)}, u32[]{:S(2)}) copy-start(bf16[3,7,8,512]{3,2,1,0:T(8,128)(2,1)S(1)} %collective-permute-done.30.refs_3_) | copy-start | bytes 516100
  425.4 25.4 %collective-permute-start.34 = (bf16[3,7,8,512]{3,2,1,0:T(8,128)(2,1)S(1)}, bf16[3,7,8,512]{3,2,1,0:T(8,128)(2,1)S(1)}, u32[]{:S(2)}, u32[]{:S(2)}) collective-permute-start(bf16[3,7,8,512]{3,2,1,0:T(8,128)(2,1)S(1)} %copy-done.18), channel_id=1, source_target_pairs={{0,14},{2,12},{4,10},{6,8},{8,6},{10,4},{12,2},{14,0},{1,15},{3,13... | collective-permute-start | bytes 516104 | tf_op jit(solution)/shard_map/ppermute | solution.py:334
  444.7 53.2 %collective-permute-start.24 = (bf16[3,7,8,512]{3,2,1,0:T(8,128)(2,1)}, bf16[3,7,8,512]{3,2,1,0:T(8,128)(2,1)S(1)}, u32[]{:S(2)}, u32[]{:S(2)}) collective-permute-start(bf16[3,7,8,512]{3,2,1,0:T(8,128)(2,1)} %get-tuple-element.40), channel_id=1, source_target_pairs={{0,8},{2,10},{4,12},{6,14},{8,0},{10,2},{12,4},{14,6},{1,9},{3,11}... | collective-permute-start | bytes 516104 | tf_op jit(solution)/shard_map/ppermute | solution.py:334
  450.1 47.8 %collective-permute-start.25 = (bf16[3,7,8,512]{3,2,1,0:T(8,128)(2,1)}, bf16[3,7,8,512]{3,2,1,0:T(8,128)(2,1)S(1)}, u32[]{:S(2)}, u32[]{:S(2)}) collective-permute-start(bf16[3,7,8,512]{3,2,1,0:T(8,128)(2,1)} %get-tuple-element.41), channel_id=1, source_target_pairs={{0,10},{2,8},{4,14},{6,12},{8,2},{10,0},{12,6},{14,4},{1,11},{3,9}... | collective-permute-start | bytes 516104 | tf_op jit(solution)/shard_map/ppermute | solution.py:334
  450.8 47.2 %collective-permute-start.26 = (bf16[3,7,8,512]{3,2,1,0:T(8,128)(2,1)}, bf16[3,7,8,512]{3,2,1,0:T(8,128)(2,1)S(1)}, u32[]{:S(2)}, u32[]{:S(2)}) collective-permute-start(bf16[3,7,8,512]{3,2,1,0:T(8,128)(2,1)} %get-tuple-element.42), channel_id=1, source_target_pairs={{0,12},{2,14},{4,8},{6,10},{8,4},{10,6},{12,0},{14,2},{1,13},{3,15... | collective-permute-start | bytes 516104 | tf_op jit(solution)/shard_map/ppermute | solution.py:334
  451.5 46.5 %collective-permute-start.27 = (bf16[3,7,8,512]{3,2,1,0:T(8,128)(2,1)}, bf16[3,7,8,512]{3,2,1,0:T(8,128)(2,1)S(1)}, u32[]{:S(2)}, u32[]{:S(2)}) collective-permute-start(bf16[3,7,8,512]{3,2,1,0:T(8,128)(2,1)} %get-tuple-element.43), channel_id=1, source_target_pairs={{0,14},{2,12},{4,10},{6,8},{8,6},{10,4},{12,2},{14,0},{1,15},{3,13... | collective-permute-start | bytes 516104 | tf_op jit(solution)/shard_map/ppermute | solution.py:334
  (32 other events, 67.3 us)

commit v3 on v1

--- a/solution.py
+++ b/solution.py
@@ -107,52 +107,342 @@
     return done.transpose(2, 0, 3, 1, 4)
 
 
-def space_kernel(core_ref, q_ref, k_ref, v_ref, g_ref, qkv_ref, grad_ref, *outs):
-    own_outs, send_ref = outs[:3], outs[3]
-    rows, lanes = q_ref.shape[1:]
-    own = (q_ref, k_ref, v_ref, g_ref)
-    for pair in range(lanes // PAIR):
-        columns = slice(pair * PAIR, (pair + 1) * PAIR)
-        operands = []
-        for index in range(4):
-            near = own[index][0, :, columns].astype(F32)
-            far = (qkv_ref[index, 0] if index < 3 else grad_ref[0])[:, columns].astype(F32)
-            operands.append(jnp.concatenate([near, far], axis=0))
-        done = pair_back(*operands)
-        for index in range(3):
-            value = done[index].astype(BF16)
-            own_outs[index][0, :, columns] = value[:rows]
-            send_ref[index, 0, :, columns] = value[rows:]
-
-
-def space_attention(core, query, keys, values, grad, far_qkv, far_grad):
-    frames, rows, width = query.shape
-    half = width // 2
-    mine = pl.BlockSpec((1, rows, half), lambda f, core_ref: (f, 0, core_ref[0]))
-    far = pl.BlockSpec((1, rows, half), lambda f, core_ref: (f, 0, 0))
-    far3 = pl.BlockSpec((3, 1, rows, half), lambda f, core_ref: (0, f, 0, 0))
-    own_shape = jax.ShapeDtypeStruct((frames, rows, half), BF16)
+def own_back(queries, keys, values, grads):
+    rows = queries[0].shape[0]
+    first = lax.broadcasted_iota(jnp.int32, (rows, PAIR), 1) < HEAD_DIM
+    zero = jnp.zeros((rows, PAIR), F32)
+
+    def stacked(parts):
+        both = []
+        for part in parts:
+            both += [jnp.where(first, part, zero), jnp.where(first, zero, part)]
+        return jnp.concatenate(both, axis=0).astype(BF16)
+
+    query2, grad2 = stacked(queries), stacked(grads)
+    keys = jnp.concatenate(keys, axis=0).astype(BF16)
+    values = jnp.concatenate(values, axis=0).astype(BF16)
+    scores = dot(keys, query2, ((1,), (1,))) * SCALE
+    expo = jnp.exp(scores - jnp.max(scores, axis=0, keepdims=True))
+    probs = expo * (1.0 / jnp.sum(expo, axis=0, keepdims=True))
+    dprob = dot(values, grad2, ((1,), (1,)))
+    delta = jnp.sum(probs * dprob, axis=0, keepdims=True)
+    dscore = (probs * (dprob - delta)).astype(BF16)
+    grad_values = dot(probs[:rows].astype(BF16), grad2, ((1,), (0,)))
+    grad_keys = dot(dscore[:rows], query2, ((1,), (0,))) * SCALE
+    both = dot(dscore[:, : 2 * rows], keys, ((0,), (0,))) * SCALE
+    grad_query = jnp.where(first, both[:rows], both[rows:])
+    return grad_query, grad_keys, grad_values
+
+
+HBM = pl.BlockSpec(memory_space=pltpu.HBM)
+SCALARS = pl.BlockSpec(memory_space=pltpu.SMEM)
+BIG = pltpu.CompilerParams(vmem_limit_bytes=48 * 2**20)
+
+
+def cost_of(microseconds):
+    return pl.CostEstimate(flops=0, transcendentals=0, bytes_accessed=int(microseconds * 3_690_000))
+
+
+def run_copies(sems, pairs):
+    copies = [pltpu.make_async_copy(src, dst, sems.at[i]) for i, (src, dst) in enumerate(pairs)]
+    for copy in copies:
+        copy.start()
+    return copies
+
+
+def run_staged(pairs):
+    count = len(pairs)
+
+    def body(*scratch):
+        stages, arrived, left = scratch[:count], scratch[count], scratch[count + 1]
+        loads = run_copies(arrived, [(src, stage) for (src, _), stage in zip(pairs, stages)])
+        stores = []
+        for index, (load, (_, dst)) in enumerate(zip(loads, pairs)):
+            load.wait()
+            stores.append(pltpu.make_async_copy(stages[index], dst, left.at[index]))
+            stores[-1].start()
+        for store in stores:
+            store.wait()
+
+    sems = [pltpu.SemaphoreType.DMA((count,))] * 2
+    pl.run_scoped(body, *[pltpu.VMEM(src.shape, BF16) for src, _ in pairs], *sems)
+
+
+def moved(spots, parts, shapes, plan, name, after=(), kept=()):
+    count = len(parts)
+
+    def kernel(spots_ref, *refs):
+        run_staged(plan(spots_ref, refs[:count], refs[len(refs) - len(shapes) :]))
+
     return pl.pallas_call(
-        space_kernel,
+        kernel,
+        in_specs=[SCALARS] + [HBM] * (count + len(after) + len(kept)),
+        out_specs=[HBM] * len(shapes),
+        out_shape=[jax.ShapeDtypeStruct(shape, BF16) for shape in shapes],
+        input_output_aliases={1 + count + len(after) + i: i for i in range(len(kept))},
+        compiler_params=BIG,
+        name=name,
+    )(spots, *parts, *after, *kept)
+
+
+def weight_copies(gathered_ref, weights):
+    space, groups, tm = gathered_ref.shape[:3]
+    return [
+        (gathered_ref.at[s, g, t], weights.at[(t * space + s) * groups + g])
+        for t in range(tm)
+        for s in range(space)
+        for g in range(groups)
+    ]
+
+
+def attend_pair(held, results, patches, total):
+    for patch in range(patches):
+        rows = pl.ds(patch, total, stride=patches)
+        done = pair_back(*[ref[rows, :] for ref in held])
+        for ref, value in zip(results, done):
+            ref[rows, :] = value
+
+
+def time_chunk(blocks, gathered, late_grad, name):
+    count = len(blocks)
+    first = late_grad is None
+    _, frames, patches, lanes = blocks[0].shape
+    total, part = count * frames, frames * patches
+    rows, width = total * patches, 2 * lanes
+    wide = [pltpu.VMEM(block.shape, BF16) for block in blocks]
+    scratch = wide + [pltpu.VMEM((3, frames, patches, lanes), BF16)] * count
+    scratch += [pltpu.VMEM((rows, PAIR), F32)] * 7
+    if first:
+        space, groups, tm, share = gathered.shape[:4]
+        scratch += [pltpu.VMEM((rows, width), BF16), pltpu.VMEM((space * groups * tm, share, width), BF16)]
+        operands = (gathered,)
+        copied = count + space * groups * tm
+    else:
+        scratch += [pltpu.VMEM((rows, lanes), BF16)]
+        operands = (late_grad,)
+        copied = count + 1
+    scratch += [pltpu.SemaphoreType.DMA((copied,)), pltpu.SemaphoreType.DMA((count,))]
+
+    def kernel(*refs):
+        refs = list(refs)
+
+        def take(number):
+            taken, refs[:number] = refs[:number], []
+            return taken
+
+        block_refs, extra_ref, out_refs = take(count), take(1)[0], take(count)
+        later_ref = take(1)[0] if first else None
+        blocks_in, results_out = take(count), take(count)
+        held, results = take(4), take(3)
+        grads = take(1)[0]
+        weights = take(1)[0] if first else None
+        arrived, left = refs
+        pairs = list(zip(block_refs, blocks_in))
+        pairs += weight_copies(extra_ref, weights) if first else [(extra_ref, grads)]
+        for copy in run_copies(arrived, pairs):
+            copy.wait()
+        if first:
+            for index, ref in enumerate(blocks_in):
+                at = slice(index * part, (index + 1) * part)
+                for side in range(2):
+                    value = ref[3 + side].astype(F32).reshape(part, lanes)
+                    grads[at, side * lanes : (side + 1) * lanes] = value.astype(BF16)
+
+        def one_pair(pair, carry):
+            columns = pl.ds(pl.multiple_of(pair * PAIR, PAIR), PAIR)
+            for index, ref in enumerate(blocks_in):
+                at = slice(index * part, (index + 1) * part)
+                for kind in range(3):
+                    held[kind][at, :] = ref[kind, :, :, columns].astype(F32).reshape(part, PAIR)
+            if first:
+                pieces = weights[pl.ds(pair * (PAIR // share), PAIR // share)].reshape(PAIR, width)
+                held[3][...] = dot(grads[...], pieces, ((1,), (1,))).astype(BF16).astype(F32)
+            else:
+                held[3][...] = grads[:, columns].astype(F32)
+            attend_pair(held, results, patches, total)
+            for index, ref in enumerate(results_out):
+                at = slice(index * part, (index + 1) * part)
+                for kind in range(3):
+                    value = results[kind][at, :].reshape(frames, patches, PAIR)
+                    ref[kind, :, :, columns] = value.astype(BF16)
+            return carry
+
+        lax.fori_loop(0, lanes // PAIR, one_pair, 0)
+        stores = run_copies(left, list(zip(results_out, out_refs)))
+        if first:
+            half = weights.shape[0] // 2
+            later = weights[half:].reshape(lanes, width)
+            later_ref[...] = dot(grads[...], later, ((1,), (1,))).astype(BF16)
+        for store in stores:
+            store.wait()
+
+    out_shapes = [jax.ShapeDtypeStruct((3, frames, patches, lanes), BF16)] * count
+    out_specs = [HBM] * count
+    if first:
+        out_shapes = out_shapes + [jax.ShapeDtypeStruct((rows, lanes), BF16)]
+        out_specs = out_specs + [pl.BlockSpec(memory_space=pltpu.VMEM)]
+    return pl.pallas_call(
+        kernel,
+        in_specs=[HBM] * (count + 1),
+        out_specs=out_specs,
+        out_shape=out_shapes,
+        scratch_shapes=scratch,
+        compiler_params=BIG,
+        cost_estimate=cost_of(16 if first else 10),
+        name=name,
+    )(*blocks, *operands)
+
+
+def space_attention(spots, core_at, own, far, own_tokens, far_tokens, weights_of, after=()):
+    frames, rows, width = own_tokens.shape
+    space, groups, tm, share = weights_of.shape[:4]
+    pieces = space * groups * tm
+
+    def kernel(spots_ref, *refs):
+        own_refs, far_refs = refs[:3], refs[3:6]
+        token_refs, gathered_ref = refs[6:8], refs[8]
+        outs = refs[9 + len(after) : 12 + len(after)]
+        weights, grads, sems = refs[12 + len(after) :]
+
+        @pl.when(pl.program_id(0) == 0)
+        def _():
+            for copy in run_copies(sems, weight_copies(gathered_ref, weights)):
+                copy.wait()
+            whole = weights[...].reshape(width, width)
+            for side in range(2):
+                flat = (token_refs[0][...] if side == 0 else token_refs[1][0]).reshape(frames * rows, width)
+                made = dot(flat, whole, ((1,), (1,))).astype(BF16)
+                grads[side] = made.reshape(frames, rows, width)
+
+        frame = pl.program_id(0)
+        for pair in range(width // PAIR):
+            columns = slice(pair * PAIR, (pair + 1) * PAIR)
+            operands = [
+                (near[0, :, columns].astype(F32), away[0, 0, :, columns].astype(F32))
+                for near, away in zip(own_refs, far_refs)
+            ]
+            operands.append(tuple(grads[side, frame, :, columns].astype(F32) for side in range(2)))
+            for out, value in zip(outs, own_back(*operands)):
+                out[0, :, columns] = value.astype(BF16)
+
+    near = pl.BlockSpec((1, rows, width), lambda f, spots_ref: (f, 0, 0))
+    away = pl.BlockSpec((1, 1, rows, width), lambda f, spots_ref: (1 - spots_ref[core_at], f, 0, 0))
+    near_all = pl.BlockSpec((frames, rows, width), lambda f, spots_ref: (0, 0, 0))
+    away_all = pl.BlockSpec((1, frames, rows, width), lambda f, spots_ref: (1 - spots_ref[core_at], 0, 0, 0))
+    return pl.pallas_call(
+        kernel,
         grid_spec=pltpu.PrefetchScalarGridSpec(
             num_scalar_prefetch=1,
             grid=(frames,),
-            in_specs=[mine] * 4 + [far3, far],
-            out_specs=[far] * 3 + [far3],
+            in_specs=[near] * 3 + [away] * 3 + [near_all, away_all] + [HBM] * (1 + len(after)),
+            out_specs=[near] * 3,
+            scratch_shapes=[
+                pltpu.VMEM((pieces, share, width), BF16),
+                pltpu.VMEM((2, frames, rows, width), BF16),
+                pltpu.SemaphoreType.DMA((pieces,)),
+            ],
         ),
-        out_shape=[own_shape] * 3 + [jax.ShapeDtypeStruct((3, frames, rows, half), BF16)],
-        compiler_params=pltpu.CompilerParams(vmem_limit_bytes=40 * 2**20),
+        out_shape=[jax.ShapeDtypeStruct((frames, rows, width), BF16)] * 3,
+        compiler_params=BIG,
+        cost_estimate=cost_of(20),
         name="space_attention",
-    )(core.reshape(1), query, keys, values, grad, far_qkv, far_grad)
+    )(spots, *own, *far, own_tokens, far_tokens, weights_of, *after)
 
 
 def per_device(sizes, grad_out, time_q, time_k, time_v, space_q, space_k, space_v, time_wo, space_wo):
     frames, rows, width = grad_out.shape
     groups, tm, space = sizes
+    patches, half = rows // tm, width // 2
+    group, me, core = (lax.axis_index(name) for name in ("groups", "tm", "space"))
+    share = time_wo.shape[0] // groups
+    spots = jnp.concatenate([me ^ jnp.arange(tm, dtype=jnp.int32), core.reshape(1)]).astype(jnp.int32)
+    core_at = tm
+    order = []
+    for low in range(tm // 2):
+        order += [tm // 2 - 1 - low, tm - 1 - low]
+
+    def to_partner(tensor, k):
+        return lax.ppermute(tensor, "tm", [(i, i ^ k) for i in range(tm)]) if k else tensor
+
+    def cut(tensor):
+        return lax.dynamic_slice_in_dim(tensor, group * share, share, 0)
+
+    def gathered(piece):
+        whole = lax.all_gather(piece, ("space", "groups", "tm"), axis=0, tiled=True)
+        return whole.reshape(space, groups, tm, share, width)
+
+    time_weights = gathered(cut(time_wo))
+
+    split = [t.reshape(frames, tm, patches, width) for t in (time_q, time_k, time_v, grad_out)]
+
+    def payloads(chunk, after=()):
+        def plan(at, parts, outs):
+            columns = pl.ds(chunk * half, half)
+            pairs = []
+            for k in order:
+                pairs += [(part.at[:, at[k], :, columns], outs[k].at[i]) for i, part in enumerate(parts[:3])]
+                if chunk == 0:
+                    for side in range(2):
+                        side_columns = pl.ds(side * half, half)
+                        pairs.append((parts[3].at[:, at[k], :, side_columns], outs[k].at[3 + side]))
+            return pairs
+
+        kinds = 5 if chunk == 0 else 3
+        shapes = [(kinds, frames, patches, half)] * tm
+        return moved(spots, split[: 4 - chunk], shapes, plan, "payloads", after)
+
+    def exchange(tensors):
+        arrived = {k: to_partner(tensors[k], k) for k in order}
+        return [arrived[k] for k in range(tm)]
+
+    first_sent = payloads(0)
+    early = exchange(first_sent)
+
+    late = exchange(payloads(1, (first_sent[0],)))
+
+    far = [lax.all_gather(tensor, "space", axis=0) for tensor in (space_q, space_k, space_v, grad_out)]
+    space_weights = gathered(cut(space_wo))
+
+    *done, late_grad = time_chunk(early, time_weights, None, "time_first")
+    back = exchange(done)
+    done = time_chunk(late, None, late_grad, "time_second")
+    back2 = exchange(done)
+
+    space_out = space_attention(
+        spots,
+        core_at,
+        (space_q, space_k, space_v),
+        far[:3],
+        grad_out,
+        far[3],
+        space_weights,
+        (late_grad,),
+    )
+
+    def place(chunk):
+        def plan(at, refs, outs):
+            columns = pl.ds(chunk * half, half)
+            return [
+                (ref.at[kind], outs[kind].at[:, at[k], :, columns])
+                for k, ref in enumerate(refs)
+                for kind in range(3)
+            ]
+
+        return plan
+
+    shapes = [(frames, tm, patches, width)] * 3
+    outs = moved(spots, back, shapes, place(0), "place_first")
+    outs = moved(spots, back2, shapes, place(1), "place_second", space_out, outs)
+    time_out = [out.reshape(frames, rows, width) for out in outs]
+    return (*time_out, *space_out)
+
+
+def per_device_plain(sizes, grad_out, time_q, time_k, time_v, space_q, space_k, space_v, time_wo, space_wo):
+    frames, rows, width = grad_out.shape
+    groups, tm, space = sizes
     patches = rows // tm
-    half = width // 2
     core = lax.axis_index("space")
-    swap = [(0, 1), (1, 0)]
+    spots = core.reshape(1).astype(jnp.int32)
 
     def to_patches(tensor):
         split = tensor.reshape(tensor.shape[:-2] + (tm, patches, width))
@@ -171,28 +461,13 @@
     else:
         whole = lax.all_gather(both_wo, ("tm", "space"), axis=0, tiled=True)
 
-    def other_half(tensor):
-        return lax.dynamic_slice_in_dim(tensor, (1 - core) * half, half, tensor.ndim - 1)
-
-    far_qkv = lax.ppermute(jnp.stack([other_half(t) for t in (space_q, space_k, space_v)]), "space", swap)
-
+    far = [lax.all_gather(tensor, "space", axis=0) for tensor in (space_q, space_k, space_v, grad_out)]
     tokens = grad_out.reshape(frames * rows, width)
     time_grad = jnp.einsum("td,cd->tc", tokens, whole[:, :width], preferred_element_type=F32)
     time_grad = exchanged(to_patches(time_grad.astype(BF16).reshape(frames, rows, width)))
-    space_grad = jnp.einsum("td,cd->tc", tokens, whole[:, width:], preferred_element_type=F32)
-    space_grad = space_grad.astype(BF16).reshape(frames, rows, width)
-    far_grad = lax.ppermute(other_half(space_grad), "space", swap)
-
-    *own, send = space_attention(core, space_q, space_k, space_v, space_grad, far_qkv, far_grad)
-    far = lax.ppermute(send, "space", swap)
-    space_out = [
-        jnp.where(
-            core == 0,
-            jnp.concatenate([own[index], far[index]], axis=-1),
-            jnp.concatenate([far[index], own[index]], axis=-1),
-        )
-        for index in range(3)
-    ]
+    pieces = whole[:, width:].reshape(tm, space, -1, 1, width)
+    pieces = jnp.moveaxis(pieces.reshape(tm, space, 1, -1, width), 0, 2)
+    space_out = space_attention(spots, 0, (space_q, space_k, space_v), far[:3], grad_out, far[3], pieces)
 
     back = exchanged(time_attention(time_qkv, time_grad))
     time_out = [jnp.moveaxis(back[:, index], 0, 1).reshape(frames, rows, width) for index in range(3)]
@@ -203,8 +478,16 @@
     tokens = P(("groups", "tm"), "space", None)
     weights = P(("tm", "space"), None)
     sizes = tuple(mesh.shape[name] for name in ("groups", "tm", "space"))
+    groups, tm, space = sizes
+    paired = groups == 2 and space == 2 and tm % 2 == 0 and tm & (tm - 1) == 0
+
+    def body(*tensors):
+        patches, rows = tensors[0].shape[1] // tm, tensors[-1].shape[0]
+        fits = paired and patches % 8 == 0 and rows % (16 * groups) == 0
+        return (per_device if fits else per_device_plain)(sizes, *tensors)
+
     return jax.shard_map(
-        functools.partial(per_device, sizes),
+        body,
         mesh=mesh,
         in_specs=(tokens,) * 7 + (weights,) * 2,
         out_specs=(tokens,) * 6,

time: 240 us -> 259 us (1.079)
  starting transfers between devices: 12.1 us -> 60.4 us
  waiting for transfers between devices: 134 us -> 93.7 us
  Pallas kernels: 27 us -> 65.7 us
  blocking collectives: 27.6 us -> 0 us
  local copies, waits for them, and re-layouts: 11.1 us -> 23.9 us
  other arithmetic: 8.93 us -> 0.08 us
  matrix products: 3.89 us -> 0 us
    all_gather x1 -> x6, waiting for transfers between devices: 93.6 us -> 17.5 us  [the longest x2 17.5 us: gathered(): whole = lax.all_gather(piece, ('space', 'groups', 'tm'), axis=0, tiled=True)]
    ppermute x3 -> x28, waiting for transfers between devices: 5.13 us -> 73.7 us  [to_partner(): lax.ppermute(tensor, 'tm', [(i, i ^ k) for i in range(tm)])]
    ppermute x3 -> x28, starting transfers between devices: 0.28 us -> 60.2 us  [to_partner(): lax.ppermute(tensor, 'tm', [(i, i ^ k) for i in range(tm)])]
    pallas_call x2 -> x7, Pallas kernels: 27 us -> 65.7 us  [the longest x2 29.2 us: time_chunk(): pl.pallas_call(kernel, in_specs=[HBM] * (count + 1), out_specs=out_specs,...]
    all_to_all x2 -> x0, waiting for transfers between devices: 35.7 us -> none  [exchanged(): return lax.all_to_all(tensor, 'tm', split_axis=0, concat_axis=0, tiled=True)]
    all_to_all x1 -> x0, blocking collectives: 27.6 us -> none  [exchanged(): return lax.all_to_all(tensor, 'tm', split_axis=0, concat_axis=0, tiled=True)]
    unnamed x20 -> x96, local copies, waits for them, and re-layouts: 3.94 us -> 22.6 us
    all_to_all x2 -> x0, starting transfers between devices: 11.8 us -> none  [exchanged(): return lax.all_to_all(tensor, 'tm', split_axis=0, concat_axis=0, tiled=True)]
  transfers between devices with their start and end apart: 6 -> 34, of which waited for: 5 -> 11; matrix products, arithmetic and copies ran while one was open for 6% -> 0% of each run, Pallas kernels for 4% -> 24%
where the time goes in v3:
time: 259 us; the launch traced here: 258 us
  waiting for transfers between devices  93.7 us (36%)
  Pallas kernels  65.7 us (25%)
  starting transfers between devices  60.4 us (23%)
  local copies, waits for them, and re-layouts  23.9 us (9%)
  between operations  14.5 us (6%)
    ppermute x28, waiting for transfers between devices, to_partner(): lax.ppermute(tensor, 'tm', [(i, i ^ k) for i in range(tm)])  73.7 us
    ppermute x28, starting transfers between devices, to_partner(): lax.ppermute(tensor, 'tm', [(i, i ^ k) for i in range(tm)])  60.2 us
    pallas_call x2, Pallas kernels, time_chunk(): pl.pallas_call(kernel, in_specs=[HBM] * (count + 1), out_specs=out_specs,...  29.2 us
    pallas_call x1, Pallas kernels, space_attention(): pl.pallas_call(kernel, grid_spec=pltpu.PrefetchScalarGridSpec(num_scalar_...  23.5 us
    unnamed x96, local copies, waits for them, and re-layouts  22.6 us
    all_gather x2, waiting for transfers between devices, gathered(): whole = lax.all_gather(piece, ('space', 'groups', 'tm'), axis=0, tiled=True)  17.5 us
    pallas_call x4, Pallas kernels, moved(): pl.pallas_call(kernel, in_specs=[SCALARS] + [HBM] * (count + len(after) +...  13 us
  transfers between devices with their start and end apart: 34, of which 11 were waited for; matrix products, arithmetic and copies ran while one was open for 0% of the time, Pallas kernels for 24%

profile of v3, /device:TPU:0, one launch (start us, length us, event | category | flops | bytes accessed | tf_op | source)
XLA Modules:
  0.0 258.4 jit_solution(14253145299503420817)
XLA Ops:
  7.2 0.8 copy-done
  8.1 0.6 constant_dynamic-slice_fusion.1
  8.8 0.7 all-gather.15.cloned.1.call-update
  9.6 0.7 all-gather.17.cloned.1.call-update
  10.3 0.5 all-gather.19.cloned.1.call-update
  10.9 0.5 all-gather.21.cloned.1.call-update
  11.5 0.6 constant_dynamic-slice_fusion
  12.3 1.2 copy-done.7
  13.4 4.2 %payloads.2 = (bf16[5,7,8,512]{3,2,1,0:T(8,128)(2,1)S(1)}, bf16[5,7,8,512]{3,2,1,0:T(8,128)(2,1)S(1)}, bf16[5,7,8,512]{3,2,1,0:T(8,128)(2,1)S(1)}, bf16[5,7,8,51...) custom-call(s32[9]{0:T(128)S(1)} %pad_add_fusion.spots_ref, ...), custom_call_target="tpu_custom_call" | custom-call | tf_op jit(solution)/shard_map/payloads/pallas_call | solution.py:177
  17.7 3.0 %collective-permute-start.7 = (bf16[5,7,8,512]{3,2,1,0:T(8,128)(2,1)S(1)}, bf16[5,7,8,512]{3,2,1,0:T(8,128)(2,1)S(1)}, u32[]{:S(2)}, u32[]{:S(2)}) collective-permute-start(bf16[5,7,8,512]{3,2,1,0:T(8,128)(2,1)S(1)} %get-tuple-element.57), channel_id=1, source_target_pairs={{0,2},{2,0},{4,6},{6,4},{8,10},{10,8},{12,14},{14,12},{1,3},{3,1},... | collective-permute-start | bytes 860168 | tf_op jit(solution)/shard_map/ppermute | solution.py:365
  20.7 1.6 collective-permute-start.8
  22.3 2.2 payloads.3
  24.5 0.7 copy-done.25
  25.7 3.0 %collective-permute-start.9 = (bf16[5,7,8,512]{3,2,1,0:T(8,128)(2,1)S(1)}, bf16[5,7,8,512]{3,2,1,0:T(8,128)(2,1)S(1)}, u32[]{:S(2)}, u32[]{:S(2)}) collective-permute-start(bf16[5,7,8,512]{3,2,1,0:T(8,128)(2,1)S(1)} %get-tuple-element.59), channel_id=1, source_target_pairs={{0,6},{2,4},{4,2},{6,0},{8,14},{10,12},{12,10},{14,8},{1,7},{3,5},... | collective-permute-start | bytes 860168 | tf_op jit(solution)/shard_map/ppermute | solution.py:365
  28.6 3.1 %collective-permute-done.refs_1_ = bf16[3,7,8,512]{3,2,1,0:T(8,128)(2,1)S(1)} collective-permute-done((bf16[3,7,8,512]{3,2,1,0:T(8,128)(2,1)S(1)}, bf16[3,7,8,512]{3,2,1,0:T(8,128)(2,1)S(1)}, u32[]{:S(2)}, u32[]{:S(2)}) %collective-permute-start) | collective-permute-done | bytes 172064 | tf_op jit(solution)/shard_map/ppermute | solution.py:365
  31.7 0.6 copy-done.27
  32.4 2.8 %collective-permute-start.10 = (bf16[5,7,8,512]{3,2,1,0:T(8,128)(2,1)S(1)}, bf16[5,7,8,512]{3,2,1,0:T(8,128)(2,1)S(1)}, u32[]{:S(2)}, u32[]{:S(2)}) collective-permute-start(bf16[5,7,8,512]{3,2,1,0:T(8,128)(2,1)S(1)} %get-tuple-element.60), channel_id=1, source_target_pairs={{0,8},{2,10},{4,12},{6,14},{8,0},{10,2},{12,4},{14,6},{1,9},{3,11}... | collective-permute-start | bytes 860168 | tf_op jit(solution)/shard_map/ppermute | solution.py:365
  35.2 6.4 %collective-permute-done.1.refs_2_ = bf16[3,7,8,512]{3,2,1,0:T(8,128)(2,1)S(1)} collective-permute-done((bf16[3,7,8,512]{3,2,1,0:T(8,128)(2,1)S(1)}, bf16[3,7,8,512]{3,2,1,0:T(8,128)(2,1)S(1)}, u32[]{:S(2)}, u32[]{:S(2)}) %collective-permute-start.1) | collective-permute-done | bytes 172064 | tf_op jit(solution)/shard_map/ppermute | solution.py:365
  41.5 0.7 copy-done.29
  42.2 0.7 copy-done.15
  42.9 1.4 collective-permute-start.12
  44.3 0.7 copy-done.17
  45.1 2.3 collective-permute-done.9.refs_3_
  47.3 0.7 collective-permute-start.2
  48.0 21.2 %collective-permute-done.10.refs_4_ = bf16[5,7,8,512]{3,2,1,0:T(8,128)(2,1)S(1)} collective-permute-done((bf16[5,7,8,512]{3,2,1,0:T(8,128)(2,1)S(1)}, bf16[5,7,8,512]{3,2,1,0:T(8,128)(2,1)S(1)}, u32[]{:S(2)}, u32[]{:S(2)}) %collective-permute-start.10) | collective-permute-done | bytes 286752 | tf_op jit(solution)/shard_map/ppermute | solution.py:365
  69.2 14.2 %collective-permute-done.11.refs_5_ = bf16[5,7,8,512]{3,2,1,0:T(8,128)(2,1)S(1)} collective-permute-done((bf16[5,7,8,512]{3,2,1,0:T(8,128)(2,1)S(1)}, bf16[5,7,8,512]{3,2,1,0:T(8,128)(2,1)S(1)}, u32[]{:S(2)}, u32[]{:S(2)}) %collective-permute-start.11) | collective-permute-done | bytes 286752 | tf_op jit(solution)/shard_map/ppermute | solution.py:365
  83.4 14.6 %collective-permute-start.5 = (bf16[3,7,8,512]{3,2,1,0:T(8,128)(2,1)}, bf16[3,7,8,512]{3,2,1,0:T(8,128)(2,1)}, u32[]{:S(2)}, u32[]{:S(2)}) collective-permute-start(bf16[3,7,8,512]{3,2,1,0:T(8,128)(2,1)} %get-tuple-element.55), channel_id=1, source_target_pairs={{0,12},{2,14},{4,8},{6,10},{8,4},{10,6},{12,0},{14,2},{1,13},{3,15... | collective-permute-start | bytes 516104 | tf_op jit(solution)/shard_map/ppermute | solution.py:365
  98.2 1.6 copy-done.8
  99.8 1.0 copy-done.11
  100.7 1.0 copy-done.16
  101.7 1.0 copy-done.18
  102.7 17.2 %time_first.1 = (bf16[3,7,8,512]{3,2,1,0:T(8,128)(2,1)S(1)}, bf16[3,7,8,512]{3,2,1,0:T(8,128)(2,1)S(1)}, bf16[3,7,8,512]{3,2,1,0:T(8,128)(2,1)S(1)}, bf16[3,7,8,...) custom-call(bf16[5,7,8,512]{3,2,1,0:T(8,128)(2,1)S(1)} %copy-done.11, ...), custom_call_target="tpu_custom_call" | custom-call | bytes 59040000 | tf_op jit(solution)/shard_map/time_first/pallas_call | solution.py:284
  119.9 0.7 copy-done.41
  120.6 0.9 copy-done.42
  121.5 12.0 %time_second.1 = (bf16[3,7,8,512]{3,2,1,0:T(8,128)(2,1)S(1)}, bf16[3,7,8,512]{3,2,1,0:T(8,128)(2,1)S(1)}, bf16[3,7,8,512]{3,2,1,0:T(8,128)(2,1)S(1)}, bf16[3,7,8...) custom-call(bf16[3,7,8,512]{3,2,1,0:T(8,128)(2,1)S(1)} %copy-done.26, ...), custom_call_target="tpu_custom_call" | custom-call | bytes 36900000 | tf_op jit(solution)/shard_map/time_second/pallas_call | solution.py:284
  133.6 1.5 collective-permute-start.14
  135.1 15.7 %collective-permute-start.15 = (bf16[3,7,8,512]{3,2,1,0:T(8,128)(2,1)S(1)}, bf16[3,7,8,512]{3,2,1,0:T(8,128)(2,1)S(1)}, u32[]{:S(2)}, u32[]{:S(2)}) collective-permute-start(bf16[3,7,8,512]{3,2,1,0:T(8,128)(2,1)S(1)} %get-tuple-element.67), channel_id=1, source_target_pairs={{0,4},{2,6},{4,0},{6,2},{8,12},{10,14},{12,8},{14,10},{1,5},{3,7},... | collective-permute-start | bytes 516104 | tf_op jit(solution)/shard_map/ppermute | solution.py:365
  151.3 3.0 %collective-permute-start.23 = (bf16[3,7,8,512]{3,2,1,0:T(8,128)(2,1)S(1)}, bf16[3,7,8,512]{3,2,1,0:T(8,128)(2,1)S(1)}, u32[]{:S(2)}, u32[]{:S(2)}) collective-permute-start(bf16[3,7,8,512]{3,2,1,0:T(8,128)(2,1)S(1)} %get-tuple-element.79), channel_id=1, source_target_pairs={{0,6},{2,4},{4,2},{6,0},{8,14},{10,12},{12,10},{14,8},{1,7},{3,5},... | collective-permute-start | bytes 516104 | tf_op jit(solution)/shard_map/ppermute | solution.py:365
  154.2 0.7 copy-done.19
  154.9 1.7 collective-permute-start.24
  156.7 0.7 copy-done.21
  157.4 1.1 collective-permute-start.25
  158.9 0.7 copy-done.31
  159.6 2.8 %collective-permute-start.26 = (bf16[3,7,8,512]{3,2,1,0:T(8,128)(2,1)S(1)}, bf16[3,7,8,512]{3,2,1,0:T(8,128)(2,1)S(1)}, u32[]{:S(2)}, u32[]{:S(2)}) collective-permute-start(bf16[3,7,8,512]{3,2,1,0:T(8,128)(2,1)S(1)} %get-tuple-element.82), channel_id=1, source_target_pairs={{0,12},{2,14},{4,8},{6,10},{8,4},{10,6},{12,0},{14,2},{1,13},{3,15... | collective-permute-start | bytes 516104 | tf_op jit(solution)/shard_map/ppermute | solution.py:365
  162.3 0.7 copy-done.33
  163.0 1.9 collective-permute-start.27
  164.9 4.6 %collective-permute-done.23.refs_3_ = bf16[3,7,8,512]{3,2,1,0:T(8,128)(2,1)S(1)} collective-permute-done((bf16[3,7,8,512]{3,2,1,0:T(8,128)(2,1)S(1)}, bf16[3,7,8,512]{3,2,1,0:T(8,128)(2,1)S(1)}, u32[]{:S(2)}, u32[]{:S(2)}) %collective-permute-start.23) | collective-permute-done | bytes 172064 | tf_op jit(solution)/shard_map/ppermute | solution.py:365
  169.5 0.7 copy-done.35
  170.2 2.6 collective-permute-done.24.refs_4_
  172.7 0.7 copy-done.37
  173.4 18.9 %collective-permute-done.25.refs_5_ = bf16[3,7,8,512]{3,2,1,0:T(8,128)(2,1)S(1)} collective-permute-done((bf16[3,7,8,512]{3,2,1,0:T(8,128)(2,1)S(1)}, bf16[3,7,8,512]{3,2,1,0:T(8,128)(2,1)S(1)}, u32[]{:S(2)}, u32[]{:S(2)}) %collective-permute-start.25) | collective-permute-done | bytes 172064 | tf_op jit(solution)/shard_map/ppermute | solution.py:365
  192.3 0.7 copy-done.39
  193.0 0.7 copy-done.43
  193.6 2.1 collective-permute-start.19
  195.7 0.7 copy-done.45
  196.4 2.2 collective-permute-start.20
  198.6 17.5 %all-gather.13.cloned.1.call-done = bf16[1024,1024]{1,0:T(8,128)(2,1)} async-done(((bf16[32,1024]{1,0:T(8,128)(2,1)}), bf16[1024,1024]{1,0:T(8,128)(2,1)}) %all-gather.13.cloned.1.call-update) | async-done | bytes 2097168 | tf_op jit(solution)/shard_map/all_gather | solution.py:371
  216.1 1.2 copy-done.4
  217.3 1.5 copy-done.9
  218.9 23.5 %space_attention.1 = (bf16[7,64,1024]{2,1,0:T(8,128)(2,1)}, bf16[7,64,1024]{2,1,0:T(8,128)(2,1)}, bf16[7,64,1024]{2,1,0:T(8,128)(2,1)}) custom-call(s32[9]{0:T(128)S(1)} %pad_add_fusion.spots_ref, bf16[7,64,1024]{2,1,0:T(8,128)(2,1)S(1)} %copy-done.2, bf16[7,64,1024]{2,1,0:T(8,128)(2,1)S(1)} %copy-done.3, bf16[7,64,1024]{2,1,0:T(8,128)(2,1)S(1)} %copy-done.4, ...), custom_call_target="tpu_custom_call" | custom-call | bytes 73800000 | tf_op jit(solution)/shard_map/space_attention/pallas_call | solution.py:332
  242.5 3.4 %place_first.1 = (bf16[7,8,8,1024]{3,2,1,0:T(8,128)(2,1)}, bf16[7,8,8,1024]{3,2,1,0:T(8,128)(2,1)}, bf16[7,8,8,1024]{3,2,1,0:T(8,128)(2,1)}) custom-call(s32[9]{0:T(128)S(1)} %pad_add_fusion.spots_ref, bf16[3,7,8,512]{3,2,1,0:T(8,128)(2,1)S(1)} %copy-done.24, bf16[3,7,8,512]{3,2,1,0:T(8,128)(2,1)S(1)} %copy-done.32, bf16[3,7,8,512]{3,2,1,0:T(8,128)(2,1)S(1)} %copy-done.34, ...), custom_call_target="tpu_custom_call" | custom-call | tf_op jit(solution)/shard_map/place_first/pallas_call | solution.py:177
  245.9 1.2 copy-done.13
  247.1 1.2 copy-done.14
  248.3 3.2 %place_second.1 = (bf16[7,8,8,1024]{3,2,1,0:T(8,128)(2,1)}, bf16[7,8,8,1024]{3,2,1,0:T(8,128)(2,1)}, bf16[7,8,8,1024]{3,2,1,0:T(8,128)(2,1)}) custom-call(s32[9]{0:T(128)S(1)} %pad_add_fusion.spots_ref, bf16[3,7,8,512]{3,2,1,0:T(8,128)(2,1)S(1)} %get-tuple-element.65.refs_0_, ...), custom_call_target="tpu_custom_call", output_to_operand_aliasing={{0}: (12, {}), {1}: (13, {}), {2}: (14, {})} | custom-call | tf_op jit(solution)/shard_map/place_second/pallas_call | solution.py:177
  (117 shorter events, 2.3 us)
Async XLA Ops:
  7.2 91.0 %all-gather.11.cloned.1.call-start = ((), (), s32[]{:S(2)}) async-start(), calls=%async_computation | async-start | bytes 2162688 | tf_op jit(solution)/shard_map/all_gather | solution.py:371
  8.7 2.7 %copy-start.47 = (bf16[64,1024]{1,0:T(8,128)(2,1)S(1)}, bf16[64,1024]{1,0:T(8,128)(2,1)}, u32[]{:S(2)}) copy-start(bf16[64,1024]{1,0:T(8,128)(2,1)} %param.17) | copy-start | bytes 393220
  8.7 3.5 %copy-start.1 = (bf16[7,64,1024]{2,1,0:T(8,128)(2,1)S(1)}, bf16[7,64,1024]{2,1,0:T(8,128)(2,1)}, u32[]{:S(2)}) copy-start(bf16[7,64,1024]{2,1,0:T(8,128)(2,1)} %refs_6_.1) | copy-start | bytes 2752516
  8.8 3.5 %copy-start.5 = (bf16[7,64,1024]{2,1,0:T(8,128)(2,1)S(1)}, bf16[7,64,1024]{2,1,0:T(8,128)(2,1)}, u32[]{:S(2)}) copy-start(bf16[7,64,1024]{2,1,0:T(8,128)(2,1)} %param.10) | copy-start | bytes 2752516
  8.8 3.5 %copy-start.6 = (bf16[7,64,1024]{2,1,0:T(8,128)(2,1)S(1)}, bf16[7,64,1024]{2,1,0:T(8,128)(2,1)}, u32[]{:S(2)}) copy-start(bf16[7,64,1024]{2,1,0:T(8,128)(2,1)} %param.11) | copy-start | bytes 2752516
  8.8 189.8 %all-gather.15.cloned.1.call-start = ((), (), s32[]{:S(2)}) async-start(), calls=%async_computation.2 | async-start | bytes 2752512 | tf_op jit(solution)/shard_map/all_gather | solution.py:403
  9.5 189.1 %all-gather.17.cloned.1.call-start = ((), (), s32[]{:S(2)}) async-start(), calls=%async_computation.3 | async-start | bytes 2752512 | tf_op jit(solution)/shard_map/all_gather | solution.py:403
  10.3 188.3 %all-gather.19.cloned.1.call-start = ((), (), s32[]{:S(2)}) async-start(), calls=%async_computation.4 | async-start | bytes 2752512 | tf_op jit(solution)/shard_map/all_gather | solution.py:403
  10.8 187.8 %all-gather.21.cloned.1.call-start = ((), (), s32[]{:S(2)}) async-start(), calls=%async_computation.5 | async-start | bytes 2752512 | tf_op jit(solution)/shard_map/all_gather | solution.py:403
  11.4 204.7 %all-gather.13.cloned.1.call-start = ((), (), s32[]{:S(2)}) async-start(), calls=%async_computation.1 | async-start | bytes 2162688 | tf_op jit(solution)/shard_map/all_gather | solution.py:371
  12.3 1.2 copy-start.7
  17.7 6.8 %copy-start.10 = (bf16[5,7,8,512]{3,2,1,0:T(8,128)(2,1)}, bf16[5,7,8,512]{3,2,1,0:T(8,128)(2,1)S(1)}, u32[]{:S(2)}) copy-start(bf16[5,7,8,512]{3,2,1,0:T(8,128)(2,1)S(1)} %get-tuple-element.48.refs_3_.refs_0_) | copy-start | bytes 860164
  17.7 24.5 %collective-permute-start.7 = (bf16[5,7,8,512]{3,2,1,0:T(8,128)(2,1)S(1)}, bf16[5,7,8,512]{3,2,1,0:T(8,128)(2,1)S(1)}, u32[]{:S(2)}, u32[]{:S(2)}) collective-permute-start(bf16[5,7,8,512]{3,2,1,0:T(8,128)(2,1)S(1)} %get-tuple-element.57), channel_id=1, source_target_pairs={{0,2},{2,0},{4,6},{6,4},{8,10},{10,8},{12,14},{14,12},{1,3},{3,1},... | collective-permute-start | bytes 860168 | tf_op jit(solution)/shard_map/ppermute | solution.py:365
  20.7 23.6 %collective-permute-start.8 = (bf16[5,7,8,512]{3,2,1,0:T(8,128)(2,1)S(1)}, bf16[5,7,8,512]{3,2,1,0:T(8,128)(2,1)S(1)}, u32[]{:S(2)}, u32[]{:S(2)}) collective-permute-start(bf16[5,7,8,512]{3,2,1,0:T(8,128)(2,1)S(1)} %get-tuple-element.58), channel_id=1, source_target_pairs={{0,4},{2,6},{4,0},{6,2},{8,12},{10,14},{12,8},{14,10},{1,5},{3,7},... | collective-permute-start | bytes 860168 | tf_op jit(solution)/shard_map/ppermute | solution.py:365
  25.2 6.5 %collective-permute-start = (bf16[3,7,8,512]{3,2,1,0:T(8,128)(2,1)S(1)}, bf16[3,7,8,512]{3,2,1,0:T(8,128)(2,1)S(1)}, u32[]{:S(2)}, u32[]{:S(2)}) collective-permute-start(bf16[3,7,8,512]{3,2,1,0:T(8,128)(2,1)S(1)} %get-tuple-element.50), channel_id=1, source_target_pairs={{0,2},{2,0},{4,6},{6,4},{8,10},{10,8},{12,14},{14,12},{1,3},{3,1},... | collective-permute-start | bytes 516104 | tf_op jit(solution)/shard_map/ppermute | solution.py:365
  25.7 15.9 %collective-permute-start.1 = (bf16[3,7,8,512]{3,2,1,0:T(8,128)(2,1)S(1)}, bf16[3,7,8,512]{3,2,1,0:T(8,128)(2,1)S(1)}, u32[]{:S(2)}, u32[]{:S(2)}) collective-permute-start(bf16[3,7,8,512]{3,2,1,0:T(8,128)(2,1)S(1)} %get-tuple-element.51), channel_id=1, source_target_pairs={{0,4},{2,6},{4,0},{6,2},{8,12},{10,14},{12,8},{14,10},{1,5},{3,7},... | collective-permute-start | bytes 516104 | tf_op jit(solution)/shard_map/ppermute | solution.py:365
  25.7 21.6 %collective-permute-start.9 = (bf16[5,7,8,512]{3,2,1,0:T(8,128)(2,1)S(1)}, bf16[5,7,8,512]{3,2,1,0:T(8,128)(2,1)S(1)}, u32[]{:S(2)}, u32[]{:S(2)}) collective-permute-start(bf16[5,7,8,512]{3,2,1,0:T(8,128)(2,1)S(1)} %get-tuple-element.59), channel_id=1, source_target_pairs={{0,6},{2,4},{4,2},{6,0},{8,14},{10,12},{12,10},{14,8},{1,7},{3,5},... | collective-permute-start | bytes 860168 | tf_op jit(solution)/shard_map/ppermute | solution.py:365
  32.4 36.9 %collective-permute-start.10 = (bf16[5,7,8,512]{3,2,1,0:T(8,128)(2,1)S(1)}, bf16[5,7,8,512]{3,2,1,0:T(8,128)(2,1)S(1)}, u32[]{:S(2)}, u32[]{:S(2)}) collective-permute-start(bf16[5,7,8,512]{3,2,1,0:T(8,128)(2,1)S(1)} %get-tuple-element.60), channel_id=1, source_target_pairs={{0,8},{2,10},{4,12},{6,14},{8,0},{10,2},{12,4},{14,6},{1,9},{3,11}... | collective-permute-start | bytes 860168 | tf_op jit(solution)/shard_map/ppermute | solution.py:365
  42.2 41.2 %collective-permute-start.11 = (bf16[5,7,8,512]{3,2,1,0:T(8,128)(2,1)S(1)}, bf16[5,7,8,512]{3,2,1,0:T(8,128)(2,1)S(1)}, u32[]{:S(2)}, u32[]{:S(2)}) collective-permute-start(bf16[5,7,8,512]{3,2,1,0:T(8,128)(2,1)S(1)} %get-tuple-element.61), channel_id=1, source_target_pairs={{0,10},{2,8},{4,14},{6,12},{8,2},{10,0},{12,6},{14,4},{1,11},{3,9}... | collective-permute-start | bytes 860168 | tf_op jit(solution)/shard_map/ppermute | solution.py:365
  42.9 40.5 %collective-permute-start.12 = (bf16[5,7,8,512]{3,2,1,0:T(8,128)(2,1)S(1)}, bf16[5,7,8,512]{3,2,1,0:T(8,128)(2,1)S(1)}, u32[]{:S(2)}, u32[]{:S(2)}) collective-permute-start(bf16[5,7,8,512]{3,2,1,0:T(8,128)(2,1)S(1)} %get-tuple-element.62), channel_id=1, source_target_pairs={{0,12},{2,14},{4,8},{6,10},{8,4},{10,6},{12,0},{14,2},{1,13},{3,15... | collective-permute-start | bytes 860168 | tf_op jit(solution)/shard_map/ppermute | solution.py:365
  45.1 53.0 %collective-permute-start.13 = (bf16[5,7,8,512]{3,2,1,0:T(8,128)(2,1)S(1)}, bf16[5,7,8,512]{3,2,1,0:T(8,128)(2,1)S(1)}, u32[]{:S(2)}, u32[]{:S(2)}) collective-permute-start(bf16[5,7,8,512]{3,2,1,0:T(8,128)(2,1)S(1)} %get-tuple-element.63), channel_id=1, source_target_pairs={{0,14},{2,12},{4,10},{6,8},{8,6},{10,4},{12,2},{14,0},{1,15},{3,13... | collective-permute-start | bytes 860168 | tf_op jit(solution)/shard_map/ppermute | solution.py:365
  47.3 72.6 %collective-permute-start.2 = (bf16[3,7,8,512]{3,2,1,0:T(8,128)(2,1)}, bf16[3,7,8,512]{3,2,1,0:T(8,128)(2,1)S(1)}, u32[]{:S(2)}, u32[]{:S(2)}) collective-permute-start(bf16[3,7,8,512]{3,2,1,0:T(8,128)(2,1)} %get-tuple-element.52), channel_id=1, source_target_pairs={{0,6},{2,4},{4,2},{6,0},{8,14},{10,12},{12,10},{14,8},{1,7},{3,5},... | collective-permute-start | bytes 516104 | tf_op jit(solution)/shard_map/ppermute | solution.py:365
  69.2 51.4 %collective-permute-start.3 = (bf16[3,7,8,512]{3,2,1,0:T(8,128)(2,1)}, bf16[3,7,8,512]{3,2,1,0:T(8,128)(2,1)}, u32[]{:S(2)}, u32[]{:S(2)}) collective-permute-start(bf16[3,7,8,512]{3,2,1,0:T(8,128)(2,1)} %get-tuple-element.53), channel_id=1, source_target_pairs={{0,8},{2,10},{4,12},{6,14},{8,0},{10,2},{12,4},{14,6},{1,9},{3,11}... | collective-permute-start | bytes 516104 | tf_op jit(solution)/shard_map/ppermute | solution.py:365
  83.4 37.2 %collective-permute-start.4 = (bf16[3,7,8,512]{3,2,1,0:T(8,128)(2,1)}, bf16[3,7,8,512]{3,2,1,0:T(8,128)(2,1)}, u32[]{:S(2)}, u32[]{:S(2)}) collective-permute-start(bf16[3,7,8,512]{3,2,1,0:T(8,128)(2,1)} %get-tuple-element.54), channel_id=1, source_target_pairs={{0,10},{2,8},{4,14},{6,12},{8,2},{10,0},{12,6},{14,4},{1,11},{3,9}... | collective-permute-start | bytes 516104 | tf_op jit(solution)/shard_map/ppermute | solution.py:365
  83.4 37.2 %collective-permute-start.5 = (bf16[3,7,8,512]{3,2,1,0:T(8,128)(2,1)}, bf16[3,7,8,512]{3,2,1,0:T(8,128)(2,1)}, u32[]{:S(2)}, u32[]{:S(2)}) collective-permute-start(bf16[3,7,8,512]{3,2,1,0:T(8,128)(2,1)} %get-tuple-element.55), channel_id=1, source_target_pairs={{0,12},{2,14},{4,8},{6,10},{8,4},{10,6},{12,0},{14,2},{1,13},{3,15... | collective-permute-start | bytes 516104 | tf_op jit(solution)/shard_map/ppermute | solution.py:365
  98.0 22.6 %collective-permute-start.6 = (bf16[3,7,8,512]{3,2,1,0:T(8,128)(2,1)}, bf16[3,7,8,512]{3,2,1,0:T(8,128)(2,1)}, u32[]{:S(2)}, u32[]{:S(2)}) collective-permute-start(bf16[3,7,8,512]{3,2,1,0:T(8,128)(2,1)} %get-tuple-element.56), channel_id=1, source_target_pairs={{0,14},{2,12},{4,10},{6,8},{8,6},{10,4},{12,2},{14,0},{1,15},{3,13... | collective-permute-start | bytes 516104 | tf_op jit(solution)/shard_map/ppermute | solution.py:365
  98.2 1.6 copy-start.8
  99.8 1.0 copy-start.11
  100.7 1.0 copy-start.16
  102.6 18.0 %copy-start.26 = (bf16[3,7,8,512]{3,2,1,0:T(8,128)(2,1)S(1)}, bf16[3,7,8,512]{3,2,1,0:T(8,128)(2,1)}, u32[]{:S(2)}) copy-start(bf16[3,7,8,512]{3,2,1,0:T(8,128)(2,1)} %copy-done.25) | copy-start | bytes 516100
  102.6 18.0 %copy-start.28 = (bf16[3,7,8,512]{3,2,1,0:T(8,128)(2,1)S(1)}, bf16[3,7,8,512]{3,2,1,0:T(8,128)(2,1)}, u32[]{:S(2)}) copy-start(bf16[3,7,8,512]{3,2,1,0:T(8,128)(2,1)} %copy-done.27) | copy-start | bytes 516100
  102.7 18.0 %copy-start.30 = (bf16[3,7,8,512]{3,2,1,0:T(8,128)(2,1)S(1)}, bf16[3,7,8,512]{3,2,1,0:T(8,128)(2,1)}, u32[]{:S(2)}) copy-start(bf16[3,7,8,512]{3,2,1,0:T(8,128)(2,1)} %copy-done.29) | copy-start | bytes 516100
  119.9 36.8 %copy-start.23 = (bf16[3,7,8,512]{3,2,1,0:T(8,128)(2,1)}, bf16[3,7,8,512]{3,2,1,0:T(8,128)(2,1)S(1)}, u32[]{:S(2)}) copy-start(bf16[3,7,8,512]{3,2,1,0:T(8,128)(2,1)S(1)} %get-tuple-element.76.refs_0_) | copy-start | bytes 516100
  119.9 96.3 %copy-start.2 = (bf16[7,64,1024]{2,1,0:T(8,128)(2,1)S(1)}, bf16[7,64,1024]{2,1,0:T(8,128)(2,1)}, u32[]{:S(2)}) copy-start(bf16[7,64,1024]{2,1,0:T(8,128)(2,1)} %refs_0_.1) | copy-start | bytes 2752516
  119.9 96.3 %copy-start.3 = (bf16[7,64,1024]{2,1,0:T(8,128)(2,1)S(1)}, bf16[7,64,1024]{2,1,0:T(8,128)(2,1)}, u32[]{:S(2)}) copy-start(bf16[7,64,1024]{2,1,0:T(8,128)(2,1)} %refs_1_.1) | copy-start | bytes 2752516
  133.6 20.6 %collective-permute-start.14 = (bf16[3,7,8,512]{3,2,1,0:T(8,128)(2,1)S(1)}, bf16[3,7,8,512]{3,2,1,0:T(8,128)(2,1)S(1)}, u32[]{:S(2)}, u32[]{:S(2)}) collective-permute-start(bf16[3,7,8,512]{3,2,1,0:T(8,128)(2,1)S(1)} %get-tuple-element.66), channel_id=1, source_target_pairs={{0,2},{2,0},{4,6},{6,4},{8,10},{10,8},{12,14},{14,12},{1,3},{3,1},... | collective-permute-start | bytes 516104 | tf_op jit(solution)/shard_map/ppermute | solution.py:365
  135.1 21.6 %collective-permute-start.15 = (bf16[3,7,8,512]{3,2,1,0:T(8,128)(2,1)S(1)}, bf16[3,7,8,512]{3,2,1,0:T(8,128)(2,1)S(1)}, u32[]{:S(2)}, u32[]{:S(2)}) collective-permute-start(bf16[3,7,8,512]{3,2,1,0:T(8,128)(2,1)S(1)} %get-tuple-element.67), channel_id=1, source_target_pairs={{0,4},{2,6},{4,0},{6,2},{8,12},{10,14},{12,8},{14,10},{1,5},{3,7},... | collective-permute-start | bytes 516104 | tf_op jit(solution)/shard_map/ppermute | solution.py:365
  150.7 8.2 %collective-permute-start.21 = (bf16[3,7,8,512]{3,2,1,0:T(8,128)(2,1)S(1)}, bf16[3,7,8,512]{3,2,1,0:T(8,128)(2,1)S(1)}, u32[]{:S(2)}, u32[]{:S(2)}) collective-permute-start(bf16[3,7,8,512]{3,2,1,0:T(8,128)(2,1)S(1)} %get-tuple-element.77), channel_id=1, source_target_pairs={{0,2},{2,0},{4,6},{6,4},{8,10},{10,8},{12,14},{14,12},{1,3},{3,1},... | collective-permute-start | bytes 516104 | tf_op jit(solution)/shard_map/ppermute | solution.py:365
  151.2 11.1 %collective-permute-start.22 = (bf16[3,7,8,512]{3,2,1,0:T(8,128)(2,1)S(1)}, bf16[3,7,8,512]{3,2,1,0:T(8,128)(2,1)S(1)}, u32[]{:S(2)}, u32[]{:S(2)}) collective-permute-start(bf16[3,7,8,512]{3,2,1,0:T(8,128)(2,1)S(1)} %get-tuple-element.78), channel_id=1, source_target_pairs={{0,4},{2,6},{4,0},{6,2},{8,12},{10,14},{12,8},{14,10},{1,5},{3,7},... | collective-permute-start | bytes 516104 | tf_op jit(solution)/shard_map/ppermute | solution.py:365
  151.3 18.2 %collective-permute-start.23 = (bf16[3,7,8,512]{3,2,1,0:T(8,128)(2,1)S(1)}, bf16[3,7,8,512]{3,2,1,0:T(8,128)(2,1)S(1)}, u32[]{:S(2)}, u32[]{:S(2)}) collective-permute-start(bf16[3,7,8,512]{3,2,1,0:T(8,128)(2,1)S(1)} %get-tuple-element.79), channel_id=1, source_target_pairs={{0,6},{2,4},{4,2},{6,0},{8,14},{10,12},{12,10},{14,8},{1,7},{3,5},... | collective-permute-start | bytes 516104 | tf_op jit(solution)/shard_map/ppermute | solution.py:365
  154.9 17.8 %collective-permute-start.24 = (bf16[3,7,8,512]{3,2,1,0:T(8,128)(2,1)S(1)}, bf16[3,7,8,512]{3,2,1,0:T(8,128)(2,1)S(1)}, u32[]{:S(2)}, u32[]{:S(2)}) collective-permute-start(bf16[3,7,8,512]{3,2,1,0:T(8,128)(2,1)S(1)} %get-tuple-element.80), channel_id=1, source_target_pairs={{0,8},{2,10},{4,12},{6,14},{8,0},{10,2},{12,4},{14,6},{1,9},{3,11}... | collective-permute-start | bytes 516104 | tf_op jit(solution)/shard_map/ppermute | solution.py:365
  157.4 34.9 %collective-permute-start.25 = (bf16[3,7,8,512]{3,2,1,0:T(8,128)(2,1)S(1)}, bf16[3,7,8,512]{3,2,1,0:T(8,128)(2,1)S(1)}, u32[]{:S(2)}, u32[]{:S(2)}) collective-permute-start(bf16[3,7,8,512]{3,2,1,0:T(8,128)(2,1)S(1)} %get-tuple-element.81), channel_id=1, source_target_pairs={{0,10},{2,8},{4,14},{6,12},{8,2},{10,0},{12,6},{14,4},{1,11},{3,9}... | collective-permute-start | bytes 516104 | tf_op jit(solution)/shard_map/ppermute | solution.py:365
  159.6 33.4 %collective-permute-start.26 = (bf16[3,7,8,512]{3,2,1,0:T(8,128)(2,1)S(1)}, bf16[3,7,8,512]{3,2,1,0:T(8,128)(2,1)S(1)}, u32[]{:S(2)}, u32[]{:S(2)}) collective-permute-start(bf16[3,7,8,512]{3,2,1,0:T(8,128)(2,1)S(1)} %get-tuple-element.82), channel_id=1, source_target_pairs={{0,12},{2,14},{4,8},{6,10},{8,4},{10,6},{12,0},{14,2},{1,13},{3,15... | collective-permute-start | bytes 516104 | tf_op jit(solution)/shard_map/ppermute | solution.py:365
  163.0 32.7 %collective-permute-start.27 = (bf16[3,7,8,512]{3,2,1,0:T(8,128)(2,1)S(1)}, bf16[3,7,8,512]{3,2,1,0:T(8,128)(2,1)S(1)}, u32[]{:S(2)}, u32[]{:S(2)}) collective-permute-start(bf16[3,7,8,512]{3,2,1,0:T(8,128)(2,1)S(1)} %get-tuple-element.83), channel_id=1, source_target_pairs={{0,14},{2,12},{4,10},{6,8},{8,6},{10,4},{12,2},{14,0},{1,15},{3,13... | collective-permute-start | bytes 516104 | tf_op jit(solution)/shard_map/ppermute | solution.py:365
  170.2 75.7 %collective-permute-start.16 = (bf16[3,7,8,512]{3,2,1,0:T(8,128)(2,1)}, bf16[3,7,8,512]{3,2,1,0:T(8,128)(2,1)}, u32[]{:S(2)}, u32[]{:S(2)}) collective-permute-start(bf16[3,7,8,512]{3,2,1,0:T(8,128)(2,1)} %get-tuple-element.68), channel_id=1, source_target_pairs={{0,6},{2,4},{4,2},{6,0},{8,14},{10,12},{12,10},{14,8},{1,7},{3,5},... | collective-permute-start | bytes 516104 | tf_op jit(solution)/shard_map/ppermute | solution.py:365
  173.4 72.5 %collective-permute-start.17 = (bf16[3,7,8,512]{3,2,1,0:T(8,128)(2,1)}, bf16[3,7,8,512]{3,2,1,0:T(8,128)(2,1)}, u32[]{:S(2)}, u32[]{:S(2)}) collective-permute-start(bf16[3,7,8,512]{3,2,1,0:T(8,128)(2,1)} %get-tuple-element.69), channel_id=1, source_target_pairs={{0,8},{2,10},{4,12},{6,14},{8,0},{10,2},{12,4},{14,6},{1,9},{3,11}... | collective-permute-start | bytes 516104 | tf_op jit(solution)/shard_map/ppermute | solution.py:365
  193.0 52.9 %collective-permute-start.18 = (bf16[3,7,8,512]{3,2,1,0:T(8,128)(2,1)}, bf16[3,7,8,512]{3,2,1,0:T(8,128)(2,1)}, u32[]{:S(2)}, u32[]{:S(2)}) collective-permute-start(bf16[3,7,8,512]{3,2,1,0:T(8,128)(2,1)} %get-tuple-element.70), channel_id=1, source_target_pairs={{0,10},{2,8},{4,14},{6,12},{8,2},{10,0},{12,6},{14,4},{1,11},{3,9}... | collective-permute-start | bytes 516104 | tf_op jit(solution)/shard_map/ppermute | solution.py:365
  193.6 52.2 %collective-permute-start.19 = (bf16[3,7,8,512]{3,2,1,0:T(8,128)(2,1)}, bf16[3,7,8,512]{3,2,1,0:T(8,128)(2,1)}, u32[]{:S(2)}, u32[]{:S(2)}) collective-permute-start(bf16[3,7,8,512]{3,2,1,0:T(8,128)(2,1)} %get-tuple-element.71), channel_id=1, source_target_pairs={{0,12},{2,14},{4,8},{6,10},{8,4},{10,6},{12,0},{14,2},{1,13},{3,15... | collective-permute-start | bytes 516104 | tf_op jit(solution)/shard_map/ppermute | solution.py:365
  196.4 49.5 %collective-permute-start.20 = (bf16[3,7,8,512]{3,2,1,0:T(8,128)(2,1)}, bf16[3,7,8,512]{3,2,1,0:T(8,128)(2,1)}, u32[]{:S(2)}, u32[]{:S(2)}) collective-permute-start(bf16[3,7,8,512]{3,2,1,0:T(8,128)(2,1)} %get-tuple-element.72), channel_id=1, source_target_pairs={{0,14},{2,12},{4,10},{6,8},{8,6},{10,4},{12,2},{14,0},{1,15},{3,13... | collective-permute-start | bytes 516104 | tf_op jit(solution)/shard_map/ppermute | solution.py:365
  216.1 1.2 copy-start.4
  217.3 1.5 copy-start.9
  218.8 23.6 %copy-start.24 = (bf16[3,7,8,512]{3,2,1,0:T(8,128)(2,1)S(1)}, bf16[3,7,8,512]{3,2,1,0:T(8,128)(2,1)}, u32[]{:S(2)}) copy-start(bf16[3,7,8,512]{3,2,1,0:T(8,128)(2,1)} %copy-done.23) | copy-start | bytes 516100
  218.8 23.6 %copy-start.32 = (bf16[3,7,8,512]{3,2,1,0:T(8,128)(2,1)S(1)}, bf16[3,7,8,512]{3,2,1,0:T(8,128)(2,1)}, u32[]{:S(2)}) copy-start(bf16[3,7,8,512]{3,2,1,0:T(8,128)(2,1)} %copy-done.31) | copy-start | bytes 516100
  218.8 23.6 %copy-start.34 = (bf16[3,7,8,512]{3,2,1,0:T(8,128)(2,1)S(1)}, bf16[3,7,8,512]{3,2,1,0:T(8,128)(2,1)}, u32[]{:S(2)}) copy-start(bf16[3,7,8,512]{3,2,1,0:T(8,128)(2,1)} %copy-done.33) | copy-start | bytes 516100
  218.8 23.6 %copy-start.36 = (bf16[3,7,8,512]{3,2,1,0:T(8,128)(2,1)S(1)}, bf16[3,7,8,512]{3,2,1,0:T(8,128)(2,1)}, u32[]{:S(2)}) copy-start(bf16[3,7,8,512]{3,2,1,0:T(8,128)(2,1)} %copy-done.35) | copy-start | bytes 516100
  218.8 23.6 %copy-start.38 = (bf16[3,7,8,512]{3,2,1,0:T(8,128)(2,1)S(1)}, bf16[3,7,8,512]{3,2,1,0:T(8,128)(2,1)}, u32[]{:S(2)}) copy-start(bf16[3,7,8,512]{3,2,1,0:T(8,128)(2,1)} %copy-done.37) | copy-start | bytes 516100
  218.8 23.6 %copy-start.40 = (bf16[3,7,8,512]{3,2,1,0:T(8,128)(2,1)S(1)}, bf16[3,7,8,512]{3,2,1,0:T(8,128)(2,1)}, u32[]{:S(2)}) copy-start(bf16[3,7,8,512]{3,2,1,0:T(8,128)(2,1)} %copy-done.39) | copy-start | bytes 516100
  218.8 23.6 %copy-start.44 = (bf16[3,7,8,512]{3,2,1,0:T(8,128)(2,1)S(1)}, bf16[3,7,8,512]{3,2,1,0:T(8,128)(2,1)}, u32[]{:S(2)}) copy-start(bf16[3,7,8,512]{3,2,1,0:T(8,128)(2,1)} %copy-done.43) | copy-start | bytes 516100
  218.9 23.6 %copy-start.46 = (bf16[3,7,8,512]{3,2,1,0:T(8,128)(2,1)S(1)}, bf16[3,7,8,512]{3,2,1,0:T(8,128)(2,1)}, u32[]{:S(2)}) copy-start(bf16[3,7,8,512]{3,2,1,0:T(8,128)(2,1)} %copy-done.45) | copy-start | bytes 516100
  218.9 27.0 %copy-start.20 = (bf16[3,7,8,512]{3,2,1,0:T(8,128)(2,1)S(1)}, bf16[3,7,8,512]{3,2,1,0:T(8,128)(2,1)}, u32[]{:S(2)}) copy-start(bf16[3,7,8,512]{3,2,1,0:T(8,128)(2,1)} %copy-done.19) | copy-start | bytes 516100
  218.9 27.0 %copy-start.22 = (bf16[3,7,8,512]{3,2,1,0:T(8,128)(2,1)S(1)}, bf16[3,7,8,512]{3,2,1,0:T(8,128)(2,1)}, u32[]{:S(2)}) copy-start(bf16[3,7,8,512]{3,2,1,0:T(8,128)(2,1)} %copy-done.21) | copy-start | bytes 516100
  242.4 3.5 %copy-start.12 = (bf16[7,64,1024]{2,1,0:T(8,128)(2,1)S(1)}, bf16[7,64,1024]{2,1,0:T(8,128)(2,1)}, u32[]{:S(2)}) copy-start(bf16[7,64,1024]{2,1,0:T(8,128)(2,1)} %get-tuple-element.45.refs_8_) | copy-start | bytes 2752516
  245.9 1.2 copy-start.13
  247.1 1.2 copy-start.14
  (18 other events, 12.9 us)
Sparse Core Ops, SparseCore 0:
  11.0 85.8 all-gather.10
  98.4 8.7 all-gather.14
  108.7 11.3 all-gather.16
  121.5 11.3 all-gather.18
  134.4 11.3 all-gather.20
  148.6 67.4 all-gather.12

commit v4 on v3

--- a/solution.py
+++ b/solution.py
@@ -203,9 +203,10 @@
             ref[rows, :] = value
 
 
-def time_chunk(blocks, gathered, late_grad, name):
-    count = len(blocks)
+def time_chunk(blocks, token_blocks, gathered, late_grad, name, after=()):
+    blocks = [*blocks, *token_blocks]
     first = late_grad is None
+    count = len(blocks) // 2 if first else len(blocks)
     _, frames, patches, lanes = blocks[0].shape
     total, part = count * frames, frames * patches
     rows, width = total * patches, 2 * lanes
@@ -216,7 +217,7 @@
         space, groups, tm, share = gathered.shape[:4]
         scratch += [pltpu.VMEM((rows, width), BF16), pltpu.VMEM((space * groups * tm, share, width), BF16)]
         operands = (gathered,)
-        copied = count + space * groups * tm
+        copied = len(blocks) + space * groups * tm
     else:
         scratch += [pltpu.VMEM((rows, lanes), BF16)]
         operands = (late_grad,)
@@ -230,23 +231,23 @@
             taken, refs[:number] = refs[:number], []
             return taken
 
-        block_refs, extra_ref, out_refs = take(count), take(1)[0], take(count)
+        block_refs, extra_ref, _ = take(len(blocks)), take(1)[0], take(len(after))
+        out_refs = take(count)
         later_ref = take(1)[0] if first else None
-        blocks_in, results_out = take(count), take(count)
+        blocks_in, results_out = take(len(blocks)), take(count)
+        blocks_in, tokens_in = blocks_in[:count], blocks_in[count:]
         held, results = take(4), take(3)
         grads = take(1)[0]
         weights = take(1)[0] if first else None
         arrived, left = refs
-        pairs = list(zip(block_refs, blocks_in))
+        pairs = list(zip(block_refs, [*blocks_in, *tokens_in]))
         pairs += weight_copies(extra_ref, weights) if first else [(extra_ref, grads)]
         for copy in run_copies(arrived, pairs):
             copy.wait()
         if first:
-            for index, ref in enumerate(blocks_in):
-                at = slice(index * part, (index + 1) * part)
-                for side in range(2):
-                    value = ref[3 + side].astype(F32).reshape(part, lanes)
-                    grads[at, side * lanes : (side + 1) * lanes] = value.astype(BF16)
+            for index, ref in enumerate(tokens_in):
+                value = ref[...].astype(F32).reshape(part, width)
+                grads[index * part : (index + 1) * part, :] = value.astype(BF16)
 
         def one_pair(pair, carry):
             columns = pl.ds(pl.multiple_of(pair * PAIR, PAIR), PAIR)
@@ -283,26 +284,25 @@
         out_specs = out_specs + [pl.BlockSpec(memory_space=pltpu.VMEM)]
     return pl.pallas_call(
         kernel,
-        in_specs=[HBM] * (count + 1),
+        in_specs=[HBM] * (len(blocks) + 1 + len(after)),
         out_specs=out_specs,
         out_shape=out_shapes,
         scratch_shapes=scratch,
         compiler_params=BIG,
         cost_estimate=cost_of(16 if first else 10),
         name=name,
-    )(*blocks, *operands)
-
-
-def space_attention(spots, core_at, own, far, own_tokens, far_tokens, weights_of, after=()):
+    )(*blocks, *operands, *after)
+
+
+def space_attention(own, far, own_tokens, weights_of, after=()):
     frames, rows, width = own_tokens.shape
     space, groups, tm, share = weights_of.shape[:4]
     pieces = space * groups * tm
 
-    def kernel(spots_ref, *refs):
-        own_refs, far_refs = refs[:3], refs[3:6]
-        token_refs, gathered_ref = refs[6:8], refs[8]
-        outs = refs[9 + len(after) : 12 + len(after)]
-        weights, grads, sems = refs[12 + len(after) :]
+    def kernel(*refs):
+        own_refs, far_ref, own_token_ref, far_token_ref, gathered_ref = refs[:3], *refs[3:7]
+        outs = refs[7 + len(after) : 10 + len(after)]
+        weights, grads, sems = refs[10 + len(after) :]
 
         @pl.when(pl.program_id(0) == 0)
         def _():
@@ -310,7 +310,7 @@
                 copy.wait()
             whole = weights[...].reshape(width, width)
             for side in range(2):
-                flat = (token_refs[0][...] if side == 0 else token_refs[1][0]).reshape(frames * rows, width)
+                flat = (far_token_ref[0] if side else own_token_ref[...]).reshape(frames * rows, width)
                 made = dot(flat, whole, ((1,), (1,))).astype(BF16)
                 grads[side] = made.reshape(frames, rows, width)
 
@@ -318,23 +318,23 @@
         for pair in range(width // PAIR):
             columns = slice(pair * PAIR, (pair + 1) * PAIR)
             operands = [
-                (near[0, :, columns].astype(F32), away[0, 0, :, columns].astype(F32))
-                for near, away in zip(own_refs, far_refs)
+                (near[0, :, columns].astype(F32), far_ref[index, 0, :, columns].astype(F32))
+                for index, near in enumerate(own_refs)
             ]
             operands.append(tuple(grads[side, frame, :, columns].astype(F32) for side in range(2)))
             for out, value in zip(outs, own_back(*operands)):
                 out[0, :, columns] = value.astype(BF16)
 
-    near = pl.BlockSpec((1, rows, width), lambda f, spots_ref: (f, 0, 0))
-    away = pl.BlockSpec((1, 1, rows, width), lambda f, spots_ref: (1 - spots_ref[core_at], f, 0, 0))
-    near_all = pl.BlockSpec((frames, rows, width), lambda f, spots_ref: (0, 0, 0))
-    away_all = pl.BlockSpec((1, frames, rows, width), lambda f, spots_ref: (1 - spots_ref[core_at], 0, 0, 0))
+    near = pl.BlockSpec((1, rows, width), lambda f: (f, 0, 0))
+    near_all = pl.BlockSpec((frames, rows, width), lambda f: (0, 0, 0))
+    away = pl.BlockSpec((3, 1, rows, width), lambda f: (0, f, 0, 0))
+    away_all = pl.BlockSpec((1, frames, rows, width), lambda f: (3, 0, 0, 0))
     return pl.pallas_call(
         kernel,
         grid_spec=pltpu.PrefetchScalarGridSpec(
-            num_scalar_prefetch=1,
+            num_scalar_prefetch=0,
             grid=(frames,),
-            in_specs=[near] * 3 + [away] * 3 + [near_all, away_all] + [HBM] * (1 + len(after)),
+            in_specs=[near] * 3 + [away, near_all, away_all] + [HBM] * (1 + len(after)),
             out_specs=[near] * 3,
             scratch_shapes=[
                 pltpu.VMEM((pieces, share, width), BF16),
@@ -346,17 +346,16 @@
         compiler_params=BIG,
         cost_estimate=cost_of(20),
         name="space_attention",
-    )(spots, *own, *far, own_tokens, far_tokens, weights_of, *after)
+    )(*own, far, own_tokens, far, weights_of, *after)
 
 
 def per_device(sizes, grad_out, time_q, time_k, time_v, space_q, space_k, space_v, time_wo, space_wo):
     frames, rows, width = grad_out.shape
     groups, tm, space = sizes
     patches, half = rows // tm, width // 2
-    group, me, core = (lax.axis_index(name) for name in ("groups", "tm", "space"))
+    group, me = lax.axis_index("groups"), lax.axis_index("tm")
     share = time_wo.shape[0] // groups
-    spots = jnp.concatenate([me ^ jnp.arange(tm, dtype=jnp.int32), core.reshape(1)]).astype(jnp.int32)
-    core_at = tm
+    spots = jnp.concatenate([me ^ jnp.arange(tm, dtype=jnp.int32), group.reshape(1)]).astype(jnp.int32)
     order = []
     for low in range(tm // 2):
         order += [tm // 2 - 1 - low, tm - 1 - low]
@@ -364,60 +363,70 @@
     def to_partner(tensor, k):
         return lax.ppermute(tensor, "tm", [(i, i ^ k) for i in range(tm)]) if k else tensor
 
-    def cut(tensor):
-        return lax.dynamic_slice_in_dim(tensor, group * share, share, 0)
-
-    def gathered(piece):
-        whole = lax.all_gather(piece, ("space", "groups", "tm"), axis=0, tiled=True)
+    def moved_one(parts, shape, plan, name, after=()):
+        return moved(spots, parts, [shape], lambda at, refs, outs: plan(at, refs, outs[0]), name, after)[0]
+
+    piece = moved_one(
+        [tensor.reshape(groups, share, width) for tensor in (time_wo, space_wo)],
+        (2, share, width),
+        lambda at, refs, out: [(ref.at[at[tm]], out.at[i]) for i, ref in enumerate(refs)],
+        "own_piece",
+    )
+    columns = lax.all_gather(piece, "tm", axis=0)
+
+    def gathered(column):
+        whole = lax.all_gather(column, ("space", "groups"), axis=0, tiled=True)
         return whole.reshape(space, groups, tm, share, width)
 
-    time_weights = gathered(cut(time_wo))
-
     split = [t.reshape(frames, tm, patches, width) for t in (time_q, time_k, time_v, grad_out)]
+
+    def token_plan(at, parts, outs):
+        return [(parts[0].at[:, at[k]], outs[k]) for k in order]
 
     def payloads(chunk, after=()):
         def plan(at, parts, outs):
             columns = pl.ds(chunk * half, half)
-            pairs = []
-            for k in order:
-                pairs += [(part.at[:, at[k], :, columns], outs[k].at[i]) for i, part in enumerate(parts[:3])]
-                if chunk == 0:
-                    for side in range(2):
-                        side_columns = pl.ds(side * half, half)
-                        pairs.append((parts[3].at[:, at[k], :, side_columns], outs[k].at[3 + side]))
-            return pairs
-
-        kinds = 5 if chunk == 0 else 3
-        shapes = [(kinds, frames, patches, half)] * tm
-        return moved(spots, split[: 4 - chunk], shapes, plan, "payloads", after)
+            return [
+                (part.at[:, at[k], :, columns], outs[k].at[i]) for k in order for i, part in enumerate(parts)
+            ]
+
+        return moved(spots, split[:3], [(3, frames, patches, half)] * tm, plan, "payloads", after)
 
     def exchange(tensors):
         arrived = {k: to_partner(tensors[k], k) for k in order}
         return [arrived[k] for k in range(tm)]
 
-    first_sent = payloads(0)
+    sent_tokens = moved(spots, split[3:], [(frames, patches, width)] * tm, token_plan, "token_payloads", (piece,))
+    tokens = exchange(sent_tokens)
+    first_sent = payloads(0, (sent_tokens[0],))
     early = exchange(first_sent)
-
-    late = exchange(payloads(1, (first_sent[0],)))
-
-    far = [lax.all_gather(tensor, "space", axis=0) for tensor in (space_q, space_k, space_v, grad_out)]
-    space_weights = gathered(cut(space_wo))
-
-    *done, late_grad = time_chunk(early, time_weights, None, "time_first")
+    second_sent = payloads(1, (first_sent[0],))
+    late = exchange(second_sent)
+    both_cores = moved_one(
+        [space_q, space_k, space_v, grad_out],
+        (4, frames, rows, width),
+        lambda at, refs, out: [(ref, out.at[i]) for i, ref in enumerate(refs)],
+        "space_payload",
+        (first_sent[0],),
+    )
+    far = lax.ppermute(both_cores, "space", [(0, 1), (1, 0)])
+
+    time_column, space_column = moved(
+        spots,
+        [columns],
+        [(tm * share, width)] * 2,
+        lambda at, refs, outs: [
+            (refs[0].at[t, i], outs[i].at[pl.ds(t * share, share)]) for i in range(2) for t in range(tm)
+        ],
+        "columns",
+        [tokens[k] for k in order if k],
+    )
+    time_weights, space_weights = gathered(time_column), gathered(space_column)
+
+    *done, late_grad = time_chunk(early, tokens, time_weights, None, "time_first", (far,))
     back = exchange(done)
-    done = time_chunk(late, None, late_grad, "time_second")
+    done = time_chunk(late, (), None, late_grad, "time_second")
     back2 = exchange(done)
-
-    space_out = space_attention(
-        spots,
-        core_at,
-        (space_q, space_k, space_v),
-        far[:3],
-        grad_out,
-        far[3],
-        space_weights,
-        (late_grad,),
-    )
 
     def place(chunk):
         def plan(at, refs, outs):
@@ -432,6 +441,13 @@
 
     shapes = [(frames, tm, patches, width)] * 3
     outs = moved(spots, back, shapes, place(0), "place_first")
+    space_out = space_attention(
+        (space_q, space_k, space_v),
+        far,
+        grad_out,
+        space_weights,
+        (outs[0],),
+    )
     outs = moved(spots, back2, shapes, place(1), "place_second", space_out, outs)
     time_out = [out.reshape(frames, rows, width) for out in outs]
     return (*time_out, *space_out)
@@ -441,8 +457,6 @@
     frames, rows, width = grad_out.shape
     groups, tm, space = sizes
     patches = rows // tm
-    core = lax.axis_index("space")
-    spots = core.reshape(1).astype(jnp.int32)
 
     def to_patches(tensor):
         split = tensor.reshape(tensor.shape[:-2] + (tm, patches, width))
@@ -461,13 +475,14 @@
     else:
         whole = lax.all_gather(both_wo, ("tm", "space"), axis=0, tiled=True)
 
-    far = [lax.all_gather(tensor, "space", axis=0) for tensor in (space_q, space_k, space_v, grad_out)]
+    swap = [(0, 1), (1, 0)]
+    far = lax.ppermute(jnp.stack([space_q, space_k, space_v, grad_out]), "space", swap)
     tokens = grad_out.reshape(frames * rows, width)
     time_grad = jnp.einsum("td,cd->tc", tokens, whole[:, :width], preferred_element_type=F32)
     time_grad = exchanged(to_patches(time_grad.astype(BF16).reshape(frames, rows, width)))
     pieces = whole[:, width:].reshape(tm, space, -1, 1, width)
     pieces = jnp.moveaxis(pieces.reshape(tm, space, 1, -1, width), 0, 2)
-    space_out = space_attention(spots, 0, (space_q, space_k, space_v), far[:3], grad_out, far[3], pieces)
+    space_out = space_attention((space_q, space_k, space_v), far, grad_out, pieces)
 
     back = exchanged(time_attention(time_qkv, time_grad))
     time_out = [jnp.moveaxis(back[:, index], 0, 1).reshape(frames, rows, width) for index in range(3)]

time: 259 us -> 251 us (0.969)
  waiting for transfers between devices: 93.7 us -> 53.9 us
  local copies, waits for them, and re-layouts: 23.9 us -> 40 us
  Pallas kernels: 65.7 us -> 74.7 us
  starting transfers between devices: 60.4 us -> 67 us
    ppermute x28 -> x35, waiting for transfers between devices: 73.7 us -> 35.7 us  [to_partner(): lax.ppermute(tensor, 'tm', [(i, i ^ k) for i in range(tm)])]
    unnamed x96 -> x110, local copies, waits for them, and re-layouts: 22.6 us -> 40 us
    ppermute x28 -> x35, starting transfers between devices: 60.2 us -> 66.8 us  [to_partner(): lax.ppermute(tensor, 'tm', [(i, i ^ k) for i in range(tm)])]
    pallas_call x4 -> x8, Pallas kernels: 13 us -> 19.5 us  [moved(): pl.pallas_call(kernel, in_specs=[SCALARS] + [HBM] * (count + len(after) +...]
    pallas_call x2, Pallas kernels: 29.2 us -> 32.3 us  [time_chunk(): pl.pallas_call(kernel, in_specs=[HBM] * (len(blocks) + 1 + len(after)), o...]
    all_gather x6 -> x3, waiting for transfers between devices: 17.5 us -> 18.2 us  [the longest x1 18.2 us: per_device(): columns = lax.all_gather(piece, 'tm', axis=0)]
  transfers between devices with their start and end apart: 34 -> 39, of which waited for: 11 -> 10; matrix products, arithmetic and copies ran while one was open for 0% -> 0% of each run, Pallas kernels for 24% -> 27%
where the time goes in v4:
time: 251 us; the launch traced here: 250 us
  Pallas kernels  74.7 us (30%)
  starting transfers between devices  67 us (27%)
  waiting for transfers between devices  53.9 us (21%)
  local copies, waits for them, and re-layouts  40 us (16%)
  between operations  14 us (6%)
    ppermute x35, starting transfers between devices, to_partner(): lax.ppermute(tensor, 'tm', [(i, i ^ k) for i in range(tm)])  66.8 us
    unnamed x110, local copies, waits for them, and re-layouts  40 us
    ppermute x35, waiting for transfers between devices, to_partner(): lax.ppermute(tensor, 'tm', [(i, i ^ k) for i in range(tm)])  35.7 us
    pallas_call x2, Pallas kernels, time_chunk(): pl.pallas_call(kernel, in_specs=[HBM] * (len(blocks) + 1 + len(after)), o...  32.3 us
    pallas_call x1, Pallas kernels, space_attention(): pl.pallas_call(kernel, grid_spec=pltpu.PrefetchScalarGridSpec(num_scalar_...  22.8 us
    pallas_call x8, Pallas kernels, moved(): pl.pallas_call(kernel, in_specs=[SCALARS] + [HBM] * (count + len(after) +...  19.5 us
    all_gather x1, waiting for transfers between devices, per_device(): columns = lax.all_gather(piece, 'tm', axis=0)  18.2 us
  transfers between devices with their start and end apart: 39, of which 10 were waited for; matrix products, arithmetic and copies ran while one was open for 0% of the time, Pallas kernels for 27%

profile of v4, /device:TPU:0, one launch (start us, length us, event | category | flops | bytes accessed | tf_op | source)
XLA Modules:
  0.0 249.6 jit_solution(2498455447465981114)
XLA Ops:
  7.3 0.9 copy-done.46
  8.2 0.9 copy-done.47
  9.1 1.2 own_piece.1.refs_1_
  10.4 1.2 copy-done
  11.6 1.9 token_payloads.1
  13.5 3.0 %collective-permute-start.14 = (bf16[7,8,1024]{2,1,0:T(8,128)(2,1)S(1)}, bf16[7,8,1024]{2,1,0:T(8,128)(2,1)S(1)}, u32[]{:S(2)}, u32[]{:S(2)}) collective-permute-start(bf16[7,8,1024]{2,1,0:T(8,128)(2,1)S(1)} %get-tuple-element.75), channel_id=1, source_target_pairs={{0,2},{2,0},{4,6},{6,4},{8,10},{10,8},{12,14},{14,12},{1,3},{3,1},... | collective-permute-start | bytes 344072 | tf_op jit(solution)/shard_map/ppermute | solution.py:364
  16.6 1.6 collective-permute-start.15
  18.1 3.0 %collective-permute-start.17 = (bf16[7,8,1024]{2,1,0:T(8,128)(2,1)S(1)}, bf16[7,8,1024]{2,1,0:T(8,128)(2,1)S(1)}, u32[]{:S(2)}, u32[]{:S(2)}) collective-permute-start(bf16[7,8,1024]{2,1,0:T(8,128)(2,1)S(1)} %get-tuple-element.78), channel_id=1, source_target_pairs={{0,8},{2,10},{4,12},{6,14},{8,0},{10,2},{12,4},{14,6},{1,9},{3,11}... | collective-permute-start | bytes 344072 | tf_op jit(solution)/shard_map/ppermute | solution.py:364
  21.1 1.3 collective-permute-start.18
  22.4 3.6 %collective-permute-start.19 = (bf16[7,8,1024]{2,1,0:T(8,128)(2,1)S(1)}, bf16[7,8,1024]{2,1,0:T(8,128)(2,1)S(1)}, u32[]{:S(2)}, u32[]{:S(2)}) collective-permute-start(bf16[7,8,1024]{2,1,0:T(8,128)(2,1)S(1)} %get-tuple-element.80), channel_id=1, source_target_pairs={{0,12},{2,14},{4,8},{6,10},{8,4},{10,6},{12,0},{14,2},{1,13},{3,15... | collective-permute-start | bytes 344072 | tf_op jit(solution)/shard_map/ppermute | solution.py:364
  27.1 2.4 collective-permute-done.17.refs_7_.refs_12_
  29.5 13.1 %collective-permute-done.18.refs_6_.refs_13_ = bf16[7,8,1024]{2,1,0:T(8,128)(2,1)S(1)} collective-permute-done((bf16[7,8,1024]{2,1,0:T(8,128)(2,1)S(1)}, bf16[7,8,1024]{2,1,0:T(8,128)(2,1)S(1)}, u32[]{:S(2)}, u32[]{:S(2)}) %collective-permute-start.18) | collective-permute-done | bytes 114720 | tf_op jit(solution)/shard_map/ppermute | solution.py:364
  43.9 18.2 %all-gather.9.cloned.1.call-done = bf16[16,32,1024]{2,1,0:T(8,128)(2,1)} async-done(((bf16[2,32,1024]{2,1,0:T(8,128)(2,1)}), bf16[16,32,1024]{2,1,0:T(8,128)(2,1)}) %all-gather.9.cloned.1.call-update) | async-done | bytes 1048592 | tf_op jit(solution)/shard_map/all_gather | solution.py:375
  62.1 1.2 copy-done.14
  63.3 0.9 copy-done.21
  64.2 0.9 copy-done.24
  65.1 1.7 columns.1
  66.9 1.2 copy-done.4
  68.1 2.7 %payloads.2 = (bf16[3,7,8,512]{3,2,1,0:T(8,128)(2,1)S(1)}, bf16[3,7,8,512]{3,2,1,0:T(8,128)(2,1)S(1)}, bf16[3,7,8,512]{3,2,1,0:T(8,128)(2,1)S(1)}, bf16[3,7,8,51...) custom-call(s32[9]{0:T(128)S(1)} %pad_add_fusion.spots_ref, ...), custom_call_target="tpu_custom_call" | custom-call | tf_op jit(solution)/shard_map/payloads/pallas_call | solution.py:177
  74.1 1.3 copy-done.6
  75.4 1.2 copy-done.8
  76.6 1.2 copy-done.10
  77.8 3.0 %space_payload.1 = bf16[4,7,64,1024]{3,2,1,0:T(8,128)(2,1)} custom-call(s32[9]{0:T(128)S(1)} %pad_add_fusion.spots_ref, bf16[7,64,1024]{2,1,0:T(8,128)(2,1)S(1)} %copy-done.6, bf16[7,64,1024]{2,1,0:T(8,128)(2,1)S(1)} %copy-done.8, bf16[7,64,1024]{2,1,0:T(8,128)(2,1)S(1)} %copy-done.10, bf16[7,64,1024]{2,1,0:T(8,128)(2,1)S(1)} %copy-done.1, ...), custom_call_target="tpu_custom_call" | custom-call | tf_op jit(solution)/shard_map/space_payload/pallas_call | solution.py:177
  81.7 2.3 collective-permute-start.11
  84.1 2.2 collective-permute-start.12
  86.2 2.3 collective-permute-start.13
  88.6 15.3 %collective-permute-done.10.refs_4_ = bf16[3,7,8,512]{3,2,1,0:T(8,128)(2,1)S(1)} collective-permute-done((bf16[3,7,8,512]{3,2,1,0:T(8,128)(2,1)}, bf16[3,7,8,512]{3,2,1,0:T(8,128)(2,1)S(1)}, u32[]{:S(2)}, u32[]{:S(2)}) %collective-permute-start.10) | collective-permute-done | bytes 172064 | tf_op jit(solution)/shard_map/ppermute | solution.py:364
  104.9 1.2 copy-done.5
  106.1 2.2 payloads.3
  110.3 3.1 %collective-permute-start.9 = (bf16[3,7,8,512]{3,2,1,0:T(8,128)(2,1)}, bf16[3,7,8,512]{3,2,1,0:T(8,128)(2,1)S(1)}, u32[]{:S(2)}, u32[]{:S(2)}) collective-permute-start(bf16[3,7,8,512]{3,2,1,0:T(8,128)(2,1)} %copy-done.48), channel_id=1, source_target_pairs={{0,6},{2,4},{4,2},{6,0},{8,14},{10,12},{12,10},{14,8},{1,7},{3,5},... | collective-permute-start | bytes 516104 | tf_op jit(solution)/shard_map/ppermute | solution.py:364
  115.2 2.8 %collective-permute-start.1 = (bf16[3,7,8,512]{3,2,1,0:T(8,128)(2,1)S(1)}, bf16[3,7,8,512]{3,2,1,0:T(8,128)(2,1)S(1)}, u32[]{:S(2)}, u32[]{:S(2)}) collective-permute-start(bf16[3,7,8,512]{3,2,1,0:T(8,128)(2,1)S(1)} %get-tuple-element.62), channel_id=1, source_target_pairs={{0,4},{2,6},{4,0},{6,2},{8,12},{10,14},{12,8},{14,10},{1,5},{3,7},... | collective-permute-start | bytes 516104 | tf_op jit(solution)/shard_map/ppermute | solution.py:364
  118.9 2.6 %collective-permute-done.9.refs_3_ = bf16[3,7,8,512]{3,2,1,0:T(8,128)(2,1)S(1)} collective-permute-done((bf16[3,7,8,512]{3,2,1,0:T(8,128)(2,1)}, bf16[3,7,8,512]{3,2,1,0:T(8,128)(2,1)S(1)}, u32[]{:S(2)}, u32[]{:S(2)}) %collective-permute-start.9) | collective-permute-done | bytes 172064 | tf_op jit(solution)/shard_map/ppermute | solution.py:364
  123.1 2.8 %collective-permute-start.4 = (bf16[3,7,8,512]{3,2,1,0:T(8,128)(2,1)}, bf16[3,7,8,512]{3,2,1,0:T(8,128)(2,1)}, u32[]{:S(2)}, u32[]{:S(2)}) collective-permute-start(bf16[3,7,8,512]{3,2,1,0:T(8,128)(2,1)} %get-tuple-element.65), channel_id=1, source_target_pairs={{0,10},{2,8},{4,14},{6,12},{8,2},{10,0},{12,6},{14,4},{1,11},{3,9}... | collective-permute-start | bytes 516104 | tf_op jit(solution)/shard_map/ppermute | solution.py:364
  127.0 2.3 collective-permute-start.5
  129.4 2.7 %collective-permute-start.6 = (bf16[3,7,8,512]{3,2,1,0:T(8,128)(2,1)}, bf16[3,7,8,512]{3,2,1,0:T(8,128)(2,1)}, u32[]{:S(2)}, u32[]{:S(2)}) collective-permute-start(bf16[3,7,8,512]{3,2,1,0:T(8,128)(2,1)} %get-tuple-element.67), channel_id=1, source_target_pairs={{0,14},{2,12},{4,10},{6,8},{8,6},{10,4},{12,2},{14,0},{1,15},{3,13... | collective-permute-start | bytes 516104 | tf_op jit(solution)/shard_map/ppermute | solution.py:364
  132.0 1.6 copy-done.13
  133.6 0.9 copy-done.19
  134.5 0.9 copy-done.22
  136.3 0.9 copy-done.33
  137.2 0.9 copy-done.35
  138.2 0.9 copy-done.37
  139.1 0.9 copy-done.39
  140.0 0.9 copy-done.41
  140.9 0.9 copy-done.43
  141.8 0.9 copy-done.45
  142.8 20.3 %time_first.1 = (bf16[3,7,8,512]{3,2,1,0:T(8,128)(2,1)S(1)}, bf16[3,7,8,512]{3,2,1,0:T(8,128)(2,1)S(1)}, bf16[3,7,8,512]{3,2,1,0:T(8,128)(2,1)S(1)}, bf16[3,7,8,...) custom-call(bf16[3,7,8,512]{3,2,1,0:T(8,128)(2,1)S(1)} %get-tuple-el, ...), custom_call_target="tpu_custom_call" | custom-call | bytes 59040000 | tf_op jit(solution)/shard_map/time_first/pallas_call | solution.py:285
  163.5 3.2 %collective-permute-start.31 = (bf16[3,7,8,512]{3,2,1,0:T(8,128)(2,1)S(1)}, bf16[3,7,8,512]{3,2,1,0:T(8,128)(2,1)S(1)}, u32[]{:S(2)}, u32[]{:S(2)}) collective-permute-start(bf16[3,7,8,512]{3,2,1,0:T(8,128)(2,1)S(1)} %get-tuple-element.96), channel_id=1, source_target_pairs={{0,6},{2,4},{4,2},{6,0},{8,14},{10,12},{12,10},{14,8},{1,7},{3,5},... | collective-permute-start | bytes 516104 | tf_op jit(solution)/shard_map/ppermute | solution.py:364
  166.7 1.0 collective-permute-start.32
  167.7 1.7 collective-permute-start.33
  169.4 12.0 %time_second.1 = (bf16[3,7,8,512]{3,2,1,0:T(8,128)(2,1)S(1)}, bf16[3,7,8,512]{3,2,1,0:T(8,128)(2,1)S(1)}, bf16[3,7,8,512]{3,2,1,0:T(8,128)(2,1)S(1)}, bf16[3,7,8...) custom-call(bf16[3,7,8,512]{3,2,1,0:T(8,128)(2,1)S(1)} %copy-done.27, ...), custom_call_target="tpu_custom_call" | custom-call | bytes 36900000 | tf_op jit(solution)/shard_map/time_second/pallas_call | solution.py:285
  181.3 2.4 collective-permute-start.34
  183.7 2.7 %collective-permute-start.35 = (bf16[3,7,8,512]{3,2,1,0:T(8,128)(2,1)S(1)}, bf16[3,7,8,512]{3,2,1,0:T(8,128)(2,1)S(1)}, u32[]{:S(2)}, u32[]{:S(2)}) collective-permute-start(bf16[3,7,8,512]{3,2,1,0:T(8,128)(2,1)S(1)} %get-tuple-element.100), channel_id=1, source_target_pairs={{0,14},{2,12},{4,10},{6,8},{8,6},{10,4},{12,2},{14,0},{1,15},{3,13... | collective-permute-start | bytes 516104 | tf_op jit(solution)/shard_map/ppermute | solution.py:364
  186.7 3.2 %collective-permute-start.24 = (bf16[3,7,8,512]{3,2,1,0:T(8,128)(2,1)}, bf16[3,7,8,512]{3,2,1,0:T(8,128)(2,1)S(1)}, u32[]{:S(2)}, u32[]{:S(2)}) collective-permute-start(bf16[3,7,8,512]{3,2,1,0:T(8,128)(2,1)} %get-tuple-element.87), channel_id=1, source_target_pairs={{0,6},{2,4},{4,2},{6,0},{8,14},{10,12},{12,10},{14,8},{1,7},{3,5},... | collective-permute-start | bytes 516104 | tf_op jit(solution)/shard_map/ppermute | solution.py:364
  190.4 5.8 %collective-permute-start.25 = (bf16[3,7,8,512]{3,2,1,0:T(8,128)(2,1)}, bf16[3,7,8,512]{3,2,1,0:T(8,128)(2,1)}, u32[]{:S(2)}, u32[]{:S(2)}) collective-permute-start(bf16[3,7,8,512]{3,2,1,0:T(8,128)(2,1)} %get-tuple-element.88), channel_id=1, source_target_pairs={{0,8},{2,10},{4,12},{6,14},{8,0},{10,2},{12,4},{14,6},{1,9},{3,11}... | collective-permute-start | bytes 516104 | tf_op jit(solution)/shard_map/ppermute | solution.py:364
  196.2 8.3 %collective-permute-start.26 = (bf16[3,7,8,512]{3,2,1,0:T(8,128)(2,1)}, bf16[3,7,8,512]{3,2,1,0:T(8,128)(2,1)}, u32[]{:S(2)}, u32[]{:S(2)}) collective-permute-start(bf16[3,7,8,512]{3,2,1,0:T(8,128)(2,1)} %get-tuple-element.89), channel_id=1, source_target_pairs={{0,10},{2,8},{4,14},{6,12},{8,2},{10,0},{12,6},{14,4},{1,11},{3,9}... | collective-permute-start | bytes 516104 | tf_op jit(solution)/shard_map/ppermute | solution.py:364
  204.5 3.0 %collective-permute-start.28 = (bf16[3,7,8,512]{3,2,1,0:T(8,128)(2,1)}, bf16[3,7,8,512]{3,2,1,0:T(8,128)(2,1)}, u32[]{:S(2)}, u32[]{:S(2)}) collective-permute-start(bf16[3,7,8,512]{3,2,1,0:T(8,128)(2,1)} %get-tuple-element.91), channel_id=1, source_target_pairs={{0,14},{2,12},{4,10},{6,8},{8,6},{10,4},{12,2},{14,0},{1,15},{3,13... | collective-permute-start | bytes 516104 | tf_op jit(solution)/shard_map/ppermute | solution.py:364
  207.5 3.4 %place_first.1 = (bf16[7,8,8,1024]{3,2,1,0:T(8,128)(2,1)}, bf16[7,8,8,1024]{3,2,1,0:T(8,128)(2,1)}, bf16[7,8,8,1024]{3,2,1,0:T(8,128)(2,1)}) custom-call(s32[9]{0:T(128)S(1)} %pad_add_fusion.spots_ref, bf16[3,7,8,512]{3,2,1,0:T(8,128)(2,1)S(1)} %get-tuple-element.93.refs_0_, bf16[3,7,8,512]{3,2,1,0:T(8,128)(2,1)S(1)} %collective-permute-done.29.refs_1_, ...), custom_call_target="tpu_custom_call" | custom-call | tf_op jit(solution)/shard_map/place_first/pallas_call | solution.py:177
  210.9 1.2 copy-done.11
  212.1 1.2 copy-done.12
  213.2 22.8 %space_attention.1 = (bf16[7,64,1024]{2,1,0:T(8,128)(2,1)}, bf16[7,64,1024]{2,1,0:T(8,128)(2,1)}, bf16[7,64,1024]{2,1,0:T(8,128)(2,1)}) custom-call(bf16[7,64,1024]{2,1,0:T(8,128)(2,1)S(1)} %copy-done.7, bf16[7,64,1024]{2,1,0:T(8,128)(2,1)S(1)} %copy-done.9, bf16[7,64,1024]{2,1,0:T(8,128)(2,1)S(1)} %copy-done.11, ...), custom_call_target="tpu_custom_call" | custom-call | bytes 73800000 | tf_op jit(solution)/shard_map/space_attention/pallas_call | solution.py:332
  236.1 1.2 copy-done.15
  237.3 1.2 copy-done.16
  238.5 1.2 copy-done.17
  239.7 3.5 %place_second.1 = (bf16[7,8,8,1024]{3,2,1,0:T(8,128)(2,1)}, bf16[7,8,8,1024]{3,2,1,0:T(8,128)(2,1)}, bf16[7,8,8,1024]{3,2,1,0:T(8,128)(2,1)}) custom-call(s32[9]{0:T(128)S(1)} %pad_add_fusion.spots_ref, bf16[3,7,8,512]{3,2,1,0:T(8,128)(2,1)S(1)} %get-tuple-element.84.refs_0_, ...), custom_call_target="tpu_custom_call", output_to_operand_aliasing={{0}: (12, {}), {1}: (13, {}), {2}: (14, {})} | custom-call | tf_op jit(solution)/shard_map/place_second/pallas_call | solution.py:177
  (140 shorter events, 17.5 us)
Async XLA Ops:
  7.2 54.9 %all-gather.9.cloned.1.call-start = ((), (), s32[]{:S(2)}) async-start(), calls=%async_computation.2 | async-start | bytes 1179648 | tf_op jit(solution)/shard_map/all_gather | solution.py:375
  10.4 121.7 %all-gather.5.cloned.1.call-start = ((), (), s32[]{:S(2)}) async-start(), calls=%async_computation | async-start | bytes 2621440 | tf_op jit(solution)/shard_map/all_gather | solution.py:378
  10.4 1.2 copy-start
  11.6 55.3 %copy-start.2 = (bf16[7,64,1024]{2,1,0:T(8,128)(2,1)S(1)}, bf16[7,64,1024]{2,1,0:T(8,128)(2,1)}, u32[]{:S(2)}) copy-start(bf16[7,64,1024]{2,1,0:T(8,128)(2,1)} %param.10) | copy-start | bytes 2752516
  11.6 55.3 %copy-start.3 = (bf16[7,64,1024]{2,1,0:T(8,128)(2,1)S(1)}, bf16[7,64,1024]{2,1,0:T(8,128)(2,1)}, u32[]{:S(2)}) copy-start(bf16[7,64,1024]{2,1,0:T(8,128)(2,1)} %param.11) | copy-start | bytes 2752516
  11.6 62.5 %copy-start.1 = (bf16[7,64,1024]{2,1,0:T(8,128)(2,1)S(1)}, bf16[7,64,1024]{2,1,0:T(8,128)(2,1)}, u32[]{:S(2)}) copy-start(bf16[7,64,1024]{2,1,0:T(8,128)(2,1)} %refs_4_.1) | copy-start | bytes 2752516
  13.5 8.9 %collective-permute-start.14 = (bf16[7,8,1024]{2,1,0:T(8,128)(2,1)S(1)}, bf16[7,8,1024]{2,1,0:T(8,128)(2,1)S(1)}, u32[]{:S(2)}, u32[]{:S(2)}) collective-permute-start(bf16[7,8,1024]{2,1,0:T(8,128)(2,1)S(1)} %get-tuple-element.75), channel_id=1, source_target_pairs={{0,2},{2,0},{4,6},{6,4},{8,10},{10,8},{12,14},{14,12},{1,3},{3,1},... | collective-permute-start | bytes 344072 | tf_op jit(solution)/shard_map/ppermute | solution.py:364
  16.6 10.3 %collective-permute-start.15 = (bf16[7,8,1024]{2,1,0:T(8,128)(2,1)S(1)}, bf16[7,8,1024]{2,1,0:T(8,128)(2,1)S(1)}, u32[]{:S(2)}, u32[]{:S(2)}) collective-permute-start(bf16[7,8,1024]{2,1,0:T(8,128)(2,1)S(1)} %get-tuple-element.76), channel_id=1, source_target_pairs={{0,4},{2,6},{4,0},{6,2},{8,12},{10,14},{12,8},{14,10},{1,5},{3,7},... | collective-permute-start | bytes 344072 | tf_op jit(solution)/shard_map/ppermute | solution.py:364
  18.1 9.0 %collective-permute-start.16 = (bf16[7,8,1024]{2,1,0:T(8,128)(2,1)S(1)}, bf16[7,8,1024]{2,1,0:T(8,128)(2,1)S(1)}, u32[]{:S(2)}, u32[]{:S(2)}) collective-permute-start(bf16[7,8,1024]{2,1,0:T(8,128)(2,1)S(1)} %get-tuple-element.77), channel_id=1, source_target_pairs={{0,6},{2,4},{4,2},{6,0},{8,14},{10,12},{12,10},{14,8},{1,7},{3,5},... | collective-permute-start | bytes 344072 | tf_op jit(solution)/shard_map/ppermute | solution.py:364
  18.1 11.4 %collective-permute-start.17 = (bf16[7,8,1024]{2,1,0:T(8,128)(2,1)S(1)}, bf16[7,8,1024]{2,1,0:T(8,128)(2,1)S(1)}, u32[]{:S(2)}, u32[]{:S(2)}) collective-permute-start(bf16[7,8,1024]{2,1,0:T(8,128)(2,1)S(1)} %get-tuple-element.78), channel_id=1, source_target_pairs={{0,8},{2,10},{4,12},{6,14},{8,0},{10,2},{12,4},{14,6},{1,9},{3,11}... | collective-permute-start | bytes 344072 | tf_op jit(solution)/shard_map/ppermute | solution.py:364
  21.1 21.5 %collective-permute-start.18 = (bf16[7,8,1024]{2,1,0:T(8,128)(2,1)S(1)}, bf16[7,8,1024]{2,1,0:T(8,128)(2,1)S(1)}, u32[]{:S(2)}, u32[]{:S(2)}) collective-permute-start(bf16[7,8,1024]{2,1,0:T(8,128)(2,1)S(1)} %get-tuple-element.79), channel_id=1, source_target_pairs={{0,10},{2,8},{4,14},{6,12},{8,2},{10,0},{12,6},{14,4},{1,11},{3,9}... | collective-permute-start | bytes 344072 | tf_op jit(solution)/shard_map/ppermute | solution.py:364
  22.4 20.2 %collective-permute-start.19 = (bf16[7,8,1024]{2,1,0:T(8,128)(2,1)S(1)}, bf16[7,8,1024]{2,1,0:T(8,128)(2,1)S(1)}, u32[]{:S(2)}, u32[]{:S(2)}) collective-permute-start(bf16[7,8,1024]{2,1,0:T(8,128)(2,1)S(1)} %get-tuple-element.80), channel_id=1, source_target_pairs={{0,12},{2,14},{4,8},{6,10},{8,4},{10,6},{12,0},{14,2},{1,13},{3,15... | collective-permute-start | bytes 344072 | tf_op jit(solution)/shard_map/ppermute | solution.py:364
  26.8 16.5 %collective-permute-start.20 = (bf16[7,8,1024]{2,1,0:T(8,128)(2,1)S(1)}, bf16[7,8,1024]{2,1,0:T(8,128)(2,1)S(1)}, u32[]{:S(2)}, u32[]{:S(2)}) collective-permute-start(bf16[7,8,1024]{2,1,0:T(8,128)(2,1)S(1)} %get-tuple-element.81), channel_id=1, source_target_pairs={{0,14},{2,12},{4,10},{6,8},{8,6},{10,4},{12,2},{14,0},{1,15},{3,13... | collective-permute-start | bytes 344072 | tf_op jit(solution)/shard_map/ppermute | solution.py:364
  42.6 24.3 %copy-start.18 = (bf16[7,8,1024]{2,1,0:T(8,128)(2,1)}, bf16[7,8,1024]{2,1,0:T(8,128)(2,1)S(1)}, u32[]{:S(2)}) copy-start(bf16[7,8,1024]{2,1,0:T(8,128)(2,1)S(1)} %collective-permute-done.18.refs_6_.refs_13_) | copy-start | bytes 344068
  62.1 1.2 copy-start.14
  66.8 144.1 %all-gather.7.cloned.1.call-start = ((), (), s32[]{:S(2)}) async-start(), calls=%async_computation.1 | async-start | bytes 2621440 | tf_op jit(solution)/shard_map/all_gather | solution.py:378
  66.9 1.2 copy-start.4
  74.1 6.7 %copy-start.48 = (bf16[3,7,8,512]{3,2,1,0:T(8,128)(2,1)}, bf16[3,7,8,512]{3,2,1,0:T(8,128)(2,1)S(1)}, u32[]{:S(2)}) copy-start(bf16[3,7,8,512]{3,2,1,0:T(8,128)(2,1)S(1)} %get-tuple-element.70) | copy-start | bytes 516100
  74.1 6.7 %copy-start.49 = (bf16[3,7,8,512]{3,2,1,0:T(8,128)(2,1)}, bf16[3,7,8,512]{3,2,1,0:T(8,128)(2,1)S(1)}, u32[]{:S(2)}) copy-start(bf16[3,7,8,512]{3,2,1,0:T(8,128)(2,1)S(1)} %get-tuple-element.69) | copy-start | bytes 516100
  74.1 1.3 copy-start.6
  75.4 1.2 copy-start.8
  76.6 1.2 copy-start.10
  80.8 48.5 %collective-permute-start.21 = (bf16[4,7,64,1024]{3,2,1,0:T(8,128)(2,1)}, bf16[4,7,64,1024]{3,2,1,0:T(8,128)(2,1)}, u32[]{:S(2)}, u32[]{:S(2)}) collective-permute-start(bf16[4,7,64,1024]{3,2,1,0:T(8,128)(2,1)} %space_payload.1), channel_id=1, source_target_pairs={{0,1},{1,0},{2,3},{3,2},{4,5},{5,4},{6,7},{7,6},{8,9},{9,8},{10,11... | collective-permute-start | bytes 11010056 | tf_op jit(solution)/shard_map/ppermute | solution.py:412
  80.9 23.0 %collective-permute-start.10 = (bf16[3,7,8,512]{3,2,1,0:T(8,128)(2,1)}, bf16[3,7,8,512]{3,2,1,0:T(8,128)(2,1)S(1)}, u32[]{:S(2)}, u32[]{:S(2)}) collective-permute-start(bf16[3,7,8,512]{3,2,1,0:T(8,128)(2,1)} %copy-done.54), channel_id=1, source_target_pairs={{0,8},{2,10},{4,12},{6,14},{8,0},{10,2},{12,4},{14,6},{1,9},{3,11}... | collective-permute-start | bytes 516104 | tf_op jit(solution)/shard_map/ppermute | solution.py:364
  81.7 27.3 %collective-permute-start.11 = (bf16[3,7,8,512]{3,2,1,0:T(8,128)(2,1)}, bf16[3,7,8,512]{3,2,1,0:T(8,128)(2,1)S(1)}, u32[]{:S(2)}, u32[]{:S(2)}) collective-permute-start(bf16[3,7,8,512]{3,2,1,0:T(8,128)(2,1)} %copy-done.53), channel_id=1, source_target_pairs={{0,10},{2,8},{4,14},{6,12},{8,2},{10,0},{12,6},{14,4},{1,11},{3,9}... | collective-permute-start | bytes 516104 | tf_op jit(solution)/shard_map/ppermute | solution.py:364
  84.1 25.6 %collective-permute-start.12 = (bf16[3,7,8,512]{3,2,1,0:T(8,128)(2,1)}, bf16[3,7,8,512]{3,2,1,0:T(8,128)(2,1)S(1)}, u32[]{:S(2)}, u32[]{:S(2)}) collective-permute-start(bf16[3,7,8,512]{3,2,1,0:T(8,128)(2,1)} %copy-done.52), channel_id=1, source_target_pairs={{0,12},{2,14},{4,8},{6,10},{8,4},{10,6},{12,0},{14,2},{1,13},{3,15... | collective-permute-start | bytes 516104 | tf_op jit(solution)/shard_map/ppermute | solution.py:364
  86.2 27.1 %collective-permute-start.13 = (bf16[3,7,8,512]{3,2,1,0:T(8,128)(2,1)}, bf16[3,7,8,512]{3,2,1,0:T(8,128)(2,1)S(1)}, u32[]{:S(2)}, u32[]{:S(2)}) collective-permute-start(bf16[3,7,8,512]{3,2,1,0:T(8,128)(2,1)} %copy-done.51), channel_id=1, source_target_pairs={{0,14},{2,12},{4,10},{6,8},{8,6},{10,4},{12,2},{14,0},{1,15},{3,13... | collective-permute-start | bytes 516104 | tf_op jit(solution)/shard_map/ppermute | solution.py:364
  104.5 10.1 %collective-permute-start.7 = (bf16[3,7,8,512]{3,2,1,0:T(8,128)(2,1)}, bf16[3,7,8,512]{3,2,1,0:T(8,128)(2,1)S(1)}, u32[]{:S(2)}, u32[]{:S(2)}) collective-permute-start(bf16[3,7,8,512]{3,2,1,0:T(8,128)(2,1)} %copy-done.50), channel_id=1, source_target_pairs={{0,2},{2,0},{4,6},{6,4},{8,10},{10,8},{12,14},{14,12},{1,3},{3,1},... | collective-permute-start | bytes 516104 | tf_op jit(solution)/shard_map/ppermute | solution.py:364
  104.9 1.2 copy-start.5
  109.7 8.3 %collective-permute-start.8 = (bf16[3,7,8,512]{3,2,1,0:T(8,128)(2,1)}, bf16[3,7,8,512]{3,2,1,0:T(8,128)(2,1)S(1)}, u32[]{:S(2)}, u32[]{:S(2)}) collective-permute-start(bf16[3,7,8,512]{3,2,1,0:T(8,128)(2,1)} %copy-done.49), channel_id=1, source_target_pairs={{0,4},{2,6},{4,0},{6,2},{8,12},{10,14},{12,8},{14,10},{1,5},{3,7},... | collective-permute-start | bytes 516104 | tf_op jit(solution)/shard_map/ppermute | solution.py:364
  110.3 11.2 %collective-permute-start.9 = (bf16[3,7,8,512]{3,2,1,0:T(8,128)(2,1)}, bf16[3,7,8,512]{3,2,1,0:T(8,128)(2,1)S(1)}, u32[]{:S(2)}, u32[]{:S(2)}) collective-permute-start(bf16[3,7,8,512]{3,2,1,0:T(8,128)(2,1)} %copy-done.48), channel_id=1, source_target_pairs={{0,6},{2,4},{4,2},{6,0},{8,14},{10,12},{12,10},{14,8},{1,7},{3,5},... | collective-permute-start | bytes 516104 | tf_op jit(solution)/shard_map/ppermute | solution.py:364
  114.1 8.4 %collective-permute-start = (bf16[3,7,8,512]{3,2,1,0:T(8,128)(2,1)S(1)}, bf16[3,7,8,512]{3,2,1,0:T(8,128)(2,1)S(1)}, u32[]{:S(2)}, u32[]{:S(2)}) collective-permute-start(bf16[3,7,8,512]{3,2,1,0:T(8,128)(2,1)S(1)} %get-tuple-element.61), channel_id=1, source_target_pairs={{0,2},{2,0},{4,6},{6,4},{8,10},{10,8},{12,14},{14,12},{1,3},{3,1},... | collective-permute-start | bytes 516104 | tf_op jit(solution)/shard_map/ppermute | solution.py:364
  115.2 11.1 %collective-permute-start.1 = (bf16[3,7,8,512]{3,2,1,0:T(8,128)(2,1)S(1)}, bf16[3,7,8,512]{3,2,1,0:T(8,128)(2,1)S(1)}, u32[]{:S(2)}, u32[]{:S(2)}) collective-permute-start(bf16[3,7,8,512]{3,2,1,0:T(8,128)(2,1)S(1)} %get-tuple-element.62), channel_id=1, source_target_pairs={{0,4},{2,6},{4,0},{6,2},{8,12},{10,14},{12,8},{14,10},{1,5},{3,7},... | collective-permute-start | bytes 516104 | tf_op jit(solution)/shard_map/ppermute | solution.py:364
  118.7 44.5 %collective-permute-start.2 = (bf16[3,7,8,512]{3,2,1,0:T(8,128)(2,1)}, bf16[3,7,8,512]{3,2,1,0:T(8,128)(2,1)}, u32[]{:S(2)}, u32[]{:S(2)}) collective-permute-start(bf16[3,7,8,512]{3,2,1,0:T(8,128)(2,1)} %get-tuple-element.63), channel_id=1, source_target_pairs={{0,6},{2,4},{4,2},{6,0},{8,14},{10,12},{12,10},{14,8},{1,7},{3,5},... | collective-permute-start | bytes 516104 | tf_op jit(solution)/shard_map/ppermute | solution.py:364
  122.2 41.3 %collective-permute-start.3 = (bf16[3,7,8,512]{3,2,1,0:T(8,128)(2,1)}, bf16[3,7,8,512]{3,2,1,0:T(8,128)(2,1)}, u32[]{:S(2)}, u32[]{:S(2)}) collective-permute-start(bf16[3,7,8,512]{3,2,1,0:T(8,128)(2,1)} %get-tuple-element.64), channel_id=1, source_target_pairs={{0,8},{2,10},{4,12},{6,14},{8,0},{10,2},{12,4},{14,6},{1,9},{3,11}... | collective-permute-start | bytes 516104 | tf_op jit(solution)/shard_map/ppermute | solution.py:364
  123.1 40.4 %collective-permute-start.4 = (bf16[3,7,8,512]{3,2,1,0:T(8,128)(2,1)}, bf16[3,7,8,512]{3,2,1,0:T(8,128)(2,1)}, u32[]{:S(2)}, u32[]{:S(2)}) collective-permute-start(bf16[3,7,8,512]{3,2,1,0:T(8,128)(2,1)} %get-tuple-element.65), channel_id=1, source_target_pairs={{0,10},{2,8},{4,14},{6,12},{8,2},{10,0},{12,6},{14,4},{1,11},{3,9}... | collective-permute-start | bytes 516104 | tf_op jit(solution)/shard_map/ppermute | solution.py:364
  127.0 39.7 %collective-permute-start.5 = (bf16[3,7,8,512]{3,2,1,0:T(8,128)(2,1)}, bf16[3,7,8,512]{3,2,1,0:T(8,128)(2,1)}, u32[]{:S(2)}, u32[]{:S(2)}) collective-permute-start(bf16[3,7,8,512]{3,2,1,0:T(8,128)(2,1)} %get-tuple-element.66), channel_id=1, source_target_pairs={{0,12},{2,14},{4,8},{6,10},{8,4},{10,6},{12,0},{14,2},{1,13},{3,15... | collective-permute-start | bytes 516104 | tf_op jit(solution)/shard_map/ppermute | solution.py:364
  129.4 38.3 %collective-permute-start.6 = (bf16[3,7,8,512]{3,2,1,0:T(8,128)(2,1)}, bf16[3,7,8,512]{3,2,1,0:T(8,128)(2,1)}, u32[]{:S(2)}, u32[]{:S(2)}) collective-permute-start(bf16[3,7,8,512]{3,2,1,0:T(8,128)(2,1)} %get-tuple-element.67), channel_id=1, source_target_pairs={{0,14},{2,12},{4,10},{6,8},{8,6},{10,4},{12,2},{14,0},{1,15},{3,13... | collective-permute-start | bytes 516104 | tf_op jit(solution)/shard_map/ppermute | solution.py:364
  132.0 1.6 copy-start.13
  140.9 0.9 copy-start.43
  142.8 26.6 %copy-start.27 = (bf16[3,7,8,512]{3,2,1,0:T(8,128)(2,1)S(1)}, bf16[3,7,8,512]{3,2,1,0:T(8,128)(2,1)}, u32[]{:S(2)}) copy-start(bf16[3,7,8,512]{3,2,1,0:T(8,128)(2,1)} %copy-done.26) | copy-start | bytes 516100
  142.8 26.6 %copy-start.29 = (bf16[3,7,8,512]{3,2,1,0:T(8,128)(2,1)S(1)}, bf16[3,7,8,512]{3,2,1,0:T(8,128)(2,1)}, u32[]{:S(2)}) copy-start(bf16[3,7,8,512]{3,2,1,0:T(8,128)(2,1)} %copy-done.28) | copy-start | bytes 516100
  142.8 26.6 %copy-start.31 = (bf16[3,7,8,512]{3,2,1,0:T(8,128)(2,1)S(1)}, bf16[3,7,8,512]{3,2,1,0:T(8,128)(2,1)}, u32[]{:S(2)}) copy-start(bf16[3,7,8,512]{3,2,1,0:T(8,128)(2,1)} %copy-done.30) | copy-start | bytes 516100
  142.8 68.1 %copy-start.7 = (bf16[7,64,1024]{2,1,0:T(8,128)(2,1)S(1)}, bf16[7,64,1024]{2,1,0:T(8,128)(2,1)}, u32[]{:S(2)}) copy-start(bf16[7,64,1024]{2,1,0:T(8,128)(2,1)} %refs_0_.3) | copy-start | bytes 2752516
  142.8 68.1 %copy-start.9 = (bf16[7,64,1024]{2,1,0:T(8,128)(2,1)S(1)}, bf16[7,64,1024]{2,1,0:T(8,128)(2,1)}, u32[]{:S(2)}) copy-start(bf16[7,64,1024]{2,1,0:T(8,128)(2,1)} %refs_1_.3) | copy-start | bytes 2752516
  163.1 18.2 %collective-permute-start.29 = (bf16[3,7,8,512]{3,2,1,0:T(8,128)(2,1)S(1)}, bf16[3,7,8,512]{3,2,1,0:T(8,128)(2,1)S(1)}, u32[]{:S(2)}, u32[]{:S(2)}) collective-permute-start(bf16[3,7,8,512]{3,2,1,0:T(8,128)(2,1)S(1)} %get-tuple-element.94), channel_id=1, source_target_pairs={{0,2},{2,0},{4,6},{6,4},{8,10},{10,8},{12,14},{14,12},{1,3},{3,1},... | collective-permute-start | bytes 516104 | tf_op jit(solution)/shard_map/ppermute | solution.py:364
  163.5 20.3 %collective-permute-start.30 = (bf16[3,7,8,512]{3,2,1,0:T(8,128)(2,1)S(1)}, bf16[3,7,8,512]{3,2,1,0:T(8,128)(2,1)S(1)}, u32[]{:S(2)}, u32[]{:S(2)}) collective-permute-start(bf16[3,7,8,512]{3,2,1,0:T(8,128)(2,1)S(1)} %get-tuple-element.95), channel_id=1, source_target_pairs={{0,4},{2,6},{4,0},{6,2},{8,12},{10,14},{12,8},{14,10},{1,5},{3,7},... | collective-permute-start | bytes 516104 | tf_op jit(solution)/shard_map/ppermute | solution.py:364
  163.5 22.9 %collective-permute-start.31 = (bf16[3,7,8,512]{3,2,1,0:T(8,128)(2,1)S(1)}, bf16[3,7,8,512]{3,2,1,0:T(8,128)(2,1)S(1)}, u32[]{:S(2)}, u32[]{:S(2)}) collective-permute-start(bf16[3,7,8,512]{3,2,1,0:T(8,128)(2,1)S(1)} %get-tuple-element.96), channel_id=1, source_target_pairs={{0,6},{2,4},{4,2},{6,0},{8,14},{10,12},{12,10},{14,8},{1,7},{3,5},... | collective-permute-start | bytes 516104 | tf_op jit(solution)/shard_map/ppermute | solution.py:364
  166.7 20.0 %collective-permute-start.32 = (bf16[3,7,8,512]{3,2,1,0:T(8,128)(2,1)S(1)}, bf16[3,7,8,512]{3,2,1,0:T(8,128)(2,1)S(1)}, u32[]{:S(2)}, u32[]{:S(2)}) collective-permute-start(bf16[3,7,8,512]{3,2,1,0:T(8,128)(2,1)S(1)} %get-tuple-element.97), channel_id=1, source_target_pairs={{0,8},{2,10},{4,12},{6,14},{8,0},{10,2},{12,4},{14,6},{1,9},{3,11}... | collective-permute-start | bytes 516104 | tf_op jit(solution)/shard_map/ppermute | solution.py:364
  167.7 19.0 %collective-permute-start.33 = (bf16[3,7,8,512]{3,2,1,0:T(8,128)(2,1)S(1)}, bf16[3,7,8,512]{3,2,1,0:T(8,128)(2,1)S(1)}, u32[]{:S(2)}, u32[]{:S(2)}) collective-permute-start(bf16[3,7,8,512]{3,2,1,0:T(8,128)(2,1)S(1)} %get-tuple-element.98), channel_id=1, source_target_pairs={{0,10},{2,8},{4,14},{6,12},{8,2},{10,0},{12,6},{14,4},{1,11},{3,9}... | collective-permute-start | bytes 516104 | tf_op jit(solution)/shard_map/ppermute | solution.py:364
  181.3 9.1 %collective-permute-start.34 = (bf16[3,7,8,512]{3,2,1,0:T(8,128)(2,1)S(1)}, bf16[3,7,8,512]{3,2,1,0:T(8,128)(2,1)S(1)}, u32[]{:S(2)}, u32[]{:S(2)}) collective-permute-start(bf16[3,7,8,512]{3,2,1,0:T(8,128)(2,1)S(1)} %get-tuple-element.99), channel_id=1, source_target_pairs={{0,12},{2,14},{4,8},{6,10},{8,4},{10,6},{12,0},{14,2},{1,13},{3,15... | collective-permute-start | bytes 516104 | tf_op jit(solution)/shard_map/ppermute | solution.py:364
  183.7 12.5 %collective-permute-start.35 = (bf16[3,7,8,512]{3,2,1,0:T(8,128)(2,1)S(1)}, bf16[3,7,8,512]{3,2,1,0:T(8,128)(2,1)S(1)}, u32[]{:S(2)}, u32[]{:S(2)}) collective-permute-start(bf16[3,7,8,512]{3,2,1,0:T(8,128)(2,1)S(1)} %get-tuple-element.100), channel_id=1, source_target_pairs={{0,14},{2,12},{4,10},{6,8},{8,6},{10,4},{12,2},{14,0},{1,15},{3,13... | collective-permute-start | bytes 516104 | tf_op jit(solution)/shard_map/ppermute | solution.py:364
  186.4 18.0 %collective-permute-start.22 = (bf16[3,7,8,512]{3,2,1,0:T(8,128)(2,1)S(1)}, bf16[3,7,8,512]{3,2,1,0:T(8,128)(2,1)S(1)}, u32[]{:S(2)}, u32[]{:S(2)}) collective-permute-start(bf16[3,7,8,512]{3,2,1,0:T(8,128)(2,1)S(1)} %get-tuple-element.85), channel_id=1, source_target_pairs={{0,2},{2,0},{4,6},{6,4},{8,10},{10,8},{12,14},{14,12},{1,3},{3,1},... | collective-permute-start | bytes 516104 | tf_op jit(solution)/shard_map/ppermute | solution.py:364
  186.7 17.8 %collective-permute-start.23 = (bf16[3,7,8,512]{3,2,1,0:T(8,128)(2,1)S(1)}, bf16[3,7,8,512]{3,2,1,0:T(8,128)(2,1)S(1)}, u32[]{:S(2)}, u32[]{:S(2)}) collective-permute-start(bf16[3,7,8,512]{3,2,1,0:T(8,128)(2,1)S(1)} %get-tuple-element.86), channel_id=1, source_target_pairs={{0,4},{2,6},{4,0},{6,2},{8,12},{10,14},{12,8},{14,10},{1,5},{3,7},... | collective-permute-start | bytes 516104 | tf_op jit(solution)/shard_map/ppermute | solution.py:364
  186.7 49.4 %collective-permute-start.24 = (bf16[3,7,8,512]{3,2,1,0:T(8,128)(2,1)}, bf16[3,7,8,512]{3,2,1,0:T(8,128)(2,1)S(1)}, u32[]{:S(2)}, u32[]{:S(2)}) collective-permute-start(bf16[3,7,8,512]{3,2,1,0:T(8,128)(2,1)} %get-tuple-element.87), channel_id=1, source_target_pairs={{0,6},{2,4},{4,2},{6,0},{8,14},{10,12},{12,10},{14,8},{1,7},{3,5},... | collective-permute-start | bytes 516104 | tf_op jit(solution)/shard_map/ppermute | solution.py:364
  190.4 45.6 %collective-permute-start.25 = (bf16[3,7,8,512]{3,2,1,0:T(8,128)(2,1)}, bf16[3,7,8,512]{3,2,1,0:T(8,128)(2,1)}, u32[]{:S(2)}, u32[]{:S(2)}) collective-permute-start(bf16[3,7,8,512]{3,2,1,0:T(8,128)(2,1)} %get-tuple-element.88), channel_id=1, source_target_pairs={{0,8},{2,10},{4,12},{6,14},{8,0},{10,2},{12,4},{14,6},{1,9},{3,11}... | collective-permute-start | bytes 516104 | tf_op jit(solution)/shard_map/ppermute | solution.py:364
  196.2 39.9 %collective-permute-start.26 = (bf16[3,7,8,512]{3,2,1,0:T(8,128)(2,1)}, bf16[3,7,8,512]{3,2,1,0:T(8,128)(2,1)}, u32[]{:S(2)}, u32[]{:S(2)}) collective-permute-start(bf16[3,7,8,512]{3,2,1,0:T(8,128)(2,1)} %get-tuple-element.89), channel_id=1, source_target_pairs={{0,10},{2,8},{4,14},{6,12},{8,2},{10,0},{12,6},{14,4},{1,11},{3,9}... | collective-permute-start | bytes 516104 | tf_op jit(solution)/shard_map/ppermute | solution.py:364
  204.5 31.6 %collective-permute-start.27 = (bf16[3,7,8,512]{3,2,1,0:T(8,128)(2,1)}, bf16[3,7,8,512]{3,2,1,0:T(8,128)(2,1)}, u32[]{:S(2)}, u32[]{:S(2)}) collective-permute-start(bf16[3,7,8,512]{3,2,1,0:T(8,128)(2,1)} %get-tuple-element.90), channel_id=1, source_target_pairs={{0,12},{2,14},{4,8},{6,10},{8,4},{10,6},{12,0},{14,2},{1,13},{3,15... | collective-permute-start | bytes 516104 | tf_op jit(solution)/shard_map/ppermute | solution.py:364
  204.5 31.6 %collective-permute-start.28 = (bf16[3,7,8,512]{3,2,1,0:T(8,128)(2,1)}, bf16[3,7,8,512]{3,2,1,0:T(8,128)(2,1)}, u32[]{:S(2)}, u32[]{:S(2)}) collective-permute-start(bf16[3,7,8,512]{3,2,1,0:T(8,128)(2,1)} %get-tuple-element.91), channel_id=1, source_target_pairs={{0,14},{2,12},{4,10},{6,8},{8,6},{10,4},{12,2},{14,0},{1,15},{3,13... | collective-permute-start | bytes 516104 | tf_op jit(solution)/shard_map/ppermute | solution.py:364
  210.9 1.2 copy-start.11
  212.1 1.2 copy-start.12
  236.1 1.2 copy-start.15
  237.3 1.2 copy-start.16
  238.5 1.2 copy-start.17
  (30 other events, 23.2 us)
Sparse Core Ops, SparseCore 0:
  10.7 51.3 all-gather.8
  66.9 21.3 all-gather.4
  90.5 22.5 all-gather.6

commit v5 on v4

--- a/solution.py
+++ b/solution.py
@@ -136,7 +136,7 @@
 
 HBM = pl.BlockSpec(memory_space=pltpu.HBM)
 SCALARS = pl.BlockSpec(memory_space=pltpu.SMEM)
-BIG = pltpu.CompilerParams(vmem_limit_bytes=48 * 2**20)
+BIG = pltpu.CompilerParams(vmem_limit_bytes=24 * 2**20)
 
 
 def cost_of(microseconds):
@@ -180,7 +180,7 @@
         out_specs=[HBM] * len(shapes),
         out_shape=[jax.ShapeDtypeStruct(shape, BF16) for shape in shapes],
         input_output_aliases={1 + count + len(after) + i: i for i in range(len(kept))},
-        compiler_params=BIG,
+        compiler_params=pltpu.CompilerParams(vmem_limit_bytes=2 * sum(math.prod(x) for x in shapes) + 2 * 2**20),
         name=name,
     )(spots, *parts, *after, *kept)
 
@@ -203,15 +203,15 @@
             ref[rows, :] = value
 
 
-def time_chunk(blocks, token_blocks, gathered, late_grad, name, after=()):
+def time_chunk(frames, blocks, token_blocks, gathered, late_grad, name, after=()):
     blocks = [*blocks, *token_blocks]
     first = late_grad is None
     count = len(blocks) // 2 if first else len(blocks)
-    _, frames, patches, lanes = blocks[0].shape
+    patches, lanes = blocks[0].shape[1:]
     total, part = count * frames, frames * patches
     rows, width = total * patches, 2 * lanes
     wide = [pltpu.VMEM(block.shape, BF16) for block in blocks]
-    scratch = wide + [pltpu.VMEM((3, frames, patches, lanes), BF16)] * count
+    scratch = wide + [pltpu.VMEM((3 * frames, patches, lanes), BF16)] * count
     scratch += [pltpu.VMEM((rows, PAIR), F32)] * 7
     if first:
         space, groups, tm, share = gathered.shape[:4]
@@ -246,7 +246,7 @@
             copy.wait()
         if first:
             for index, ref in enumerate(tokens_in):
-                value = ref[...].astype(F32).reshape(part, width)
+                value = ref[:frames].astype(F32).reshape(part, width)
                 grads[index * part : (index + 1) * part, :] = value.astype(BF16)
 
         def one_pair(pair, carry):
@@ -254,7 +254,8 @@
             for index, ref in enumerate(blocks_in):
                 at = slice(index * part, (index + 1) * part)
                 for kind in range(3):
-                    held[kind][at, :] = ref[kind, :, :, columns].astype(F32).reshape(part, PAIR)
+                    value = ref[kind * frames : (kind + 1) * frames, :, columns]
+                    held[kind][at, :] = value.astype(F32).reshape(part, PAIR)
             if first:
                 pieces = weights[pl.ds(pair * (PAIR // share), PAIR // share)].reshape(PAIR, width)
                 held[3][...] = dot(grads[...], pieces, ((1,), (1,))).astype(BF16).astype(F32)
@@ -265,7 +266,7 @@
                 at = slice(index * part, (index + 1) * part)
                 for kind in range(3):
                     value = results[kind][at, :].reshape(frames, patches, PAIR)
-                    ref[kind, :, :, columns] = value.astype(BF16)
+                    ref[kind * frames : (kind + 1) * frames, :, columns] = value.astype(BF16)
             return carry
 
         lax.fori_loop(0, lanes // PAIR, one_pair, 0)
@@ -277,7 +278,7 @@
         for store in stores:
             store.wait()
 
-    out_shapes = [jax.ShapeDtypeStruct((3, frames, patches, lanes), BF16)] * count
+    out_shapes = [jax.ShapeDtypeStruct((3 * frames, patches, lanes), BF16)] * count
     out_specs = [HBM] * count
     if first:
         out_shapes = out_shapes + [jax.ShapeDtypeStruct((rows, lanes), BF16)]
@@ -366,42 +367,46 @@
     def moved_one(parts, shape, plan, name, after=()):
         return moved(spots, parts, [shape], lambda at, refs, outs: plan(at, refs, outs[0]), name, after)[0]
 
-    piece = moved_one(
-        [tensor.reshape(groups, share, width) for tensor in (time_wo, space_wo)],
-        (2, share, width),
-        lambda at, refs, out: [(ref.at[at[tm]], out.at[i]) for i, ref in enumerate(refs)],
-        "own_piece",
-    )
-    columns = lax.all_gather(piece, "tm", axis=0)
-
-    def gathered(column):
-        whole = lax.all_gather(column, ("space", "groups"), axis=0, tiled=True)
-        return whole.reshape(space, groups, tm, share, width)
-
     split = [t.reshape(frames, tm, patches, width) for t in (time_q, time_k, time_v, grad_out)]
+    blocks = share // patches
+    time_pieces, space_pieces = (t.reshape(groups, blocks, patches, width) for t in (time_wo, space_wo))
 
     def token_plan(at, parts, outs):
-        return [(parts[0].at[:, at[k]], outs[k]) for k in order]
-
-    def payloads(chunk, after=()):
+        pairs = []
+        for k in order:
+            pairs.append((parts[0].at[:, at[k]], outs[k].at[pl.ds(0, frames)]))
+            pairs.append((parts[1].at[at[tm]], outs[k].at[pl.ds(frames, blocks)]))
+        return pairs
+
+    def payloads(chunk, more=(), after=()):
         def plan(at, parts, outs):
             columns = pl.ds(chunk * half, half)
-            return [
-                (part.at[:, at[k], :, columns], outs[k].at[i]) for k in order for i, part in enumerate(parts)
-            ]
-
-        return moved(spots, split[:3], [(3, frames, patches, half)] * tm, plan, "payloads", after)
+            pairs = []
+            for k in order:
+                for i in range(3):
+                    pairs.append((parts[i].at[:, at[k], :, columns], outs[k].at[pl.ds(i * frames, frames)]))
+                for part in parts[3:]:
+                    for side in range(2):
+                        kept = outs[k].at[pl.ds(3 * frames + side * blocks, blocks)]
+                        pairs.append((part.at[at[tm], :, :, pl.ds(side * half, half)], kept))
+            return pairs
+
+        shape = (3 * frames + 2 * blocks * len(more), patches, half)
+        return moved(spots, [*split[:3], *more], [shape] * tm, plan, "payloads", after)
 
     def exchange(tensors):
         arrived = {k: to_partner(tensors[k], k) for k in order}
         return [arrived[k] for k in range(tm)]
 
-    sent_tokens = moved(spots, split[3:], [(frames, patches, width)] * tm, token_plan, "token_payloads", (piece,))
+    sent_tokens = moved(
+        spots, [split[3], time_pieces], [(frames + blocks, patches, width)] * tm, token_plan, "token_payloads"
+    )
     tokens = exchange(sent_tokens)
-    first_sent = payloads(0, (sent_tokens[0],))
+    first_sent = payloads(0, (space_pieces,), (sent_tokens[0],))
     early = exchange(first_sent)
-    second_sent = payloads(1, (first_sent[0],))
+    second_sent = payloads(1, (), (first_sent[0],))
     late = exchange(second_sent)
+
     both_cores = moved_one(
         [space_q, space_k, space_v, grad_out],
         (4, frames, rows, width),
@@ -411,28 +416,48 @@
     )
     far = lax.ppermute(both_cores, "space", [(0, 1), (1, 0)])
 
-    time_column, space_column = moved(
-        spots,
-        [columns],
-        [(tm * share, width)] * 2,
-        lambda at, refs, outs: [
-            (refs[0].at[t, i], outs[i].at[pl.ds(t * share, share)]) for i in range(2) for t in range(tm)
-        ],
-        "columns",
-        [tokens[k] for k in order if k],
+    def gathered(column):
+        whole = lax.all_gather(column, ("space", "groups"), axis=0, tiled=True)
+        return whole.reshape(space, groups, tm, share, width)
+
+    time_weights = gathered(
+        moved_one(
+            tokens,
+            (tm, blocks, patches, width),
+            lambda at, refs, out: [
+                (ref.at[pl.ds(frames, blocks)], out.at[at[k]]) for k, ref in enumerate(refs)
+            ],
+            "time_column",
+            (first_sent[0], both_cores),
+        )
     )
-    time_weights, space_weights = gathered(time_column), gathered(space_column)
-
-    *done, late_grad = time_chunk(early, tokens, time_weights, None, "time_first", (far,))
+    space_weights = gathered(
+        moved_one(
+            early,
+            (tm, blocks, patches, width),
+            lambda at, refs, out: [
+                (
+                    ref.at[pl.ds(3 * frames + side * blocks, blocks)],
+                    out.at[at[k], :, :, pl.ds(side * half, half)],
+                )
+                for k, ref in enumerate(refs)
+                for side in range(2)
+            ],
+            "space_column",
+            (second_sent[0],),
+        )
+    )
+
+    *done, late_grad = time_chunk(frames, early, tokens, time_weights, None, "time_first", (far,))
     back = exchange(done)
-    done = time_chunk(late, (), None, late_grad, "time_second")
+    done = time_chunk(frames, late, (), None, late_grad, "time_second")
     back2 = exchange(done)
 
     def place(chunk):
         def plan(at, refs, outs):
             columns = pl.ds(chunk * half, half)
             return [
-                (ref.at[kind], outs[kind].at[:, at[k], :, columns])
+                (ref.at[pl.ds(kind * frames, frames)], outs[kind].at[:, at[k], :, columns])
                 for k, ref in enumerate(refs)
                 for kind in range(3)
             ]
@@ -498,7 +523,7 @@
 
     def body(*tensors):
         patches, rows = tensors[0].shape[1] // tm, tensors[-1].shape[0]
-        fits = paired and patches % 8 == 0 and rows % (16 * groups) == 0
+        fits = paired and patches % 8 == 0 and rows % (16 * groups) == 0 and rows % (groups * patches) == 0
         return (per_device if fits else per_device_plain)(sizes, *tensors)
 
     return jax.shard_map(

time: 251 us -> 264 us (1.052)
  waiting for transfers between devices: 53.9 us -> 40 us
  starting transfers between devices: 67 us -> 79.1 us
  local copies, waits for them, and re-layouts: 40 us -> 48.4 us
  Pallas kernels: 74.7 us -> 80.7 us
    all_gather x1 -> x0, waiting for transfers between devices: 18.2 us -> none  [per_device(): columns = lax.all_gather(piece, 'tm', axis=0)]
    ppermute x35, starting transfers between devices: 66.8 us -> 78.7 us  [to_partner(): lax.ppermute(tensor, 'tm', [(i, i ^ k) for i in range(tm)])]
    unnamed x110 -> x138, local copies, waits for them, and re-layouts: 40 us -> 48.4 us
    ppermute x35, waiting for transfers between devices: 35.7 us -> 40 us  [to_partner(): lax.ppermute(tensor, 'tm', [(i, i ^ k) for i in range(tm)])]
    pallas_call x8, Pallas kernels: 19.5 us -> 22.3 us  [moved(): pl.pallas_call(kernel, in_specs=[SCALARS] + [HBM] * (count + len(after) +...]
  transfers between devices with their start and end apart: 39 -> 38, of which waited for: 10 -> 7; matrix products, arithmetic and copies ran while one was open for 0% -> 0% of each run, Pallas kernels for 27% -> 27%
where the time goes in v5:
time: 264 us; the launch traced here: 263 us
  Pallas kernels  80.7 us (31%)
  starting transfers between devices  79.1 us (30%)
  local copies, waits for them, and re-layouts  48.4 us (18%)
  waiting for transfers between devices  40 us (15%)
  between operations  14.4 us (5%)
    ppermute x35, starting transfers between devices, to_partner(): lax.ppermute(tensor, 'tm', [(i, i ^ k) for i in range(tm)])  78.7 us
    unnamed x138, local copies, waits for them, and re-layouts  48.4 us
    ppermute x35, waiting for transfers between devices, to_partner(): lax.ppermute(tensor, 'tm', [(i, i ^ k) for i in range(tm)])  40 us
    pallas_call x2, Pallas kernels, time_chunk(): pl.pallas_call(kernel, in_specs=[HBM] * (len(blocks) + 1 + len(after)), o...  33.8 us
    pallas_call x1, Pallas kernels, space_attention(): pl.pallas_call(kernel, grid_spec=pltpu.PrefetchScalarGridSpec(num_scalar_...  24.5 us
    pallas_call x8, Pallas kernels, moved(): pl.pallas_call(kernel, in_specs=[SCALARS] + [HBM] * (count + len(after) +...  22.3 us
  transfers between devices with their start and end apart: 38, of which 7 were waited for; matrix products, arithmetic and copies ran while one was open for 0% of the time, Pallas kernels for 27%

profile of v5, /device:TPU:0, one launch (start us, length us, event | category | flops | bytes accessed | tf_op | source)
XLA Modules:
  0.0 262.7 jit_solution(9985419494525513095)
XLA Ops:
  7.3 1.2 copy-done.1
  9.4 3.3 %token_payloads.1 = (bf16[11,8,1024]{2,1,0:T(8,128)(2,1)S(1)}, bf16[11,8,1024]{2,1,0:T(8,128)(2,1)S(1)}, bf16[11,8,1024]{2,1,0:T(8,128)(2,1)S(1)}, bf16[11,8,102...) custom-call(s32[9]{0:T(128)S(1)} %pad_add_fusion.spots_ref, ...), custom_call_target="tpu_custom_call" | custom-call | tf_op jit(solution)/shard_map/token_payloads/pallas_call | solution.py:177
  12.7 3.0 %collective-permute-start.14 = (bf16[11,8,1024]{2,1,0:T(8,128)(2,1)S(1)}, bf16[11,8,1024]{2,1,0:T(8,128)(2,1)S(1)}, u32[]{:S(2)}, u32[]{:S(2)}) collective-permute-start(bf16[11,8,1024]{2,1,0:T(8,128)(2,1)S(1)} %get-tuple-element.73), channel_id=1, source_target_pairs={{0,2},{2,0},{4,6},{6,4},{8,10},{10,8},{12,14},{14,12},{1,3},{3,1},... | collective-permute-start | bytes 540680 | tf_op jit(solution)/shard_map/ppermute | solution.py:365
  15.8 1.6 collective-permute-start.15
  17.3 3.0 %collective-permute-start.17 = (bf16[11,8,1024]{2,1,0:T(8,128)(2,1)S(1)}, bf16[11,8,1024]{2,1,0:T(8,128)(2,1)S(1)}, u32[]{:S(2)}, u32[]{:S(2)}) collective-permute-start(bf16[11,8,1024]{2,1,0:T(8,128)(2,1)S(1)} %get-tuple-element.76), channel_id=1, source_target_pairs={{0,8},{2,10},{4,12},{6,14},{8,0},{10,2},{12,4},{14,6},{1,9},{3,11}... | collective-permute-start | bytes 540680 | tf_op jit(solution)/shard_map/ppermute | solution.py:365
  20.3 1.3 collective-permute-start.18
  21.6 3.6 %collective-permute-start.19 = (bf16[11,8,1024]{2,1,0:T(8,128)(2,1)S(1)}, bf16[11,8,1024]{2,1,0:T(8,128)(2,1)S(1)}, u32[]{:S(2)}, u32[]{:S(2)}) collective-permute-start(bf16[11,8,1024]{2,1,0:T(8,128)(2,1)S(1)} %get-tuple-element.78), channel_id=1, source_target_pairs={{0,12},{2,14},{4,8},{6,10},{8,4},{10,6},{12,0},{14,2},{1,13},{3,15... | collective-permute-start | bytes 540680 | tf_op jit(solution)/shard_map/ppermute | solution.py:365
  25.2 4.8 %collective-permute-done.15.refs_2_.refs_10_ = bf16[11,8,1024]{2,1,0:T(8,128)(2,1)S(1)} collective-permute-done((bf16[11,8,1024]{2,1,0:T(8,128)(2,1)S(1)}, bf16[11,8,1024]{2,1,0:T(8,128)(2,1)S(1)}, u32[]{:S(2)}, u32[]{:S(2)}) %collective-permute-start.15) | collective-permute-done | bytes 180256 | tf_op jit(solution)/shard_map/ppermute | solution.py:365
  30.0 1.0 collective-permute-start.20
  31.0 1.2 copy-done.3
  32.2 1.2 copy-done.5
  33.4 1.2 copy-done.7
  35.5 3.8 %payloads.2 = (bf16[29,8,512]{2,1,0:T(8,128)(2,1)S(1)}, bf16[29,8,512]{2,1,0:T(8,128)(2,1)S(1)}, bf16[29,8,512]{2,1,0:T(8,128)(2,1)S(1)}, bf16[29,8,512]{2,1,0:T...) custom-call(s32[9]{0:T(128)S(1)} %pad_add_fusion.spots_ref, ...), custom_call_target="tpu_custom_call" | custom-call | tf_op jit(solution)/shard_map/payloads/pallas_call | solution.py:177
  44.1 1.7 space_payload.1.refs_9_
  46.1 2.0 time_column.1
  48.1 1.9 copy-done
  53.6 8.8 %collective-permute-start.10 = (bf16[29,8,512]{2,1,0:T(8,128)(2,1)}, bf16[29,8,512]{2,1,0:T(8,128)(2,1)S(1)}, u32[]{:S(2)}, u32[]{:S(2)}) collective-permute-start(bf16[29,8,512]{2,1,0:T(8,128)(2,1)} %copy-done.61), channel_id=1, source_target_pairs={{0,8},{2,10},{4,12},{6,14},{8,0},{10,2},{12,4},{14,6},{1,9},{3,11}... | collective-permute-start | bytes 712712 | tf_op jit(solution)/shard_map/ppermute | solution.py:365
  63.0 4.3 %collective-permute-start.13 = (bf16[29,8,512]{2,1,0:T(8,128)(2,1)}, bf16[29,8,512]{2,1,0:T(8,128)(2,1)S(1)}, u32[]{:S(2)}, u32[]{:S(2)}) collective-permute-start(bf16[29,8,512]{2,1,0:T(8,128)(2,1)} %copy-done.58), channel_id=1, source_target_pairs={{0,14},{2,12},{4,10},{6,8},{8,6},{10,4},{12,2},{14,0},{1,15},{3,13... | collective-permute-start | bytes 712712 | tf_op jit(solution)/shard_map/ppermute | solution.py:365
  67.3 22.1 %collective-permute-done.10.refs_4_ = bf16[29,8,512]{2,1,0:T(8,128)(2,1)S(1)} collective-permute-done((bf16[29,8,512]{2,1,0:T(8,128)(2,1)}, bf16[29,8,512]{2,1,0:T(8,128)(2,1)S(1)}, u32[]{:S(2)}, u32[]{:S(2)}) %collective-permute-start.10) | collective-permute-done | bytes 237600 | tf_op jit(solution)/shard_map/ppermute | solution.py:365
  90.2 4.5 %collective-permute-done.11.refs_5_ = bf16[29,8,512]{2,1,0:T(8,128)(2,1)S(1)} collective-permute-done((bf16[29,8,512]{2,1,0:T(8,128)(2,1)}, bf16[29,8,512]{2,1,0:T(8,128)(2,1)S(1)}, u32[]{:S(2)}, u32[]{:S(2)}) %collective-permute-start.11) | collective-permute-done | bytes 237600 | tf_op jit(solution)/shard_map/ppermute | solution.py:365
  94.7 5.6 %collective-permute-start.9 = (bf16[29,8,512]{2,1,0:T(8,128)(2,1)}, bf16[29,8,512]{2,1,0:T(8,128)(2,1)S(1)}, u32[]{:S(2)}, u32[]{:S(2)}) collective-permute-start(bf16[29,8,512]{2,1,0:T(8,128)(2,1)} %copy-done.55), channel_id=1, source_target_pairs={{0,6},{2,4},{4,2},{6,0},{8,14},{10,12},{12,10},{14,8},{1,7},{3,5},... | collective-permute-start | bytes 712712 | tf_op jit(solution)/shard_map/ppermute | solution.py:365
  100.3 1.2 copy-done.8
  101.5 2.7 %payloads.3 = (bf16[21,8,512]{2,1,0:T(8,128)(2,1)S(1)}, bf16[21,8,512]{2,1,0:T(8,128)(2,1)S(1)}, bf16[21,8,512]{2,1,0:T(8,128)(2,1)S(1)}, bf16[21,8,512]{2,1,0:T...) custom-call(s32[9]{0:T(128)S(1)} %pad_add_fusion.spots_ref, ...), custom_call_target="tpu_custom_call" | custom-call | tf_op jit(solution)/shard_map/payloads/pallas_call | solution.py:177
  109.0 2.0 space_column.1
  114.4 1.3 collective-permute-start
  115.7 1.5 collective-permute-start.1
  118.3 2.7 %collective-permute-done.refs_1_ = bf16[21,8,512]{2,1,0:T(8,128)(2,1)S(1)} collective-permute-done((bf16[21,8,512]{2,1,0:T(8,128)(2,1)}, bf16[21,8,512]{2,1,0:T(8,128)(2,1)S(1)}, u32[]{:S(2)}, u32[]{:S(2)}) %collective-permute-start) | collective-permute-done | bytes 172064 | tf_op jit(solution)/shard_map/ppermute | solution.py:365
  121.7 1.5 collective-permute-start.4
  123.2 4.0 %collective-permute-done.1.refs_2_ = bf16[21,8,512]{2,1,0:T(8,128)(2,1)S(1)} collective-permute-done((bf16[21,8,512]{2,1,0:T(8,128)(2,1)}, bf16[21,8,512]{2,1,0:T(8,128)(2,1)S(1)}, u32[]{:S(2)}, u32[]{:S(2)}) %collective-permute-start.1) | collective-permute-done | bytes 172064 | tf_op jit(solution)/shard_map/ppermute | solution.py:365
  127.9 2.5 collective-permute-start.5
  131.2 1.6 copy-done.16
  132.8 0.9 copy-done.19
  133.8 1.0 copy-done.21
  134.7 0.9 copy-done.23
  135.7 0.9 copy-done.25
  136.6 0.9 copy-done.27
  137.5 0.9 copy-done.29
  138.5 0.9 copy-done.34
  139.4 0.9 copy-done.36
  141.3 0.9 copy-done.40
  142.2 0.9 copy-done.42
  144.9 21.9 %time_first.1 = (bf16[21,8,512]{2,1,0:T(8,128)(2,1)S(1)}, bf16[21,8,512]{2,1,0:T(8,128)(2,1)S(1)}, bf16[21,8,512]{2,1,0:T(8,128)(2,1)S(1)}, bf16[21,8,512]{2,1,0...) custom-call(bf16[29,8,512]{2,1,0:T(8,128)(2,1)S(1)} %get-tuple-eleme, ...), custom_call_target="tpu_custom_call" | custom-call | bytes 59040000 | tf_op jit(solution)/shard_map/time_first/pallas_call | solution.py:286
  166.9 2.0 collective-permute-start.29
  168.9 1.5 collective-permute-start.31
  170.5 1.6 collective-permute-start.32
  172.0 2.7 %collective-permute-start.33 = (bf16[21,8,512]{2,1,0:T(8,128)(2,1)S(1)}, bf16[21,8,512]{2,1,0:T(8,128)(2,1)S(1)}, u32[]{:S(2)}, u32[]{:S(2)}) collective-permute-start(bf16[21,8,512]{2,1,0:T(8,128)(2,1)S(1)} %get-tuple-element.94), channel_id=1, source_target_pairs={{0,10},{2,8},{4,14},{6,12},{8,2},{10,0},{12,6},{14,4},{1,11},{3,9}... | collective-permute-start | bytes 516104 | tf_op jit(solution)/shard_map/ppermute | solution.py:365
  174.8 12.0 %time_second.1 = (bf16[21,8,512]{2,1,0:T(8,128)(2,1)S(1)}, bf16[21,8,512]{2,1,0:T(8,128)(2,1)S(1)}, bf16[21,8,512]{2,1,0:T(8,128)(2,1)S(1)}, bf16[21,8,512]{2,1,...) custom-call(bf16[21,8,512]{2,1,0:T(8,128)(2,1)S(1)} %copy-done.48, ...), custom_call_target="tpu_custom_call" | custom-call | bytes 36900000 | tf_op jit(solution)/shard_map/time_second/pallas_call | solution.py:286
  186.7 2.5 collective-permute-start.34
  190.2 1.9 collective-permute-start.22
  192.1 1.5 collective-permute-start.24
  193.7 1.5 collective-permute-done.34.refs_6_
  195.2 7.3 %collective-permute-start.25 = (bf16[21,8,512]{2,1,0:T(8,128)(2,1)}, bf16[21,8,512]{2,1,0:T(8,128)(2,1)}, u32[]{:S(2)}, u32[]{:S(2)}) collective-permute-start(bf16[21,8,512]{2,1,0:T(8,128)(2,1)} %get-tuple-element.85), channel_id=1, source_target_pairs={{0,8},{2,10},{4,12},{6,14},{8,0},{10,2},{12,4},{14,6},{1,9},{3,11}... | collective-permute-start | bytes 516104 | tf_op jit(solution)/shard_map/ppermute | solution.py:365
  202.5 10.3 %collective-permute-start.26 = (bf16[21,8,512]{2,1,0:T(8,128)(2,1)}, bf16[21,8,512]{2,1,0:T(8,128)(2,1)}, u32[]{:S(2)}, u32[]{:S(2)}) collective-permute-start(bf16[21,8,512]{2,1,0:T(8,128)(2,1)} %get-tuple-element.86), channel_id=1, source_target_pairs={{0,10},{2,8},{4,14},{6,12},{8,2},{10,0},{12,6},{14,4},{1,11},{3,9}... | collective-permute-start | bytes 516104 | tf_op jit(solution)/shard_map/ppermute | solution.py:365
  212.8 1.5 collective-permute-start.27
  214.2 2.7 %collective-permute-start.28 = (bf16[21,8,512]{2,1,0:T(8,128)(2,1)}, bf16[21,8,512]{2,1,0:T(8,128)(2,1)}, u32[]{:S(2)}, u32[]{:S(2)}) collective-permute-start(bf16[21,8,512]{2,1,0:T(8,128)(2,1)} %get-tuple-element.88), channel_id=1, source_target_pairs={{0,14},{2,12},{4,10},{6,8},{8,6},{10,4},{12,2},{14,0},{1,15},{3,13... | collective-permute-start | bytes 516104 | tf_op jit(solution)/shard_map/ppermute | solution.py:365
  216.9 3.4 %place_first.1 = (bf16[7,8,8,1024]{3,2,1,0:T(8,128)(2,1)}, bf16[7,8,8,1024]{3,2,1,0:T(8,128)(2,1)}, bf16[7,8,8,1024]{3,2,1,0:T(8,128)(2,1)}) custom-call(s32[9]{0:T(128)S(1)} %pad_add_fusion.spots_ref, bf16[21,8,512]{2,1,0:T(8,128)(2,1)S(1)} %get-tuple-element.89.refs_0_, bf16[21,8,512]{2,1,0:T(8,128)(2,1)S(1)} %collective-permute-done.29.refs_1_, ...), custom_call_target="tpu_custom_call" | custom-call | tf_op jit(solution)/shard_map/place_first/pallas_call | solution.py:177
  220.3 1.2 copy-done.14
  221.5 1.2 copy-done.15
  222.6 1.6 copy-done.17
  224.2 24.5 %space_attention.1 = (bf16[7,64,1024]{2,1,0:T(8,128)(2,1)}, bf16[7,64,1024]{2,1,0:T(8,128)(2,1)}, bf16[7,64,1024]{2,1,0:T(8,128)(2,1)}) custom-call(bf16[7,64,1024]{2,1,0:T(8,128)(2,1)S(1)} %copy-done.10, bf16[7,64,1024]{2,1,0:T(8,128)(2,1)S(1)} %copy-done.12, bf16[7,64,1024]{2,1,0:T(8,128)(2,1)S(1)} %copy-done.14, ...), custom_call_target="tpu_custom_call" | custom-call | bytes 73800000 | tf_op jit(solution)/shard_map/space_attention/pallas_call | solution.py:333
  248.8 1.2 copy-done.30
  250.0 1.2 copy-done.31
  251.2 1.2 copy-done.32
  252.4 3.5 %place_second.1 = (bf16[7,8,8,1024]{3,2,1,0:T(8,128)(2,1)}, bf16[7,8,8,1024]{3,2,1,0:T(8,128)(2,1)}, bf16[7,8,8,1024]{3,2,1,0:T(8,128)(2,1)}) custom-call(s32[9]{0:T(128)S(1)} %pad_add_fusion.spots_ref, bf16[21,8,512]{2,1,0:T(8,128)(2,1)S(1)} %get-tuple-element.81.refs_0_, ...), custom_call_target="tpu_custom_call", output_to_operand_aliasing={{0}: (12, {}), {1}: (13, {}), {2}: (14, {})} | custom-call | tf_op jit(solution)/shard_map/place_second/pallas_call | solution.py:177
  (165 shorter events, 27.1 us)
Async XLA Ops:
  7.2 124.1 %all-gather.3.cloned.1.call-start = ((), (), s32[]{:S(2)}) async-start(), calls=%async_computation | async-start | bytes 2621440 | tf_op jit(solution)/shard_map/all_gather | solution.py:420
  7.3 1.2 copy-start.1
  9.4 34.7 %copy-start.2 = (bf16[7,64,1024]{2,1,0:T(8,128)(2,1)S(1)}, bf16[7,64,1024]{2,1,0:T(8,128)(2,1)}, u32[]{:S(2)}) copy-start(bf16[7,64,1024]{2,1,0:T(8,128)(2,1)} %refs_4_.1) | copy-start | bytes 2752516
  12.7 8.9 %collective-permute-start.14 = (bf16[11,8,1024]{2,1,0:T(8,128)(2,1)S(1)}, bf16[11,8,1024]{2,1,0:T(8,128)(2,1)S(1)}, u32[]{:S(2)}, u32[]{:S(2)}) collective-permute-start(bf16[11,8,1024]{2,1,0:T(8,128)(2,1)S(1)} %get-tuple-element.73), channel_id=1, source_target_pairs={{0,2},{2,0},{4,6},{6,4},{8,10},{10,8},{12,14},{14,12},{1,3},{3,1},... | collective-permute-start | bytes 540680 | tf_op jit(solution)/shard_map/ppermute | solution.py:365
  15.8 14.2 %collective-permute-start.15 = (bf16[11,8,1024]{2,1,0:T(8,128)(2,1)S(1)}, bf16[11,8,1024]{2,1,0:T(8,128)(2,1)S(1)}, u32[]{:S(2)}, u32[]{:S(2)}) collective-permute-start(bf16[11,8,1024]{2,1,0:T(8,128)(2,1)S(1)} %get-tuple-element.74), channel_id=1, source_target_pairs={{0,4},{2,6},{4,0},{6,2},{8,12},{10,14},{12,8},{14,10},{1,5},{3,7},... | collective-permute-start | bytes 540680 | tf_op jit(solution)/shard_map/ppermute | solution.py:365
  17.3 28.5 %collective-permute-start.16 = (bf16[11,8,1024]{2,1,0:T(8,128)(2,1)S(1)}, bf16[11,8,1024]{2,1,0:T(8,128)(2,1)S(1)}, u32[]{:S(2)}, u32[]{:S(2)}) collective-permute-start(bf16[11,8,1024]{2,1,0:T(8,128)(2,1)S(1)} %get-tuple-element.75), channel_id=1, source_target_pairs={{0,6},{2,4},{4,2},{6,0},{8,14},{10,12},{12,10},{14,8},{1,7},{3,5},... | collective-permute-start | bytes 540680 | tf_op jit(solution)/shard_map/ppermute | solution.py:365
  17.3 28.5 %collective-permute-start.17 = (bf16[11,8,1024]{2,1,0:T(8,128)(2,1)S(1)}, bf16[11,8,1024]{2,1,0:T(8,128)(2,1)S(1)}, u32[]{:S(2)}, u32[]{:S(2)}) collective-permute-start(bf16[11,8,1024]{2,1,0:T(8,128)(2,1)S(1)} %get-tuple-element.76), channel_id=1, source_target_pairs={{0,8},{2,10},{4,12},{6,14},{8,0},{10,2},{12,4},{14,6},{1,9},{3,11}... | collective-permute-start | bytes 540680 | tf_op jit(solution)/shard_map/ppermute | solution.py:365
  20.3 25.7 %collective-permute-start.18 = (bf16[11,8,1024]{2,1,0:T(8,128)(2,1)S(1)}, bf16[11,8,1024]{2,1,0:T(8,128)(2,1)S(1)}, u32[]{:S(2)}, u32[]{:S(2)}) collective-permute-start(bf16[11,8,1024]{2,1,0:T(8,128)(2,1)S(1)} %get-tuple-element.77), channel_id=1, source_target_pairs={{0,10},{2,8},{4,14},{6,12},{8,2},{10,0},{12,6},{14,4},{1,11},{3,9}... | collective-permute-start | bytes 540680 | tf_op jit(solution)/shard_map/ppermute | solution.py:365
  21.6 24.4 %copy-start.33 = (bf16[11,8,1024]{2,1,0:T(8,128)(2,1)}, bf16[11,8,1024]{2,1,0:T(8,128)(2,1)S(1)}, u32[]{:S(2)}) copy-start(bf16[11,8,1024]{2,1,0:T(8,128)(2,1)S(1)} %collective-permute-done.14.refs_1_.refs_9_) | copy-start | bytes 540676
  21.6 24.4 %collective-permute-start.19 = (bf16[11,8,1024]{2,1,0:T(8,128)(2,1)S(1)}, bf16[11,8,1024]{2,1,0:T(8,128)(2,1)S(1)}, u32[]{:S(2)}, u32[]{:S(2)}) collective-permute-start(bf16[11,8,1024]{2,1,0:T(8,128)(2,1)S(1)} %get-tuple-element.78), channel_id=1, source_target_pairs={{0,12},{2,14},{4,8},{6,10},{8,4},{10,6},{12,0},{14,2},{1,13},{3,15... | collective-permute-start | bytes 540680 | tf_op jit(solution)/shard_map/ppermute | solution.py:365
  30.0 16.1 %copy-start.35 = (bf16[11,8,1024]{2,1,0:T(8,128)(2,1)}, bf16[11,8,1024]{2,1,0:T(8,128)(2,1)S(1)}, u32[]{:S(2)}) copy-start(bf16[11,8,1024]{2,1,0:T(8,128)(2,1)S(1)} %collective-permute-done.15.refs_2_.refs_10_) | copy-start | bytes 540676
  30.0 16.0 %collective-permute-start.20 = (bf16[11,8,1024]{2,1,0:T(8,128)(2,1)S(1)}, bf16[11,8,1024]{2,1,0:T(8,128)(2,1)S(1)}, u32[]{:S(2)}, u32[]{:S(2)}) collective-permute-start(bf16[11,8,1024]{2,1,0:T(8,128)(2,1)S(1)} %get-tuple-element.79), channel_id=1, source_target_pairs={{0,14},{2,12},{4,10},{6,8},{8,6},{10,4},{12,2},{14,0},{1,15},{3,13... | collective-permute-start | bytes 540680 | tf_op jit(solution)/shard_map/ppermute | solution.py:365
  31.0 1.2 copy-start.3
  32.2 1.2 copy-start.5
  33.4 1.2 copy-start.7
  35.5 8.6 %copy-start.9 = (bf16[7,64,1024]{2,1,0:T(8,128)(2,1)S(1)}, bf16[7,64,1024]{2,1,0:T(8,128)(2,1)}, u32[]{:S(2)}) copy-start(bf16[7,64,1024]{2,1,0:T(8,128)(2,1)} %refs_0_.3) | copy-start | bytes 2752516
  35.5 8.6 %copy-start.11 = (bf16[7,64,1024]{2,1,0:T(8,128)(2,1)S(1)}, bf16[7,64,1024]{2,1,0:T(8,128)(2,1)}, u32[]{:S(2)}) copy-start(bf16[7,64,1024]{2,1,0:T(8,128)(2,1)} %refs_1_.3) | copy-start | bytes 2752516
  35.5 8.6 %copy-start.13 = (bf16[7,64,1024]{2,1,0:T(8,128)(2,1)S(1)}, bf16[7,64,1024]{2,1,0:T(8,128)(2,1)}, u32[]{:S(2)}) copy-start(bf16[7,64,1024]{2,1,0:T(8,128)(2,1)} %refs_2_.3) | copy-start | bytes 2752516
  45.8 54.5 %copy-start.4 = (bf16[7,64,1024]{2,1,0:T(8,128)(2,1)S(1)}, bf16[7,64,1024]{2,1,0:T(8,128)(2,1)}, u32[]{:S(2)}) copy-start(bf16[7,64,1024]{2,1,0:T(8,128)(2,1)} %param.10) | copy-start | bytes 2752516
  45.8 54.5 %copy-start.6 = (bf16[7,64,1024]{2,1,0:T(8,128)(2,1)S(1)}, bf16[7,64,1024]{2,1,0:T(8,128)(2,1)}, u32[]{:S(2)}) copy-start(bf16[7,64,1024]{2,1,0:T(8,128)(2,1)} %param.11) | copy-start | bytes 2752516
  48.1 1.9 copy-start
  53.3 167.0 %all-gather.5.cloned.1.call-start = ((), (), s32[]{:S(2)}) async-start(), calls=%async_computation.1 | async-start | bytes 2621440 | tf_op jit(solution)/shard_map/all_gather | solution.py:420
  53.6 76.8 %collective-permute-start.21 = (bf16[4,7,64,1024]{3,2,1,0:T(8,128)(2,1)}, bf16[4,7,64,1024]{3,2,1,0:T(8,128)(2,1)}, u32[]{:S(2)}, u32[]{:S(2)}) collective-permute-start(bf16[4,7,64,1024]{3,2,1,0:T(8,128)(2,1)} %copy-done), channel_id=1, source_target_pairs={{0,1},{1,0},{2,3},{3,2},{4,5},{5,4},{6,7},{7,6},{8,9},{9,8},{10,11... | collective-permute-start | bytes 11010056 | tf_op jit(solution)/shard_map/ppermute | solution.py:417
  53.6 35.7 %collective-permute-start.10 = (bf16[29,8,512]{2,1,0:T(8,128)(2,1)}, bf16[29,8,512]{2,1,0:T(8,128)(2,1)S(1)}, u32[]{:S(2)}, u32[]{:S(2)}) collective-permute-start(bf16[29,8,512]{2,1,0:T(8,128)(2,1)} %copy-done.61), channel_id=1, source_target_pairs={{0,8},{2,10},{4,12},{6,14},{8,0},{10,2},{12,4},{14,6},{1,9},{3,11}... | collective-permute-start | bytes 712712 | tf_op jit(solution)/shard_map/ppermute | solution.py:365
  62.5 32.2 %collective-permute-start.11 = (bf16[29,8,512]{2,1,0:T(8,128)(2,1)}, bf16[29,8,512]{2,1,0:T(8,128)(2,1)S(1)}, u32[]{:S(2)}, u32[]{:S(2)}) collective-permute-start(bf16[29,8,512]{2,1,0:T(8,128)(2,1)} %copy-done.60), channel_id=1, source_target_pairs={{0,10},{2,8},{4,14},{6,12},{8,2},{10,0},{12,6},{14,4},{1,11},{3,9}... | collective-permute-start | bytes 712712 | tf_op jit(solution)/shard_map/ppermute | solution.py:365
  62.5 32.2 %collective-permute-start.12 = (bf16[29,8,512]{2,1,0:T(8,128)(2,1)}, bf16[29,8,512]{2,1,0:T(8,128)(2,1)S(1)}, u32[]{:S(2)}, u32[]{:S(2)}) collective-permute-start(bf16[29,8,512]{2,1,0:T(8,128)(2,1)} %copy-done.59), channel_id=1, source_target_pairs={{0,12},{2,14},{4,8},{6,10},{8,4},{10,6},{12,0},{14,2},{1,13},{3,15... | collective-permute-start | bytes 712712 | tf_op jit(solution)/shard_map/ppermute | solution.py:365
  63.0 45.9 %collective-permute-start.13 = (bf16[29,8,512]{2,1,0:T(8,128)(2,1)}, bf16[29,8,512]{2,1,0:T(8,128)(2,1)S(1)}, u32[]{:S(2)}, u32[]{:S(2)}) collective-permute-start(bf16[29,8,512]{2,1,0:T(8,128)(2,1)} %copy-done.58), channel_id=1, source_target_pairs={{0,14},{2,12},{4,10},{6,8},{8,6},{10,4},{12,2},{14,0},{1,15},{3,13... | collective-permute-start | bytes 712712 | tf_op jit(solution)/shard_map/ppermute | solution.py:365
  89.4 19.6 %collective-permute-start.7 = (bf16[29,8,512]{2,1,0:T(8,128)(2,1)}, bf16[29,8,512]{2,1,0:T(8,128)(2,1)S(1)}, u32[]{:S(2)}, u32[]{:S(2)}) collective-permute-start(bf16[29,8,512]{2,1,0:T(8,128)(2,1)} %copy-done.57), channel_id=1, source_target_pairs={{0,2},{2,0},{4,6},{6,4},{8,10},{10,8},{12,14},{14,12},{1,3},{3,1},... | collective-permute-start | bytes 712712 | tf_op jit(solution)/shard_map/ppermute | solution.py:365
  94.7 14.3 %copy-start.18 = (bf16[29,8,512]{2,1,0:T(8,128)(2,1)}, bf16[29,8,512]{2,1,0:T(8,128)(2,1)S(1)}, u32[]{:S(2)}) copy-start(bf16[29,8,512]{2,1,0:T(8,128)(2,1)S(1)} %collective-permute-done.11.refs_5_) | copy-start | bytes 712708
  94.7 14.2 %collective-permute-start.8 = (bf16[29,8,512]{2,1,0:T(8,128)(2,1)}, bf16[29,8,512]{2,1,0:T(8,128)(2,1)S(1)}, u32[]{:S(2)}, u32[]{:S(2)}) collective-permute-start(bf16[29,8,512]{2,1,0:T(8,128)(2,1)} %copy-done.56), channel_id=1, source_target_pairs={{0,4},{2,6},{4,0},{6,2},{8,12},{10,14},{12,8},{14,10},{1,5},{3,7},... | collective-permute-start | bytes 712712 | tf_op jit(solution)/shard_map/ppermute | solution.py:365
  94.7 14.3 %copy-start.20 = (bf16[29,8,512]{2,1,0:T(8,128)(2,1)}, bf16[29,8,512]{2,1,0:T(8,128)(2,1)S(1)}, u32[]{:S(2)}) copy-start(bf16[29,8,512]{2,1,0:T(8,128)(2,1)S(1)} %collective-permute-done.12.refs_6_) | copy-start | bytes 712708
  94.7 14.2 %collective-permute-start.9 = (bf16[29,8,512]{2,1,0:T(8,128)(2,1)}, bf16[29,8,512]{2,1,0:T(8,128)(2,1)S(1)}, u32[]{:S(2)}, u32[]{:S(2)}) collective-permute-start(bf16[29,8,512]{2,1,0:T(8,128)(2,1)} %copy-done.55), channel_id=1, source_target_pairs={{0,6},{2,4},{4,2},{6,0},{8,14},{10,12},{12,10},{14,8},{1,7},{3,5},... | collective-permute-start | bytes 712712 | tf_op jit(solution)/shard_map/ppermute | solution.py:365
  100.3 1.2 copy-start.8
  114.4 6.6 %collective-permute-start = (bf16[21,8,512]{2,1,0:T(8,128)(2,1)}, bf16[21,8,512]{2,1,0:T(8,128)(2,1)S(1)}, u32[]{:S(2)}, u32[]{:S(2)}) collective-permute-start(bf16[21,8,512]{2,1,0:T(8,128)(2,1)} %copy-done.68), channel_id=1, source_target_pairs={{0,2},{2,0},{4,6},{6,4},{8,10},{10,8},{12,14},{14,12},{1,3},{3,1},... | collective-permute-start | bytes 516104 | tf_op jit(solution)/shard_map/ppermute | solution.py:365
  115.7 11.5 %collective-permute-start.1 = (bf16[21,8,512]{2,1,0:T(8,128)(2,1)}, bf16[21,8,512]{2,1,0:T(8,128)(2,1)S(1)}, u32[]{:S(2)}, u32[]{:S(2)}) collective-permute-start(bf16[21,8,512]{2,1,0:T(8,128)(2,1)} %copy-done.67), channel_id=1, source_target_pairs={{0,4},{2,6},{4,0},{6,2},{8,12},{10,14},{12,8},{14,10},{1,5},{3,7},... | collective-permute-start | bytes 516104 | tf_op jit(solution)/shard_map/ppermute | solution.py:365
  117.3 49.6 %collective-permute-start.2 = (bf16[21,8,512]{2,1,0:T(8,128)(2,1)}, bf16[21,8,512]{2,1,0:T(8,128)(2,1)}, u32[]{:S(2)}, u32[]{:S(2)}) collective-permute-start(bf16[21,8,512]{2,1,0:T(8,128)(2,1)} %copy-done.66), channel_id=1, source_target_pairs={{0,6},{2,4},{4,2},{6,0},{8,14},{10,12},{12,10},{14,8},{1,7},{3,5},... | collective-permute-start | bytes 516104 | tf_op jit(solution)/shard_map/ppermute | solution.py:365
  118.0 50.9 %collective-permute-start.3 = (bf16[21,8,512]{2,1,0:T(8,128)(2,1)}, bf16[21,8,512]{2,1,0:T(8,128)(2,1)}, u32[]{:S(2)}, u32[]{:S(2)}) collective-permute-start(bf16[21,8,512]{2,1,0:T(8,128)(2,1)} %copy-done.65), channel_id=1, source_target_pairs={{0,8},{2,10},{4,12},{6,14},{8,0},{10,2},{12,4},{14,6},{1,9},{3,11}... | collective-permute-start | bytes 516104 | tf_op jit(solution)/shard_map/ppermute | solution.py:365
  121.7 47.2 %collective-permute-start.4 = (bf16[21,8,512]{2,1,0:T(8,128)(2,1)}, bf16[21,8,512]{2,1,0:T(8,128)(2,1)}, u32[]{:S(2)}, u32[]{:S(2)}) collective-permute-start(bf16[21,8,512]{2,1,0:T(8,128)(2,1)} %copy-done.64), channel_id=1, source_target_pairs={{0,10},{2,8},{4,14},{6,12},{8,2},{10,0},{12,6},{14,4},{1,11},{3,9}... | collective-permute-start | bytes 516104 | tf_op jit(solution)/shard_map/ppermute | solution.py:365
  127.9 42.5 %collective-permute-start.5 = (bf16[21,8,512]{2,1,0:T(8,128)(2,1)}, bf16[21,8,512]{2,1,0:T(8,128)(2,1)}, u32[]{:S(2)}, u32[]{:S(2)}) collective-permute-start(bf16[21,8,512]{2,1,0:T(8,128)(2,1)} %copy-done.63), channel_id=1, source_target_pairs={{0,12},{2,14},{4,8},{6,10},{8,4},{10,6},{12,0},{14,2},{1,13},{3,15... | collective-permute-start | bytes 516104 | tf_op jit(solution)/shard_map/ppermute | solution.py:365
  130.4 41.6 %collective-permute-start.6 = (bf16[21,8,512]{2,1,0:T(8,128)(2,1)}, bf16[21,8,512]{2,1,0:T(8,128)(2,1)}, u32[]{:S(2)}, u32[]{:S(2)}) collective-permute-start(bf16[21,8,512]{2,1,0:T(8,128)(2,1)} %copy-done.62), channel_id=1, source_target_pairs={{0,14},{2,12},{4,10},{6,8},{8,6},{10,4},{12,2},{14,0},{1,15},{3,13... | collective-permute-start | bytes 516104 | tf_op jit(solution)/shard_map/ppermute | solution.py:365
  131.2 1.6 copy-start.16
  144.9 29.8 %copy-start.48 = (bf16[21,8,512]{2,1,0:T(8,128)(2,1)S(1)}, bf16[21,8,512]{2,1,0:T(8,128)(2,1)}, u32[]{:S(2)}) copy-start(bf16[21,8,512]{2,1,0:T(8,128)(2,1)} %copy-done.47) | copy-start | bytes 516100
  144.9 29.8 %copy-start.50 = (bf16[21,8,512]{2,1,0:T(8,128)(2,1)S(1)}, bf16[21,8,512]{2,1,0:T(8,128)(2,1)}, u32[]{:S(2)}) copy-start(bf16[21,8,512]{2,1,0:T(8,128)(2,1)} %copy-done.49) | copy-start | bytes 516100
  144.9 29.8 %copy-start.52 = (bf16[21,8,512]{2,1,0:T(8,128)(2,1)S(1)}, bf16[21,8,512]{2,1,0:T(8,128)(2,1)}, u32[]{:S(2)}) copy-start(bf16[21,8,512]{2,1,0:T(8,128)(2,1)} %copy-done.51) | copy-start | bytes 516100
  166.8 53.5 %copy-start.10 = (bf16[7,64,1024]{2,1,0:T(8,128)(2,1)S(1)}, bf16[7,64,1024]{2,1,0:T(8,128)(2,1)}, u32[]{:S(2)}) copy-start(bf16[7,64,1024]{2,1,0:T(8,128)(2,1)} %refs_0_.3) | copy-start | bytes 2752516
  166.8 53.4 %copy-start.12 = (bf16[7,64,1024]{2,1,0:T(8,128)(2,1)S(1)}, bf16[7,64,1024]{2,1,0:T(8,128)(2,1)}, u32[]{:S(2)}) copy-start(bf16[7,64,1024]{2,1,0:T(8,128)(2,1)} %refs_1_.3) | copy-start | bytes 2752516
  166.9 19.9 %collective-permute-start.29 = (bf16[21,8,512]{2,1,0:T(8,128)(2,1)S(1)}, bf16[21,8,512]{2,1,0:T(8,128)(2,1)S(1)}, u32[]{:S(2)}, u32[]{:S(2)}) collective-permute-start(bf16[21,8,512]{2,1,0:T(8,128)(2,1)S(1)} %get-tuple-element.90), channel_id=1, source_target_pairs={{0,2},{2,0},{4,6},{6,4},{8,10},{10,8},{12,14},{14,12},{1,3},{3,1},... | collective-permute-start | bytes 516104 | tf_op jit(solution)/shard_map/ppermute | solution.py:365
  168.9 20.4 %collective-permute-start.30 = (bf16[21,8,512]{2,1,0:T(8,128)(2,1)S(1)}, bf16[21,8,512]{2,1,0:T(8,128)(2,1)S(1)}, u32[]{:S(2)}, u32[]{:S(2)}) collective-permute-start(bf16[21,8,512]{2,1,0:T(8,128)(2,1)S(1)} %get-tuple-element.91), channel_id=1, source_target_pairs={{0,4},{2,6},{4,0},{6,2},{8,12},{10,14},{12,8},{14,10},{1,5},{3,7},... | collective-permute-start | bytes 516104 | tf_op jit(solution)/shard_map/ppermute | solution.py:365
  168.9 21.2 %collective-permute-start.31 = (bf16[21,8,512]{2,1,0:T(8,128)(2,1)S(1)}, bf16[21,8,512]{2,1,0:T(8,128)(2,1)S(1)}, u32[]{:S(2)}, u32[]{:S(2)}) collective-permute-start(bf16[21,8,512]{2,1,0:T(8,128)(2,1)S(1)} %get-tuple-element.92), channel_id=1, source_target_pairs={{0,6},{2,4},{4,2},{6,0},{8,14},{10,12},{12,10},{14,8},{1,7},{3,5},... | collective-permute-start | bytes 516104 | tf_op jit(solution)/shard_map/ppermute | solution.py:365
  170.5 21.6 %collective-permute-start.32 = (bf16[21,8,512]{2,1,0:T(8,128)(2,1)S(1)}, bf16[21,8,512]{2,1,0:T(8,128)(2,1)S(1)}, u32[]{:S(2)}, u32[]{:S(2)}) collective-permute-start(bf16[21,8,512]{2,1,0:T(8,128)(2,1)S(1)} %get-tuple-element.93), channel_id=1, source_target_pairs={{0,8},{2,10},{4,12},{6,14},{8,0},{10,2},{12,4},{14,6},{1,9},{3,11}... | collective-permute-start | bytes 516104 | tf_op jit(solution)/shard_map/ppermute | solution.py:365
  172.0 20.1 %collective-permute-start.33 = (bf16[21,8,512]{2,1,0:T(8,128)(2,1)S(1)}, bf16[21,8,512]{2,1,0:T(8,128)(2,1)S(1)}, u32[]{:S(2)}, u32[]{:S(2)}) collective-permute-start(bf16[21,8,512]{2,1,0:T(8,128)(2,1)S(1)} %get-tuple-element.94), channel_id=1, source_target_pairs={{0,10},{2,8},{4,14},{6,12},{8,2},{10,0},{12,6},{14,4},{1,11},{3,9}... | collective-permute-start | bytes 516104 | tf_op jit(solution)/shard_map/ppermute | solution.py:365
  186.7 8.4 %collective-permute-start.34 = (bf16[21,8,512]{2,1,0:T(8,128)(2,1)S(1)}, bf16[21,8,512]{2,1,0:T(8,128)(2,1)S(1)}, u32[]{:S(2)}, u32[]{:S(2)}) collective-permute-start(bf16[21,8,512]{2,1,0:T(8,128)(2,1)S(1)} %get-tuple-element.95), channel_id=1, source_target_pairs={{0,12},{2,14},{4,8},{6,10},{8,4},{10,6},{12,0},{14,2},{1,13},{3,15... | collective-permute-start | bytes 516104 | tf_op jit(solution)/shard_map/ppermute | solution.py:365
  189.3 13.2 %collective-permute-start.35 = (bf16[21,8,512]{2,1,0:T(8,128)(2,1)S(1)}, bf16[21,8,512]{2,1,0:T(8,128)(2,1)S(1)}, u32[]{:S(2)}, u32[]{:S(2)}) collective-permute-start(bf16[21,8,512]{2,1,0:T(8,128)(2,1)S(1)} %get-tuple-element.96), channel_id=1, source_target_pairs={{0,14},{2,12},{4,10},{6,8},{8,6},{10,4},{12,2},{14,0},{1,15},{3,13... | collective-permute-start | bytes 516104 | tf_op jit(solution)/shard_map/ppermute | solution.py:365
  190.2 22.6 %collective-permute-start.22 = (bf16[21,8,512]{2,1,0:T(8,128)(2,1)S(1)}, bf16[21,8,512]{2,1,0:T(8,128)(2,1)S(1)}, u32[]{:S(2)}, u32[]{:S(2)}) collective-permute-start(bf16[21,8,512]{2,1,0:T(8,128)(2,1)S(1)} %get-tuple-element.82), channel_id=1, source_target_pairs={{0,2},{2,0},{4,6},{6,4},{8,10},{10,8},{12,14},{14,12},{1,3},{3,1},... | collective-permute-start | bytes 516104 | tf_op jit(solution)/shard_map/ppermute | solution.py:365
  192.1 22.1 %collective-permute-start.23 = (bf16[21,8,512]{2,1,0:T(8,128)(2,1)S(1)}, bf16[21,8,512]{2,1,0:T(8,128)(2,1)S(1)}, u32[]{:S(2)}, u32[]{:S(2)}) collective-permute-start(bf16[21,8,512]{2,1,0:T(8,128)(2,1)S(1)} %get-tuple-element.83), channel_id=1, source_target_pairs={{0,4},{2,6},{4,0},{6,2},{8,12},{10,14},{12,8},{14,10},{1,5},{3,7},... | collective-permute-start | bytes 516104 | tf_op jit(solution)/shard_map/ppermute | solution.py:365
  192.1 56.7 %collective-permute-start.24 = (bf16[21,8,512]{2,1,0:T(8,128)(2,1)}, bf16[21,8,512]{2,1,0:T(8,128)(2,1)S(1)}, u32[]{:S(2)}, u32[]{:S(2)}) collective-permute-start(bf16[21,8,512]{2,1,0:T(8,128)(2,1)} %get-tuple-element.84), channel_id=1, source_target_pairs={{0,6},{2,4},{4,2},{6,0},{8,14},{10,12},{12,10},{14,8},{1,7},{3,5},... | collective-permute-start | bytes 516104 | tf_op jit(solution)/shard_map/ppermute | solution.py:365
  195.2 53.6 %collective-permute-start.25 = (bf16[21,8,512]{2,1,0:T(8,128)(2,1)}, bf16[21,8,512]{2,1,0:T(8,128)(2,1)}, u32[]{:S(2)}, u32[]{:S(2)}) collective-permute-start(bf16[21,8,512]{2,1,0:T(8,128)(2,1)} %get-tuple-element.85), channel_id=1, source_target_pairs={{0,8},{2,10},{4,12},{6,14},{8,0},{10,2},{12,4},{14,6},{1,9},{3,11}... | collective-permute-start | bytes 516104 | tf_op jit(solution)/shard_map/ppermute | solution.py:365
  202.5 46.3 %collective-permute-start.26 = (bf16[21,8,512]{2,1,0:T(8,128)(2,1)}, bf16[21,8,512]{2,1,0:T(8,128)(2,1)}, u32[]{:S(2)}, u32[]{:S(2)}) collective-permute-start(bf16[21,8,512]{2,1,0:T(8,128)(2,1)} %get-tuple-element.86), channel_id=1, source_target_pairs={{0,10},{2,8},{4,14},{6,12},{8,2},{10,0},{12,6},{14,4},{1,11},{3,9}... | collective-permute-start | bytes 516104 | tf_op jit(solution)/shard_map/ppermute | solution.py:365
  212.8 36.0 %collective-permute-start.27 = (bf16[21,8,512]{2,1,0:T(8,128)(2,1)}, bf16[21,8,512]{2,1,0:T(8,128)(2,1)}, u32[]{:S(2)}, u32[]{:S(2)}) collective-permute-start(bf16[21,8,512]{2,1,0:T(8,128)(2,1)} %get-tuple-element.87), channel_id=1, source_target_pairs={{0,12},{2,14},{4,8},{6,10},{8,4},{10,6},{12,0},{14,2},{1,13},{3,15... | collective-permute-start | bytes 516104 | tf_op jit(solution)/shard_map/ppermute | solution.py:365
  214.2 34.6 %collective-permute-start.28 = (bf16[21,8,512]{2,1,0:T(8,128)(2,1)}, bf16[21,8,512]{2,1,0:T(8,128)(2,1)}, u32[]{:S(2)}, u32[]{:S(2)}) collective-permute-start(bf16[21,8,512]{2,1,0:T(8,128)(2,1)} %get-tuple-element.88), channel_id=1, source_target_pairs={{0,14},{2,12},{4,10},{6,8},{8,6},{10,4},{12,2},{14,0},{1,15},{3,13... | collective-permute-start | bytes 516104 | tf_op jit(solution)/shard_map/ppermute | solution.py:365
  220.3 1.2 copy-start.14
  222.6 1.6 copy-start.17
  248.8 1.2 copy-start.30
  251.2 1.2 copy-start.32
  (43 other events, 34.0 us)
Sparse Core Ops, SparseCore 0:
  53.4 28.0 all-gather.2
  114.5 21.4 all-gather.4

commit v6 on v5

--- a/solution.py
+++ b/solution.py
@@ -134,9 +134,18 @@
     return grad_query, grad_keys, grad_values
 
 
-HBM = pl.BlockSpec(memory_space=pltpu.HBM)
+ANYWHERE = pl.BlockSpec(memory_space=pl.ANY)
 SCALARS = pl.BlockSpec(memory_space=pltpu.SMEM)
 BIG = pltpu.CompilerParams(vmem_limit_bytes=24 * 2**20)
+
+
+def settled(tensors):
+    return [
+        tensor
+        if jax.typeof(tensor).memory_space == pltpu.VMEM
+        else pltpu.with_memory_space_constraint(tensor, pltpu.HBM)
+        for tensor in tensors
+    ]
 
 
 def cost_of(microseconds):
@@ -150,39 +159,27 @@
     return copies
 
 
-def run_staged(pairs):
-    count = len(pairs)
-
-    def body(*scratch):
-        stages, arrived, left = scratch[:count], scratch[count], scratch[count + 1]
-        loads = run_copies(arrived, [(src, stage) for (src, _), stage in zip(pairs, stages)])
-        stores = []
-        for index, (load, (_, dst)) in enumerate(zip(loads, pairs)):
-            load.wait()
-            stores.append(pltpu.make_async_copy(stages[index], dst, left.at[index]))
-            stores[-1].start()
-        for store in stores:
-            store.wait()
-
-    sems = [pltpu.SemaphoreType.DMA((count,))] * 2
-    pl.run_scoped(body, *[pltpu.VMEM(src.shape, BF16) for src, _ in pairs], *sems)
-
-
-def moved(spots, parts, shapes, plan, name, after=(), kept=()):
+def moved(spots, parts, shapes, plan, name, after=(), kept=(), space=pltpu.VMEM):
     count = len(parts)
 
     def kernel(spots_ref, *refs):
-        run_staged(plan(spots_ref, refs[:count], refs[len(refs) - len(shapes) :]))
+        pairs = plan(spots_ref, refs[:count], refs[len(refs) - len(shapes) :])
+
+        def body(sems):
+            for copy in run_copies(sems, pairs):
+                copy.wait()
+
+        pl.run_scoped(body, pltpu.SemaphoreType.DMA((len(pairs),)))
 
     return pl.pallas_call(
         kernel,
-        in_specs=[SCALARS] + [HBM] * (count + len(after) + len(kept)),
-        out_specs=[HBM] * len(shapes),
-        out_shape=[jax.ShapeDtypeStruct(shape, BF16) for shape in shapes],
+        in_specs=[SCALARS] + [ANYWHERE] * (count + len(after) + len(kept)),
+        out_specs=[ANYWHERE] * len(shapes),
+        out_shape=[space(shape, BF16) for shape in shapes],
         input_output_aliases={1 + count + len(after) + i: i for i in range(len(kept))},
-        compiler_params=pltpu.CompilerParams(vmem_limit_bytes=2 * sum(math.prod(x) for x in shapes) + 2 * 2**20),
+        compiler_params=pltpu.CompilerParams(vmem_limit_bytes=4 * 2**20),
         name=name,
-    )(spots, *parts, *after, *kept)
+    )(spots, *settled(parts), *after, *settled(kept))
 
 
 def weight_copies(gathered_ref, weights):
@@ -216,7 +213,7 @@
     if first:
         space, groups, tm, share = gathered.shape[:4]
         scratch += [pltpu.VMEM((rows, width), BF16), pltpu.VMEM((space * groups * tm, share, width), BF16)]
-        operands = (gathered,)
+        operands = settled((gathered,))
         copied = len(blocks) + space * groups * tm
     else:
         scratch += [pltpu.VMEM((rows, lanes), BF16)]
@@ -278,21 +275,21 @@
         for store in stores:
             store.wait()
 
-    out_shapes = [jax.ShapeDtypeStruct((3 * frames, patches, lanes), BF16)] * count
-    out_specs = [HBM] * count
+    out_shapes = [pltpu.VMEM((3 * frames, patches, lanes), BF16)] * count
+    out_specs = [ANYWHERE] * count
     if first:
         out_shapes = out_shapes + [jax.ShapeDtypeStruct((rows, lanes), BF16)]
         out_specs = out_specs + [pl.BlockSpec(memory_space=pltpu.VMEM)]
     return pl.pallas_call(
         kernel,
-        in_specs=[HBM] * (len(blocks) + 1 + len(after)),
+        in_specs=[ANYWHERE] * (len(blocks) + 1 + len(after)),
         out_specs=out_specs,
         out_shape=out_shapes,
         scratch_shapes=scratch,
         compiler_params=BIG,
         cost_estimate=cost_of(16 if first else 10),
         name=name,
-    )(*blocks, *operands, *after)
+    )(*blocks, *operands, *settled(after))
 
 
 def space_attention(own, far, own_tokens, weights_of, after=()):
@@ -335,7 +332,7 @@
         grid_spec=pltpu.PrefetchScalarGridSpec(
             num_scalar_prefetch=0,
             grid=(frames,),
-            in_specs=[near] * 3 + [away, near_all, away_all] + [HBM] * (1 + len(after)),
+            in_specs=[near] * 3 + [away, near_all, away_all] + [ANYWHERE] * (1 + len(after)),
             out_specs=[near] * 3,
             scratch_shapes=[
                 pltpu.VMEM((pieces, share, width), BF16),
@@ -347,7 +344,7 @@
         compiler_params=BIG,
         cost_estimate=cost_of(20),
         name="space_attention",
-    )(*own, far, own_tokens, far, weights_of, *after)
+    )(*settled([*own, far, own_tokens, far, weights_of, *after]))
 
 
 def per_device(sizes, grad_out, time_q, time_k, time_v, space_q, space_k, space_v, time_wo, space_wo):
@@ -364,8 +361,9 @@
     def to_partner(tensor, k):
         return lax.ppermute(tensor, "tm", [(i, i ^ k) for i in range(tm)]) if k else tensor
 
-    def moved_one(parts, shape, plan, name, after=()):
-        return moved(spots, parts, [shape], lambda at, refs, outs: plan(at, refs, outs[0]), name, after)[0]
+    def moved_one(parts, shape, plan, name, after=(), space=pltpu.HBM):
+        one = lambda at, refs, outs: plan(at, refs, outs[0])
+        return moved(spots, parts, [shape], one, name, after, (), space)[0]
 
     split = [t.reshape(frames, tm, patches, width) for t in (time_q, time_k, time_v, grad_out)]
     blocks = share // patches
@@ -396,7 +394,7 @@
 
     def exchange(tensors):
         arrived = {k: to_partner(tensors[k], k) for k in order}
-        return [arrived[k] for k in range(tm)]
+        return [pltpu.with_memory_space_constraint(arrived[k], pltpu.VMEM) for k in range(tm)]
 
     sent_tokens = moved(
         spots, [split[3], time_pieces], [(frames + blocks, patches, width)] * tm, token_plan, "token_payloads"
@@ -413,6 +411,7 @@
         lambda at, refs, out: [(ref, out.at[i]) for i, ref in enumerate(refs)],
         "space_payload",
         (first_sent[0],),
+        pltpu.VMEM,
     )
     far = lax.ppermute(both_cores, "space", [(0, 1), (1, 0)])
 
@@ -465,7 +464,7 @@
         return plan
 
     shapes = [(frames, tm, patches, width)] * 3
-    outs = moved(spots, back, shapes, place(0), "place_first")
+    outs = moved(spots, back, shapes, place(0), "place_first", (), (), pltpu.HBM)
     space_out = space_attention(
         (space_q, space_k, space_v),
         far,
@@ -473,7 +472,7 @@
         space_weights,
         (outs[0],),
     )
-    outs = moved(spots, back2, shapes, place(1), "place_second", space_out, outs)
+    outs = moved(spots, back2, shapes, place(1), "place_second", settled(space_out), outs, pltpu.HBM)
     time_out = [out.reshape(frames, rows, width) for out in outs]
     return (*time_out, *space_out)
 

time: 264 us -> 231 us (0.88)
  local copies, waits for them, and re-layouts: 48.4 us -> 8.55 us
  Pallas kernels: 80.7 us -> 92.1 us
  waiting for transfers between devices: 40 us -> 33.6 us
  starting transfers between devices: 79.1 us -> 82 us
    unnamed x138 -> x26, local copies, waits for them, and re-layouts: 48.4 us -> 8.55 us
    pallas_call x10, Pallas kernels: 56.1 us -> 68.4 us  [the longest x8 35.6 us: moved(): pl.pallas_call(kernel, in_specs=[SCALARS] + [ANYWHERE] * (count + len(aft...]
    ppermute x35, waiting for transfers between devices: 40 us -> 33.6 us  [to_partner(): lax.ppermute(tensor, 'tm', [(i, i ^ k) for i in range(tm)])]
    ppermute x35, starting transfers between devices: 78.7 us -> 81.8 us  [to_partner(): lax.ppermute(tensor, 'tm', [(i, i ^ k) for i in range(tm)])]
  transfers between devices with their start and end apart: 38 -> 38, of which waited for: 7 -> 5; matrix products, arithmetic and copies ran while one was open for 0% -> 0% of each run, Pallas kernels for 27% -> 38%
where the time goes in v6:
time: 231 us
  Pallas kernels  92.1 us (40%)
  starting transfers between devices  82 us (35%)
  waiting for transfers between devices  33.6 us (15%)
  between operations  14.3 us (6%)
  local copies, waits for them, and re-layouts  8.55 us (4%)
    ppermute x35, starting transfers between devices, to_partner(): lax.ppermute(tensor, 'tm', [(i, i ^ k) for i in range(tm)])  81.8 us
    pallas_call x8, Pallas kernels, moved(): pl.pallas_call(kernel, in_specs=[SCALARS] + [ANYWHERE] * (count + len(aft...  35.6 us
    ppermute x35, waiting for transfers between devices, to_partner(): lax.ppermute(tensor, 'tm', [(i, i ^ k) for i in range(tm)])  33.6 us
    pallas_call x2, Pallas kernels, time_chunk(): pl.pallas_call(kernel, in_specs=[ANYWHERE] * (len(blocks) + 1 + len(after...  32.8 us
    pallas_call x1, Pallas kernels, space_attention(): pl.pallas_call(kernel, grid_spec=pltpu.PrefetchScalarGridSpec(num_scalar_...  23.8 us
    unnamed x26, local copies, waits for them, and re-layouts  8.55 us
  transfers between devices with their start and end apart: 38, of which 5 were waited for; matrix products, arithmetic and copies ran while one was open for 0% of the time, Pallas kernels for 38%

profile of v6, /device:TPU:0, one launch (start us, length us, event | category | flops | bytes accessed | tf_op | source)
XLA Modules:
  0.0 230.6 jit_solution(3957389194162012825)
XLA Ops:
  7.2 0.0 all-gather.3.cloned.1.call-start
  7.2 0.1 pad_add_fusion.spots_ref
  7.3 2.0 token_payloads.1
  9.4 3.0 %collective-permute-start.14 = (bf16[11,8,1024]{2,1,0:T(8,128)(2,1)S(1)}, bf16[11,8,1024]{2,1,0:T(8,128)(2,1)S(1)}, u32[]{:S(2)}, u32[]{:S(2)}) collective-permute-start(bf16[11,8,1024]{2,1,0:T(8,128)(2,1)S(1)} %get-tuple-element.73), channel_id=1, source_target_pairs={{0,2},{2,0},{4,6},{6,4},{8,10},{10,8},{12,14},{14,12},{1,3},{3,1},... | collective-permute-start | bytes 540680 | tf_op jit(solution)/shard_map/ppermute | solution.py:362
  12.3 1.6 collective-permute-start.15
  13.9 3.0 %collective-permute-start.17 = (bf16[11,8,1024]{2,1,0:T(8,128)(2,1)S(1)}, bf16[11,8,1024]{2,1,0:T(8,128)(2,1)S(1)}, u32[]{:S(2)}, u32[]{:S(2)}) collective-permute-start(bf16[11,8,1024]{2,1,0:T(8,128)(2,1)S(1)} %get-tuple-element.76), channel_id=1, source_target_pairs={{0,8},{2,10},{4,12},{6,14},{8,0},{10,2},{12,4},{14,6},{1,9},{3,11}... | collective-permute-start | bytes 540680 | tf_op jit(solution)/shard_map/ppermute | solution.py:362
  16.9 1.3 collective-permute-start.18
  18.2 3.6 %collective-permute-start.19 = (bf16[11,8,1024]{2,1,0:T(8,128)(2,1)S(1)}, bf16[11,8,1024]{2,1,0:T(8,128)(2,1)S(1)}, u32[]{:S(2)}, u32[]{:S(2)}) collective-permute-start(bf16[11,8,1024]{2,1,0:T(8,128)(2,1)S(1)} %get-tuple-element.78), channel_id=1, source_target_pairs={{0,12},{2,14},{4,8},{6,10},{8,4},{10,6},{12,0},{14,2},{1,13},{3,15... | collective-permute-start | bytes 540680 | tf_op jit(solution)/shard_map/ppermute | solution.py:362
  21.8 4.8 %collective-permute-done.15.refs_2_.refs_10_ = bf16[11,8,1024]{2,1,0:T(8,128)(2,1)S(1)} collective-permute-done((bf16[11,8,1024]{2,1,0:T(8,128)(2,1)S(1)}, bf16[11,8,1024]{2,1,0:T(8,128)(2,1)S(1)}, u32[]{:S(2)}, u32[]{:S(2)}) %collective-permute-start.15) | collective-permute-done | bytes 180256 | tf_op jit(solution)/shard_map/ppermute | solution.py:362
  26.6 1.0 collective-permute-start.20
  27.6 23.3 %payloads.2 = (bf16[29,8,512]{2,1,0:T(8,128)(2,1)S(1)}, bf16[29,8,512]{2,1,0:T(8,128)(2,1)}, bf16[29,8,512]{2,1,0:T(8,128)(2,1)}, bf16[29,8,512]{2,1,0:T(8,128)(...) custom-call(s32[9]{0:T(128)S(1)} %pad_add_fusion.spots_ref, ...), custom_call_target="tpu_custom_call" | custom-call | tf_op jit(solution)/shard_map/payloads/pallas_call | solution.py:174
  50.9 0.7 copy-done.5
  51.5 2.5 %space_payload.1.refs_9_ = bf16[4,7,64,1024]{3,2,1,0:T(8,128)(2,1)S(1)} custom-call(s32[9]{0:T(128)S(1)} %pad_add_fusion.spots_ref, bf16[7,64,1024]{2,1,0:T(8,128)(2,1)} %refs_0_.3, bf16[7,64,1024]{2,1,0:T(8,128)(2,1)} %refs_1_.3, bf16[7,64,1024]{2,1,0:T(8,128)(2,1)} %refs_2_.3, bf16[7,64,1024]{2,1,0:T(8,128)(2,1)} %refs_4_.1, ...), custom_call_target="tpu_custom_call" | custom-call | tf_op jit(solution)/shard_map/space_payload/pallas_call | solution.py:174
  54.1 1.3 time_column.1
  55.4 1.8 copy-done
  57.3 0.0 all-gather.3.cloned.1.call-update
  57.3 0.0 all-gather.5.cloned.1.call-start
  57.3 0.1 collective-permute-start.21
  57.4 0.1 collective-permute-start.10
  57.5 4.9 %collective-permute-start.11 = (bf16[29,8,512]{2,1,0:T(8,128)(2,1)S(1)}, bf16[29,8,512]{2,1,0:T(8,128)(2,1)S(1)}, u32[]{:S(2)}, u32[]{:S(2)}) collective-permute-start(bf16[29,8,512]{2,1,0:T(8,128)(2,1)S(1)} %get-tuple-element.70), channel_id=1, source_target_pairs={{0,10},{2,8},{4,14},{6,12},{8,2},{10,0},{12,6},{14,4},{1,11},{3,9}... | collective-permute-start | bytes 712712 | tf_op jit(solution)/shard_map/ppermute | solution.py:362
  62.4 1.7 collective-permute-start.12
  64.1 1.0 collective-permute-start.13
  65.1 20.8 %collective-permute-done.10.refs_4_ = bf16[29,8,512]{2,1,0:T(8,128)(2,1)S(1)} collective-permute-done((bf16[29,8,512]{2,1,0:T(8,128)(2,1)S(1)}, bf16[29,8,512]{2,1,0:T(8,128)(2,1)S(1)}, u32[]{:S(2)}, u32[]{:S(2)}) %collective-permute-start.10) | collective-permute-done | bytes 237600 | tf_op jit(solution)/shard_map/ppermute | solution.py:362
  85.9 2.6 %collective-permute-start.7 = (bf16[29,8,512]{2,1,0:T(8,128)(2,1)}, bf16[29,8,512]{2,1,0:T(8,128)(2,1)S(1)}, u32[]{:S(2)}, u32[]{:S(2)}) collective-permute-start(bf16[29,8,512]{2,1,0:T(8,128)(2,1)} %get-tuple-element.66), channel_id=1, source_target_pairs={{0,2},{2,0},{4,6},{6,4},{8,10},{10,8},{12,14},{14,12},{1,3},{3,1},... | collective-permute-start | bytes 712712 | tf_op jit(solution)/shard_map/ppermute | solution.py:362
  88.5 4.6 %collective-permute-done.11.refs_5_ = bf16[29,8,512]{2,1,0:T(8,128)(2,1)S(1)} collective-permute-done((bf16[29,8,512]{2,1,0:T(8,128)(2,1)S(1)}, bf16[29,8,512]{2,1,0:T(8,128)(2,1)S(1)}, u32[]{:S(2)}, u32[]{:S(2)}) %collective-permute-start.11) | collective-permute-done | bytes 237600 | tf_op jit(solution)/shard_map/ppermute | solution.py:362
  93.1 5.6 %collective-permute-start.9 = (bf16[29,8,512]{2,1,0:T(8,128)(2,1)}, bf16[29,8,512]{2,1,0:T(8,128)(2,1)S(1)}, u32[]{:S(2)}, u32[]{:S(2)}) collective-permute-start(bf16[29,8,512]{2,1,0:T(8,128)(2,1)} %copy-done.5), channel_id=1, source_target_pairs={{0,6},{2,4},{4,2},{6,0},{8,14},{10,12},{12,10},{14,8},{1,7},{3,5},... | collective-permute-start | bytes 712712 | tf_op jit(solution)/shard_map/ppermute | solution.py:362
  98.7 1.9 payloads.3
  100.6 0.7 copy-done.6
  101.3 0.7 copy-done.7
  102.0 0.7 copy-done.8
  102.7 0.7 copy-done.9
  103.3 0.7 copy-done.10
  104.0 0.7 copy-done.11
  104.6 0.7 copy-done.12
  105.3 1.3 space_column.1
  106.7 2.3 collective-permute-start
  108.9 1.4 collective-permute-start.1
  110.3 1.4 collective-permute-start.2
  111.7 2.6 %collective-permute-start.3 = (bf16[21,8,512]{2,1,0:T(8,128)(2,1)}, bf16[21,8,512]{2,1,0:T(8,128)(2,1)}, u32[]{:S(2)}, u32[]{:S(2)}) collective-permute-start(bf16[21,8,512]{2,1,0:T(8,128)(2,1)} %copy-done.9), channel_id=1, source_target_pairs={{0,8},{2,10},{4,12},{6,14},{8,0},{10,2},{12,4},{14,6},{1,9},{3,11}... | collective-permute-start | bytes 516104 | tf_op jit(solution)/shard_map/ppermute | solution.py:362
  114.4 0.7 copy-done.1
  115.0 2.5 %collective-permute-start.4 = (bf16[21,8,512]{2,1,0:T(8,128)(2,1)}, bf16[21,8,512]{2,1,0:T(8,128)(2,1)}, u32[]{:S(2)}, u32[]{:S(2)}) collective-permute-start(bf16[21,8,512]{2,1,0:T(8,128)(2,1)} %copy-done.8), channel_id=1, source_target_pairs={{0,10},{2,8},{4,14},{6,12},{8,2},{10,0},{12,6},{14,4},{1,11},{3,9}... | collective-permute-start | bytes 516104 | tf_op jit(solution)/shard_map/ppermute | solution.py:362
  117.5 3.2 %collective-permute-done.1.refs_2_ = bf16[21,8,512]{2,1,0:T(8,128)(2,1)S(1)} collective-permute-done((bf16[21,8,512]{2,1,0:T(8,128)(2,1)}, bf16[21,8,512]{2,1,0:T(8,128)(2,1)S(1)}, u32[]{:S(2)}, u32[]{:S(2)}) %collective-permute-start.1) | collective-permute-done | bytes 172064 | tf_op jit(solution)/shard_map/ppermute | solution.py:362
  120.8 0.7 copy-done.3
  121.4 1.7 collective-permute-start.5
  123.1 4.3 %collective-permute-start.6 = (bf16[21,8,512]{2,1,0:T(8,128)(2,1)}, bf16[21,8,512]{2,1,0:T(8,128)(2,1)}, u32[]{:S(2)}, u32[]{:S(2)}) collective-permute-start(bf16[21,8,512]{2,1,0:T(8,128)(2,1)} %copy-done.6), channel_id=1, source_target_pairs={{0,14},{2,12},{4,10},{6,8},{8,6},{10,4},{12,2},{14,0},{1,15},{3,13... | collective-permute-start | bytes 516104 | tf_op jit(solution)/shard_map/ppermute | solution.py:362
  127.4 20.6 %time_first.1 = (bf16[21,8,512]{2,1,0:T(8,128)(2,1)S(1)}, bf16[21,8,512]{2,1,0:T(8,128)(2,1)S(1)}, bf16[21,8,512]{2,1,0:T(8,128)(2,1)S(1)}, bf16[21,8,512]{2,1,0...) custom-call(bf16[29,8,512]{2,1,0:T(8,128)(2,1)S(1)} %get-tuple-eleme, ...), custom_call_target="tpu_custom_call" | custom-call | bytes 59040000 | tf_op jit(solution)/shard_map/time_first/pallas_call | solution.py:283
  148.1 0.1 collective-permute-start.29
  148.2 0.1 collective-permute-start.30
  148.3 3.4 %collective-permute-start.31 = (bf16[21,8,512]{2,1,0:T(8,128)(2,1)S(1)}, bf16[21,8,512]{2,1,0:T(8,128)(2,1)S(1)}, u32[]{:S(2)}, u32[]{:S(2)}) collective-permute-start(bf16[21,8,512]{2,1,0:T(8,128)(2,1)S(1)} %get-tuple-element.92), channel_id=1, source_target_pairs={{0,6},{2,4},{4,2},{6,0},{8,14},{10,12},{12,10},{14,8},{1,7},{3,5},... | collective-permute-start | bytes 516104 | tf_op jit(solution)/shard_map/ppermute | solution.py:362
  151.6 0.4 collective-permute-start.32
  152.0 2.1 collective-permute-start.33
  154.1 12.1 %time_second.1 = (bf16[21,8,512]{2,1,0:T(8,128)(2,1)S(1)}, bf16[21,8,512]{2,1,0:T(8,128)(2,1)S(1)}, bf16[21,8,512]{2,1,0:T(8,128)(2,1)S(1)}, bf16[21,8,512]{2,1,...) custom-call(bf16[21,8,512]{2,1,0:T(8,128)(2,1)S(1)} %get-tuple-eleme, ...), custom_call_target="tpu_custom_call" | custom-call | bytes 36900000 | tf_op jit(solution)/shard_map/time_second/pallas_call | solution.py:283
  166.3 1.8 collective-permute-start.34
  168.1 3.5 %collective-permute-start.35 = (bf16[21,8,512]{2,1,0:T(8,128)(2,1)S(1)}, bf16[21,8,512]{2,1,0:T(8,128)(2,1)S(1)}, u32[]{:S(2)}, u32[]{:S(2)}) collective-permute-start(bf16[21,8,512]{2,1,0:T(8,128)(2,1)S(1)} %get-tuple-element.96), channel_id=1, source_target_pairs={{0,14},{2,12},{4,10},{6,8},{8,6},{10,4},{12,2},{14,0},{1,15},{3,13... | collective-permute-start | bytes 516104 | tf_op jit(solution)/shard_map/ppermute | solution.py:362
  171.5 0.1 collective-permute-start.22
  171.6 3.4 %collective-permute-start.24 = (bf16[21,8,512]{2,1,0:T(8,128)(2,1)S(1)}, bf16[21,8,512]{2,1,0:T(8,128)(2,1)S(1)}, u32[]{:S(2)}, u32[]{:S(2)}) collective-permute-start(bf16[21,8,512]{2,1,0:T(8,128)(2,1)S(1)} %get-tuple-element.84), channel_id=1, source_target_pairs={{0,6},{2,4},{4,2},{6,0},{8,14},{10,12},{12,10},{14,8},{1,7},{3,5},... | collective-permute-start | bytes 516104 | tf_op jit(solution)/shard_map/ppermute | solution.py:362
  175.0 0.1 collective-permute-done.34.refs_6_
  175.1 4.9 %collective-permute-start.25 = (bf16[21,8,512]{2,1,0:T(8,128)(2,1)S(1)}, bf16[21,8,512]{2,1,0:T(8,128)(2,1)S(1)}, u32[]{:S(2)}, u32[]{:S(2)}) collective-permute-start(bf16[21,8,512]{2,1,0:T(8,128)(2,1)S(1)} %get-tuple-element.85), channel_id=1, source_target_pairs={{0,8},{2,10},{4,12},{6,14},{8,0},{10,2},{12,4},{14,6},{1,9},{3,11}... | collective-permute-start | bytes 516104 | tf_op jit(solution)/shard_map/ppermute | solution.py:362
  180.0 12.0 %collective-permute-start.26 = (bf16[21,8,512]{2,1,0:T(8,128)(2,1)S(1)}, bf16[21,8,512]{2,1,0:T(8,128)(2,1)S(1)}, u32[]{:S(2)}, u32[]{:S(2)}) collective-permute-start(bf16[21,8,512]{2,1,0:T(8,128)(2,1)S(1)} %get-tuple-element.86), channel_id=1, source_target_pairs={{0,10},{2,8},{4,14},{6,12},{8,2},{10,0},{12,6},{14,4},{1,11},{3,9}... | collective-permute-start | bytes 516104 | tf_op jit(solution)/shard_map/ppermute | solution.py:362
  192.0 2.2 collective-permute-start.27
  194.1 2.6 %collective-permute-start.28 = (bf16[21,8,512]{2,1,0:T(8,128)(2,1)S(1)}, bf16[21,8,512]{2,1,0:T(8,128)(2,1)S(1)}, u32[]{:S(2)}, u32[]{:S(2)}) collective-permute-start(bf16[21,8,512]{2,1,0:T(8,128)(2,1)S(1)} %get-tuple-element.88), channel_id=1, source_target_pairs={{0,14},{2,12},{4,10},{6,8},{8,6},{10,4},{12,2},{14,0},{1,15},{3,13... | collective-permute-start | bytes 516104 | tf_op jit(solution)/shard_map/ppermute | solution.py:362
  196.7 1.6 place_first.1
  198.3 23.8 %space_attention.1 = (bf16[7,64,1024]{2,1,0:T(8,128)(2,1)}, bf16[7,64,1024]{2,1,0:T(8,128)(2,1)}, bf16[7,64,1024]{2,1,0:T(8,128)(2,1)}) custom-call(bf16[7,64,1024]{2,1,0:T(8,128)(2,1)} %refs_0_.3, bf16[7,64,1024]{2,1,0:T(8,128)(2,1)} %refs_1_.3, bf16[7,64,1024]{2,1,0:T(8,128)(2,1)} %refs_2_.3, ...), custom_call_target="tpu_custom_call" | custom-call | bytes 73800000 | tf_op jit(solution)/shard_map/space_attention/pallas_call | solution.py:330
  222.2 1.6 place_second.1
  (53 shorter events, 0.1 us)
Async XLA Ops:
  7.2 120.3 %all-gather.3.cloned.1.call-start = ((), (), s32[]{:S(2)}) async-start(), calls=%async_computation | async-start | bytes 2621440 | tf_op jit(solution)/shard_map/all_gather | solution.py:419
  9.4 8.8 %collective-permute-start.14 = (bf16[11,8,1024]{2,1,0:T(8,128)(2,1)S(1)}, bf16[11,8,1024]{2,1,0:T(8,128)(2,1)S(1)}, u32[]{:S(2)}, u32[]{:S(2)}) collective-permute-start(bf16[11,8,1024]{2,1,0:T(8,128)(2,1)S(1)} %get-tuple-element.73), channel_id=1, source_target_pairs={{0,2},{2,0},{4,6},{6,4},{8,10},{10,8},{12,14},{14,12},{1,3},{3,1},... | collective-permute-start | bytes 540680 | tf_op jit(solution)/shard_map/ppermute | solution.py:362
  12.3 14.2 %collective-permute-start.15 = (bf16[11,8,1024]{2,1,0:T(8,128)(2,1)S(1)}, bf16[11,8,1024]{2,1,0:T(8,128)(2,1)S(1)}, u32[]{:S(2)}, u32[]{:S(2)}) collective-permute-start(bf16[11,8,1024]{2,1,0:T(8,128)(2,1)S(1)} %get-tuple-element.74), channel_id=1, source_target_pairs={{0,4},{2,6},{4,0},{6,2},{8,12},{10,14},{12,8},{14,10},{1,5},{3,7},... | collective-permute-start | bytes 540680 | tf_op jit(solution)/shard_map/ppermute | solution.py:362
  13.9 40.2 %collective-permute-start.16 = (bf16[11,8,1024]{2,1,0:T(8,128)(2,1)S(1)}, bf16[11,8,1024]{2,1,0:T(8,128)(2,1)S(1)}, u32[]{:S(2)}, u32[]{:S(2)}) collective-permute-start(bf16[11,8,1024]{2,1,0:T(8,128)(2,1)S(1)} %get-tuple-element.75), channel_id=1, source_target_pairs={{0,6},{2,4},{4,2},{6,0},{8,14},{10,12},{12,10},{14,8},{1,7},{3,5},... | collective-permute-start | bytes 540680 | tf_op jit(solution)/shard_map/ppermute | solution.py:362
  13.9 40.2 %collective-permute-start.17 = (bf16[11,8,1024]{2,1,0:T(8,128)(2,1)S(1)}, bf16[11,8,1024]{2,1,0:T(8,128)(2,1)S(1)}, u32[]{:S(2)}, u32[]{:S(2)}) collective-permute-start(bf16[11,8,1024]{2,1,0:T(8,128)(2,1)S(1)} %get-tuple-element.76), channel_id=1, source_target_pairs={{0,8},{2,10},{4,12},{6,14},{8,0},{10,2},{12,4},{14,6},{1,9},{3,11}... | collective-permute-start | bytes 540680 | tf_op jit(solution)/shard_map/ppermute | solution.py:362
  16.9 37.2 %collective-permute-start.18 = (bf16[11,8,1024]{2,1,0:T(8,128)(2,1)S(1)}, bf16[11,8,1024]{2,1,0:T(8,128)(2,1)S(1)}, u32[]{:S(2)}, u32[]{:S(2)}) collective-permute-start(bf16[11,8,1024]{2,1,0:T(8,128)(2,1)S(1)} %get-tuple-element.77), channel_id=1, source_target_pairs={{0,10},{2,8},{4,14},{6,12},{8,2},{10,0},{12,6},{14,4},{1,11},{3,9}... | collective-permute-start | bytes 540680 | tf_op jit(solution)/shard_map/ppermute | solution.py:362
  18.2 35.9 %collective-permute-start.19 = (bf16[11,8,1024]{2,1,0:T(8,128)(2,1)S(1)}, bf16[11,8,1024]{2,1,0:T(8,128)(2,1)S(1)}, u32[]{:S(2)}, u32[]{:S(2)}) collective-permute-start(bf16[11,8,1024]{2,1,0:T(8,128)(2,1)S(1)} %get-tuple-element.78), channel_id=1, source_target_pairs={{0,12},{2,14},{4,8},{6,10},{8,4},{10,6},{12,0},{14,2},{1,13},{3,15... | collective-permute-start | bytes 540680 | tf_op jit(solution)/shard_map/ppermute | solution.py:362
  26.6 27.5 %collective-permute-start.20 = (bf16[11,8,1024]{2,1,0:T(8,128)(2,1)S(1)}, bf16[11,8,1024]{2,1,0:T(8,128)(2,1)S(1)}, u32[]{:S(2)}, u32[]{:S(2)}) collective-permute-start(bf16[11,8,1024]{2,1,0:T(8,128)(2,1)S(1)} %get-tuple-element.79), channel_id=1, source_target_pairs={{0,14},{2,12},{4,10},{6,8},{8,6},{10,4},{12,2},{14,0},{1,15},{3,13... | collective-permute-start | bytes 540680 | tf_op jit(solution)/shard_map/ppermute | solution.py:362
  50.8 0.7 copy-start.5
  55.4 1.8 copy-start
  57.3 141.0 %all-gather.5.cloned.1.call-start = ((), (), s32[]{:S(2)}) async-start(), calls=%async_computation.1 | async-start | bytes 2621440 | tf_op jit(solution)/shard_map/all_gather | solution.py:419
  57.3 65.8 %collective-permute-start.21 = (bf16[4,7,64,1024]{3,2,1,0:T(8,128)(2,1)}, bf16[4,7,64,1024]{3,2,1,0:T(8,128)(2,1)}, u32[]{:S(2)}, u32[]{:S(2)}) collective-permute-start(bf16[4,7,64,1024]{3,2,1,0:T(8,128)(2,1)} %copy-done), channel_id=1, source_target_pairs={{0,1},{1,0},{2,3},{3,2},{4,5},{5,4},{6,7},{7,6},{8,9},{9,8},{10,11... | collective-permute-start | bytes 11010056 | tf_op jit(solution)/shard_map/ppermute | solution.py:416
  57.4 28.5 %collective-permute-start.10 = (bf16[29,8,512]{2,1,0:T(8,128)(2,1)S(1)}, bf16[29,8,512]{2,1,0:T(8,128)(2,1)S(1)}, u32[]{:S(2)}, u32[]{:S(2)}) collective-permute-start(bf16[29,8,512]{2,1,0:T(8,128)(2,1)S(1)} %get-tuple-element.69), channel_id=1, source_target_pairs={{0,8},{2,10},{4,12},{6,14},{8,0},{10,2},{12,4},{14,6},{1,9},{3,11}... | collective-permute-start | bytes 712712 | tf_op jit(solution)/shard_map/ppermute | solution.py:362
  57.5 35.6 %collective-permute-start.11 = (bf16[29,8,512]{2,1,0:T(8,128)(2,1)S(1)}, bf16[29,8,512]{2,1,0:T(8,128)(2,1)S(1)}, u32[]{:S(2)}, u32[]{:S(2)}) collective-permute-start(bf16[29,8,512]{2,1,0:T(8,128)(2,1)S(1)} %get-tuple-element.70), channel_id=1, source_target_pairs={{0,10},{2,8},{4,14},{6,12},{8,2},{10,0},{12,6},{14,4},{1,11},{3,9}... | collective-permute-start | bytes 712712 | tf_op jit(solution)/shard_map/ppermute | solution.py:362
  62.4 30.8 %collective-permute-start.12 = (bf16[29,8,512]{2,1,0:T(8,128)(2,1)S(1)}, bf16[29,8,512]{2,1,0:T(8,128)(2,1)S(1)}, u32[]{:S(2)}, u32[]{:S(2)}) collective-permute-start(bf16[29,8,512]{2,1,0:T(8,128)(2,1)S(1)} %get-tuple-element.71), channel_id=1, source_target_pairs={{0,12},{2,14},{4,8},{6,10},{8,4},{10,6},{12,0},{14,2},{1,13},{3,15... | collective-permute-start | bytes 712712 | tf_op jit(solution)/shard_map/ppermute | solution.py:362
  64.1 41.2 %collective-permute-start.13 = (bf16[29,8,512]{2,1,0:T(8,128)(2,1)}, bf16[29,8,512]{2,1,0:T(8,128)(2,1)S(1)}, u32[]{:S(2)}, u32[]{:S(2)}) collective-permute-start(bf16[29,8,512]{2,1,0:T(8,128)(2,1)} %get-tuple-element.72), channel_id=1, source_target_pairs={{0,14},{2,12},{4,10},{6,8},{8,6},{10,4},{12,2},{14,0},{1,15},{3,13... | collective-permute-start | bytes 712712 | tf_op jit(solution)/shard_map/ppermute | solution.py:362
  85.9 19.4 %collective-permute-start.7 = (bf16[29,8,512]{2,1,0:T(8,128)(2,1)}, bf16[29,8,512]{2,1,0:T(8,128)(2,1)S(1)}, u32[]{:S(2)}, u32[]{:S(2)}) collective-permute-start(bf16[29,8,512]{2,1,0:T(8,128)(2,1)} %get-tuple-element.66), channel_id=1, source_target_pairs={{0,2},{2,0},{4,6},{6,4},{8,10},{10,8},{12,14},{14,12},{1,3},{3,1},... | collective-permute-start | bytes 712712 | tf_op jit(solution)/shard_map/ppermute | solution.py:362
  93.1 12.2 %collective-permute-start.8 = (bf16[29,8,512]{2,1,0:T(8,128)(2,1)}, bf16[29,8,512]{2,1,0:T(8,128)(2,1)S(1)}, u32[]{:S(2)}, u32[]{:S(2)}) collective-permute-start(bf16[29,8,512]{2,1,0:T(8,128)(2,1)} %get-tuple-element.67), channel_id=1, source_target_pairs={{0,4},{2,6},{4,0},{6,2},{8,12},{10,14},{12,8},{14,10},{1,5},{3,7},... | collective-permute-start | bytes 712712 | tf_op jit(solution)/shard_map/ppermute | solution.py:362
  93.1 12.2 %collective-permute-start.9 = (bf16[29,8,512]{2,1,0:T(8,128)(2,1)}, bf16[29,8,512]{2,1,0:T(8,128)(2,1)S(1)}, u32[]{:S(2)}, u32[]{:S(2)}) collective-permute-start(bf16[29,8,512]{2,1,0:T(8,128)(2,1)} %copy-done.5), channel_id=1, source_target_pairs={{0,6},{2,4},{4,2},{6,0},{8,14},{10,12},{12,10},{14,8},{1,7},{3,5},... | collective-permute-start | bytes 712712 | tf_op jit(solution)/shard_map/ppermute | solution.py:362
  100.6 0.7 copy-start.6
  101.3 0.7 copy-start.7
  102.0 0.7 copy-start.8
  102.7 0.7 copy-start.9
  103.3 0.7 copy-start.10
  104.0 0.7 copy-start.11
  104.6 0.7 copy-start.12
  106.7 7.7 %collective-permute-start = (bf16[21,8,512]{2,1,0:T(8,128)(2,1)}, bf16[21,8,512]{2,1,0:T(8,128)(2,1)S(1)}, u32[]{:S(2)}, u32[]{:S(2)}) collective-permute-start(bf16[21,8,512]{2,1,0:T(8,128)(2,1)} %copy-done.12), channel_id=1, source_target_pairs={{0,2},{2,0},{4,6},{6,4},{8,10},{10,8},{12,14},{14,12},{1,3},{3,1},... | collective-permute-start | bytes 516104 | tf_op jit(solution)/shard_map/ppermute | solution.py:362
  108.9 11.8 %collective-permute-start.1 = (bf16[21,8,512]{2,1,0:T(8,128)(2,1)}, bf16[21,8,512]{2,1,0:T(8,128)(2,1)S(1)}, u32[]{:S(2)}, u32[]{:S(2)}) collective-permute-start(bf16[21,8,512]{2,1,0:T(8,128)(2,1)} %copy-done.11), channel_id=1, source_target_pairs={{0,4},{2,6},{4,0},{6,2},{8,12},{10,14},{12,8},{14,10},{1,5},{3,7},... | collective-permute-start | bytes 516104 | tf_op jit(solution)/shard_map/ppermute | solution.py:362
  110.3 37.7 %collective-permute-start.2 = (bf16[21,8,512]{2,1,0:T(8,128)(2,1)}, bf16[21,8,512]{2,1,0:T(8,128)(2,1)}, u32[]{:S(2)}, u32[]{:S(2)}) collective-permute-start(bf16[21,8,512]{2,1,0:T(8,128)(2,1)} %copy-done.10), channel_id=1, source_target_pairs={{0,6},{2,4},{4,2},{6,0},{8,14},{10,12},{12,10},{14,8},{1,7},{3,5},... | collective-permute-start | bytes 516104 | tf_op jit(solution)/shard_map/ppermute | solution.py:362
  111.7 36.4 %collective-permute-start.3 = (bf16[21,8,512]{2,1,0:T(8,128)(2,1)}, bf16[21,8,512]{2,1,0:T(8,128)(2,1)}, u32[]{:S(2)}, u32[]{:S(2)}) collective-permute-start(bf16[21,8,512]{2,1,0:T(8,128)(2,1)} %copy-done.9), channel_id=1, source_target_pairs={{0,8},{2,10},{4,12},{6,14},{8,0},{10,2},{12,4},{14,6},{1,9},{3,11}... | collective-permute-start | bytes 516104 | tf_op jit(solution)/shard_map/ppermute | solution.py:362
  114.4 0.7 copy-start.1
  115.0 33.2 %collective-permute-start.4 = (bf16[21,8,512]{2,1,0:T(8,128)(2,1)}, bf16[21,8,512]{2,1,0:T(8,128)(2,1)}, u32[]{:S(2)}, u32[]{:S(2)}) collective-permute-start(bf16[21,8,512]{2,1,0:T(8,128)(2,1)} %copy-done.8), channel_id=1, source_target_pairs={{0,10},{2,8},{4,14},{6,12},{8,2},{10,0},{12,6},{14,4},{1,11},{3,9}... | collective-permute-start | bytes 516104 | tf_op jit(solution)/shard_map/ppermute | solution.py:362
  120.8 0.7 copy-start.3
  121.4 30.2 %collective-permute-start.5 = (bf16[21,8,512]{2,1,0:T(8,128)(2,1)}, bf16[21,8,512]{2,1,0:T(8,128)(2,1)}, u32[]{:S(2)}, u32[]{:S(2)}) collective-permute-start(bf16[21,8,512]{2,1,0:T(8,128)(2,1)} %copy-done.7), channel_id=1, source_target_pairs={{0,12},{2,14},{4,8},{6,10},{8,4},{10,6},{12,0},{14,2},{1,13},{3,15... | collective-permute-start | bytes 516104 | tf_op jit(solution)/shard_map/ppermute | solution.py:362
  123.1 28.9 %collective-permute-start.6 = (bf16[21,8,512]{2,1,0:T(8,128)(2,1)}, bf16[21,8,512]{2,1,0:T(8,128)(2,1)}, u32[]{:S(2)}, u32[]{:S(2)}) collective-permute-start(bf16[21,8,512]{2,1,0:T(8,128)(2,1)} %copy-done.6), channel_id=1, source_target_pairs={{0,14},{2,12},{4,10},{6,8},{8,6},{10,4},{12,2},{14,0},{1,15},{3,13... | collective-permute-start | bytes 516104 | tf_op jit(solution)/shard_map/ppermute | solution.py:362
  127.4 26.7 %copy-start.2 = (bf16[21,8,512]{2,1,0:T(8,128)(2,1)S(1)}, bf16[21,8,512]{2,1,0:T(8,128)(2,1)}, u32[]{:S(2)}) copy-start(bf16[21,8,512]{2,1,0:T(8,128)(2,1)} %copy-done.1) | copy-start | bytes 516100
  127.4 26.7 %copy-start.4 = (bf16[21,8,512]{2,1,0:T(8,128)(2,1)S(1)}, bf16[21,8,512]{2,1,0:T(8,128)(2,1)}, u32[]{:S(2)}) copy-start(bf16[21,8,512]{2,1,0:T(8,128)(2,1)} %copy-done.3) | copy-start | bytes 516100
  148.1 18.2 %collective-permute-start.29 = (bf16[21,8,512]{2,1,0:T(8,128)(2,1)S(1)}, bf16[21,8,512]{2,1,0:T(8,128)(2,1)S(1)}, u32[]{:S(2)}, u32[]{:S(2)}) collective-permute-start(bf16[21,8,512]{2,1,0:T(8,128)(2,1)S(1)} %get-tuple-element.90), channel_id=1, source_target_pairs={{0,2},{2,0},{4,6},{6,4},{8,10},{10,8},{12,14},{14,12},{1,3},{3,1},... | collective-permute-start | bytes 516104 | tf_op jit(solution)/shard_map/ppermute | solution.py:362
  148.2 19.9 %collective-permute-start.30 = (bf16[21,8,512]{2,1,0:T(8,128)(2,1)S(1)}, bf16[21,8,512]{2,1,0:T(8,128)(2,1)S(1)}, u32[]{:S(2)}, u32[]{:S(2)}) collective-permute-start(bf16[21,8,512]{2,1,0:T(8,128)(2,1)S(1)} %get-tuple-element.91), channel_id=1, source_target_pairs={{0,4},{2,6},{4,0},{6,2},{8,12},{10,14},{12,8},{14,10},{1,5},{3,7},... | collective-permute-start | bytes 516104 | tf_op jit(solution)/shard_map/ppermute | solution.py:362
  148.3 23.3 %collective-permute-start.31 = (bf16[21,8,512]{2,1,0:T(8,128)(2,1)S(1)}, bf16[21,8,512]{2,1,0:T(8,128)(2,1)S(1)}, u32[]{:S(2)}, u32[]{:S(2)}) collective-permute-start(bf16[21,8,512]{2,1,0:T(8,128)(2,1)S(1)} %get-tuple-element.92), channel_id=1, source_target_pairs={{0,6},{2,4},{4,2},{6,0},{8,14},{10,12},{12,10},{14,8},{1,7},{3,5},... | collective-permute-start | bytes 516104 | tf_op jit(solution)/shard_map/ppermute | solution.py:362
  151.6 20.0 %collective-permute-start.32 = (bf16[21,8,512]{2,1,0:T(8,128)(2,1)S(1)}, bf16[21,8,512]{2,1,0:T(8,128)(2,1)S(1)}, u32[]{:S(2)}, u32[]{:S(2)}) collective-permute-start(bf16[21,8,512]{2,1,0:T(8,128)(2,1)S(1)} %get-tuple-element.93), channel_id=1, source_target_pairs={{0,8},{2,10},{4,12},{6,14},{8,0},{10,2},{12,4},{14,6},{1,9},{3,11}... | collective-permute-start | bytes 516104 | tf_op jit(solution)/shard_map/ppermute | solution.py:362
  152.0 19.6 %collective-permute-start.33 = (bf16[21,8,512]{2,1,0:T(8,128)(2,1)S(1)}, bf16[21,8,512]{2,1,0:T(8,128)(2,1)S(1)}, u32[]{:S(2)}, u32[]{:S(2)}) collective-permute-start(bf16[21,8,512]{2,1,0:T(8,128)(2,1)S(1)} %get-tuple-element.94), channel_id=1, source_target_pairs={{0,10},{2,8},{4,14},{6,12},{8,2},{10,0},{12,6},{14,4},{1,11},{3,9}... | collective-permute-start | bytes 516104 | tf_op jit(solution)/shard_map/ppermute | solution.py:362
  166.3 8.8 %collective-permute-start.34 = (bf16[21,8,512]{2,1,0:T(8,128)(2,1)S(1)}, bf16[21,8,512]{2,1,0:T(8,128)(2,1)S(1)}, u32[]{:S(2)}, u32[]{:S(2)}) collective-permute-start(bf16[21,8,512]{2,1,0:T(8,128)(2,1)S(1)} %get-tuple-element.95), channel_id=1, source_target_pairs={{0,12},{2,14},{4,8},{6,10},{8,4},{10,6},{12,0},{14,2},{1,13},{3,15... | collective-permute-start | bytes 516104 | tf_op jit(solution)/shard_map/ppermute | solution.py:362
  168.1 11.9 %collective-permute-start.35 = (bf16[21,8,512]{2,1,0:T(8,128)(2,1)S(1)}, bf16[21,8,512]{2,1,0:T(8,128)(2,1)S(1)}, u32[]{:S(2)}, u32[]{:S(2)}) collective-permute-start(bf16[21,8,512]{2,1,0:T(8,128)(2,1)S(1)} %get-tuple-element.96), channel_id=1, source_target_pairs={{0,14},{2,12},{4,10},{6,8},{8,6},{10,4},{12,2},{14,0},{1,15},{3,13... | collective-permute-start | bytes 516104 | tf_op jit(solution)/shard_map/ppermute | solution.py:362
  171.5 20.4 %collective-permute-start.22 = (bf16[21,8,512]{2,1,0:T(8,128)(2,1)S(1)}, bf16[21,8,512]{2,1,0:T(8,128)(2,1)S(1)}, u32[]{:S(2)}, u32[]{:S(2)}) collective-permute-start(bf16[21,8,512]{2,1,0:T(8,128)(2,1)S(1)} %get-tuple-element.82), channel_id=1, source_target_pairs={{0,2},{2,0},{4,6},{6,4},{8,10},{10,8},{12,14},{14,12},{1,3},{3,1},... | collective-permute-start | bytes 516104 | tf_op jit(solution)/shard_map/ppermute | solution.py:362
  171.6 22.5 %collective-permute-start.23 = (bf16[21,8,512]{2,1,0:T(8,128)(2,1)S(1)}, bf16[21,8,512]{2,1,0:T(8,128)(2,1)S(1)}, u32[]{:S(2)}, u32[]{:S(2)}) collective-permute-start(bf16[21,8,512]{2,1,0:T(8,128)(2,1)S(1)} %get-tuple-element.83), channel_id=1, source_target_pairs={{0,4},{2,6},{4,0},{6,2},{8,12},{10,14},{12,8},{14,10},{1,5},{3,7},... | collective-permute-start | bytes 516104 | tf_op jit(solution)/shard_map/ppermute | solution.py:362
  171.6 50.5 %collective-permute-start.24 = (bf16[21,8,512]{2,1,0:T(8,128)(2,1)S(1)}, bf16[21,8,512]{2,1,0:T(8,128)(2,1)S(1)}, u32[]{:S(2)}, u32[]{:S(2)}) collective-permute-start(bf16[21,8,512]{2,1,0:T(8,128)(2,1)S(1)} %get-tuple-element.84), channel_id=1, source_target_pairs={{0,6},{2,4},{4,2},{6,0},{8,14},{10,12},{12,10},{14,8},{1,7},{3,5},... | collective-permute-start | bytes 516104 | tf_op jit(solution)/shard_map/ppermute | solution.py:362
  175.1 47.0 %collective-permute-start.25 = (bf16[21,8,512]{2,1,0:T(8,128)(2,1)S(1)}, bf16[21,8,512]{2,1,0:T(8,128)(2,1)S(1)}, u32[]{:S(2)}, u32[]{:S(2)}) collective-permute-start(bf16[21,8,512]{2,1,0:T(8,128)(2,1)S(1)} %get-tuple-element.85), channel_id=1, source_target_pairs={{0,8},{2,10},{4,12},{6,14},{8,0},{10,2},{12,4},{14,6},{1,9},{3,11}... | collective-permute-start | bytes 516104 | tf_op jit(solution)/shard_map/ppermute | solution.py:362
  180.0 42.1 %collective-permute-start.26 = (bf16[21,8,512]{2,1,0:T(8,128)(2,1)S(1)}, bf16[21,8,512]{2,1,0:T(8,128)(2,1)S(1)}, u32[]{:S(2)}, u32[]{:S(2)}) collective-permute-start(bf16[21,8,512]{2,1,0:T(8,128)(2,1)S(1)} %get-tuple-element.86), channel_id=1, source_target_pairs={{0,10},{2,8},{4,14},{6,12},{8,2},{10,0},{12,6},{14,4},{1,11},{3,9}... | collective-permute-start | bytes 516104 | tf_op jit(solution)/shard_map/ppermute | solution.py:362
  192.0 30.2 %collective-permute-start.27 = (bf16[21,8,512]{2,1,0:T(8,128)(2,1)S(1)}, bf16[21,8,512]{2,1,0:T(8,128)(2,1)S(1)}, u32[]{:S(2)}, u32[]{:S(2)}) collective-permute-start(bf16[21,8,512]{2,1,0:T(8,128)(2,1)S(1)} %get-tuple-element.87), channel_id=1, source_target_pairs={{0,12},{2,14},{4,8},{6,10},{8,4},{10,6},{12,0},{14,2},{1,13},{3,15... | collective-permute-start | bytes 516104 | tf_op jit(solution)/shard_map/ppermute | solution.py:362
  194.1 28.0 %collective-permute-start.28 = (bf16[21,8,512]{2,1,0:T(8,128)(2,1)S(1)}, bf16[21,8,512]{2,1,0:T(8,128)(2,1)S(1)}, u32[]{:S(2)}, u32[]{:S(2)}) collective-permute-start(bf16[21,8,512]{2,1,0:T(8,128)(2,1)S(1)} %get-tuple-element.88), channel_id=1, source_target_pairs={{0,14},{2,12},{4,10},{6,8},{8,6},{10,4},{12,2},{14,0},{1,15},{3,13... | collective-permute-start | bytes 516104 | tf_op jit(solution)/shard_map/ppermute | solution.py:362
Sparse Core Ops, SparseCore 0:
  57.4 22.9 all-gather.2
  106.8 23.4 all-gather.4

commit v7 on v6

--- a/solution.py
+++ b/solution.py
@@ -292,15 +292,15 @@
     )(*blocks, *operands, *settled(after))
 
 
-def space_attention(own, far, own_tokens, weights_of, after=()):
+def space_attention(other_core, own, far, own_tokens, weights_of, after=()):
     frames, rows, width = own_tokens.shape
     space, groups, tm, share = weights_of.shape[:4]
     pieces = space * groups * tm
 
-    def kernel(*refs):
-        own_refs, far_ref, own_token_ref, far_token_ref, gathered_ref = refs[:3], *refs[3:7]
-        outs = refs[7 + len(after) : 10 + len(after)]
-        weights, grads, sems = refs[10 + len(after) :]
+    def kernel(core_ref, *refs):
+        own_refs, far_refs, own_token_ref, far_token_ref, gathered_ref = refs[:3], refs[3:6], *refs[6:9]
+        outs = refs[9 + len(after) : 12 + len(after)]
+        weights, grads, sems = refs[12 + len(after) :]
 
         @pl.when(pl.program_id(0) == 0)
         def _():
@@ -316,23 +316,23 @@
         for pair in range(width // PAIR):
             columns = slice(pair * PAIR, (pair + 1) * PAIR)
             operands = [
-                (near[0, :, columns].astype(F32), far_ref[index, 0, :, columns].astype(F32))
-                for index, near in enumerate(own_refs)
+                (near[0, :, columns].astype(F32), away[0, 0, :, columns].astype(F32))
+                for near, away in zip(own_refs, far_refs)
             ]
             operands.append(tuple(grads[side, frame, :, columns].astype(F32) for side in range(2)))
             for out, value in zip(outs, own_back(*operands)):
                 out[0, :, columns] = value.astype(BF16)
 
-    near = pl.BlockSpec((1, rows, width), lambda f: (f, 0, 0))
-    near_all = pl.BlockSpec((frames, rows, width), lambda f: (0, 0, 0))
-    away = pl.BlockSpec((3, 1, rows, width), lambda f: (0, f, 0, 0))
-    away_all = pl.BlockSpec((1, frames, rows, width), lambda f: (3, 0, 0, 0))
+    near = pl.BlockSpec((1, rows, width), lambda f, core_ref: (f, 0, 0))
+    near_all = pl.BlockSpec((frames, rows, width), lambda f, core_ref: (0, 0, 0))
+    away = pl.BlockSpec((1, 1, rows, width), lambda f, core_ref: (core_ref[0], f, 0, 0))
+    away_all = pl.BlockSpec((1, frames, rows, width), lambda f, core_ref: (core_ref[0], 0, 0, 0))
     return pl.pallas_call(
         kernel,
         grid_spec=pltpu.PrefetchScalarGridSpec(
-            num_scalar_prefetch=0,
+            num_scalar_prefetch=1,
             grid=(frames,),
-            in_specs=[near] * 3 + [away, near_all, away_all] + [ANYWHERE] * (1 + len(after)),
+            in_specs=[near] * 3 + [away] * 3 + [near_all, away_all] + [ANYWHERE] * (1 + len(after)),
             out_specs=[near] * 3,
             scratch_shapes=[
                 pltpu.VMEM((pieces, share, width), BF16),
@@ -344,7 +344,7 @@
         compiler_params=BIG,
         cost_estimate=cost_of(20),
         name="space_attention",
-    )(*settled([*own, far, own_tokens, far, weights_of, *after]))
+    )(other_core, *settled([*own, *far[:3], own_tokens, far[3], weights_of, *after]))
 
 
 def per_device(sizes, grad_out, time_q, time_k, time_v, space_q, space_k, space_v, time_wo, space_wo):
@@ -354,6 +354,7 @@
     group, me = lax.axis_index("groups"), lax.axis_index("tm")
     share = time_wo.shape[0] // groups
     spots = jnp.concatenate([me ^ jnp.arange(tm, dtype=jnp.int32), group.reshape(1)]).astype(jnp.int32)
+    other_core = (1 - lax.axis_index("space")).reshape(1).astype(jnp.int32)
     order = []
     for low in range(tm // 2):
         order += [tm // 2 - 1 - low, tm - 1 - low]
@@ -405,15 +406,7 @@
     second_sent = payloads(1, (), (first_sent[0],))
     late = exchange(second_sent)
 
-    both_cores = moved_one(
-        [space_q, space_k, space_v, grad_out],
-        (4, frames, rows, width),
-        lambda at, refs, out: [(ref, out.at[i]) for i, ref in enumerate(refs)],
-        "space_payload",
-        (first_sent[0],),
-        pltpu.VMEM,
-    )
-    far = lax.ppermute(both_cores, "space", [(0, 1), (1, 0)])
+    far = [lax.all_gather(tensor, "space", axis=0) for tensor in (space_q, space_k, space_v, grad_out)]
 
     def gathered(column):
         whole = lax.all_gather(column, ("space", "groups"), axis=0, tiled=True)
@@ -427,7 +420,7 @@
                 (ref.at[pl.ds(frames, blocks)], out.at[at[k]]) for k, ref in enumerate(refs)
             ],
             "time_column",
-            (first_sent[0], both_cores),
+            (first_sent[0],),
         )
     )
     space_weights = gathered(
@@ -447,7 +440,7 @@
         )
     )
 
-    *done, late_grad = time_chunk(frames, early, tokens, time_weights, None, "time_first", (far,))
+    *done, late_grad = time_chunk(frames, early, tokens, time_weights, None, "time_first")
     back = exchange(done)
     done = time_chunk(frames, late, (), None, late_grad, "time_second")
     back2 = exchange(done)
@@ -466,6 +459,7 @@
     shapes = [(frames, tm, patches, width)] * 3
     outs = moved(spots, back, shapes, place(0), "place_first", (), (), pltpu.HBM)
     space_out = space_attention(
+        other_core,
         (space_q, space_k, space_v),
         far,
         grad_out,
@@ -499,14 +493,15 @@
     else:
         whole = lax.all_gather(both_wo, ("tm", "space"), axis=0, tiled=True)
 
-    swap = [(0, 1), (1, 0)]
-    far = lax.ppermute(jnp.stack([space_q, space_k, space_v, grad_out]), "space", swap)
+    far = [lax.all_gather(tensor, "space", axis=0) for tensor in (space_q, space_k, space_v, grad_out)]
     tokens = grad_out.reshape(frames * rows, width)
     time_grad = jnp.einsum("td,cd->tc", tokens, whole[:, :width], preferred_element_type=F32)
     time_grad = exchanged(to_patches(time_grad.astype(BF16).reshape(frames, rows, width)))
     pieces = whole[:, width:].reshape(tm, space, -1, 1, width)
     pieces = jnp.moveaxis(pieces.reshape(tm, space, 1, -1, width), 0, 2)
-    space_out = space_attention((space_q, space_k, space_v), far, grad_out, pieces)
+    space_out = space_attention(
+        (1 - lax.axis_index("space")).reshape(1).astype(jnp.int32), (space_q, space_k, space_v), far, grad_out, pieces
+    )
 
     back = exchanged(time_attention(time_qkv, time_grad))
     time_out = [jnp.moveaxis(back[:, index], 0, 1).reshape(frames, rows, width) for index in range(3)]

time: 231 us -> 227 us (0.983)
  Pallas kernels: 92.1 us -> 96.9 us
  waiting for transfers between devices: 33.6 us -> 30.3 us
  local copies, waits for them, and re-layouts: 8.55 us -> 5.61 us
  starting transfers between devices: 82 us -> 79.6 us
    ppermute x35, waiting for transfers between devices: 33.6 us -> 27.8 us  [to_partner(): lax.ppermute(tensor, 'tm', [(i, i ^ k) for i in range(tm)])]
    pallas_call x8 -> x7, Pallas kernels: 35.6 us -> 40.3 us  [moved(): pl.pallas_call(kernel, in_specs=[SCALARS] + [ANYWHERE] * (count + len(aft...]
    unnamed x26 -> x28, local copies, waits for them, and re-layouts: 8.55 us -> 5.61 us
    ppermute x35, starting transfers between devices: 81.8 us -> 79.4 us  [to_partner(): lax.ppermute(tensor, 'tm', [(i, i ^ k) for i in range(tm)])]
    unnamed x2 -> x6, waiting for transfers between devices: 0.03 us -> 2.47 us
  transfers between devices with their start and end apart: 38 -> 41, of which waited for: 5 -> 7; matrix products, arithmetic and copies ran while one was open for 0% -> 0% of each run, Pallas kernels for 38% -> 41%
where the time goes in v7:
time: 227 us
  Pallas kernels  96.9 us (43%)
  starting transfers between devices  79.6 us (35%)
  waiting for transfers between devices  30.3 us (13%)
  between operations  14.3 us (6%)
  local copies, waits for them, and re-layouts  5.61 us (2%)
    ppermute x35, starting transfers between devices, to_partner(): lax.ppermute(tensor, 'tm', [(i, i ^ k) for i in range(tm)])  79.4 us
    pallas_call x7, Pallas kernels, moved(): pl.pallas_call(kernel, in_specs=[SCALARS] + [ANYWHERE] * (count + len(aft...  40.3 us
    pallas_call x2, Pallas kernels, time_chunk(): pl.pallas_call(kernel, in_specs=[ANYWHERE] * (len(blocks) + 1 + len(after...  32.5 us
    ppermute x35, waiting for transfers between devices, to_partner(): lax.ppermute(tensor, 'tm', [(i, i ^ k) for i in range(tm)])  27.8 us
    pallas_call x1, Pallas kernels, space_attention(): pl.pallas_call(kernel, grid_spec=pltpu.PrefetchScalarGridSpec(num_scalar_...  24.1 us
    unnamed x28, local copies, waits for them, and re-layouts  5.61 us
  transfers between devices with their start and end apart: 41, of which 7 were waited for; matrix products, arithmetic and copies ran while one was open for 0% of the time, Pallas kernels for 41%

profile of v7, /device:TPU:0, one launch (start us, length us, event | category | flops | bytes accessed | tf_op | source)
XLA Modules:
  0.0 226.9 jit_solution(13336960791085990000)
XLA Ops:
  7.2 0.0 all-gather.11.cloned.1.call-start
  7.2 0.1 pad_add_fusion.spots_ref
  7.3 2.1 token_payloads.1
  9.4 3.0 %collective-permute-start.14 = (bf16[11,8,1024]{2,1,0:T(8,128)(2,1)S(1)}, bf16[11,8,1024]{2,1,0:T(8,128)(2,1)S(1)}, u32[]{:S(2)}, u32[]{:S(2)}) collective-permute-start(bf16[11,8,1024]{2,1,0:T(8,128)(2,1)S(1)} %get-tuple-element.73), channel_id=1, source_target_pairs={{0,2},{2,0},{4,6},{6,4},{8,10},{10,8},{12,14},{14,12},{1,3},{3,1},... | collective-permute-start | bytes 540680 | tf_op jit(solution)/shard_map/ppermute | solution.py:363
  12.4 1.6 collective-permute-start.15
  13.9 3.0 %collective-permute-start.17 = (bf16[11,8,1024]{2,1,0:T(8,128)(2,1)S(1)}, bf16[11,8,1024]{2,1,0:T(8,128)(2,1)S(1)}, u32[]{:S(2)}, u32[]{:S(2)}) collective-permute-start(bf16[11,8,1024]{2,1,0:T(8,128)(2,1)S(1)} %get-tuple-element.76), channel_id=1, source_target_pairs={{0,8},{2,10},{4,12},{6,14},{8,0},{10,2},{12,4},{14,6},{1,9},{3,11}... | collective-permute-start | bytes 540680 | tf_op jit(solution)/shard_map/ppermute | solution.py:363
  16.9 1.3 collective-permute-start.18
  18.2 3.6 %collective-permute-start.19 = (bf16[11,8,1024]{2,1,0:T(8,128)(2,1)S(1)}, bf16[11,8,1024]{2,1,0:T(8,128)(2,1)S(1)}, u32[]{:S(2)}, u32[]{:S(2)}) collective-permute-start(bf16[11,8,1024]{2,1,0:T(8,128)(2,1)S(1)} %get-tuple-element.78), channel_id=1, source_target_pairs={{0,12},{2,14},{4,8},{6,10},{8,4},{10,6},{12,0},{14,2},{1,13},{3,15... | collective-permute-start | bytes 540680 | tf_op jit(solution)/shard_map/ppermute | solution.py:363
  21.8 4.8 %collective-permute-done.15.refs_2_.refs_10_ = bf16[11,8,1024]{2,1,0:T(8,128)(2,1)S(1)} collective-permute-done((bf16[11,8,1024]{2,1,0:T(8,128)(2,1)S(1)}, bf16[11,8,1024]{2,1,0:T(8,128)(2,1)S(1)}, u32[]{:S(2)}, u32[]{:S(2)}) %collective-permute-start.15) | collective-permute-done | bytes 180256 | tf_op jit(solution)/shard_map/ppermute | solution.py:363
  26.6 1.0 collective-permute-start.20
  27.6 30.4 %payloads.2 = (bf16[29,8,512]{2,1,0:T(8,128)(2,1)S(1)}, bf16[29,8,512]{2,1,0:T(8,128)(2,1)S(1)}, bf16[29,8,512]{2,1,0:T(8,128)(2,1)S(1)}, bf16[29,8,512]{2,1,0:T...) custom-call(s32[9]{0:T(128)S(1)} %pad_add_fusion.spots_ref, ...), custom_call_target="tpu_custom_call" | custom-call | tf_op jit(solution)/shard_map/payloads/pallas_call | solution.py:174
  58.0 0.7 copy-done.6
  58.8 1.3 time_column.1
  60.1 0.0 all-gather.15.cloned.1.call-start
  60.2 0.7 all-gather.15.cloned.1.call-update
  60.9 0.0 all-gather.17.cloned.1.call-start
  60.9 0.7 all-gather.17.cloned.1.call-update
  61.6 0.0 all-gather.19.cloned.1.call-start
  61.6 0.5 all-gather.19.cloned.1.call-update
  62.2 0.0 all-gather.21.cloned.1.call-start
  62.2 0.5 all-gather.21.cloned.1.call-update
  62.8 0.0 all-gather.13.cloned.1.call-start
  62.8 2.6 %collective-permute-start.7 = (bf16[29,8,512]{2,1,0:T(8,128)(2,1)S(1)}, bf16[29,8,512]{2,1,0:T(8,128)(2,1)S(1)}, u32[]{:S(2)}, u32[]{:S(2)}) collective-permute-start(bf16[29,8,512]{2,1,0:T(8,128)(2,1)S(1)} %get-tuple-element.66), channel_id=1, source_target_pairs={{0,2},{2,0},{4,6},{6,4},{8,10},{10,8},{12,14},{14,12},{1,3},{3,1},... | collective-permute-start | bytes 712712 | tf_op jit(solution)/shard_map/ppermute | solution.py:363
  65.4 1.5 collective-permute-start.9
  67.0 0.8 collective-permute-start.10
  67.7 3.5 %collective-permute-start.11 = (bf16[29,8,512]{2,1,0:T(8,128)(2,1)}, bf16[29,8,512]{2,1,0:T(8,128)(2,1)S(1)}, u32[]{:S(2)}, u32[]{:S(2)}) collective-permute-start(bf16[29,8,512]{2,1,0:T(8,128)(2,1)} %get-tuple-element.70), channel_id=1, source_target_pairs={{0,10},{2,8},{4,14},{6,12},{8,2},{10,0},{12,6},{14,4},{1,11},{3,9}... | collective-permute-start | bytes 712712 | tf_op jit(solution)/shard_map/ppermute | solution.py:363
  71.3 2.3 %collective-permute-done.7.refs_1_ = bf16[29,8,512]{2,1,0:T(8,128)(2,1)S(1)} collective-permute-done((bf16[29,8,512]{2,1,0:T(8,128)(2,1)S(1)}, bf16[29,8,512]{2,1,0:T(8,128)(2,1)S(1)}, u32[]{:S(2)}, u32[]{:S(2)}) %collective-permute-start.7) | collective-permute-done | bytes 237600 | tf_op jit(solution)/shard_map/ppermute | solution.py:363
  73.5 0.9 collective-permute-done.8.refs_2_
  74.4 4.0 %collective-permute-start.13 = (bf16[29,8,512]{2,1,0:T(8,128)(2,1)}, bf16[29,8,512]{2,1,0:T(8,128)(2,1)S(1)}, u32[]{:S(2)}, u32[]{:S(2)}) collective-permute-start(bf16[29,8,512]{2,1,0:T(8,128)(2,1)} %copy-done.6), channel_id=1, source_target_pairs={{0,14},{2,12},{4,10},{6,8},{8,6},{10,4},{12,2},{14,0},{1,15},{3,13... | collective-permute-start | bytes 712712 | tf_op jit(solution)/shard_map/ppermute | solution.py:363
  78.4 1.9 payloads.3
  80.3 0.7 copy-done.10
  81.0 0.7 copy-done.11
  81.7 0.7 copy-done.12
  82.3 0.7 copy-done.13
  83.0 13.0 %collective-permute-done.10.refs_4_ = bf16[29,8,512]{2,1,0:T(8,128)(2,1)S(1)} collective-permute-done((bf16[29,8,512]{2,1,0:T(8,128)(2,1)}, bf16[29,8,512]{2,1,0:T(8,128)(2,1)S(1)}, u32[]{:S(2)}, u32[]{:S(2)}) %collective-permute-start.10) | collective-permute-done | bytes 237600 | tf_op jit(solution)/shard_map/ppermute | solution.py:363
  96.0 5.0 %collective-permute-done.11.refs_5_ = bf16[29,8,512]{2,1,0:T(8,128)(2,1)S(1)} collective-permute-done((bf16[29,8,512]{2,1,0:T(8,128)(2,1)}, bf16[29,8,512]{2,1,0:T(8,128)(2,1)S(1)}, u32[]{:S(2)}, u32[]{:S(2)}) %collective-permute-start.11) | collective-permute-done | bytes 237600 | tf_op jit(solution)/shard_map/ppermute | solution.py:363
  101.0 1.3 space_column.1
  102.4 1.3 collective-permute-start
  103.6 5.6 %collective-permute-start.1 = (bf16[21,8,512]{2,1,0:T(8,128)(2,1)}, bf16[21,8,512]{2,1,0:T(8,128)(2,1)S(1)}, u32[]{:S(2)}, u32[]{:S(2)}) collective-permute-start(bf16[21,8,512]{2,1,0:T(8,128)(2,1)} %copy-done.12), channel_id=1, source_target_pairs={{0,4},{2,6},{4,0},{6,2},{8,12},{10,14},{12,8},{14,10},{1,5},{3,7},... | collective-permute-start | bytes 516104 | tf_op jit(solution)/shard_map/ppermute | solution.py:363
  109.3 0.3 collective-permute-start.2
  109.5 4.3 %collective-permute-start.3 = (bf16[21,8,512]{2,1,0:T(8,128)(2,1)}, bf16[21,8,512]{2,1,0:T(8,128)(2,1)}, u32[]{:S(2)}, u32[]{:S(2)}) collective-permute-start(bf16[21,8,512]{2,1,0:T(8,128)(2,1)} %copy-done.10), channel_id=1, source_target_pairs={{0,8},{2,10},{4,12},{6,14},{8,0},{10,2},{12,4},{14,6},{1,9},{3,11}... | collective-permute-start | bytes 516104 | tf_op jit(solution)/shard_map/ppermute | solution.py:363
  113.9 0.7 copy-done.2
  114.6 2.4 %collective-permute-start.5 = (bf16[21,8,512]{2,1,0:T(8,128)(2,1)}, bf16[21,8,512]{2,1,0:T(8,128)(2,1)}, u32[]{:S(2)}, u32[]{:S(2)}) collective-permute-start(bf16[21,8,512]{2,1,0:T(8,128)(2,1)} %copy-done.8), channel_id=1, source_target_pairs={{0,12},{2,14},{4,8},{6,10},{8,4},{10,6},{12,0},{14,2},{1,13},{3,15... | collective-permute-start | bytes 516104 | tf_op jit(solution)/shard_map/ppermute | solution.py:363
  116.9 0.7 copy-done.4
  117.6 4.3 %collective-permute-start.6 = (bf16[21,8,512]{2,1,0:T(8,128)(2,1)}, bf16[21,8,512]{2,1,0:T(8,128)(2,1)}, u32[]{:S(2)}, u32[]{:S(2)}) collective-permute-start(bf16[21,8,512]{2,1,0:T(8,128)(2,1)} %copy-done.7), channel_id=1, source_target_pairs={{0,14},{2,12},{4,10},{6,8},{8,6},{10,4},{12,2},{14,0},{1,15},{3,13... | collective-permute-start | bytes 516104 | tf_op jit(solution)/shard_map/ppermute | solution.py:363
  121.9 20.6 %time_first.1 = (bf16[21,8,512]{2,1,0:T(8,128)(2,1)S(1)}, bf16[21,8,512]{2,1,0:T(8,128)(2,1)S(1)}, bf16[21,8,512]{2,1,0:T(8,128)(2,1)S(1)}, bf16[21,8,512]{2,1,0...) custom-call(bf16[29,8,512]{2,1,0:T(8,128)(2,1)S(1)} %get-tuple-eleme, ...), custom_call_target="tpu_custom_call" | custom-call | bytes 59040000 | tf_op jit(solution)/shard_map/time_first/pallas_call | solution.py:283
  142.6 1.0 collective-permute-start.28
  143.6 2.6 %collective-permute-start.30 = (bf16[21,8,512]{2,1,0:T(8,128)(2,1)S(1)}, bf16[21,8,512]{2,1,0:T(8,128)(2,1)S(1)}, u32[]{:S(2)}, u32[]{:S(2)}) collective-permute-start(bf16[21,8,512]{2,1,0:T(8,128)(2,1)S(1)} %get-tuple-element.92), channel_id=1, source_target_pairs={{0,6},{2,4},{4,2},{6,0},{8,14},{10,12},{12,10},{14,8},{1,7},{3,5},... | collective-permute-start | bytes 516104 | tf_op jit(solution)/shard_map/ppermute | solution.py:363
  146.1 3.3 %collective-permute-start.32 = (bf16[21,8,512]{2,1,0:T(8,128)(2,1)S(1)}, bf16[21,8,512]{2,1,0:T(8,128)(2,1)S(1)}, u32[]{:S(2)}, u32[]{:S(2)}) collective-permute-start(bf16[21,8,512]{2,1,0:T(8,128)(2,1)S(1)} %get-tuple-element.94), channel_id=1, source_target_pairs={{0,10},{2,8},{4,14},{6,12},{8,2},{10,0},{12,6},{14,4},{1,11},{3,9}... | collective-permute-start | bytes 516104 | tf_op jit(solution)/shard_map/ppermute | solution.py:363
  149.4 11.9 %time_second.1 = (bf16[21,8,512]{2,1,0:T(8,128)(2,1)S(1)}, bf16[21,8,512]{2,1,0:T(8,128)(2,1)S(1)}, bf16[21,8,512]{2,1,0:T(8,128)(2,1)S(1)}, bf16[21,8,512]{2,1,...) custom-call(bf16[21,8,512]{2,1,0:T(8,128)(2,1)S(1)} %get-tuple-eleme, ...), custom_call_target="tpu_custom_call" | custom-call | bytes 36900000 | tf_op jit(solution)/shard_map/time_second/pallas_call | solution.py:283
  161.4 0.1 collective-permute-start.33
  161.5 4.3 %collective-permute-start.34 = (bf16[21,8,512]{2,1,0:T(8,128)(2,1)S(1)}, bf16[21,8,512]{2,1,0:T(8,128)(2,1)S(1)}, u32[]{:S(2)}, u32[]{:S(2)}) collective-permute-start(bf16[21,8,512]{2,1,0:T(8,128)(2,1)S(1)} %get-tuple-element.96), channel_id=1, source_target_pairs={{0,14},{2,12},{4,10},{6,8},{8,6},{10,4},{12,2},{14,0},{1,15},{3,13... | collective-permute-start | bytes 516104 | tf_op jit(solution)/shard_map/ppermute | solution.py:363
  165.8 0.9 collective-permute-start.21
  166.7 2.6 %collective-permute-start.23 = (bf16[21,8,512]{2,1,0:T(8,128)(2,1)}, bf16[21,8,512]{2,1,0:T(8,128)(2,1)S(1)}, u32[]{:S(2)}, u32[]{:S(2)}) collective-permute-start(bf16[21,8,512]{2,1,0:T(8,128)(2,1)} %get-tuple-element.84), channel_id=1, source_target_pairs={{0,6},{2,4},{4,2},{6,0},{8,14},{10,12},{12,10},{14,8},{1,7},{3,5},... | collective-permute-start | bytes 516104 | tf_op jit(solution)/shard_map/ppermute | solution.py:363
  169.3 1.3 collective-permute-done.33.refs_6_
  170.7 3.7 %collective-permute-start.24 = (bf16[21,8,512]{2,1,0:T(8,128)(2,1)S(1)}, bf16[21,8,512]{2,1,0:T(8,128)(2,1)S(1)}, u32[]{:S(2)}, u32[]{:S(2)}) collective-permute-start(bf16[21,8,512]{2,1,0:T(8,128)(2,1)S(1)} %get-tuple-element.85), channel_id=1, source_target_pairs={{0,8},{2,10},{4,12},{6,14},{8,0},{10,2},{12,4},{14,6},{1,9},{3,11}... | collective-permute-start | bytes 516104 | tf_op jit(solution)/shard_map/ppermute | solution.py:363
  174.3 0.5 collective-permute-done.34.refs_7_
  174.8 11.8 %collective-permute-start.25 = (bf16[21,8,512]{2,1,0:T(8,128)(2,1)S(1)}, bf16[21,8,512]{2,1,0:T(8,128)(2,1)S(1)}, u32[]{:S(2)}, u32[]{:S(2)}) collective-permute-start(bf16[21,8,512]{2,1,0:T(8,128)(2,1)S(1)} %get-tuple-element.86), channel_id=1, source_target_pairs={{0,10},{2,8},{4,14},{6,12},{8,2},{10,0},{12,6},{14,4},{1,11},{3,9}... | collective-permute-start | bytes 516104 | tf_op jit(solution)/shard_map/ppermute | solution.py:363
  186.7 2.6 %collective-permute-start.26 = (bf16[21,8,512]{2,1,0:T(8,128)(2,1)S(1)}, bf16[21,8,512]{2,1,0:T(8,128)(2,1)S(1)}, u32[]{:S(2)}, u32[]{:S(2)}) collective-permute-start(bf16[21,8,512]{2,1,0:T(8,128)(2,1)S(1)} %get-tuple-element.87), channel_id=1, source_target_pairs={{0,12},{2,14},{4,8},{6,10},{8,4},{10,6},{12,0},{14,2},{1,13},{3,15... | collective-permute-start | bytes 516104 | tf_op jit(solution)/shard_map/ppermute | solution.py:363
  189.3 2.5 %collective-permute-start.27 = (bf16[21,8,512]{2,1,0:T(8,128)(2,1)S(1)}, bf16[21,8,512]{2,1,0:T(8,128)(2,1)S(1)}, u32[]{:S(2)}, u32[]{:S(2)}) collective-permute-start(bf16[21,8,512]{2,1,0:T(8,128)(2,1)S(1)} %get-tuple-element.88), channel_id=1, source_target_pairs={{0,14},{2,12},{4,10},{6,8},{8,6},{10,4},{12,2},{14,0},{1,15},{3,13... | collective-permute-start | bytes 516104 | tf_op jit(solution)/shard_map/ppermute | solution.py:363
  191.7 0.9 copy-done.1
  192.6 1.6 place_first.1
  194.3 24.1 %space_attention.1 = (bf16[7,64,1024]{2,1,0:T(8,128)(2,1)}, bf16[7,64,1024]{2,1,0:T(8,128)(2,1)}, bf16[7,64,1024]{2,1,0:T(8,128)(2,1)}) custom-call(s32[1]{0:T(128)} %bitcast.8.core_ref, bf16[7,64,1024]{2,1,0:T(8,128)(2,1)} %refs_0_.1, bf16[7,64,1024]{2,1,0:T(8,128)(2,1)} %refs_1_.1, bf16[7,64,1024]{2,1,0:T(8,128)(2,1)} %refs_2_.1, ...), custom_call_target="tpu_custom_call" | custom-call | bytes 73800000 | tf_op jit(solution)/shard_map/space_attention/pallas_call | solution.py:330
  218.5 1.6 place_second.1
  (64 shorter events, 0.2 us)
Async XLA Ops:
  7.2 114.7 %all-gather.11.cloned.1.call-start = ((), (), s32[]{:S(2)}) async-start(), calls=%async_computation | async-start | bytes 2621440 | tf_op jit(solution)/shard_map/all_gather | solution.py:412
  9.4 8.8 %collective-permute-start.14 = (bf16[11,8,1024]{2,1,0:T(8,128)(2,1)S(1)}, bf16[11,8,1024]{2,1,0:T(8,128)(2,1)S(1)}, u32[]{:S(2)}, u32[]{:S(2)}) collective-permute-start(bf16[11,8,1024]{2,1,0:T(8,128)(2,1)S(1)} %get-tuple-element.73), channel_id=1, source_target_pairs={{0,2},{2,0},{4,6},{6,4},{8,10},{10,8},{12,14},{14,12},{1,3},{3,1},... | collective-permute-start | bytes 540680 | tf_op jit(solution)/shard_map/ppermute | solution.py:363
  12.4 14.2 %collective-permute-start.15 = (bf16[11,8,1024]{2,1,0:T(8,128)(2,1)S(1)}, bf16[11,8,1024]{2,1,0:T(8,128)(2,1)S(1)}, u32[]{:S(2)}, u32[]{:S(2)}) collective-permute-start(bf16[11,8,1024]{2,1,0:T(8,128)(2,1)S(1)} %get-tuple-element.74), channel_id=1, source_target_pairs={{0,4},{2,6},{4,0},{6,2},{8,12},{10,14},{12,8},{14,10},{1,5},{3,7},... | collective-permute-start | bytes 540680 | tf_op jit(solution)/shard_map/ppermute | solution.py:363
  13.9 44.8 %collective-permute-start.16 = (bf16[11,8,1024]{2,1,0:T(8,128)(2,1)S(1)}, bf16[11,8,1024]{2,1,0:T(8,128)(2,1)S(1)}, u32[]{:S(2)}, u32[]{:S(2)}) collective-permute-start(bf16[11,8,1024]{2,1,0:T(8,128)(2,1)S(1)} %get-tuple-element.75), channel_id=1, source_target_pairs={{0,6},{2,4},{4,2},{6,0},{8,14},{10,12},{12,10},{14,8},{1,7},{3,5},... | collective-permute-start | bytes 540680 | tf_op jit(solution)/shard_map/ppermute | solution.py:363
  13.9 44.8 %collective-permute-start.17 = (bf16[11,8,1024]{2,1,0:T(8,128)(2,1)S(1)}, bf16[11,8,1024]{2,1,0:T(8,128)(2,1)S(1)}, u32[]{:S(2)}, u32[]{:S(2)}) collective-permute-start(bf16[11,8,1024]{2,1,0:T(8,128)(2,1)S(1)} %get-tuple-element.76), channel_id=1, source_target_pairs={{0,8},{2,10},{4,12},{6,14},{8,0},{10,2},{12,4},{14,6},{1,9},{3,11}... | collective-permute-start | bytes 540680 | tf_op jit(solution)/shard_map/ppermute | solution.py:363
  16.9 41.8 %collective-permute-start.18 = (bf16[11,8,1024]{2,1,0:T(8,128)(2,1)S(1)}, bf16[11,8,1024]{2,1,0:T(8,128)(2,1)S(1)}, u32[]{:S(2)}, u32[]{:S(2)}) collective-permute-start(bf16[11,8,1024]{2,1,0:T(8,128)(2,1)S(1)} %get-tuple-element.77), channel_id=1, source_target_pairs={{0,10},{2,8},{4,14},{6,12},{8,2},{10,0},{12,6},{14,4},{1,11},{3,9}... | collective-permute-start | bytes 540680 | tf_op jit(solution)/shard_map/ppermute | solution.py:363
  18.2 40.5 %collective-permute-start.19 = (bf16[11,8,1024]{2,1,0:T(8,128)(2,1)S(1)}, bf16[11,8,1024]{2,1,0:T(8,128)(2,1)S(1)}, u32[]{:S(2)}, u32[]{:S(2)}) collective-permute-start(bf16[11,8,1024]{2,1,0:T(8,128)(2,1)S(1)} %get-tuple-element.78), channel_id=1, source_target_pairs={{0,12},{2,14},{4,8},{6,10},{8,4},{10,6},{12,0},{14,2},{1,13},{3,15... | collective-permute-start | bytes 540680 | tf_op jit(solution)/shard_map/ppermute | solution.py:363
  26.6 32.2 %collective-permute-start.20 = (bf16[11,8,1024]{2,1,0:T(8,128)(2,1)S(1)}, bf16[11,8,1024]{2,1,0:T(8,128)(2,1)S(1)}, u32[]{:S(2)}, u32[]{:S(2)}) collective-permute-start(bf16[11,8,1024]{2,1,0:T(8,128)(2,1)S(1)} %get-tuple-element.79), channel_id=1, source_target_pairs={{0,14},{2,12},{4,10},{6,8},{8,6},{10,4},{12,2},{14,0},{1,15},{3,13... | collective-permute-start | bytes 540680 | tf_op jit(solution)/shard_map/ppermute | solution.py:363
  58.0 0.7 copy-start.6
  60.1 134.1 %all-gather.15.cloned.1.call-start = ((), (), s32[]{:S(2)}) async-start(), calls=%async_computation.2 | async-start | bytes 2752512 | tf_op jit(solution)/shard_map/all_gather | solution.py:409
  60.9 133.4 %all-gather.17.cloned.1.call-start = ((), (), s32[]{:S(2)}) async-start(), calls=%async_computation.3 | async-start | bytes 2752512 | tf_op jit(solution)/shard_map/all_gather | solution.py:409
  61.6 132.6 %all-gather.19.cloned.1.call-start = ((), (), s32[]{:S(2)}) async-start(), calls=%async_computation.4 | async-start | bytes 2752512 | tf_op jit(solution)/shard_map/all_gather | solution.py:409
  62.2 132.1 %all-gather.21.cloned.1.call-start = ((), (), s32[]{:S(2)}) async-start(), calls=%async_computation.5 | async-start | bytes 2752512 | tf_op jit(solution)/shard_map/all_gather | solution.py:409
  62.8 131.5 %all-gather.13.cloned.1.call-start = ((), (), s32[]{:S(2)}) async-start(), calls=%async_computation.1 | async-start | bytes 2621440 | tf_op jit(solution)/shard_map/all_gather | solution.py:412
  62.8 10.7 %collective-permute-start.7 = (bf16[29,8,512]{2,1,0:T(8,128)(2,1)S(1)}, bf16[29,8,512]{2,1,0:T(8,128)(2,1)S(1)}, u32[]{:S(2)}, u32[]{:S(2)}) collective-permute-start(bf16[29,8,512]{2,1,0:T(8,128)(2,1)S(1)} %get-tuple-element.66), channel_id=1, source_target_pairs={{0,2},{2,0},{4,6},{6,4},{8,10},{10,8},{12,14},{14,12},{1,3},{3,1},... | collective-permute-start | bytes 712712 | tf_op jit(solution)/shard_map/ppermute | solution.py:363
  65.4 9.0 %collective-permute-start.8 = (bf16[29,8,512]{2,1,0:T(8,128)(2,1)S(1)}, bf16[29,8,512]{2,1,0:T(8,128)(2,1)S(1)}, u32[]{:S(2)}, u32[]{:S(2)}) collective-permute-start(bf16[29,8,512]{2,1,0:T(8,128)(2,1)S(1)} %get-tuple-element.67), channel_id=1, source_target_pairs={{0,4},{2,6},{4,0},{6,2},{8,12},{10,14},{12,8},{14,10},{1,5},{3,7},... | collective-permute-start | bytes 712712 | tf_op jit(solution)/shard_map/ppermute | solution.py:363
  65.4 17.6 %collective-permute-start.9 = (bf16[29,8,512]{2,1,0:T(8,128)(2,1)}, bf16[29,8,512]{2,1,0:T(8,128)(2,1)S(1)}, u32[]{:S(2)}, u32[]{:S(2)}) collective-permute-start(bf16[29,8,512]{2,1,0:T(8,128)(2,1)} %get-tuple-element.68), channel_id=1, source_target_pairs={{0,6},{2,4},{4,2},{6,0},{8,14},{10,12},{12,10},{14,8},{1,7},{3,5},... | collective-permute-start | bytes 712712 | tf_op jit(solution)/shard_map/ppermute | solution.py:363
  67.0 29.0 %collective-permute-start.10 = (bf16[29,8,512]{2,1,0:T(8,128)(2,1)}, bf16[29,8,512]{2,1,0:T(8,128)(2,1)S(1)}, u32[]{:S(2)}, u32[]{:S(2)}) collective-permute-start(bf16[29,8,512]{2,1,0:T(8,128)(2,1)} %get-tuple-element.69), channel_id=1, source_target_pairs={{0,8},{2,10},{4,12},{6,14},{8,0},{10,2},{12,4},{14,6},{1,9},{3,11}... | collective-permute-start | bytes 712712 | tf_op jit(solution)/shard_map/ppermute | solution.py:363
  67.7 33.3 %collective-permute-start.11 = (bf16[29,8,512]{2,1,0:T(8,128)(2,1)}, bf16[29,8,512]{2,1,0:T(8,128)(2,1)S(1)}, u32[]{:S(2)}, u32[]{:S(2)}) collective-permute-start(bf16[29,8,512]{2,1,0:T(8,128)(2,1)} %get-tuple-element.70), channel_id=1, source_target_pairs={{0,10},{2,8},{4,14},{6,12},{8,2},{10,0},{12,6},{14,4},{1,11},{3,9}... | collective-permute-start | bytes 712712 | tf_op jit(solution)/shard_map/ppermute | solution.py:363
  73.5 27.5 %collective-permute-start.12 = (bf16[29,8,512]{2,1,0:T(8,128)(2,1)}, bf16[29,8,512]{2,1,0:T(8,128)(2,1)S(1)}, u32[]{:S(2)}, u32[]{:S(2)}) collective-permute-start(bf16[29,8,512]{2,1,0:T(8,128)(2,1)} %get-tuple-element.71), channel_id=1, source_target_pairs={{0,12},{2,14},{4,8},{6,10},{8,4},{10,6},{12,0},{14,2},{1,13},{3,15... | collective-permute-start | bytes 712712 | tf_op jit(solution)/shard_map/ppermute | solution.py:363
  74.4 26.6 %collective-permute-start.13 = (bf16[29,8,512]{2,1,0:T(8,128)(2,1)}, bf16[29,8,512]{2,1,0:T(8,128)(2,1)S(1)}, u32[]{:S(2)}, u32[]{:S(2)}) collective-permute-start(bf16[29,8,512]{2,1,0:T(8,128)(2,1)} %copy-done.6), channel_id=1, source_target_pairs={{0,14},{2,12},{4,10},{6,8},{8,6},{10,4},{12,2},{14,0},{1,15},{3,13... | collective-permute-start | bytes 712712 | tf_op jit(solution)/shard_map/ppermute | solution.py:363
  80.3 0.7 copy-start.10
  81.0 0.7 copy-start.11
  81.7 0.7 copy-start.12
  82.3 0.7 copy-start.13
  83.0 18.0 %copy-start.7 = (bf16[21,8,512]{2,1,0:T(8,128)(2,1)}, bf16[21,8,512]{2,1,0:T(8,128)(2,1)S(1)}, u32[]{:S(2)}) copy-start(bf16[21,8,512]{2,1,0:T(8,128)(2,1)S(1)} %get-tuple-element.65) | copy-start | bytes 516100
  83.0 18.0 %copy-start.8 = (bf16[21,8,512]{2,1,0:T(8,128)(2,1)}, bf16[21,8,512]{2,1,0:T(8,128)(2,1)S(1)}, u32[]{:S(2)}) copy-start(bf16[21,8,512]{2,1,0:T(8,128)(2,1)S(1)} %get-tuple-element.64) | copy-start | bytes 516100
  83.0 18.0 %copy-start.9 = (bf16[21,8,512]{2,1,0:T(8,128)(2,1)}, bf16[21,8,512]{2,1,0:T(8,128)(2,1)S(1)}, u32[]{:S(2)}) copy-start(bf16[21,8,512]{2,1,0:T(8,128)(2,1)S(1)} %get-tuple-element.63) | copy-start | bytes 516100
  102.4 11.5 %collective-permute-start = (bf16[21,8,512]{2,1,0:T(8,128)(2,1)}, bf16[21,8,512]{2,1,0:T(8,128)(2,1)S(1)}, u32[]{:S(2)}, u32[]{:S(2)}) collective-permute-start(bf16[21,8,512]{2,1,0:T(8,128)(2,1)} %copy-done.13), channel_id=1, source_target_pairs={{0,2},{2,0},{4,6},{6,4},{8,10},{10,8},{12,14},{14,12},{1,3},{3,1},... | collective-permute-start | bytes 516104 | tf_op jit(solution)/shard_map/ppermute | solution.py:363
  103.6 13.3 %collective-permute-start.1 = (bf16[21,8,512]{2,1,0:T(8,128)(2,1)}, bf16[21,8,512]{2,1,0:T(8,128)(2,1)S(1)}, u32[]{:S(2)}, u32[]{:S(2)}) collective-permute-start(bf16[21,8,512]{2,1,0:T(8,128)(2,1)} %copy-done.12), channel_id=1, source_target_pairs={{0,4},{2,6},{4,0},{6,2},{8,12},{10,14},{12,8},{14,10},{1,5},{3,7},... | collective-permute-start | bytes 516104 | tf_op jit(solution)/shard_map/ppermute | solution.py:363
  109.3 33.3 %collective-permute-start.2 = (bf16[21,8,512]{2,1,0:T(8,128)(2,1)}, bf16[21,8,512]{2,1,0:T(8,128)(2,1)}, u32[]{:S(2)}, u32[]{:S(2)}) collective-permute-start(bf16[21,8,512]{2,1,0:T(8,128)(2,1)} %copy-done.11), channel_id=1, source_target_pairs={{0,6},{2,4},{4,2},{6,0},{8,14},{10,12},{12,10},{14,8},{1,7},{3,5},... | collective-permute-start | bytes 516104 | tf_op jit(solution)/shard_map/ppermute | solution.py:363
  109.5 34.0 %collective-permute-start.3 = (bf16[21,8,512]{2,1,0:T(8,128)(2,1)}, bf16[21,8,512]{2,1,0:T(8,128)(2,1)}, u32[]{:S(2)}, u32[]{:S(2)}) collective-permute-start(bf16[21,8,512]{2,1,0:T(8,128)(2,1)} %copy-done.10), channel_id=1, source_target_pairs={{0,8},{2,10},{4,12},{6,14},{8,0},{10,2},{12,4},{14,6},{1,9},{3,11}... | collective-permute-start | bytes 516104 | tf_op jit(solution)/shard_map/ppermute | solution.py:363
  113.9 29.7 %collective-permute-start.4 = (bf16[21,8,512]{2,1,0:T(8,128)(2,1)}, bf16[21,8,512]{2,1,0:T(8,128)(2,1)}, u32[]{:S(2)}, u32[]{:S(2)}) collective-permute-start(bf16[21,8,512]{2,1,0:T(8,128)(2,1)} %copy-done.9), channel_id=1, source_target_pairs={{0,10},{2,8},{4,14},{6,12},{8,2},{10,0},{12,6},{14,4},{1,11},{3,9}... | collective-permute-start | bytes 516104 | tf_op jit(solution)/shard_map/ppermute | solution.py:363
  113.9 0.7 copy-start.2
  114.6 31.6 %collective-permute-start.5 = (bf16[21,8,512]{2,1,0:T(8,128)(2,1)}, bf16[21,8,512]{2,1,0:T(8,128)(2,1)}, u32[]{:S(2)}, u32[]{:S(2)}) collective-permute-start(bf16[21,8,512]{2,1,0:T(8,128)(2,1)} %copy-done.8), channel_id=1, source_target_pairs={{0,12},{2,14},{4,8},{6,10},{8,4},{10,6},{12,0},{14,2},{1,13},{3,15... | collective-permute-start | bytes 516104 | tf_op jit(solution)/shard_map/ppermute | solution.py:363
  116.9 0.7 copy-start.4
  117.6 28.5 %collective-permute-start.6 = (bf16[21,8,512]{2,1,0:T(8,128)(2,1)}, bf16[21,8,512]{2,1,0:T(8,128)(2,1)}, u32[]{:S(2)}, u32[]{:S(2)}) collective-permute-start(bf16[21,8,512]{2,1,0:T(8,128)(2,1)} %copy-done.7), channel_id=1, source_target_pairs={{0,14},{2,12},{4,10},{6,8},{8,6},{10,4},{12,2},{14,0},{1,15},{3,13... | collective-permute-start | bytes 516104 | tf_op jit(solution)/shard_map/ppermute | solution.py:363
  121.9 27.5 %copy-start.3 = (bf16[21,8,512]{2,1,0:T(8,128)(2,1)S(1)}, bf16[21,8,512]{2,1,0:T(8,128)(2,1)}, u32[]{:S(2)}) copy-start(bf16[21,8,512]{2,1,0:T(8,128)(2,1)} %copy-done.2) | copy-start | bytes 516100
  121.9 27.5 %copy-start.5 = (bf16[21,8,512]{2,1,0:T(8,128)(2,1)S(1)}, bf16[21,8,512]{2,1,0:T(8,128)(2,1)}, u32[]{:S(2)}) copy-start(bf16[21,8,512]{2,1,0:T(8,128)(2,1)} %copy-done.4) | copy-start | bytes 516100
  142.5 46.7 %copy-start = (bf16[21,8,512]{2,1,0:T(8,128)(2,1)}, bf16[21,8,512]{2,1,0:T(8,128)(2,1)S(1)}, u32[]{:S(2)}) copy-start(bf16[21,8,512]{2,1,0:T(8,128)(2,1)S(1)} %get-tuple-element.89.refs_0_) | copy-start | bytes 516100
  142.6 18.8 %collective-permute-start.28 = (bf16[21,8,512]{2,1,0:T(8,128)(2,1)S(1)}, bf16[21,8,512]{2,1,0:T(8,128)(2,1)S(1)}, u32[]{:S(2)}, u32[]{:S(2)}) collective-permute-start(bf16[21,8,512]{2,1,0:T(8,128)(2,1)S(1)} %get-tuple-element.90), channel_id=1, source_target_pairs={{0,2},{2,0},{4,6},{6,4},{8,10},{10,8},{12,14},{14,12},{1,3},{3,1},... | collective-permute-start | bytes 516104 | tf_op jit(solution)/shard_map/ppermute | solution.py:363
  143.6 17.9 %collective-permute-start.29 = (bf16[21,8,512]{2,1,0:T(8,128)(2,1)S(1)}, bf16[21,8,512]{2,1,0:T(8,128)(2,1)S(1)}, u32[]{:S(2)}, u32[]{:S(2)}) collective-permute-start(bf16[21,8,512]{2,1,0:T(8,128)(2,1)S(1)} %get-tuple-element.91), channel_id=1, source_target_pairs={{0,4},{2,6},{4,0},{6,2},{8,12},{10,14},{12,8},{14,10},{1,5},{3,7},... | collective-permute-start | bytes 516104 | tf_op jit(solution)/shard_map/ppermute | solution.py:363
  143.6 22.2 %collective-permute-start.30 = (bf16[21,8,512]{2,1,0:T(8,128)(2,1)S(1)}, bf16[21,8,512]{2,1,0:T(8,128)(2,1)S(1)}, u32[]{:S(2)}, u32[]{:S(2)}) collective-permute-start(bf16[21,8,512]{2,1,0:T(8,128)(2,1)S(1)} %get-tuple-element.92), channel_id=1, source_target_pairs={{0,6},{2,4},{4,2},{6,0},{8,14},{10,12},{12,10},{14,8},{1,7},{3,5},... | collective-permute-start | bytes 516104 | tf_op jit(solution)/shard_map/ppermute | solution.py:363
  146.1 20.6 %collective-permute-start.31 = (bf16[21,8,512]{2,1,0:T(8,128)(2,1)S(1)}, bf16[21,8,512]{2,1,0:T(8,128)(2,1)S(1)}, u32[]{:S(2)}, u32[]{:S(2)}) collective-permute-start(bf16[21,8,512]{2,1,0:T(8,128)(2,1)S(1)} %get-tuple-element.93), channel_id=1, source_target_pairs={{0,8},{2,10},{4,12},{6,14},{8,0},{10,2},{12,4},{14,6},{1,9},{3,11}... | collective-permute-start | bytes 516104 | tf_op jit(solution)/shard_map/ppermute | solution.py:363
  146.1 20.6 %collective-permute-start.32 = (bf16[21,8,512]{2,1,0:T(8,128)(2,1)S(1)}, bf16[21,8,512]{2,1,0:T(8,128)(2,1)S(1)}, u32[]{:S(2)}, u32[]{:S(2)}) collective-permute-start(bf16[21,8,512]{2,1,0:T(8,128)(2,1)S(1)} %get-tuple-element.94), channel_id=1, source_target_pairs={{0,10},{2,8},{4,14},{6,12},{8,2},{10,0},{12,6},{14,4},{1,11},{3,9}... | collective-permute-start | bytes 516104 | tf_op jit(solution)/shard_map/ppermute | solution.py:363
  161.4 9.3 %collective-permute-start.33 = (bf16[21,8,512]{2,1,0:T(8,128)(2,1)S(1)}, bf16[21,8,512]{2,1,0:T(8,128)(2,1)S(1)}, u32[]{:S(2)}, u32[]{:S(2)}) collective-permute-start(bf16[21,8,512]{2,1,0:T(8,128)(2,1)S(1)} %get-tuple-element.95), channel_id=1, source_target_pairs={{0,12},{2,14},{4,8},{6,10},{8,4},{10,6},{12,0},{14,2},{1,13},{3,15... | collective-permute-start | bytes 516104 | tf_op jit(solution)/shard_map/ppermute | solution.py:363
  161.5 13.4 %collective-permute-start.34 = (bf16[21,8,512]{2,1,0:T(8,128)(2,1)S(1)}, bf16[21,8,512]{2,1,0:T(8,128)(2,1)S(1)}, u32[]{:S(2)}, u32[]{:S(2)}) collective-permute-start(bf16[21,8,512]{2,1,0:T(8,128)(2,1)S(1)} %get-tuple-element.96), channel_id=1, source_target_pairs={{0,14},{2,12},{4,10},{6,8},{8,6},{10,4},{12,2},{14,0},{1,15},{3,13... | collective-permute-start | bytes 516104 | tf_op jit(solution)/shard_map/ppermute | solution.py:363
  165.8 20.9 %collective-permute-start.21 = (bf16[21,8,512]{2,1,0:T(8,128)(2,1)S(1)}, bf16[21,8,512]{2,1,0:T(8,128)(2,1)S(1)}, u32[]{:S(2)}, u32[]{:S(2)}) collective-permute-start(bf16[21,8,512]{2,1,0:T(8,128)(2,1)S(1)} %get-tuple-element.82), channel_id=1, source_target_pairs={{0,2},{2,0},{4,6},{6,4},{8,10},{10,8},{12,14},{14,12},{1,3},{3,1},... | collective-permute-start | bytes 516104 | tf_op jit(solution)/shard_map/ppermute | solution.py:363
  166.7 22.5 %collective-permute-start.22 = (bf16[21,8,512]{2,1,0:T(8,128)(2,1)S(1)}, bf16[21,8,512]{2,1,0:T(8,128)(2,1)S(1)}, u32[]{:S(2)}, u32[]{:S(2)}) collective-permute-start(bf16[21,8,512]{2,1,0:T(8,128)(2,1)S(1)} %get-tuple-element.83), channel_id=1, source_target_pairs={{0,4},{2,6},{4,0},{6,2},{8,12},{10,14},{12,8},{14,10},{1,5},{3,7},... | collective-permute-start | bytes 516104 | tf_op jit(solution)/shard_map/ppermute | solution.py:363
  166.7 51.7 %collective-permute-start.23 = (bf16[21,8,512]{2,1,0:T(8,128)(2,1)}, bf16[21,8,512]{2,1,0:T(8,128)(2,1)S(1)}, u32[]{:S(2)}, u32[]{:S(2)}) collective-permute-start(bf16[21,8,512]{2,1,0:T(8,128)(2,1)} %get-tuple-element.84), channel_id=1, source_target_pairs={{0,6},{2,4},{4,2},{6,0},{8,14},{10,12},{12,10},{14,8},{1,7},{3,5},... | collective-permute-start | bytes 516104 | tf_op jit(solution)/shard_map/ppermute | solution.py:363
  170.7 47.8 %collective-permute-start.24 = (bf16[21,8,512]{2,1,0:T(8,128)(2,1)S(1)}, bf16[21,8,512]{2,1,0:T(8,128)(2,1)S(1)}, u32[]{:S(2)}, u32[]{:S(2)}) collective-permute-start(bf16[21,8,512]{2,1,0:T(8,128)(2,1)S(1)} %get-tuple-element.85), channel_id=1, source_target_pairs={{0,8},{2,10},{4,12},{6,14},{8,0},{10,2},{12,4},{14,6},{1,9},{3,11}... | collective-permute-start | bytes 516104 | tf_op jit(solution)/shard_map/ppermute | solution.py:363
  174.8 43.6 %collective-permute-start.25 = (bf16[21,8,512]{2,1,0:T(8,128)(2,1)S(1)}, bf16[21,8,512]{2,1,0:T(8,128)(2,1)S(1)}, u32[]{:S(2)}, u32[]{:S(2)}) collective-permute-start(bf16[21,8,512]{2,1,0:T(8,128)(2,1)S(1)} %get-tuple-element.86), channel_id=1, source_target_pairs={{0,10},{2,8},{4,14},{6,12},{8,2},{10,0},{12,6},{14,4},{1,11},{3,9}... | collective-permute-start | bytes 516104 | tf_op jit(solution)/shard_map/ppermute | solution.py:363
  186.7 31.8 %collective-permute-start.26 = (bf16[21,8,512]{2,1,0:T(8,128)(2,1)S(1)}, bf16[21,8,512]{2,1,0:T(8,128)(2,1)S(1)}, u32[]{:S(2)}, u32[]{:S(2)}) collective-permute-start(bf16[21,8,512]{2,1,0:T(8,128)(2,1)S(1)} %get-tuple-element.87), channel_id=1, source_target_pairs={{0,12},{2,14},{4,8},{6,10},{8,4},{10,6},{12,0},{14,2},{1,13},{3,15... | collective-permute-start | bytes 516104 | tf_op jit(solution)/shard_map/ppermute | solution.py:363
  189.3 29.2 %collective-permute-start.27 = (bf16[21,8,512]{2,1,0:T(8,128)(2,1)S(1)}, bf16[21,8,512]{2,1,0:T(8,128)(2,1)S(1)}, u32[]{:S(2)}, u32[]{:S(2)}) collective-permute-start(bf16[21,8,512]{2,1,0:T(8,128)(2,1)S(1)} %get-tuple-element.88), channel_id=1, source_target_pairs={{0,14},{2,12},{4,10},{6,8},{8,6},{10,4},{12,2},{14,0},{1,15},{3,13... | collective-permute-start | bytes 516104 | tf_op jit(solution)/shard_map/ppermute | solution.py:363
  191.7 0.9 copy-start.1
Sparse Core Ops, SparseCore 0:
  60.2 22.8 all-gather.10
  84.7 10.1 all-gather.14
  96.5 11.3 all-gather.16
  109.3 11.3 all-gather.18
  122.1 11.3 all-gather.20
  135.5 23.7 all-gather.12

commit v8 on v7

--- a/solution.py
+++ b/solution.py
@@ -355,9 +355,10 @@
     share = time_wo.shape[0] // groups
     spots = jnp.concatenate([me ^ jnp.arange(tm, dtype=jnp.int32), group.reshape(1)]).astype(jnp.int32)
     other_core = (1 - lax.axis_index("space")).reshape(1).astype(jnp.int32)
-    order = []
-    for low in range(tm // 2):
-        order += [tm // 2 - 1 - low, tm - 1 - low]
+    order = [0]
+    for k in range(1, tm // 2):
+        order += [k, k + tm // 2 - 1]
+    order.append(tm - 1)
 
     def to_partner(tensor, k):
         return lax.ppermute(tensor, "tm", [(i, i ^ k) for i in range(tm)]) if k else tensor
@@ -372,38 +373,42 @@
 
     def token_plan(at, parts, outs):
         pairs = []
-        for k in order:
-            pairs.append((parts[0].at[:, at[k]], outs[k].at[pl.ds(0, frames)]))
-            pairs.append((parts[1].at[at[tm]], outs[k].at[pl.ds(frames, blocks)]))
+        for k, out in zip(order, outs):
+            pairs.append((parts[0].at[:, at[k]], out.at[pl.ds(0, frames)]))
+            pairs.append((parts[1].at[at[tm]], out.at[pl.ds(frames, blocks)]))
         return pairs
 
-    def payloads(chunk, more=(), after=()):
-        def plan(at, parts, outs):
-            columns = pl.ds(chunk * half, half)
-            pairs = []
-            for k in order:
-                for i in range(3):
-                    pairs.append((parts[i].at[:, at[k], :, columns], outs[k].at[pl.ds(i * frames, frames)]))
-                for part in parts[3:]:
-                    for side in range(2):
-                        kept = outs[k].at[pl.ds(3 * frames + side * blocks, blocks)]
-                        pairs.append((part.at[at[tm], :, :, pl.ds(side * half, half)], kept))
-            return pairs
-
-        shape = (3 * frames + 2 * blocks * len(more), patches, half)
-        return moved(spots, [*split[:3], *more], [shape] * tm, plan, "payloads", after)
+    def chunk_plan(chunk, at, parts, outs):
+        columns = pl.ds(chunk * half, half)
+        pairs = []
+        for k, out in zip(order, outs):
+            for i in range(3):
+                pairs.append((parts[i].at[:, at[k], :, columns], out.at[pl.ds(i * frames, frames)]))
+            for part in parts[3:]:
+                for side in range(2):
+                    kept = out.at[pl.ds(3 * frames + side * blocks, blocks)]
+                    pairs.append((part.at[at[tm], :, :, pl.ds(side * half, half)], kept))
+        return pairs
+
+    def first_plan(at, parts, outs):
+        return token_plan(at, parts[:2], outs[:tm]) + chunk_plan(0, at, parts[2:], outs[tm:])
 
     def exchange(tensors):
-        arrived = {k: to_partner(tensors[k], k) for k in order}
-        return [pltpu.with_memory_space_constraint(arrived[k], pltpu.VMEM) for k in range(tm)]
-
-    sent_tokens = moved(
-        spots, [split[3], time_pieces], [(frames + blocks, patches, width)] * tm, token_plan, "token_payloads"
+        arrived = [to_partner(tensor, k) for k, tensor in zip(order, tensors)]
+        return [pltpu.with_memory_space_constraint(tensor, pltpu.VMEM) for tensor in arrived]
+
+    first_sent = moved(
+        spots,
+        [split[3], time_pieces, *split[:3], space_pieces],
+        [(frames + blocks, patches, width)] * tm + [(3 * frames + 2 * blocks, patches, half)] * tm,
+        first_plan,
+        "first_payloads",
     )
-    tokens = exchange(sent_tokens)
-    first_sent = payloads(0, (space_pieces,), (sent_tokens[0],))
-    early = exchange(first_sent)
-    second_sent = payloads(1, (), (first_sent[0],))
+    tokens = exchange(first_sent[:tm])
+    early = exchange(first_sent[tm:])
+    second_plan = functools.partial(chunk_plan, 1)
+    shapes = [(3 * frames, patches, half)] * tm
+    second_sent = moved(spots, split[:3], shapes, second_plan, "second_payloads", (first_sent[0],))
     late = exchange(second_sent)
 
     far = [lax.all_gather(tensor, "space", axis=0) for tensor in (space_q, space_k, space_v, grad_out)]
@@ -417,10 +422,9 @@
             tokens,
             (tm, blocks, patches, width),
             lambda at, refs, out: [
-                (ref.at[pl.ds(frames, blocks)], out.at[at[k]]) for k, ref in enumerate(refs)
+                (ref.at[pl.ds(frames, blocks)], out.at[at[k]]) for k, ref in zip(order, refs)
             ],
             "time_column",
-            (first_sent[0],),
         )
     )
     space_weights = gathered(
@@ -432,7 +436,7 @@
                     ref.at[pl.ds(3 * frames + side * blocks, blocks)],
                     out.at[at[k], :, :, pl.ds(side * half, half)],
                 )
-                for k, ref in enumerate(refs)
+                for k, ref in zip(order, refs)
                 for side in range(2)
             ],
             "space_column",
@@ -450,7 +454,7 @@
             columns = pl.ds(chunk * half, half)
             return [
                 (ref.at[pl.ds(kind * frames, frames)], outs[kind].at[:, at[k], :, columns])
-                for k, ref in enumerate(refs)
+                for k, ref in zip(order, refs)
                 for kind in range(3)
             ]
 

time: 227 us -> 249 us (1.097)
  waiting for transfers between devices: 30.3 us -> 52.2 us
    ppermute x35, waiting for transfers between devices: 27.8 us -> 49.7 us  [to_partner(): lax.ppermute(tensor, 'tm', [(i, i ^ k) for i in range(tm)])]
    pallas_call x7 -> x6, Pallas kernels: 40.3 us -> 38.2 us  [moved(): pl.pallas_call(kernel, in_specs=[SCALARS] + [ANYWHERE] * (count + len(aft...]
  transfers between devices with their start and end apart: 41 -> 41, of which waited for: 7 -> 12; matrix products, arithmetic and copies ran while one was open for 0% -> 0% of each run, Pallas kernels for 41% -> 25%
where the time goes in v8:
time: 249 us
  Pallas kernels  95.1 us (38%)
  starting transfers between devices  81.3 us (33%)
  waiting for transfers between devices  52.2 us (21%)
  between operations  14.3 us (6%)
  local copies, waits for them, and re-layouts  5.63 us (2%)
    ppermute x35, starting transfers between devices, to_partner(): lax.ppermute(tensor, 'tm', [(i, i ^ k) for i in range(tm)])  81.1 us
    ppermute x35, waiting for transfers between devices, to_partner(): lax.ppermute(tensor, 'tm', [(i, i ^ k) for i in range(tm)])  49.7 us
    pallas_call x6, Pallas kernels, moved(): pl.pallas_call(kernel, in_specs=[SCALARS] + [ANYWHERE] * (count + len(aft...  38.2 us
    pallas_call x2, Pallas kernels, time_chunk(): pl.pallas_call(kernel, in_specs=[ANYWHERE] * (len(blocks) + 1 + len(after...  32.8 us
    pallas_call x1, Pallas kernels, space_attention(): pl.pallas_call(kernel, grid_spec=pltpu.PrefetchScalarGridSpec(num_scalar_...  24.1 us
    unnamed x28, local copies, waits for them, and re-layouts  5.63 us
  transfers between devices with their start and end apart: 41, of which 12 were waited for; matrix products, arithmetic and copies ran while one was open for 0% of the time, Pallas kernels for 25%

profile of v8, /device:TPU:0, one launch (start us, length us, event | category | flops | bytes accessed | tf_op | source)
XLA Modules:
  0.0 248.7 jit_solution(7262464073189605293)
XLA Ops:
  7.2 0.1 pad_add_fusion.spots_ref
  7.3 30.5 %first_payloads.1 = (bf16[11,8,1024]{2,1,0:T(8,128)(2,1)S(1)}, bf16[11,8,1024]{2,1,0:T(8,128)(2,1)S(1)}, bf16[11,8,1024]{2,1,0:T(8,128)(2,1)S(1)}, bf16[11,8,102...) custom-call(s32[9]{0:T(128)S(1)} %pad_add_fusion.spots_ref, ...), custom_call_target="tpu_custom_call" | custom-call | tf_op jit(solution)/shard_map/first_payloads/pallas_call | solution.py:174
  37.8 0.7 copy-done.6
  38.5 3.0 %collective-permute-start.14 = (bf16[11,8,1024]{2,1,0:T(8,128)(2,1)S(1)}, bf16[11,8,1024]{2,1,0:T(8,128)(2,1)S(1)}, u32[]{:S(2)}, u32[]{:S(2)}) collective-permute-start(bf16[11,8,1024]{2,1,0:T(8,128)(2,1)S(1)} %get-tuple-element.73), channel_id=1, source_target_pairs={{0,2},{2,0},{4,6},{6,4},{8,10},{10,8},{12,14},{14,12},{1,3},{3,1},... | collective-permute-start | bytes 540680 | tf_op jit(solution)/shard_map/ppermute | solution.py:364
  41.5 2.6 %collective-permute-start.15 = (bf16[11,8,1024]{2,1,0:T(8,128)(2,1)S(1)}, bf16[11,8,1024]{2,1,0:T(8,128)(2,1)S(1)}, u32[]{:S(2)}, u32[]{:S(2)}) collective-permute-start(bf16[11,8,1024]{2,1,0:T(8,128)(2,1)S(1)} %get-tuple-element.74), channel_id=1, source_target_pairs={{0,8},{2,10},{4,12},{6,14},{8,0},{10,2},{12,4},{14,6},{1,9},{3,11}... | collective-permute-start | bytes 540680 | tf_op jit(solution)/shard_map/ppermute | solution.py:364
  44.0 1.6 collective-permute-start.16
  45.6 0.3 collective-permute-start.17
  45.9 1.4 collective-permute-start.18
  47.3 3.6 %collective-permute-start.19 = (bf16[11,8,1024]{2,1,0:T(8,128)(2,1)S(1)}, bf16[11,8,1024]{2,1,0:T(8,128)(2,1)S(1)}, u32[]{:S(2)}, u32[]{:S(2)}) collective-permute-start(bf16[11,8,1024]{2,1,0:T(8,128)(2,1)S(1)} %get-tuple-element.78), channel_id=1, source_target_pairs={{0,12},{2,14},{4,8},{6,10},{8,4},{10,6},{12,0},{14,2},{1,13},{3,15... | collective-permute-start | bytes 540680 | tf_op jit(solution)/shard_map/ppermute | solution.py:364
  50.9 5.1 %collective-permute-done.15.refs_2_.refs_10_ = bf16[11,8,1024]{2,1,0:T(8,128)(2,1)S(1)} collective-permute-done((bf16[11,8,1024]{2,1,0:T(8,128)(2,1)S(1)}, bf16[11,8,1024]{2,1,0:T(8,128)(2,1)S(1)}, u32[]{:S(2)}, u32[]{:S(2)}) %collective-permute-start.15) | collective-permute-done | bytes 180256 | tf_op jit(solution)/shard_map/ppermute | solution.py:364
  56.0 2.2 collective-permute-start.20
  58.2 3.8 %collective-permute-done.17.refs_4_.refs_12_ = bf16[11,8,1024]{2,1,0:T(8,128)(2,1)S(1)} collective-permute-done((bf16[11,8,1024]{2,1,0:T(8,128)(2,1)S(1)}, bf16[11,8,1024]{2,1,0:T(8,128)(2,1)S(1)}, u32[]{:S(2)}, u32[]{:S(2)}) %collective-permute-start.17) | collective-permute-done | bytes 180256 | tf_op jit(solution)/shard_map/ppermute | solution.py:364
  62.0 4.8 %collective-permute-done.19.refs_6_.refs_14_ = bf16[11,8,1024]{2,1,0:T(8,128)(2,1)S(1)} collective-permute-done((bf16[11,8,1024]{2,1,0:T(8,128)(2,1)S(1)}, bf16[11,8,1024]{2,1,0:T(8,128)(2,1)S(1)}, u32[]{:S(2)}, u32[]{:S(2)}) %collective-permute-start.19) | collective-permute-done | bytes 180256 | tf_op jit(solution)/shard_map/ppermute | solution.py:364
  66.9 2.4 collective-permute-done.20.refs_7_.refs_15_
  69.3 1.3 time_column.1
  70.7 0.7 all-gather.15.cloned.1.call-update
  71.4 0.7 all-gather.17.cloned.1.call-update
  72.1 0.5 all-gather.19.cloned.1.call-update
  72.7 0.5 all-gather.21.cloned.1.call-update
  73.3 1.6 collective-permute-start.7
  74.9 8.7 %collective-permute-start.8 = (bf16[29,8,512]{2,1,0:T(8,128)(2,1)S(1)}, bf16[29,8,512]{2,1,0:T(8,128)(2,1)S(1)}, u32[]{:S(2)}, u32[]{:S(2)}) collective-permute-start(bf16[29,8,512]{2,1,0:T(8,128)(2,1)S(1)} %get-tuple-element.67), channel_id=1, source_target_pairs={{0,8},{2,10},{4,12},{6,14},{8,0},{10,2},{12,4},{14,6},{1,9},{3,11}... | collective-permute-start | bytes 712712 | tf_op jit(solution)/shard_map/ppermute | solution.py:364
  83.6 1.0 collective-permute-start.10
  84.6 1.9 collective-permute-start.11
  86.5 2.4 collective-permute-start.12
  88.9 7.0 %collective-permute-done.8.refs_2_ = bf16[29,8,512]{2,1,0:T(8,128)(2,1)S(1)} collective-permute-done((bf16[29,8,512]{2,1,0:T(8,128)(2,1)S(1)}, bf16[29,8,512]{2,1,0:T(8,128)(2,1)S(1)}, u32[]{:S(2)}, u32[]{:S(2)}) %collective-permute-start.8) | collective-permute-done | bytes 237600 | tf_op jit(solution)/shard_map/ppermute | solution.py:364
  95.8 1.9 second_payloads.1
  97.7 0.7 copy-done.10
  98.4 0.7 copy-done.11
  99.0 0.7 copy-done.12
  99.7 0.7 copy-done.13
  100.4 4.5 %collective-permute-done.10.refs_4_ = bf16[29,8,512]{2,1,0:T(8,128)(2,1)S(1)} collective-permute-done((bf16[29,8,512]{2,1,0:T(8,128)(2,1)}, bf16[29,8,512]{2,1,0:T(8,128)(2,1)S(1)}, u32[]{:S(2)}, u32[]{:S(2)}) %collective-permute-start.10) | collective-permute-done | bytes 237600 | tf_op jit(solution)/shard_map/ppermute | solution.py:364
  104.9 1.4 collective-permute-done.11.refs_5_
  106.2 5.8 %collective-permute-done.12.refs_6_ = bf16[29,8,512]{2,1,0:T(8,128)(2,1)S(1)} collective-permute-done((bf16[29,8,512]{2,1,0:T(8,128)(2,1)}, bf16[29,8,512]{2,1,0:T(8,128)(2,1)S(1)}, u32[]{:S(2)}, u32[]{:S(2)}) %collective-permute-start.12) | collective-permute-done | bytes 237600 | tf_op jit(solution)/shard_map/ppermute | solution.py:364
  112.0 4.9 %collective-permute-done.13.refs_7_ = bf16[29,8,512]{2,1,0:T(8,128)(2,1)S(1)} collective-permute-done((bf16[29,8,512]{2,1,0:T(8,128)(2,1)}, bf16[29,8,512]{2,1,0:T(8,128)(2,1)S(1)}, u32[]{:S(2)}, u32[]{:S(2)}) %collective-permute-start.13) | collective-permute-done | bytes 237600 | tf_op jit(solution)/shard_map/ppermute | solution.py:364
  116.9 1.3 space_column.1
  118.3 0.9 collective-permute-start
  119.2 7.4 %collective-permute-start.1 = (bf16[21,8,512]{2,1,0:T(8,128)(2,1)}, bf16[21,8,512]{2,1,0:T(8,128)(2,1)S(1)}, u32[]{:S(2)}, u32[]{:S(2)}) collective-permute-start(bf16[21,8,512]{2,1,0:T(8,128)(2,1)} %copy-done.12), channel_id=1, source_target_pairs={{0,8},{2,10},{4,12},{6,14},{8,0},{10,2},{12,4},{14,6},{1,9},{3,11}... | collective-permute-start | bytes 516104 | tf_op jit(solution)/shard_map/ppermute | solution.py:364
  126.5 1.0 collective-permute-start.2
  127.6 3.7 %collective-permute-start.3 = (bf16[21,8,512]{2,1,0:T(8,128)(2,1)}, bf16[21,8,512]{2,1,0:T(8,128)(2,1)}, u32[]{:S(2)}, u32[]{:S(2)}) collective-permute-start(bf16[21,8,512]{2,1,0:T(8,128)(2,1)} %copy-done.10), channel_id=1, source_target_pairs={{0,10},{2,8},{4,14},{6,12},{8,2},{10,0},{12,6},{14,4},{1,11},{3,9}... | collective-permute-start | bytes 516104 | tf_op jit(solution)/shard_map/ppermute | solution.py:364
  131.3 0.1 collective-permute-start.4
  131.4 0.7 copy-done.2
  132.1 1.5 collective-permute-start.5
  133.5 0.6 collective-permute-done.1.refs_2_
  134.1 0.7 copy-done.4
  134.8 6.2 %collective-permute-start.6 = (bf16[21,8,512]{2,1,0:T(8,128)(2,1)}, bf16[21,8,512]{2,1,0:T(8,128)(2,1)}, u32[]{:S(2)}, u32[]{:S(2)}) collective-permute-start(bf16[21,8,512]{2,1,0:T(8,128)(2,1)} %copy-done.7), channel_id=1, source_target_pairs={{0,14},{2,12},{4,10},{6,8},{8,6},{10,4},{12,2},{14,0},{1,15},{3,13... | collective-permute-start | bytes 516104 | tf_op jit(solution)/shard_map/ppermute | solution.py:364
  141.0 20.9 %time_first.1 = (bf16[21,8,512]{2,1,0:T(8,128)(2,1)S(1)}, bf16[21,8,512]{2,1,0:T(8,128)(2,1)S(1)}, bf16[21,8,512]{2,1,0:T(8,128)(2,1)S(1)}, bf16[21,8,512]{2,1,0...) custom-call(bf16[29,8,512]{2,1,0:T(8,128)(2,1)S(1)} %get-tuple-eleme, ...), custom_call_target="tpu_custom_call" | custom-call | bytes 59040000 | tf_op jit(solution)/shard_map/time_first/pallas_call | solution.py:283
  161.9 0.8 collective-permute-start.28
  162.7 0.2 collective-permute-start.30
  162.9 3.5 %collective-permute-start.31 = (bf16[21,8,512]{2,1,0:T(8,128)(2,1)S(1)}, bf16[21,8,512]{2,1,0:T(8,128)(2,1)S(1)}, u32[]{:S(2)}, u32[]{:S(2)}) collective-permute-start(bf16[21,8,512]{2,1,0:T(8,128)(2,1)S(1)} %get-tuple-element.93), channel_id=1, source_target_pairs={{0,10},{2,8},{4,14},{6,12},{8,2},{10,0},{12,6},{14,4},{1,11},{3,9}... | collective-permute-start | bytes 516104 | tf_op jit(solution)/shard_map/ppermute | solution.py:364
  166.4 2.1 collective-permute-start.32
  168.6 11.9 %time_second.1 = (bf16[21,8,512]{2,1,0:T(8,128)(2,1)S(1)}, bf16[21,8,512]{2,1,0:T(8,128)(2,1)S(1)}, bf16[21,8,512]{2,1,0:T(8,128)(2,1)S(1)}, bf16[21,8,512]{2,1,...) custom-call(bf16[21,8,512]{2,1,0:T(8,128)(2,1)S(1)} %get-tuple-eleme, ...), custom_call_target="tpu_custom_call" | custom-call | bytes 36900000 | tf_op jit(solution)/shard_map/time_second/pallas_call | solution.py:283
  180.5 0.1 collective-permute-start.33
  180.6 4.5 %collective-permute-start.34 = (bf16[21,8,512]{2,1,0:T(8,128)(2,1)S(1)}, bf16[21,8,512]{2,1,0:T(8,128)(2,1)S(1)}, u32[]{:S(2)}, u32[]{:S(2)}) collective-permute-start(bf16[21,8,512]{2,1,0:T(8,128)(2,1)S(1)} %get-tuple-element.96), channel_id=1, source_target_pairs={{0,14},{2,12},{4,10},{6,8},{8,6},{10,4},{12,2},{14,0},{1,15},{3,13... | collective-permute-start | bytes 516104 | tf_op jit(solution)/shard_map/ppermute | solution.py:364
  185.2 0.7 collective-permute-start.21
  185.9 0.6 collective-permute-start.23
  186.5 3.3 %collective-permute-done.33.refs_6_ = bf16[21,8,512]{2,1,0:T(8,128)(2,1)S(1)} collective-permute-done((bf16[21,8,512]{2,1,0:T(8,128)(2,1)S(1)}, bf16[21,8,512]{2,1,0:T(8,128)(2,1)S(1)}, u32[]{:S(2)}, u32[]{:S(2)}) %collective-permute-start.33) | collective-permute-done | bytes 172064 | tf_op jit(solution)/shard_map/ppermute | solution.py:364
  189.9 10.4 %collective-permute-start.24 = (bf16[21,8,512]{2,1,0:T(8,128)(2,1)S(1)}, bf16[21,8,512]{2,1,0:T(8,128)(2,1)S(1)}, u32[]{:S(2)}, u32[]{:S(2)}) collective-permute-start(bf16[21,8,512]{2,1,0:T(8,128)(2,1)S(1)} %get-tuple-element.85), channel_id=1, source_target_pairs={{0,10},{2,8},{4,14},{6,12},{8,2},{10,0},{12,6},{14,4},{1,11},{3,9}... | collective-permute-start | bytes 516104 | tf_op jit(solution)/shard_map/ppermute | solution.py:364
  200.2 5.2 %collective-permute-start.25 = (bf16[21,8,512]{2,1,0:T(8,128)(2,1)S(1)}, bf16[21,8,512]{2,1,0:T(8,128)(2,1)S(1)}, u32[]{:S(2)}, u32[]{:S(2)}) collective-permute-start(bf16[21,8,512]{2,1,0:T(8,128)(2,1)S(1)} %get-tuple-element.86), channel_id=1, source_target_pairs={{0,6},{2,4},{4,2},{6,0},{8,14},{10,12},{12,10},{14,8},{1,7},{3,5},... | collective-permute-start | bytes 516104 | tf_op jit(solution)/shard_map/ppermute | solution.py:364
  205.5 6.2 %collective-permute-done.22.refs_2_ = bf16[21,8,512]{2,1,0:T(8,128)(2,1)S(1)} collective-permute-done((bf16[21,8,512]{2,1,0:T(8,128)(2,1)S(1)}, bf16[21,8,512]{2,1,0:T(8,128)(2,1)S(1)}, u32[]{:S(2)}, u32[]{:S(2)}) %collective-permute-start.22) | collective-permute-done | bytes 172064 | tf_op jit(solution)/shard_map/ppermute | solution.py:364
  211.6 1.9 collective-permute-start.27
  213.5 0.9 copy-done.1
  214.4 1.6 place_first.1
  216.0 24.1 %space_attention.1 = (bf16[7,64,1024]{2,1,0:T(8,128)(2,1)}, bf16[7,64,1024]{2,1,0:T(8,128)(2,1)}, bf16[7,64,1024]{2,1,0:T(8,128)(2,1)}) custom-call(s32[1]{0:T(128)} %bitcast.8.core_ref, bf16[7,64,1024]{2,1,0:T(8,128)(2,1)} %refs_0_.1, bf16[7,64,1024]{2,1,0:T(8,128)(2,1)} %refs_1_.1, bf16[7,64,1024]{2,1,0:T(8,128)(2,1)} %refs_2_.1, ...), custom_call_target="tpu_custom_call" | custom-call | bytes 73800000 | tf_op jit(solution)/shard_map/space_attention/pallas_call | solution.py:330
  240.2 1.6 place_second.1
  (63 shorter events, 0.4 us)
Async XLA Ops:
  7.2 133.8 %all-gather.11.cloned.1.call-start = ((), (), s32[]{:S(2)}) async-start(), calls=%async_computation | async-start | bytes 2621440 | tf_op jit(solution)/shard_map/all_gather | solution.py:417
  37.8 0.7 copy-start.6
  38.5 8.8 %collective-permute-start.14 = (bf16[11,8,1024]{2,1,0:T(8,128)(2,1)S(1)}, bf16[11,8,1024]{2,1,0:T(8,128)(2,1)S(1)}, u32[]{:S(2)}, u32[]{:S(2)}) collective-permute-start(bf16[11,8,1024]{2,1,0:T(8,128)(2,1)S(1)} %get-tuple-element.73), channel_id=1, source_target_pairs={{0,2},{2,0},{4,6},{6,4},{8,10},{10,8},{12,14},{14,12},{1,3},{3,1},... | collective-permute-start | bytes 540680 | tf_op jit(solution)/shard_map/ppermute | solution.py:364
  41.5 14.5 %collective-permute-start.15 = (bf16[11,8,1024]{2,1,0:T(8,128)(2,1)S(1)}, bf16[11,8,1024]{2,1,0:T(8,128)(2,1)S(1)}, u32[]{:S(2)}, u32[]{:S(2)}) collective-permute-start(bf16[11,8,1024]{2,1,0:T(8,128)(2,1)S(1)} %get-tuple-element.74), channel_id=1, source_target_pairs={{0,8},{2,10},{4,12},{6,14},{8,0},{10,2},{12,4},{14,6},{1,9},{3,11}... | collective-permute-start | bytes 540680 | tf_op jit(solution)/shard_map/ppermute | solution.py:364
  44.0 14.2 %collective-permute-start.16 = (bf16[11,8,1024]{2,1,0:T(8,128)(2,1)S(1)}, bf16[11,8,1024]{2,1,0:T(8,128)(2,1)S(1)}, u32[]{:S(2)}, u32[]{:S(2)}) collective-permute-start(bf16[11,8,1024]{2,1,0:T(8,128)(2,1)S(1)} %get-tuple-element.75), channel_id=1, source_target_pairs={{0,4},{2,6},{4,0},{6,2},{8,12},{10,14},{12,8},{14,10},{1,5},{3,7},... | collective-permute-start | bytes 540680 | tf_op jit(solution)/shard_map/ppermute | solution.py:364
  45.6 16.4 %collective-permute-start.17 = (bf16[11,8,1024]{2,1,0:T(8,128)(2,1)S(1)}, bf16[11,8,1024]{2,1,0:T(8,128)(2,1)S(1)}, u32[]{:S(2)}, u32[]{:S(2)}) collective-permute-start(bf16[11,8,1024]{2,1,0:T(8,128)(2,1)S(1)} %get-tuple-element.76), channel_id=1, source_target_pairs={{0,10},{2,8},{4,14},{6,12},{8,2},{10,0},{12,6},{14,4},{1,11},{3,9}... | collective-permute-start | bytes 540680 | tf_op jit(solution)/shard_map/ppermute | solution.py:364
  45.9 16.1 %collective-permute-start.18 = (bf16[11,8,1024]{2,1,0:T(8,128)(2,1)S(1)}, bf16[11,8,1024]{2,1,0:T(8,128)(2,1)S(1)}, u32[]{:S(2)}, u32[]{:S(2)}) collective-permute-start(bf16[11,8,1024]{2,1,0:T(8,128)(2,1)S(1)} %get-tuple-element.77), channel_id=1, source_target_pairs={{0,6},{2,4},{4,2},{6,0},{8,14},{10,12},{12,10},{14,8},{1,7},{3,5},... | collective-permute-start | bytes 540680 | tf_op jit(solution)/shard_map/ppermute | solution.py:364
  47.3 19.6 %collective-permute-start.19 = (bf16[11,8,1024]{2,1,0:T(8,128)(2,1)S(1)}, bf16[11,8,1024]{2,1,0:T(8,128)(2,1)S(1)}, u32[]{:S(2)}, u32[]{:S(2)}) collective-permute-start(bf16[11,8,1024]{2,1,0:T(8,128)(2,1)S(1)} %get-tuple-element.78), channel_id=1, source_target_pairs={{0,12},{2,14},{4,8},{6,10},{8,4},{10,6},{12,0},{14,2},{1,13},{3,15... | collective-permute-start | bytes 540680 | tf_op jit(solution)/shard_map/ppermute | solution.py:364
  56.0 13.3 %collective-permute-start.20 = (bf16[11,8,1024]{2,1,0:T(8,128)(2,1)S(1)}, bf16[11,8,1024]{2,1,0:T(8,128)(2,1)S(1)}, u32[]{:S(2)}, u32[]{:S(2)}) collective-permute-start(bf16[11,8,1024]{2,1,0:T(8,128)(2,1)S(1)} %get-tuple-element.79), channel_id=1, source_target_pairs={{0,14},{2,12},{4,10},{6,8},{8,6},{10,4},{12,2},{14,0},{1,15},{3,13... | collective-permute-start | bytes 540680 | tf_op jit(solution)/shard_map/ppermute | solution.py:364
  70.6 145.4 %all-gather.15.cloned.1.call-start = ((), (), s32[]{:S(2)}) async-start(), calls=%async_computation.2 | async-start | bytes 2752512 | tf_op jit(solution)/shard_map/all_gather | solution.py:414
  71.4 144.6 %all-gather.17.cloned.1.call-start = ((), (), s32[]{:S(2)}) async-start(), calls=%async_computation.3 | async-start | bytes 2752512 | tf_op jit(solution)/shard_map/all_gather | solution.py:414
  72.1 143.9 %all-gather.19.cloned.1.call-start = ((), (), s32[]{:S(2)}) async-start(), calls=%async_computation.4 | async-start | bytes 2752512 | tf_op jit(solution)/shard_map/all_gather | solution.py:414
  72.7 143.3 %all-gather.21.cloned.1.call-start = ((), (), s32[]{:S(2)}) async-start(), calls=%async_computation.5 | async-start | bytes 2752512 | tf_op jit(solution)/shard_map/all_gather | solution.py:414
  73.3 142.8 %all-gather.13.cloned.1.call-start = ((), (), s32[]{:S(2)}) async-start(), calls=%async_computation.1 | async-start | bytes 2621440 | tf_op jit(solution)/shard_map/all_gather | solution.py:417
  73.3 13.2 %collective-permute-start.7 = (bf16[29,8,512]{2,1,0:T(8,128)(2,1)S(1)}, bf16[29,8,512]{2,1,0:T(8,128)(2,1)S(1)}, u32[]{:S(2)}, u32[]{:S(2)}) collective-permute-start(bf16[29,8,512]{2,1,0:T(8,128)(2,1)S(1)} %get-tuple-element.66), channel_id=1, source_target_pairs={{0,2},{2,0},{4,6},{6,4},{8,10},{10,8},{12,14},{14,12},{1,3},{3,1},... | collective-permute-start | bytes 712712 | tf_op jit(solution)/shard_map/ppermute | solution.py:364
  74.9 20.9 %collective-permute-start.8 = (bf16[29,8,512]{2,1,0:T(8,128)(2,1)S(1)}, bf16[29,8,512]{2,1,0:T(8,128)(2,1)S(1)}, u32[]{:S(2)}, u32[]{:S(2)}) collective-permute-start(bf16[29,8,512]{2,1,0:T(8,128)(2,1)S(1)} %get-tuple-element.67), channel_id=1, source_target_pairs={{0,8},{2,10},{4,12},{6,14},{8,0},{10,2},{12,4},{14,6},{1,9},{3,11}... | collective-permute-start | bytes 712712 | tf_op jit(solution)/shard_map/ppermute | solution.py:364
  83.6 16.8 %collective-permute-start.9 = (bf16[29,8,512]{2,1,0:T(8,128)(2,1)}, bf16[29,8,512]{2,1,0:T(8,128)(2,1)S(1)}, u32[]{:S(2)}, u32[]{:S(2)}) collective-permute-start(bf16[29,8,512]{2,1,0:T(8,128)(2,1)} %get-tuple-element.68), channel_id=1, source_target_pairs={{0,4},{2,6},{4,0},{6,2},{8,12},{10,14},{12,8},{14,10},{1,5},{3,7},... | collective-permute-start | bytes 712712 | tf_op jit(solution)/shard_map/ppermute | solution.py:364
  83.6 21.3 %collective-permute-start.10 = (bf16[29,8,512]{2,1,0:T(8,128)(2,1)}, bf16[29,8,512]{2,1,0:T(8,128)(2,1)S(1)}, u32[]{:S(2)}, u32[]{:S(2)}) collective-permute-start(bf16[29,8,512]{2,1,0:T(8,128)(2,1)} %get-tuple-element.69), channel_id=1, source_target_pairs={{0,10},{2,8},{4,14},{6,12},{8,2},{10,0},{12,6},{14,4},{1,11},{3,9}... | collective-permute-start | bytes 712712 | tf_op jit(solution)/shard_map/ppermute | solution.py:364
  84.6 21.6 %collective-permute-start.11 = (bf16[29,8,512]{2,1,0:T(8,128)(2,1)}, bf16[29,8,512]{2,1,0:T(8,128)(2,1)S(1)}, u32[]{:S(2)}, u32[]{:S(2)}) collective-permute-start(bf16[29,8,512]{2,1,0:T(8,128)(2,1)} %get-tuple-element.70), channel_id=1, source_target_pairs={{0,6},{2,4},{4,2},{6,0},{8,14},{10,12},{12,10},{14,8},{1,7},{3,5},... | collective-permute-start | bytes 712712 | tf_op jit(solution)/shard_map/ppermute | solution.py:364
  86.5 25.5 %collective-permute-start.12 = (bf16[29,8,512]{2,1,0:T(8,128)(2,1)}, bf16[29,8,512]{2,1,0:T(8,128)(2,1)S(1)}, u32[]{:S(2)}, u32[]{:S(2)}) collective-permute-start(bf16[29,8,512]{2,1,0:T(8,128)(2,1)} %get-tuple-element.71), channel_id=1, source_target_pairs={{0,12},{2,14},{4,8},{6,10},{8,4},{10,6},{12,0},{14,2},{1,13},{3,15... | collective-permute-start | bytes 712712 | tf_op jit(solution)/shard_map/ppermute | solution.py:364
  95.8 21.1 %collective-permute-start.13 = (bf16[29,8,512]{2,1,0:T(8,128)(2,1)}, bf16[29,8,512]{2,1,0:T(8,128)(2,1)S(1)}, u32[]{:S(2)}, u32[]{:S(2)}) collective-permute-start(bf16[29,8,512]{2,1,0:T(8,128)(2,1)} %copy-done.6), channel_id=1, source_target_pairs={{0,14},{2,12},{4,10},{6,8},{8,6},{10,4},{12,2},{14,0},{1,15},{3,13... | collective-permute-start | bytes 712712 | tf_op jit(solution)/shard_map/ppermute | solution.py:364
  97.7 0.7 copy-start.10
  98.4 0.7 copy-start.11
  99.0 0.7 copy-start.12
  99.7 0.7 copy-start.13
  100.4 16.6 %copy-start.7 = (bf16[21,8,512]{2,1,0:T(8,128)(2,1)}, bf16[21,8,512]{2,1,0:T(8,128)(2,1)S(1)}, u32[]{:S(2)}) copy-start(bf16[21,8,512]{2,1,0:T(8,128)(2,1)S(1)} %get-tuple-element.64) | copy-start | bytes 516100
  100.4 16.6 %copy-start.8 = (bf16[21,8,512]{2,1,0:T(8,128)(2,1)}, bf16[21,8,512]{2,1,0:T(8,128)(2,1)S(1)}, u32[]{:S(2)}) copy-start(bf16[21,8,512]{2,1,0:T(8,128)(2,1)S(1)} %get-tuple-element.63) | copy-start | bytes 516100
  100.4 16.6 %copy-start.9 = (bf16[21,8,512]{2,1,0:T(8,128)(2,1)}, bf16[21,8,512]{2,1,0:T(8,128)(2,1)S(1)}, u32[]{:S(2)}) copy-start(bf16[21,8,512]{2,1,0:T(8,128)(2,1)S(1)} %get-tuple-element.62) | copy-start | bytes 516100
  118.3 13.1 %collective-permute-start = (bf16[21,8,512]{2,1,0:T(8,128)(2,1)}, bf16[21,8,512]{2,1,0:T(8,128)(2,1)S(1)}, u32[]{:S(2)}, u32[]{:S(2)}) collective-permute-start(bf16[21,8,512]{2,1,0:T(8,128)(2,1)} %copy-done.13), channel_id=1, source_target_pairs={{0,2},{2,0},{4,6},{6,4},{8,10},{10,8},{12,14},{14,12},{1,3},{3,1},... | collective-permute-start | bytes 516104 | tf_op jit(solution)/shard_map/ppermute | solution.py:364
  119.2 14.9 %collective-permute-start.1 = (bf16[21,8,512]{2,1,0:T(8,128)(2,1)}, bf16[21,8,512]{2,1,0:T(8,128)(2,1)S(1)}, u32[]{:S(2)}, u32[]{:S(2)}) collective-permute-start(bf16[21,8,512]{2,1,0:T(8,128)(2,1)} %copy-done.12), channel_id=1, source_target_pairs={{0,8},{2,10},{4,12},{6,14},{8,0},{10,2},{12,4},{14,6},{1,9},{3,11}... | collective-permute-start | bytes 516104 | tf_op jit(solution)/shard_map/ppermute | solution.py:364
  126.5 35.4 %collective-permute-start.2 = (bf16[21,8,512]{2,1,0:T(8,128)(2,1)}, bf16[21,8,512]{2,1,0:T(8,128)(2,1)}, u32[]{:S(2)}, u32[]{:S(2)}) collective-permute-start(bf16[21,8,512]{2,1,0:T(8,128)(2,1)} %copy-done.11), channel_id=1, source_target_pairs={{0,4},{2,6},{4,0},{6,2},{8,12},{10,14},{12,8},{14,10},{1,5},{3,7},... | collective-permute-start | bytes 516104 | tf_op jit(solution)/shard_map/ppermute | solution.py:364
  127.6 35.1 %collective-permute-start.3 = (bf16[21,8,512]{2,1,0:T(8,128)(2,1)}, bf16[21,8,512]{2,1,0:T(8,128)(2,1)}, u32[]{:S(2)}, u32[]{:S(2)}) collective-permute-start(bf16[21,8,512]{2,1,0:T(8,128)(2,1)} %copy-done.10), channel_id=1, source_target_pairs={{0,10},{2,8},{4,14},{6,12},{8,2},{10,0},{12,6},{14,4},{1,11},{3,9}... | collective-permute-start | bytes 516104 | tf_op jit(solution)/shard_map/ppermute | solution.py:364
  131.3 31.4 %collective-permute-start.4 = (bf16[21,8,512]{2,1,0:T(8,128)(2,1)}, bf16[21,8,512]{2,1,0:T(8,128)(2,1)}, u32[]{:S(2)}, u32[]{:S(2)}) collective-permute-start(bf16[21,8,512]{2,1,0:T(8,128)(2,1)} %copy-done.9), channel_id=1, source_target_pairs={{0,6},{2,4},{4,2},{6,0},{8,14},{10,12},{12,10},{14,8},{1,7},{3,5},... | collective-permute-start | bytes 516104 | tf_op jit(solution)/shard_map/ppermute | solution.py:364
  131.4 0.7 copy-start.2
  132.1 30.8 %collective-permute-start.5 = (bf16[21,8,512]{2,1,0:T(8,128)(2,1)}, bf16[21,8,512]{2,1,0:T(8,128)(2,1)}, u32[]{:S(2)}, u32[]{:S(2)}) collective-permute-start(bf16[21,8,512]{2,1,0:T(8,128)(2,1)} %copy-done.8), channel_id=1, source_target_pairs={{0,12},{2,14},{4,8},{6,10},{8,4},{10,6},{12,0},{14,2},{1,13},{3,15... | collective-permute-start | bytes 516104 | tf_op jit(solution)/shard_map/ppermute | solution.py:364
  134.1 0.7 copy-start.4
  134.8 31.7 %collective-permute-start.6 = (bf16[21,8,512]{2,1,0:T(8,128)(2,1)}, bf16[21,8,512]{2,1,0:T(8,128)(2,1)}, u32[]{:S(2)}, u32[]{:S(2)}) collective-permute-start(bf16[21,8,512]{2,1,0:T(8,128)(2,1)} %copy-done.7), channel_id=1, source_target_pairs={{0,14},{2,12},{4,10},{6,8},{8,6},{10,4},{12,2},{14,0},{1,15},{3,13... | collective-permute-start | bytes 516104 | tf_op jit(solution)/shard_map/ppermute | solution.py:364
  141.0 27.6 %copy-start.3 = (bf16[21,8,512]{2,1,0:T(8,128)(2,1)S(1)}, bf16[21,8,512]{2,1,0:T(8,128)(2,1)}, u32[]{:S(2)}) copy-start(bf16[21,8,512]{2,1,0:T(8,128)(2,1)} %copy-done.2) | copy-start | bytes 516100
  141.0 27.6 %copy-start.5 = (bf16[21,8,512]{2,1,0:T(8,128)(2,1)S(1)}, bf16[21,8,512]{2,1,0:T(8,128)(2,1)}, u32[]{:S(2)}) copy-start(bf16[21,8,512]{2,1,0:T(8,128)(2,1)} %copy-done.4) | copy-start | bytes 516100
  161.9 49.7 %copy-start = (bf16[21,8,512]{2,1,0:T(8,128)(2,1)}, bf16[21,8,512]{2,1,0:T(8,128)(2,1)S(1)}, u32[]{:S(2)}) copy-start(bf16[21,8,512]{2,1,0:T(8,128)(2,1)S(1)} %get-tuple-element.89.refs_0_) | copy-start | bytes 516100
  161.9 18.6 %collective-permute-start.28 = (bf16[21,8,512]{2,1,0:T(8,128)(2,1)S(1)}, bf16[21,8,512]{2,1,0:T(8,128)(2,1)S(1)}, u32[]{:S(2)}, u32[]{:S(2)}) collective-permute-start(bf16[21,8,512]{2,1,0:T(8,128)(2,1)S(1)} %get-tuple-element.90), channel_id=1, source_target_pairs={{0,2},{2,0},{4,6},{6,4},{8,10},{10,8},{12,14},{14,12},{1,3},{3,1},... | collective-permute-start | bytes 516104 | tf_op jit(solution)/shard_map/ppermute | solution.py:364
  162.7 17.9 %collective-permute-start.29 = (bf16[21,8,512]{2,1,0:T(8,128)(2,1)S(1)}, bf16[21,8,512]{2,1,0:T(8,128)(2,1)S(1)}, u32[]{:S(2)}, u32[]{:S(2)}) collective-permute-start(bf16[21,8,512]{2,1,0:T(8,128)(2,1)S(1)} %get-tuple-element.91), channel_id=1, source_target_pairs={{0,8},{2,10},{4,12},{6,14},{8,0},{10,2},{12,4},{14,6},{1,9},{3,11}... | collective-permute-start | bytes 516104 | tf_op jit(solution)/shard_map/ppermute | solution.py:364
  162.7 22.4 %collective-permute-start.30 = (bf16[21,8,512]{2,1,0:T(8,128)(2,1)S(1)}, bf16[21,8,512]{2,1,0:T(8,128)(2,1)S(1)}, u32[]{:S(2)}, u32[]{:S(2)}) collective-permute-start(bf16[21,8,512]{2,1,0:T(8,128)(2,1)S(1)} %get-tuple-element.92), channel_id=1, source_target_pairs={{0,4},{2,6},{4,0},{6,2},{8,12},{10,14},{12,8},{14,10},{1,5},{3,7},... | collective-permute-start | bytes 516104 | tf_op jit(solution)/shard_map/ppermute | solution.py:364
  162.9 23.0 %collective-permute-start.31 = (bf16[21,8,512]{2,1,0:T(8,128)(2,1)S(1)}, bf16[21,8,512]{2,1,0:T(8,128)(2,1)S(1)}, u32[]{:S(2)}, u32[]{:S(2)}) collective-permute-start(bf16[21,8,512]{2,1,0:T(8,128)(2,1)S(1)} %get-tuple-element.93), channel_id=1, source_target_pairs={{0,10},{2,8},{4,14},{6,12},{8,2},{10,0},{12,6},{14,4},{1,11},{3,9}... | collective-permute-start | bytes 516104 | tf_op jit(solution)/shard_map/ppermute | solution.py:364
  166.4 19.5 %collective-permute-start.32 = (bf16[21,8,512]{2,1,0:T(8,128)(2,1)S(1)}, bf16[21,8,512]{2,1,0:T(8,128)(2,1)S(1)}, u32[]{:S(2)}, u32[]{:S(2)}) collective-permute-start(bf16[21,8,512]{2,1,0:T(8,128)(2,1)S(1)} %get-tuple-element.94), channel_id=1, source_target_pairs={{0,6},{2,4},{4,2},{6,0},{8,14},{10,12},{12,10},{14,8},{1,7},{3,5},... | collective-permute-start | bytes 516104 | tf_op jit(solution)/shard_map/ppermute | solution.py:364
  180.5 9.3 %collective-permute-start.33 = (bf16[21,8,512]{2,1,0:T(8,128)(2,1)S(1)}, bf16[21,8,512]{2,1,0:T(8,128)(2,1)S(1)}, u32[]{:S(2)}, u32[]{:S(2)}) collective-permute-start(bf16[21,8,512]{2,1,0:T(8,128)(2,1)S(1)} %get-tuple-element.95), channel_id=1, source_target_pairs={{0,12},{2,14},{4,8},{6,10},{8,4},{10,6},{12,0},{14,2},{1,13},{3,15... | collective-permute-start | bytes 516104 | tf_op jit(solution)/shard_map/ppermute | solution.py:364
  180.6 19.6 %collective-permute-start.34 = (bf16[21,8,512]{2,1,0:T(8,128)(2,1)S(1)}, bf16[21,8,512]{2,1,0:T(8,128)(2,1)S(1)}, u32[]{:S(2)}, u32[]{:S(2)}) collective-permute-start(bf16[21,8,512]{2,1,0:T(8,128)(2,1)S(1)} %get-tuple-element.96), channel_id=1, source_target_pairs={{0,14},{2,12},{4,10},{6,8},{8,6},{10,4},{12,2},{14,0},{1,15},{3,13... | collective-permute-start | bytes 516104 | tf_op jit(solution)/shard_map/ppermute | solution.py:364
  185.2 20.3 %collective-permute-start.21 = (bf16[21,8,512]{2,1,0:T(8,128)(2,1)S(1)}, bf16[21,8,512]{2,1,0:T(8,128)(2,1)S(1)}, u32[]{:S(2)}, u32[]{:S(2)}) collective-permute-start(bf16[21,8,512]{2,1,0:T(8,128)(2,1)S(1)} %get-tuple-element.82), channel_id=1, source_target_pairs={{0,2},{2,0},{4,6},{6,4},{8,10},{10,8},{12,14},{14,12},{1,3},{3,1},... | collective-permute-start | bytes 516104 | tf_op jit(solution)/shard_map/ppermute | solution.py:364
  185.9 25.7 %collective-permute-start.22 = (bf16[21,8,512]{2,1,0:T(8,128)(2,1)S(1)}, bf16[21,8,512]{2,1,0:T(8,128)(2,1)S(1)}, u32[]{:S(2)}, u32[]{:S(2)}) collective-permute-start(bf16[21,8,512]{2,1,0:T(8,128)(2,1)S(1)} %get-tuple-element.83), channel_id=1, source_target_pairs={{0,8},{2,10},{4,12},{6,14},{8,0},{10,2},{12,4},{14,6},{1,9},{3,11}... | collective-permute-start | bytes 516104 | tf_op jit(solution)/shard_map/ppermute | solution.py:364
  185.9 54.3 %collective-permute-start.23 = (bf16[21,8,512]{2,1,0:T(8,128)(2,1)}, bf16[21,8,512]{2,1,0:T(8,128)(2,1)S(1)}, u32[]{:S(2)}, u32[]{:S(2)}) collective-permute-start(bf16[21,8,512]{2,1,0:T(8,128)(2,1)} %get-tuple-element.84), channel_id=1, source_target_pairs={{0,4},{2,6},{4,0},{6,2},{8,12},{10,14},{12,8},{14,10},{1,5},{3,7},... | collective-permute-start | bytes 516104 | tf_op jit(solution)/shard_map/ppermute | solution.py:364
  189.9 50.3 %collective-permute-start.24 = (bf16[21,8,512]{2,1,0:T(8,128)(2,1)S(1)}, bf16[21,8,512]{2,1,0:T(8,128)(2,1)S(1)}, u32[]{:S(2)}, u32[]{:S(2)}) collective-permute-start(bf16[21,8,512]{2,1,0:T(8,128)(2,1)S(1)} %get-tuple-element.85), channel_id=1, source_target_pairs={{0,10},{2,8},{4,14},{6,12},{8,2},{10,0},{12,6},{14,4},{1,11},{3,9}... | collective-permute-start | bytes 516104 | tf_op jit(solution)/shard_map/ppermute | solution.py:364
  200.2 40.0 %collective-permute-start.25 = (bf16[21,8,512]{2,1,0:T(8,128)(2,1)S(1)}, bf16[21,8,512]{2,1,0:T(8,128)(2,1)S(1)}, u32[]{:S(2)}, u32[]{:S(2)}) collective-permute-start(bf16[21,8,512]{2,1,0:T(8,128)(2,1)S(1)} %get-tuple-element.86), channel_id=1, source_target_pairs={{0,6},{2,4},{4,2},{6,0},{8,14},{10,12},{12,10},{14,8},{1,7},{3,5},... | collective-permute-start | bytes 516104 | tf_op jit(solution)/shard_map/ppermute | solution.py:364
  205.5 34.7 %collective-permute-start.26 = (bf16[21,8,512]{2,1,0:T(8,128)(2,1)S(1)}, bf16[21,8,512]{2,1,0:T(8,128)(2,1)S(1)}, u32[]{:S(2)}, u32[]{:S(2)}) collective-permute-start(bf16[21,8,512]{2,1,0:T(8,128)(2,1)S(1)} %get-tuple-element.87), channel_id=1, source_target_pairs={{0,12},{2,14},{4,8},{6,10},{8,4},{10,6},{12,0},{14,2},{1,13},{3,15... | collective-permute-start | bytes 516104 | tf_op jit(solution)/shard_map/ppermute | solution.py:364
  211.6 28.6 %collective-permute-start.27 = (bf16[21,8,512]{2,1,0:T(8,128)(2,1)S(1)}, bf16[21,8,512]{2,1,0:T(8,128)(2,1)S(1)}, u32[]{:S(2)}, u32[]{:S(2)}) collective-permute-start(bf16[21,8,512]{2,1,0:T(8,128)(2,1)S(1)} %get-tuple-element.88), channel_id=1, source_target_pairs={{0,14},{2,12},{4,10},{6,8},{8,6},{10,4},{12,2},{14,0},{1,15},{3,13... | collective-permute-start | bytes 516104 | tf_op jit(solution)/shard_map/ppermute | solution.py:364
  213.5 0.9 copy-start.1
Sparse Core Ops, SparseCore 0:
  70.7 28.8 all-gather.10
  101.2 10.1 all-gather.14
  113.0 11.3 all-gather.16
  125.8 11.3 all-gather.18
  138.6 11.3 all-gather.20
  152.0 23.9 all-gather.12

commit v9 on v8

--- a/solution.py
+++ b/solution.py
@@ -363,10 +363,6 @@
     def to_partner(tensor, k):
         return lax.ppermute(tensor, "tm", [(i, i ^ k) for i in range(tm)]) if k else tensor
 
-    def moved_one(parts, shape, plan, name, after=(), space=pltpu.HBM):
-        one = lambda at, refs, outs: plan(at, refs, outs[0])
-        return moved(spots, parts, [shape], one, name, after, (), space)[0]
-
     split = [t.reshape(frames, tm, patches, width) for t in (time_q, time_k, time_v, grad_out)]
     blocks = share // patches
     time_pieces, space_pieces = (t.reshape(groups, blocks, patches, width) for t in (time_wo, space_wo))
@@ -375,41 +371,36 @@
         pairs = []
         for k, out in zip(order, outs):
             pairs.append((parts[0].at[:, at[k]], out.at[pl.ds(0, frames)]))
-            pairs.append((parts[1].at[at[tm]], out.at[pl.ds(frames, blocks)]))
+            for i, part in enumerate(parts[1:]):
+                pairs.append((part.at[at[tm]], out.at[pl.ds(frames + i * blocks, blocks)]))
         return pairs
 
-    def chunk_plan(chunk, at, parts, outs):
-        columns = pl.ds(chunk * half, half)
-        pairs = []
-        for k, out in zip(order, outs):
-            for i in range(3):
-                pairs.append((parts[i].at[:, at[k], :, columns], out.at[pl.ds(i * frames, frames)]))
-            for part in parts[3:]:
-                for side in range(2):
-                    kept = out.at[pl.ds(3 * frames + side * blocks, blocks)]
-                    pairs.append((part.at[at[tm], :, :, pl.ds(side * half, half)], kept))
-        return pairs
-
-    def first_plan(at, parts, outs):
-        return token_plan(at, parts[:2], outs[:tm]) + chunk_plan(0, at, parts[2:], outs[tm:])
+    def chunk_payloads(chunk, name, after):
+        def plan(at, parts, outs):
+            columns = pl.ds(chunk * half, half)
+            return [
+                (part.at[:, at[k], :, columns], out.at[pl.ds(i * frames, frames)])
+                for k, out in zip(order, outs)
+                for i, part in enumerate(parts)
+            ]
+
+        return moved(spots, split[:3], [(3 * frames, patches, half)] * tm, plan, name, after)
 
     def exchange(tensors):
         arrived = [to_partner(tensor, k) for k, tensor in zip(order, tensors)]
         return [pltpu.with_memory_space_constraint(tensor, pltpu.VMEM) for tensor in arrived]
 
-    first_sent = moved(
+    sent = moved(
         spots,
-        [split[3], time_pieces, *split[:3], space_pieces],
-        [(frames + blocks, patches, width)] * tm + [(3 * frames + 2 * blocks, patches, half)] * tm,
-        first_plan,
-        "first_payloads",
+        [split[3], time_pieces, space_pieces],
+        [(frames + 2 * blocks, patches, width)] * tm,
+        token_plan,
+        "token_payloads",
     )
-    tokens = exchange(first_sent[:tm])
-    early = exchange(first_sent[tm:])
-    second_plan = functools.partial(chunk_plan, 1)
-    shapes = [(3 * frames, patches, half)] * tm
-    second_sent = moved(spots, split[:3], shapes, second_plan, "second_payloads", (first_sent[0],))
-    late = exchange(second_sent)
+    tokens = exchange(sent)
+    first_sent = chunk_payloads(0, "first_payloads", (sent[0],))
+    early = exchange(first_sent)
+    late = exchange(chunk_payloads(1, "second_payloads", (first_sent[0],)))
 
     far = [lax.all_gather(tensor, "space", axis=0) for tensor in (space_q, space_k, space_v, grad_out)]
 
@@ -417,32 +408,21 @@
         whole = lax.all_gather(column, ("space", "groups"), axis=0, tiled=True)
         return whole.reshape(space, groups, tm, share, width)
 
-    time_weights = gathered(
-        moved_one(
-            tokens,
-            (tm, blocks, patches, width),
-            lambda at, refs, out: [
-                (ref.at[pl.ds(frames, blocks)], out.at[at[k]]) for k, ref in zip(order, refs)
-            ],
-            "time_column",
-        )
+    columns = moved(
+        spots,
+        tokens,
+        [(tm, blocks, patches, width)] * 2,
+        lambda at, refs, outs: [
+            (ref.at[pl.ds(frames + i * blocks, blocks)], out.at[at[k]])
+            for k, ref in zip(order, refs)
+            for i, out in enumerate(outs)
+        ],
+        "columns",
+        (first_sent[0],),
+        (),
+        pltpu.HBM,
     )
-    space_weights = gathered(
-        moved_one(
-            early,
-            (tm, blocks, patches, width),
-            lambda at, refs, out: [
-                (
-                    ref.at[pl.ds(3 * frames + side * blocks, blocks)],
-                    out.at[at[k], :, :, pl.ds(side * half, half)],
-                )
-                for k, ref in zip(order, refs)
-                for side in range(2)
-            ],
-            "space_column",
-            (second_sent[0],),
-        )
-    )
+    time_weights, space_weights = (gathered(column) for column in columns)
 
     *done, late_grad = time_chunk(frames, early, tokens, time_weights, None, "time_first")
     back = exchange(done)

time: 249 us -> 240 us (0.964)
  waiting for transfers between devices: 52.2 us -> 32.8 us
  local copies, waits for them, and re-layouts: 5.63 us -> 15.4 us
  starting transfers between devices: 81.3 us -> 78.1 us
  Pallas kernels: 95.1 us -> 98.2 us
    ppermute x35, waiting for transfers between devices: 49.7 us -> 29.8 us  [to_partner(): lax.ppermute(tensor, 'tm', [(i, i ^ k) for i in range(tm)])]
    unnamed x28 -> x48, local copies, waits for them, and re-layouts: 5.63 us -> 15.4 us
    pallas_call x6, Pallas kernels: 38.2 us -> 41.6 us  [moved(): pl.pallas_call(kernel, in_specs=[SCALARS] + [ANYWHERE] * (count + len(aft...]
    ppermute x35, starting transfers between devices: 81.1 us -> 77.8 us  [to_partner(): lax.ppermute(tensor, 'tm', [(i, i ^ k) for i in range(tm)])]
  transfers between devices with their start and end apart: 41 -> 41, of which waited for: 12 -> 8; matrix products, arithmetic and copies ran while one was open for 0% -> 0% of each run, Pallas kernels for 25% -> 39%
where the time goes in v9:
time: 240 us; the launch traced here: 239 us
  Pallas kernels  98.2 us (41%)
  starting transfers between devices  78.1 us (33%)
  waiting for transfers between devices  32.8 us (14%)
  local copies, waits for them, and re-layouts  15.4 us (6%)
  between operations  14.3 us (6%)
    ppermute x35, starting transfers between devices, to_partner(): lax.ppermute(tensor, 'tm', [(i, i ^ k) for i in range(tm)])  77.8 us
    pallas_call x6, Pallas kernels, moved(): pl.pallas_call(kernel, in_specs=[SCALARS] + [ANYWHERE] * (count + len(aft...  41.6 us
    pallas_call x2, Pallas kernels, time_chunk(): pl.pallas_call(kernel, in_specs=[ANYWHERE] * (len(blocks) + 1 + len(after...  32.9 us
    ppermute x35, waiting for transfers between devices, to_partner(): lax.ppermute(tensor, 'tm', [(i, i ^ k) for i in range(tm)])  29.8 us
    pallas_call x1, Pallas kernels, space_attention(): pl.pallas_call(kernel, grid_spec=pltpu.PrefetchScalarGridSpec(num_scalar_...  23.7 us
    unnamed x48, local copies, waits for them, and re-layouts  15.4 us
  transfers between devices with their start and end apart: 41, of which 8 were waited for; matrix products, arithmetic and copies ran while one was open for 0% of the time, Pallas kernels for 39%

profile of v9, /device:TPU:0, one launch (start us, length us, event | category | flops | bytes accessed | tf_op | source)
XLA Modules:
  0.0 238.9 jit_solution(11683874733973539504)
XLA Ops:
  7.3 2.3 token_payloads.1
  9.6 3.0 %collective-permute-start.14 = (bf16[15,8,1024]{2,1,0:T(8,128)(2,1)S(1)}, bf16[15,8,1024]{2,1,0:T(8,128)(2,1)S(1)}, u32[]{:S(2)}, u32[]{:S(2)}) collective-permute-start(bf16[15,8,1024]{2,1,0:T(8,128)(2,1)S(1)} %get-tuple-element.75), channel_id=1, source_target_pairs={{0,2},{2,0},{4,6},{6,4},{8,10},{10,8},{12,14},{14,12},{1,3},{3,1},... | collective-permute-start | bytes 737288 | tf_op jit(solution)/shard_map/ppermute | solution.py:364
  12.6 2.6 %collective-permute-start.15 = (bf16[15,8,1024]{2,1,0:T(8,128)(2,1)S(1)}, bf16[15,8,1024]{2,1,0:T(8,128)(2,1)S(1)}, u32[]{:S(2)}, u32[]{:S(2)}) collective-permute-start(bf16[15,8,1024]{2,1,0:T(8,128)(2,1)S(1)} %get-tuple-element.76), channel_id=1, source_target_pairs={{0,8},{2,10},{4,12},{6,14},{8,0},{10,2},{12,4},{14,6},{1,9},{3,11}... | collective-permute-start | bytes 737288 | tf_op jit(solution)/shard_map/ppermute | solution.py:364
  15.2 1.6 collective-permute-start.16
  17.0 1.4 collective-permute-start.18
  18.5 4.2 %collective-permute-start.19 = (bf16[15,8,1024]{2,1,0:T(8,128)(2,1)S(1)}, bf16[15,8,1024]{2,1,0:T(8,128)(2,1)S(1)}, u32[]{:S(2)}, u32[]{:S(2)}) collective-permute-start(bf16[15,8,1024]{2,1,0:T(8,128)(2,1)S(1)} %get-tuple-element.80), channel_id=1, source_target_pairs={{0,12},{2,14},{4,8},{6,10},{8,4},{10,6},{12,0},{14,2},{1,13},{3,15... | collective-permute-start | bytes 737288 | tf_op jit(solution)/shard_map/ppermute | solution.py:364
  22.7 8.6 %collective-permute-done.15.refs_2_.refs_10_ = bf16[15,8,1024]{2,1,0:T(8,128)(2,1)S(1)} collective-permute-done((bf16[15,8,1024]{2,1,0:T(8,128)(2,1)S(1)}, bf16[15,8,1024]{2,1,0:T(8,128)(2,1)S(1)}, u32[]{:S(2)}, u32[]{:S(2)}) %collective-permute-start.15) | collective-permute-done | bytes 245792 | tf_op jit(solution)/shard_map/ppermute | solution.py:364
  31.3 6.9 %first_payloads.1 = (bf16[21,8,512]{2,1,0:T(8,128)(2,1)S(1)}, bf16[21,8,512]{2,1,0:T(8,128)(2,1)S(1)}, bf16[21,8,512]{2,1,0:T(8,128)(2,1)S(1)}, bf16[21,8,512]{2...) custom-call(s32[9]{0:T(128)S(1)} %pad_add_fusion.spots_ref, ...), custom_call_target="tpu_custom_call" | custom-call | tf_op jit(solution)/shard_map/first_payloads/pallas_call | solution.py:174
  38.2 0.7 copy-done.16
  38.9 0.7 copy-done.18
  39.6 0.7 copy-done.20
  40.2 0.7 copy-done.22
  40.9 4.7 %collective-permute-done.19.refs_6_.refs_14_ = bf16[15,8,1024]{2,1,0:T(8,128)(2,1)S(1)} collective-permute-done((bf16[15,8,1024]{2,1,0:T(8,128)(2,1)S(1)}, bf16[15,8,1024]{2,1,0:T(8,128)(2,1)S(1)}, u32[]{:S(2)}, u32[]{:S(2)}) %collective-permute-start.19) | collective-permute-done | bytes 245792 | tf_op jit(solution)/shard_map/ppermute | solution.py:364
  45.6 3.8 %collective-permute-done.20.refs_7_.refs_15_ = bf16[15,8,1024]{2,1,0:T(8,128)(2,1)S(1)} collective-permute-done((bf16[15,8,1024]{2,1,0:T(8,128)(2,1)S(1)}, bf16[15,8,1024]{2,1,0:T(8,128)(2,1)S(1)}, u32[]{:S(2)}, u32[]{:S(2)}) %collective-permute-start.20) | collective-permute-done | bytes 245792 | tf_op jit(solution)/shard_map/ppermute | solution.py:364
  49.4 1.5 columns.1
  51.0 0.7 all-gather.17.cloned.1.call-update
  51.8 0.7 all-gather.19.cloned.1.call-update
  54.2 12.0 %collective-permute-start.10 = (bf16[21,8,512]{2,1,0:T(8,128)(2,1)}, bf16[21,8,512]{2,1,0:T(8,128)(2,1)S(1)}, u32[]{:S(2)}, u32[]{:S(2)}) collective-permute-start(bf16[21,8,512]{2,1,0:T(8,128)(2,1)} %get-tuple-element.71), channel_id=1, source_target_pairs={{0,10},{2,8},{4,14},{6,12},{8,2},{10,0},{12,6},{14,4},{1,11},{3,9}... | collective-permute-start | bytes 516104 | tf_op jit(solution)/shard_map/ppermute | solution.py:364
  66.2 1.5 collective-permute-start.12
  67.7 2.3 collective-permute-start.13
  70.0 1.5 collective-permute-start.7
  71.5 27.7 %second_payloads.1 = (bf16[21,8,512]{2,1,0:T(8,128)(2,1)S(1)}, bf16[21,8,512]{2,1,0:T(8,128)(2,1)S(1)}, bf16[21,8,512]{2,1,0:T(8,128)(2,1)S(1)}, bf16[21,8,512]{...) custom-call(s32[9]{0:T(128)S(1)} %pad_add_fusion.spots_ref, ...), custom_call_target="tpu_custom_call" | custom-call | tf_op jit(solution)/shard_map/second_payloads/pallas_call | solution.py:174
  99.2 0.7 copy-done.2
  99.9 0.7 copy-done.4
  100.6 2.0 collective-permute-start.9
  102.6 0.7 copy-done.6
  103.8 0.7 copy-done.8
  104.5 2.0 collective-permute-start.1
  106.5 0.7 copy-done.10
  107.1 0.9 collective-permute-start.2
  108.0 3.8 %collective-permute-done.8.refs_2_ = bf16[21,8,512]{2,1,0:T(8,128)(2,1)S(1)} collective-permute-done((bf16[21,8,512]{2,1,0:T(8,128)(2,1)S(1)}, bf16[21,8,512]{2,1,0:T(8,128)(2,1)S(1)}, u32[]{:S(2)}, u32[]{:S(2)}) %collective-permute-start.8) | collective-permute-done | bytes 172064 | tf_op jit(solution)/shard_map/ppermute | solution.py:364
  111.9 0.7 copy-done.12
  112.6 0.7 copy-done.14
  113.2 2.8 %collective-permute-start.4 = (bf16[21,8,512]{2,1,0:T(8,128)(2,1)}, bf16[21,8,512]{2,1,0:T(8,128)(2,1)S(1)}, u32[]{:S(2)}, u32[]{:S(2)}) collective-permute-start(bf16[21,8,512]{2,1,0:T(8,128)(2,1)} %get-tuple-element.65), channel_id=1, source_target_pairs={{0,6},{2,4},{4,2},{6,0},{8,14},{10,12},{12,10},{14,8},{1,7},{3,5},... | collective-permute-start | bytes 516104 | tf_op jit(solution)/shard_map/ppermute | solution.py:364
  116.0 2.5 %collective-permute-start.5 = (bf16[21,8,512]{2,1,0:T(8,128)(2,1)}, bf16[21,8,512]{2,1,0:T(8,128)(2,1)S(1)}, u32[]{:S(2)}, u32[]{:S(2)}) collective-permute-start(bf16[21,8,512]{2,1,0:T(8,128)(2,1)} %get-tuple-element.66), channel_id=1, source_target_pairs={{0,12},{2,14},{4,8},{6,10},{8,4},{10,6},{12,0},{14,2},{1,13},{3,15... | collective-permute-start | bytes 516104 | tf_op jit(solution)/shard_map/ppermute | solution.py:364
  118.5 0.7 collective-permute-done.1.refs_2_
  119.2 1.4 collective-permute-start.6
  120.7 0.9 copy-done.3
  121.6 0.9 copy-done.5
  122.5 0.9 copy-done.7
  123.4 0.9 copy-done.9
  124.3 0.9 copy-done.11
  125.2 0.9 copy-done.13
  126.2 0.9 copy-done.15
  127.1 20.5 %time_first.1 = (bf16[21,8,512]{2,1,0:T(8,128)(2,1)S(1)}, bf16[21,8,512]{2,1,0:T(8,128)(2,1)S(1)}, bf16[21,8,512]{2,1,0:T(8,128)(2,1)S(1)}, bf16[21,8,512]{2,1,0...) custom-call(bf16[21,8,512]{2,1,0:T(8,128)(2,1)S(1)} %get-tuple-eleme, ...), custom_call_target="tpu_custom_call" | custom-call | bytes 59040000 | tf_op jit(solution)/shard_map/time_first/pallas_call | solution.py:283
  147.6 1.5 collective-permute-start.28
  149.1 3.2 %collective-permute-start.30 = (bf16[21,8,512]{2,1,0:T(8,128)(2,1)S(1)}, bf16[21,8,512]{2,1,0:T(8,128)(2,1)S(1)}, u32[]{:S(2)}, u32[]{:S(2)}) collective-permute-start(bf16[21,8,512]{2,1,0:T(8,128)(2,1)S(1)} %get-tuple-element.96), channel_id=1, source_target_pairs={{0,4},{2,6},{4,0},{6,2},{8,12},{10,14},{12,8},{14,10},{1,5},{3,7},... | collective-permute-start | bytes 516104 | tf_op jit(solution)/shard_map/ppermute | solution.py:364
  152.3 0.7 copy-done
  153.0 2.6 %collective-permute-start.32 = (bf16[21,8,512]{2,1,0:T(8,128)(2,1)S(1)}, bf16[21,8,512]{2,1,0:T(8,128)(2,1)S(1)}, u32[]{:S(2)}, u32[]{:S(2)}) collective-permute-start(bf16[21,8,512]{2,1,0:T(8,128)(2,1)S(1)} %get-tuple-element.98), channel_id=1, source_target_pairs={{0,6},{2,4},{4,2},{6,0},{8,14},{10,12},{12,10},{14,8},{1,7},{3,5},... | collective-permute-start | bytes 516104 | tf_op jit(solution)/shard_map/ppermute | solution.py:364
  155.6 0.9 copy-done.1
  156.5 12.5 %time_second.1 = (bf16[21,8,512]{2,1,0:T(8,128)(2,1)S(1)}, bf16[21,8,512]{2,1,0:T(8,128)(2,1)S(1)}, bf16[21,8,512]{2,1,0:T(8,128)(2,1)S(1)}, bf16[21,8,512]{2,1,...) custom-call(bf16[21,8,512]{2,1,0:T(8,128)(2,1)S(1)} %get-tuple-eleme, ...), custom_call_target="tpu_custom_call" | custom-call | bytes 36900000 | tf_op jit(solution)/shard_map/time_second/pallas_call | solution.py:283
  169.0 2.7 %collective-permute-start.33 = (bf16[21,8,512]{2,1,0:T(8,128)(2,1)S(1)}, bf16[21,8,512]{2,1,0:T(8,128)(2,1)S(1)}, u32[]{:S(2)}, u32[]{:S(2)}) collective-permute-start(bf16[21,8,512]{2,1,0:T(8,128)(2,1)S(1)} %get-tuple-element.99), channel_id=1, source_target_pairs={{0,12},{2,14},{4,8},{6,10},{8,4},{10,6},{12,0},{14,2},{1,13},{3,15... | collective-permute-start | bytes 516104 | tf_op jit(solution)/shard_map/ppermute | solution.py:364
  171.7 1.2 collective-permute-start.34
  172.9 1.4 collective-permute-start.21
  174.3 3.2 %collective-permute-start.23 = (bf16[21,8,512]{2,1,0:T(8,128)(2,1)}, bf16[21,8,512]{2,1,0:T(8,128)(2,1)S(1)}, u32[]{:S(2)}, u32[]{:S(2)}) collective-permute-start(bf16[21,8,512]{2,1,0:T(8,128)(2,1)} %get-tuple-element.87), channel_id=1, source_target_pairs={{0,4},{2,6},{4,0},{6,2},{8,12},{10,14},{12,8},{14,10},{1,5},{3,7},... | collective-permute-start | bytes 516104 | tf_op jit(solution)/shard_map/ppermute | solution.py:364
  177.6 0.6 collective-permute-done.33.refs_6_
  178.2 11.2 %collective-permute-start.24 = (bf16[21,8,512]{2,1,0:T(8,128)(2,1)}, bf16[21,8,512]{2,1,0:T(8,128)(2,1)S(1)}, u32[]{:S(2)}, u32[]{:S(2)}) collective-permute-start(bf16[21,8,512]{2,1,0:T(8,128)(2,1)} %get-tuple-element.88), channel_id=1, source_target_pairs={{0,10},{2,8},{4,14},{6,12},{8,2},{10,0},{12,6},{14,4},{1,11},{3,9}... | collective-permute-start | bytes 516104 | tf_op jit(solution)/shard_map/ppermute | solution.py:364
  189.3 4.1 %collective-permute-start.25 = (bf16[21,8,512]{2,1,0:T(8,128)(2,1)}, bf16[21,8,512]{2,1,0:T(8,128)(2,1)S(1)}, u32[]{:S(2)}, u32[]{:S(2)}) collective-permute-start(bf16[21,8,512]{2,1,0:T(8,128)(2,1)} %get-tuple-element.89), channel_id=1, source_target_pairs={{0,6},{2,4},{4,2},{6,0},{8,14},{10,12},{12,10},{14,8},{1,7},{3,5},... | collective-permute-start | bytes 516104 | tf_op jit(solution)/shard_map/ppermute | solution.py:364
  193.4 1.8 collective-permute-start.26
  195.2 7.4 %collective-permute-done.22.refs_2_ = bf16[21,8,512]{2,1,0:T(8,128)(2,1)S(1)} collective-permute-done((bf16[21,8,512]{2,1,0:T(8,128)(2,1)S(1)}, bf16[21,8,512]{2,1,0:T(8,128)(2,1)S(1)}, u32[]{:S(2)}, u32[]{:S(2)}) %collective-permute-start.22) | collective-permute-done | bytes 172064 | tf_op jit(solution)/shard_map/ppermute | solution.py:364
  202.6 2.4 %collective-permute-start.27 = (bf16[21,8,512]{2,1,0:T(8,128)(2,1)}, bf16[21,8,512]{2,1,0:T(8,128)(2,1)S(1)}, u32[]{:S(2)}, u32[]{:S(2)}) collective-permute-start(bf16[21,8,512]{2,1,0:T(8,128)(2,1)} %get-tuple-element.91), channel_id=1, source_target_pairs={{0,14},{2,12},{4,10},{6,8},{8,6},{10,4},{12,2},{14,0},{1,15},{3,13... | collective-permute-start | bytes 516104 | tf_op jit(solution)/shard_map/ppermute | solution.py:364
  205.0 1.6 place_first.1
  206.7 23.7 %space_attention.1 = (bf16[7,64,1024]{2,1,0:T(8,128)(2,1)}, bf16[7,64,1024]{2,1,0:T(8,128)(2,1)}, bf16[7,64,1024]{2,1,0:T(8,128)(2,1)}) custom-call(s32[1]{0:T(128)} %bitcast.8.core_ref, bf16[7,64,1024]{2,1,0:T(8,128)(2,1)} %refs_0_.1, bf16[7,64,1024]{2,1,0:T(8,128)(2,1)} %refs_1_.1, bf16[7,64,1024]{2,1,0:T(8,128)(2,1)} %refs_2_.1, ...), custom_call_target="tpu_custom_call" | custom-call | bytes 73800000 | tf_op jit(solution)/shard_map/space_attention/pallas_call | solution.py:330
  230.4 1.6 place_second.1
  (83 shorter events, 3.0 us)
Async XLA Ops:
  7.2 113.5 %all-gather.11.cloned.1.call-start = ((), (), s32[]{:S(2)}) async-start(), calls=%async_computation | async-start | bytes 2621440 | tf_op jit(solution)/shard_map/all_gather | solution.py:408
  9.6 8.9 %collective-permute-start.14 = (bf16[15,8,1024]{2,1,0:T(8,128)(2,1)S(1)}, bf16[15,8,1024]{2,1,0:T(8,128)(2,1)S(1)}, u32[]{:S(2)}, u32[]{:S(2)}) collective-permute-start(bf16[15,8,1024]{2,1,0:T(8,128)(2,1)S(1)} %get-tuple-element.75), channel_id=1, source_target_pairs={{0,2},{2,0},{4,6},{6,4},{8,10},{10,8},{12,14},{14,12},{1,3},{3,1},... | collective-permute-start | bytes 737288 | tf_op jit(solution)/shard_map/ppermute | solution.py:364
  12.6 18.7 %collective-permute-start.15 = (bf16[15,8,1024]{2,1,0:T(8,128)(2,1)S(1)}, bf16[15,8,1024]{2,1,0:T(8,128)(2,1)S(1)}, u32[]{:S(2)}, u32[]{:S(2)}) collective-permute-start(bf16[15,8,1024]{2,1,0:T(8,128)(2,1)S(1)} %get-tuple-element.76), channel_id=1, source_target_pairs={{0,8},{2,10},{4,12},{6,14},{8,0},{10,2},{12,4},{14,6},{1,9},{3,11}... | collective-permute-start | bytes 737288 | tf_op jit(solution)/shard_map/ppermute | solution.py:364
  15.2 25.7 %collective-permute-start.16 = (bf16[15,8,1024]{2,1,0:T(8,128)(2,1)S(1)}, bf16[15,8,1024]{2,1,0:T(8,128)(2,1)S(1)}, u32[]{:S(2)}, u32[]{:S(2)}) collective-permute-start(bf16[15,8,1024]{2,1,0:T(8,128)(2,1)S(1)} %get-tuple-element.77), channel_id=1, source_target_pairs={{0,4},{2,6},{4,0},{6,2},{8,12},{10,14},{12,8},{14,10},{1,5},{3,7},... | collective-permute-start | bytes 737288 | tf_op jit(solution)/shard_map/ppermute | solution.py:364
  16.7 24.2 %collective-permute-start.17 = (bf16[15,8,1024]{2,1,0:T(8,128)(2,1)S(1)}, bf16[15,8,1024]{2,1,0:T(8,128)(2,1)S(1)}, u32[]{:S(2)}, u32[]{:S(2)}) collective-permute-start(bf16[15,8,1024]{2,1,0:T(8,128)(2,1)S(1)} %get-tuple-element.78), channel_id=1, source_target_pairs={{0,10},{2,8},{4,14},{6,12},{8,2},{10,0},{12,6},{14,4},{1,11},{3,9}... | collective-permute-start | bytes 737288 | tf_op jit(solution)/shard_map/ppermute | solution.py:364
  17.0 23.9 %collective-permute-start.18 = (bf16[15,8,1024]{2,1,0:T(8,128)(2,1)S(1)}, bf16[15,8,1024]{2,1,0:T(8,128)(2,1)S(1)}, u32[]{:S(2)}, u32[]{:S(2)}) collective-permute-start(bf16[15,8,1024]{2,1,0:T(8,128)(2,1)S(1)} %get-tuple-element.79), channel_id=1, source_target_pairs={{0,6},{2,4},{4,2},{6,0},{8,14},{10,12},{12,10},{14,8},{1,7},{3,5},... | collective-permute-start | bytes 737288 | tf_op jit(solution)/shard_map/ppermute | solution.py:364
  18.5 27.1 %collective-permute-start.19 = (bf16[15,8,1024]{2,1,0:T(8,128)(2,1)S(1)}, bf16[15,8,1024]{2,1,0:T(8,128)(2,1)S(1)}, u32[]{:S(2)}, u32[]{:S(2)}) collective-permute-start(bf16[15,8,1024]{2,1,0:T(8,128)(2,1)S(1)} %get-tuple-element.80), channel_id=1, source_target_pairs={{0,12},{2,14},{4,8},{6,10},{8,4},{10,6},{12,0},{14,2},{1,13},{3,15... | collective-permute-start | bytes 737288 | tf_op jit(solution)/shard_map/ppermute | solution.py:364
  31.3 18.1 %collective-permute-start.20 = (bf16[15,8,1024]{2,1,0:T(8,128)(2,1)S(1)}, bf16[15,8,1024]{2,1,0:T(8,128)(2,1)S(1)}, u32[]{:S(2)}, u32[]{:S(2)}) collective-permute-start(bf16[15,8,1024]{2,1,0:T(8,128)(2,1)S(1)} %get-tuple-element.81), channel_id=1, source_target_pairs={{0,14},{2,12},{4,10},{6,8},{8,6},{10,4},{12,2},{14,0},{1,15},{3,13... | collective-permute-start | bytes 737288 | tf_op jit(solution)/shard_map/ppermute | solution.py:364
  38.2 0.7 copy-start.16
  38.9 0.7 copy-start.18
  39.6 0.7 copy-start.20
  40.2 0.7 copy-start.22
  50.9 155.7 %all-gather.17.cloned.1.call-start = ((), (), s32[]{:S(2)}) async-start(), calls=%async_computation.3 | async-start | bytes 2752512 | tf_op jit(solution)/shard_map/all_gather | solution.py:405
  51.7 14.5 %copy-start.23 = (bf16[21,8,512]{2,1,0:T(8,128)(2,1)S(1)}, bf16[21,8,512]{2,1,0:T(8,128)(2,1)}, u32[]{:S(2)}) copy-start(bf16[21,8,512]{2,1,0:T(8,128)(2,1)} %copy-done.22) | copy-start | bytes 516100
  51.7 14.5 %copy-start.21 = (bf16[21,8,512]{2,1,0:T(8,128)(2,1)S(1)}, bf16[21,8,512]{2,1,0:T(8,128)(2,1)}, u32[]{:S(2)}) copy-start(bf16[21,8,512]{2,1,0:T(8,128)(2,1)} %copy-done.20) | copy-start | bytes 516100
  51.7 16.0 %copy-start.19 = (bf16[21,8,512]{2,1,0:T(8,128)(2,1)S(1)}, bf16[21,8,512]{2,1,0:T(8,128)(2,1)}, u32[]{:S(2)}) copy-start(bf16[21,8,512]{2,1,0:T(8,128)(2,1)} %copy-done.18) | copy-start | bytes 516100
  51.7 18.3 %copy-start.17 = (bf16[21,8,512]{2,1,0:T(8,128)(2,1)S(1)}, bf16[21,8,512]{2,1,0:T(8,128)(2,1)}, u32[]{:S(2)}) copy-start(bf16[21,8,512]{2,1,0:T(8,128)(2,1)} %copy-done.16) | copy-start | bytes 516100
  51.7 154.9 %all-gather.19.cloned.1.call-start = ((), (), s32[]{:S(2)}) async-start(), calls=%async_computation.4 | async-start | bytes 2752512 | tf_op jit(solution)/shard_map/all_gather | solution.py:405
  52.4 154.2 %all-gather.21.cloned.1.call-start = ((), (), s32[]{:S(2)}) async-start(), calls=%async_computation.5 | async-start | bytes 2752512 | tf_op jit(solution)/shard_map/all_gather | solution.py:405
  53.0 153.6 %all-gather.15.cloned.1.call-start = ((), (), s32[]{:S(2)}) async-start(), calls=%async_computation.2 | async-start | bytes 2752512 | tf_op jit(solution)/shard_map/all_gather | solution.py:405
  53.6 153.0 %all-gather.13.cloned.1.call-start = ((), (), s32[]{:S(2)}) async-start(), calls=%async_computation.1 | async-start | bytes 2621440 | tf_op jit(solution)/shard_map/all_gather | solution.py:408
  54.2 45.1 %collective-permute-start.10 = (bf16[21,8,512]{2,1,0:T(8,128)(2,1)}, bf16[21,8,512]{2,1,0:T(8,128)(2,1)S(1)}, u32[]{:S(2)}, u32[]{:S(2)}) collective-permute-start(bf16[21,8,512]{2,1,0:T(8,128)(2,1)} %get-tuple-element.71), channel_id=1, source_target_pairs={{0,10},{2,8},{4,14},{6,12},{8,2},{10,0},{12,6},{14,4},{1,11},{3,9}... | collective-permute-start | bytes 516104 | tf_op jit(solution)/shard_map/ppermute | solution.py:364
  66.2 33.8 %collective-permute-start.11 = (bf16[21,8,512]{2,1,0:T(8,128)(2,1)S(1)}, bf16[21,8,512]{2,1,0:T(8,128)(2,1)S(1)}, u32[]{:S(2)}, u32[]{:S(2)}) collective-permute-start(bf16[21,8,512]{2,1,0:T(8,128)(2,1)S(1)} %copy-done.23), channel_id=1, source_target_pairs={{0,6},{2,4},{4,2},{6,0},{8,14},{10,12},{12,10},{14,8},{1,7},{3,5},... | collective-permute-start | bytes 516104 | tf_op jit(solution)/shard_map/ppermute | solution.py:364
  66.2 36.5 %collective-permute-start.12 = (bf16[21,8,512]{2,1,0:T(8,128)(2,1)S(1)}, bf16[21,8,512]{2,1,0:T(8,128)(2,1)S(1)}, u32[]{:S(2)}, u32[]{:S(2)}) collective-permute-start(bf16[21,8,512]{2,1,0:T(8,128)(2,1)S(1)} %copy-done.21), channel_id=1, source_target_pairs={{0,12},{2,14},{4,8},{6,10},{8,4},{10,6},{12,0},{14,2},{1,13},{3,15... | collective-permute-start | bytes 516104 | tf_op jit(solution)/shard_map/ppermute | solution.py:364
  67.7 36.1 %collective-permute-start.13 = (bf16[21,8,512]{2,1,0:T(8,128)(2,1)S(1)}, bf16[21,8,512]{2,1,0:T(8,128)(2,1)S(1)}, u32[]{:S(2)}, u32[]{:S(2)}) collective-permute-start(bf16[21,8,512]{2,1,0:T(8,128)(2,1)S(1)} %copy-done.19), channel_id=1, source_target_pairs={{0,14},{2,12},{4,10},{6,8},{8,6},{10,4},{12,2},{14,0},{1,15},{3,13... | collective-permute-start | bytes 516104 | tf_op jit(solution)/shard_map/ppermute | solution.py:364
  70.0 36.5 %collective-permute-start.7 = (bf16[21,8,512]{2,1,0:T(8,128)(2,1)S(1)}, bf16[21,8,512]{2,1,0:T(8,128)(2,1)S(1)}, u32[]{:S(2)}, u32[]{:S(2)}) collective-permute-start(bf16[21,8,512]{2,1,0:T(8,128)(2,1)S(1)} %copy-done.17), channel_id=1, source_target_pairs={{0,2},{2,0},{4,6},{6,4},{8,10},{10,8},{12,14},{14,12},{1,3},{3,1},... | collective-permute-start | bytes 516104 | tf_op jit(solution)/shard_map/ppermute | solution.py:364
  99.2 0.7 copy-start.2
  99.9 12.0 %collective-permute-start.8 = (bf16[21,8,512]{2,1,0:T(8,128)(2,1)S(1)}, bf16[21,8,512]{2,1,0:T(8,128)(2,1)S(1)}, u32[]{:S(2)}, u32[]{:S(2)}) collective-permute-start(bf16[21,8,512]{2,1,0:T(8,128)(2,1)S(1)} %get-tuple-element.69), channel_id=1, source_target_pairs={{0,8},{2,10},{4,12},{6,14},{8,0},{10,2},{12,4},{14,6},{1,9},{3,11}... | collective-permute-start | bytes 516104 | tf_op jit(solution)/shard_map/ppermute | solution.py:364
  99.9 0.7 copy-start.4
  100.6 12.0 %collective-permute-start.9 = (bf16[21,8,512]{2,1,0:T(8,128)(2,1)S(1)}, bf16[21,8,512]{2,1,0:T(8,128)(2,1)S(1)}, u32[]{:S(2)}, u32[]{:S(2)}) collective-permute-start(bf16[21,8,512]{2,1,0:T(8,128)(2,1)S(1)} %get-tuple-element.70), channel_id=1, source_target_pairs={{0,4},{2,6},{4,0},{6,2},{8,12},{10,14},{12,8},{14,10},{1,5},{3,7},... | collective-permute-start | bytes 516104 | tf_op jit(solution)/shard_map/ppermute | solution.py:364
  102.6 0.7 copy-start.6
  103.3 12.7 %collective-permute-start = (bf16[21,8,512]{2,1,0:T(8,128)(2,1)S(1)}, bf16[21,8,512]{2,1,0:T(8,128)(2,1)S(1)}, u32[]{:S(2)}, u32[]{:S(2)}) collective-permute-start(bf16[21,8,512]{2,1,0:T(8,128)(2,1)S(1)} %get-tuple-element.61), channel_id=1, source_target_pairs={{0,2},{2,0},{4,6},{6,4},{8,10},{10,8},{12,14},{14,12},{1,3},{3,1},... | collective-permute-start | bytes 516104 | tf_op jit(solution)/shard_map/ppermute | solution.py:364
  104.5 14.8 %collective-permute-start.1 = (bf16[21,8,512]{2,1,0:T(8,128)(2,1)S(1)}, bf16[21,8,512]{2,1,0:T(8,128)(2,1)S(1)}, u32[]{:S(2)}, u32[]{:S(2)}) collective-permute-start(bf16[21,8,512]{2,1,0:T(8,128)(2,1)S(1)} %get-tuple-element.62), channel_id=1, source_target_pairs={{0,8},{2,10},{4,12},{6,14},{8,0},{10,2},{12,4},{14,6},{1,9},{3,11}... | collective-permute-start | bytes 516104 | tf_op jit(solution)/shard_map/ppermute | solution.py:364
  106.5 0.7 copy-start.10
  107.1 40.4 %collective-permute-start.2 = (bf16[21,8,512]{2,1,0:T(8,128)(2,1)}, bf16[21,8,512]{2,1,0:T(8,128)(2,1)S(1)}, u32[]{:S(2)}, u32[]{:S(2)}) collective-permute-start(bf16[21,8,512]{2,1,0:T(8,128)(2,1)} %get-tuple-element.63), channel_id=1, source_target_pairs={{0,4},{2,6},{4,0},{6,2},{8,12},{10,14},{12,8},{14,10},{1,5},{3,7},... | collective-permute-start | bytes 516104 | tf_op jit(solution)/shard_map/ppermute | solution.py:364
  111.9 0.7 copy-start.12
  112.5 36.5 %collective-permute-start.3 = (bf16[21,8,512]{2,1,0:T(8,128)(2,1)}, bf16[21,8,512]{2,1,0:T(8,128)(2,1)S(1)}, u32[]{:S(2)}, u32[]{:S(2)}) collective-permute-start(bf16[21,8,512]{2,1,0:T(8,128)(2,1)} %get-tuple-element.64), channel_id=1, source_target_pairs={{0,10},{2,8},{4,14},{6,12},{8,2},{10,0},{12,6},{14,4},{1,11},{3,9}... | collective-permute-start | bytes 516104 | tf_op jit(solution)/shard_map/ppermute | solution.py:364
  112.6 0.7 copy-start.14
  113.2 35.8 %collective-permute-start.4 = (bf16[21,8,512]{2,1,0:T(8,128)(2,1)}, bf16[21,8,512]{2,1,0:T(8,128)(2,1)S(1)}, u32[]{:S(2)}, u32[]{:S(2)}) collective-permute-start(bf16[21,8,512]{2,1,0:T(8,128)(2,1)} %get-tuple-element.65), channel_id=1, source_target_pairs={{0,6},{2,4},{4,2},{6,0},{8,14},{10,12},{12,10},{14,8},{1,7},{3,5},... | collective-permute-start | bytes 516104 | tf_op jit(solution)/shard_map/ppermute | solution.py:364
  116.0 36.2 %collective-permute-start.5 = (bf16[21,8,512]{2,1,0:T(8,128)(2,1)}, bf16[21,8,512]{2,1,0:T(8,128)(2,1)S(1)}, u32[]{:S(2)}, u32[]{:S(2)}) collective-permute-start(bf16[21,8,512]{2,1,0:T(8,128)(2,1)} %get-tuple-element.66), channel_id=1, source_target_pairs={{0,12},{2,14},{4,8},{6,10},{8,4},{10,6},{12,0},{14,2},{1,13},{3,15... | collective-permute-start | bytes 516104 | tf_op jit(solution)/shard_map/ppermute | solution.py:364
  119.2 33.8 %collective-permute-start.6 = (bf16[21,8,512]{2,1,0:T(8,128)(2,1)}, bf16[21,8,512]{2,1,0:T(8,128)(2,1)}, u32[]{:S(2)}, u32[]{:S(2)}) collective-permute-start(bf16[21,8,512]{2,1,0:T(8,128)(2,1)} %get-tuple-element.67), channel_id=1, source_target_pairs={{0,14},{2,12},{4,10},{6,8},{8,6},{10,4},{12,2},{14,0},{1,15},{3,13... | collective-permute-start | bytes 516104 | tf_op jit(solution)/shard_map/ppermute | solution.py:364
  120.6 0.9 copy-start.3
  121.6 0.9 copy-start.5
  122.5 0.9 copy-start.7
  123.4 0.9 copy-start.9
  124.3 0.9 copy-start.11
  125.2 0.9 copy-start.13
  126.2 0.9 copy-start.15
  147.6 21.4 %collective-permute-start.28 = (bf16[21,8,512]{2,1,0:T(8,128)(2,1)S(1)}, bf16[21,8,512]{2,1,0:T(8,128)(2,1)S(1)}, u32[]{:S(2)}, u32[]{:S(2)}) collective-permute-start(bf16[21,8,512]{2,1,0:T(8,128)(2,1)S(1)} %get-tuple-element.94), channel_id=1, source_target_pairs={{0,2},{2,0},{4,6},{6,4},{8,10},{10,8},{12,14},{14,12},{1,3},{3,1},... | collective-permute-start | bytes 516104 | tf_op jit(solution)/shard_map/ppermute | solution.py:364
  149.1 22.7 %collective-permute-start.29 = (bf16[21,8,512]{2,1,0:T(8,128)(2,1)S(1)}, bf16[21,8,512]{2,1,0:T(8,128)(2,1)S(1)}, u32[]{:S(2)}, u32[]{:S(2)}) collective-permute-start(bf16[21,8,512]{2,1,0:T(8,128)(2,1)S(1)} %get-tuple-element.95), channel_id=1, source_target_pairs={{0,8},{2,10},{4,12},{6,14},{8,0},{10,2},{12,4},{14,6},{1,9},{3,11}... | collective-permute-start | bytes 516104 | tf_op jit(solution)/shard_map/ppermute | solution.py:364
  149.1 23.9 %collective-permute-start.30 = (bf16[21,8,512]{2,1,0:T(8,128)(2,1)S(1)}, bf16[21,8,512]{2,1,0:T(8,128)(2,1)S(1)}, u32[]{:S(2)}, u32[]{:S(2)}) collective-permute-start(bf16[21,8,512]{2,1,0:T(8,128)(2,1)S(1)} %get-tuple-element.96), channel_id=1, source_target_pairs={{0,4},{2,6},{4,0},{6,2},{8,12},{10,14},{12,8},{14,10},{1,5},{3,7},... | collective-permute-start | bytes 516104 | tf_op jit(solution)/shard_map/ppermute | solution.py:364
  152.3 0.7 copy-start
  152.9 21.4 %collective-permute-start.31 = (bf16[21,8,512]{2,1,0:T(8,128)(2,1)S(1)}, bf16[21,8,512]{2,1,0:T(8,128)(2,1)S(1)}, u32[]{:S(2)}, u32[]{:S(2)}) collective-permute-start(bf16[21,8,512]{2,1,0:T(8,128)(2,1)S(1)} %get-tuple-element.97), channel_id=1, source_target_pairs={{0,10},{2,8},{4,14},{6,12},{8,2},{10,0},{12,6},{14,4},{1,11},{3,9}... | collective-permute-start | bytes 516104 | tf_op jit(solution)/shard_map/ppermute | solution.py:364
  153.0 21.3 %collective-permute-start.32 = (bf16[21,8,512]{2,1,0:T(8,128)(2,1)S(1)}, bf16[21,8,512]{2,1,0:T(8,128)(2,1)S(1)}, u32[]{:S(2)}, u32[]{:S(2)}) collective-permute-start(bf16[21,8,512]{2,1,0:T(8,128)(2,1)S(1)} %get-tuple-element.98), channel_id=1, source_target_pairs={{0,6},{2,4},{4,2},{6,0},{8,14},{10,12},{12,10},{14,8},{1,7},{3,5},... | collective-permute-start | bytes 516104 | tf_op jit(solution)/shard_map/ppermute | solution.py:364
  155.6 0.9 copy-start.1
  169.0 9.2 %collective-permute-start.33 = (bf16[21,8,512]{2,1,0:T(8,128)(2,1)S(1)}, bf16[21,8,512]{2,1,0:T(8,128)(2,1)S(1)}, u32[]{:S(2)}, u32[]{:S(2)}) collective-permute-start(bf16[21,8,512]{2,1,0:T(8,128)(2,1)S(1)} %get-tuple-element.99), channel_id=1, source_target_pairs={{0,12},{2,14},{4,8},{6,10},{8,4},{10,6},{12,0},{14,2},{1,13},{3,15... | collective-permute-start | bytes 516104 | tf_op jit(solution)/shard_map/ppermute | solution.py:364
  171.7 17.6 %collective-permute-start.34 = (bf16[21,8,512]{2,1,0:T(8,128)(2,1)S(1)}, bf16[21,8,512]{2,1,0:T(8,128)(2,1)S(1)}, u32[]{:S(2)}, u32[]{:S(2)}) collective-permute-start(bf16[21,8,512]{2,1,0:T(8,128)(2,1)S(1)} %get-tuple-element.100), channel_id=1, source_target_pairs={{0,14},{2,12},{4,10},{6,8},{8,6},{10,4},{12,2},{14,0},{1,15},{3,13... | collective-permute-start | bytes 516104 | tf_op jit(solution)/shard_map/ppermute | solution.py:364
  172.9 20.5 %collective-permute-start.21 = (bf16[21,8,512]{2,1,0:T(8,128)(2,1)S(1)}, bf16[21,8,512]{2,1,0:T(8,128)(2,1)S(1)}, u32[]{:S(2)}, u32[]{:S(2)}) collective-permute-start(bf16[21,8,512]{2,1,0:T(8,128)(2,1)S(1)} %get-tuple-element.85), channel_id=1, source_target_pairs={{0,2},{2,0},{4,6},{6,4},{8,10},{10,8},{12,14},{14,12},{1,3},{3,1},... | collective-permute-start | bytes 516104 | tf_op jit(solution)/shard_map/ppermute | solution.py:364
  174.3 28.3 %collective-permute-start.22 = (bf16[21,8,512]{2,1,0:T(8,128)(2,1)S(1)}, bf16[21,8,512]{2,1,0:T(8,128)(2,1)S(1)}, u32[]{:S(2)}, u32[]{:S(2)}) collective-permute-start(bf16[21,8,512]{2,1,0:T(8,128)(2,1)S(1)} %get-tuple-element.86), channel_id=1, source_target_pairs={{0,8},{2,10},{4,12},{6,14},{8,0},{10,2},{12,4},{14,6},{1,9},{3,11}... | collective-permute-start | bytes 516104 | tf_op jit(solution)/shard_map/ppermute | solution.py:364
  174.3 56.0 %collective-permute-start.23 = (bf16[21,8,512]{2,1,0:T(8,128)(2,1)}, bf16[21,8,512]{2,1,0:T(8,128)(2,1)S(1)}, u32[]{:S(2)}, u32[]{:S(2)}) collective-permute-start(bf16[21,8,512]{2,1,0:T(8,128)(2,1)} %get-tuple-element.87), channel_id=1, source_target_pairs={{0,4},{2,6},{4,0},{6,2},{8,12},{10,14},{12,8},{14,10},{1,5},{3,7},... | collective-permute-start | bytes 516104 | tf_op jit(solution)/shard_map/ppermute | solution.py:364
  178.2 52.2 %collective-permute-start.24 = (bf16[21,8,512]{2,1,0:T(8,128)(2,1)}, bf16[21,8,512]{2,1,0:T(8,128)(2,1)S(1)}, u32[]{:S(2)}, u32[]{:S(2)}) collective-permute-start(bf16[21,8,512]{2,1,0:T(8,128)(2,1)} %get-tuple-element.88), channel_id=1, source_target_pairs={{0,10},{2,8},{4,14},{6,12},{8,2},{10,0},{12,6},{14,4},{1,11},{3,9}... | collective-permute-start | bytes 516104 | tf_op jit(solution)/shard_map/ppermute | solution.py:364
  189.3 41.1 %collective-permute-start.25 = (bf16[21,8,512]{2,1,0:T(8,128)(2,1)}, bf16[21,8,512]{2,1,0:T(8,128)(2,1)S(1)}, u32[]{:S(2)}, u32[]{:S(2)}) collective-permute-start(bf16[21,8,512]{2,1,0:T(8,128)(2,1)} %get-tuple-element.89), channel_id=1, source_target_pairs={{0,6},{2,4},{4,2},{6,0},{8,14},{10,12},{12,10},{14,8},{1,7},{3,5},... | collective-permute-start | bytes 516104 | tf_op jit(solution)/shard_map/ppermute | solution.py:364
  193.4 37.0 %collective-permute-start.26 = (bf16[21,8,512]{2,1,0:T(8,128)(2,1)}, bf16[21,8,512]{2,1,0:T(8,128)(2,1)S(1)}, u32[]{:S(2)}, u32[]{:S(2)}) collective-permute-start(bf16[21,8,512]{2,1,0:T(8,128)(2,1)} %get-tuple-element.90), channel_id=1, source_target_pairs={{0,12},{2,14},{4,8},{6,10},{8,4},{10,6},{12,0},{14,2},{1,13},{3,15... | collective-permute-start | bytes 516104 | tf_op jit(solution)/shard_map/ppermute | solution.py:364
  202.6 27.8 %collective-permute-start.27 = (bf16[21,8,512]{2,1,0:T(8,128)(2,1)}, bf16[21,8,512]{2,1,0:T(8,128)(2,1)S(1)}, u32[]{:S(2)}, u32[]{:S(2)}) collective-permute-start(bf16[21,8,512]{2,1,0:T(8,128)(2,1)} %get-tuple-element.91), channel_id=1, source_target_pairs={{0,14},{2,12},{4,10},{6,8},{8,6},{10,4},{12,2},{14,0},{1,15},{3,13... | collective-permute-start | bytes 516104 | tf_op jit(solution)/shard_map/ppermute | solution.py:364
  (1 other events, 0.7 us)
Sparse Core Ops, SparseCore 0:
  51.0 31.3 all-gather.10
  83.9 10.1 all-gather.16
  95.7 11.3 all-gather.18
  108.5 11.3 all-gather.20
  121.3 11.3 all-gather.14
  134.7 23.7 all-gather.12

commit v10 on v8

--- a/solution.py
+++ b/solution.py
@@ -390,22 +390,23 @@
                     pairs.append((part.at[at[tm], :, :, pl.ds(side * half, half)], kept))
         return pairs
 
-    def first_plan(at, parts, outs):
-        return token_plan(at, parts[:2], outs[:tm]) + chunk_plan(0, at, parts[2:], outs[tm:])
-
     def exchange(tensors):
         arrived = [to_partner(tensor, k) for k, tensor in zip(order, tensors)]
         return [pltpu.with_memory_space_constraint(tensor, pltpu.VMEM) for tensor in arrived]
 
+    sent_tokens = moved(
+        spots, [split[3], time_pieces], [(frames + blocks, patches, width)] * tm, token_plan, "token_payloads"
+    )
+    tokens = exchange(sent_tokens)
     first_sent = moved(
         spots,
-        [split[3], time_pieces, *split[:3], space_pieces],
-        [(frames + blocks, patches, width)] * tm + [(3 * frames + 2 * blocks, patches, half)] * tm,
-        first_plan,
+        [*split[:3], space_pieces],
+        [(3 * frames + 2 * blocks, patches, half)] * tm,
+        functools.partial(chunk_plan, 0),
         "first_payloads",
-    )
-    tokens = exchange(first_sent[:tm])
-    early = exchange(first_sent[tm:])
+        (sent_tokens[0],),
+    )
+    early = exchange(first_sent)
     second_plan = functools.partial(chunk_plan, 1)
     shapes = [(3 * frames, patches, half)] * tm
     second_sent = moved(spots, split[:3], shapes, second_plan, "second_payloads", (first_sent[0],))
@@ -425,6 +426,7 @@
                 (ref.at[pl.ds(frames, blocks)], out.at[at[k]]) for k, ref in zip(order, refs)
             ],
             "time_column",
+            (first_sent[0],),
         )
     )
     space_weights = gathered(

time: 249 us -> 233 us (0.936)
  waiting for transfers between devices: 52.2 us -> 40.2 us
  starting transfers between devices: 81.3 us -> 75.7 us
    ppermute x35, waiting for transfers between devices: 49.7 us -> 37.7 us  [to_partner(): lax.ppermute(tensor, 'tm', [(i, i ^ k) for i in range(tm)])]
    ppermute x35, starting transfers between devices: 81.1 us -> 75.4 us  [to_partner(): lax.ppermute(tensor, 'tm', [(i, i ^ k) for i in range(tm)])]
    pallas_call x6 -> x7, Pallas kernels: 38.2 us -> 40.3 us  [moved(): pl.pallas_call(kernel, in_specs=[SCALARS] + [ANYWHERE] * (count + len(aft...]
  transfers between devices with their start and end apart: 41 -> 41, of which waited for: 12 -> 7; matrix products, arithmetic and copies ran while one was open for 0% -> 0% of each run, Pallas kernels for 25% -> 39%
where the time goes in v10:
time: 233 us
  Pallas kernels  96.9 us (42%)
  starting transfers between devices  75.7 us (32%)
  waiting for transfers between devices  40.2 us (17%)
  between operations  14.3 us (6%)
  local copies, waits for them, and re-layouts  5.62 us (2%)
    ppermute x35, starting transfers between devices, to_partner(): lax.ppermute(tensor, 'tm', [(i, i ^ k) for i in range(tm)])  75.4 us
    pallas_call x7, Pallas kernels, moved(): pl.pallas_call(kernel, in_specs=[SCALARS] + [ANYWHERE] * (count + len(aft...  40.3 us
    ppermute x35, waiting for transfers between devices, to_partner(): lax.ppermute(tensor, 'tm', [(i, i ^ k) for i in range(tm)])  37.7 us
    pallas_call x2, Pallas kernels, time_chunk(): pl.pallas_call(kernel, in_specs=[ANYWHERE] * (len(blocks) + 1 + len(after...  32.6 us
    pallas_call x1, Pallas kernels, space_attention(): pl.pallas_call(kernel, grid_spec=pltpu.PrefetchScalarGridSpec(num_scalar_...  24.1 us
    unnamed x28, local copies, waits for them, and re-layouts  5.62 us
  transfers between devices with their start and end apart: 41, of which 7 were waited for; matrix products, arithmetic and copies ran while one was open for 0% of the time, Pallas kernels for 39%

profile of v10, /device:TPU:0, one launch (start us, length us, event | category | flops | bytes accessed | tf_op | source)
XLA Modules:
  0.0 232.8 jit_solution(16785403612219803157)
XLA Ops:
  7.2 0.0 all-gather.11.cloned.1.call-start
  7.2 0.1 pad_add_fusion.spots_ref
  7.3 2.1 token_payloads.1
  9.4 3.0 %collective-permute-start.14 = (bf16[11,8,1024]{2,1,0:T(8,128)(2,1)S(1)}, bf16[11,8,1024]{2,1,0:T(8,128)(2,1)S(1)}, u32[]{:S(2)}, u32[]{:S(2)}) collective-permute-start(bf16[11,8,1024]{2,1,0:T(8,128)(2,1)S(1)} %get-tuple-element.73), channel_id=1, source_target_pairs={{0,2},{2,0},{4,6},{6,4},{8,10},{10,8},{12,14},{14,12},{1,3},{3,1},... | collective-permute-start | bytes 540680 | tf_op jit(solution)/shard_map/ppermute | solution.py:364
  12.4 2.6 %collective-permute-start.15 = (bf16[11,8,1024]{2,1,0:T(8,128)(2,1)S(1)}, bf16[11,8,1024]{2,1,0:T(8,128)(2,1)S(1)}, u32[]{:S(2)}, u32[]{:S(2)}) collective-permute-start(bf16[11,8,1024]{2,1,0:T(8,128)(2,1)S(1)} %get-tuple-element.74), channel_id=1, source_target_pairs={{0,8},{2,10},{4,12},{6,14},{8,0},{10,2},{12,4},{14,6},{1,9},{3,11}... | collective-permute-start | bytes 540680 | tf_op jit(solution)/shard_map/ppermute | solution.py:364
  14.9 1.6 collective-permute-start.16
  16.5 0.3 collective-permute-start.17
  16.8 1.4 collective-permute-start.18
  18.2 3.6 %collective-permute-start.19 = (bf16[11,8,1024]{2,1,0:T(8,128)(2,1)S(1)}, bf16[11,8,1024]{2,1,0:T(8,128)(2,1)S(1)}, u32[]{:S(2)}, u32[]{:S(2)}) collective-permute-start(bf16[11,8,1024]{2,1,0:T(8,128)(2,1)S(1)} %get-tuple-element.78), channel_id=1, source_target_pairs={{0,12},{2,14},{4,8},{6,10},{8,4},{10,6},{12,0},{14,2},{1,13},{3,15... | collective-permute-start | bytes 540680 | tf_op jit(solution)/shard_map/ppermute | solution.py:364
  21.8 5.1 %collective-permute-done.15.refs_2_.refs_10_ = bf16[11,8,1024]{2,1,0:T(8,128)(2,1)S(1)} collective-permute-done((bf16[11,8,1024]{2,1,0:T(8,128)(2,1)S(1)}, bf16[11,8,1024]{2,1,0:T(8,128)(2,1)S(1)}, u32[]{:S(2)}, u32[]{:S(2)}) %collective-permute-start.15) | collective-permute-done | bytes 180256 | tf_op jit(solution)/shard_map/ppermute | solution.py:364
  26.9 2.2 collective-permute-start.20
  29.1 30.5 %first_payloads.1 = (bf16[29,8,512]{2,1,0:T(8,128)(2,1)S(1)}, bf16[29,8,512]{2,1,0:T(8,128)(2,1)S(1)}, bf16[29,8,512]{2,1,0:T(8,128)(2,1)S(1)}, bf16[29,8,512]{2...) custom-call(s32[9]{0:T(128)S(1)} %pad_add_fusion.spots_ref, ...), custom_call_target="tpu_custom_call" | custom-call | tf_op jit(solution)/shard_map/first_payloads/pallas_call | solution.py:174
  59.6 0.7 copy-done.6
  60.3 1.3 time_column.1
  61.6 0.0 all-gather.15.cloned.1.call-start
  61.7 0.7 all-gather.15.cloned.1.call-update
  62.4 0.7 all-gather.17.cloned.1.call-update
  63.2 0.5 all-gather.19.cloned.1.call-update
  63.8 0.5 all-gather.21.cloned.1.call-update
  64.3 0.0 all-gather.13.cloned.1.call-start
  64.3 1.6 collective-permute-start.7
  65.9 2.1 collective-permute-start.9
  68.0 0.8 collective-permute-start.10
  68.8 3.0 %collective-permute-start.11 = (bf16[29,8,512]{2,1,0:T(8,128)(2,1)}, bf16[29,8,512]{2,1,0:T(8,128)(2,1)S(1)}, u32[]{:S(2)}, u32[]{:S(2)}) collective-permute-start(bf16[29,8,512]{2,1,0:T(8,128)(2,1)} %get-tuple-element.70), channel_id=1, source_target_pairs={{0,6},{2,4},{4,2},{6,0},{8,14},{10,12},{12,10},{14,8},{1,7},{3,5},... | collective-permute-start | bytes 712712 | tf_op jit(solution)/shard_map/ppermute | solution.py:364
  71.8 1.5 collective-permute-start.12
  73.3 7.4 %collective-permute-done.8.refs_2_ = bf16[29,8,512]{2,1,0:T(8,128)(2,1)S(1)} collective-permute-done((bf16[29,8,512]{2,1,0:T(8,128)(2,1)S(1)}, bf16[29,8,512]{2,1,0:T(8,128)(2,1)S(1)}, u32[]{:S(2)}, u32[]{:S(2)}) %collective-permute-start.8) | collective-permute-done | bytes 237600 | tf_op jit(solution)/shard_map/ppermute | solution.py:364
  80.7 1.2 collective-permute-start.13
  81.9 1.9 second_payloads.1
  83.8 0.7 copy-done.10
  84.4 0.7 copy-done.11
  85.1 0.7 copy-done.12
  85.7 0.7 copy-done.13
  86.4 10.9 %collective-permute-done.10.refs_4_ = bf16[29,8,512]{2,1,0:T(8,128)(2,1)S(1)} collective-permute-done((bf16[29,8,512]{2,1,0:T(8,128)(2,1)}, bf16[29,8,512]{2,1,0:T(8,128)(2,1)S(1)}, u32[]{:S(2)}, u32[]{:S(2)}) %collective-permute-start.10) | collective-permute-done | bytes 237600 | tf_op jit(solution)/shard_map/ppermute | solution.py:364
  97.3 0.2 collective-permute-done.11.refs_5_
  97.5 1.3 space_column.1
  98.8 1.8 collective-permute-start
  100.7 9.0 %collective-permute-start.1 = (bf16[21,8,512]{2,1,0:T(8,128)(2,1)}, bf16[21,8,512]{2,1,0:T(8,128)(2,1)S(1)}, u32[]{:S(2)}, u32[]{:S(2)}) collective-permute-start(bf16[21,8,512]{2,1,0:T(8,128)(2,1)} %copy-done.12), channel_id=1, source_target_pairs={{0,8},{2,10},{4,12},{6,14},{8,0},{10,2},{12,4},{14,6},{1,9},{3,11}... | collective-permute-start | bytes 516104 | tf_op jit(solution)/shard_map/ppermute | solution.py:364
  109.7 2.7 %collective-permute-start.3 = (bf16[21,8,512]{2,1,0:T(8,128)(2,1)}, bf16[21,8,512]{2,1,0:T(8,128)(2,1)}, u32[]{:S(2)}, u32[]{:S(2)}) collective-permute-start(bf16[21,8,512]{2,1,0:T(8,128)(2,1)} %copy-done.10), channel_id=1, source_target_pairs={{0,10},{2,8},{4,14},{6,12},{8,2},{10,0},{12,6},{14,4},{1,11},{3,9}... | collective-permute-start | bytes 516104 | tf_op jit(solution)/shard_map/ppermute | solution.py:364
  112.4 0.8 collective-permute-start.4
  113.2 0.7 copy-done.2
  113.8 1.9 collective-permute-start.5
  115.7 4.1 %collective-permute-done.1.refs_2_ = bf16[21,8,512]{2,1,0:T(8,128)(2,1)S(1)} collective-permute-done((bf16[21,8,512]{2,1,0:T(8,128)(2,1)}, bf16[21,8,512]{2,1,0:T(8,128)(2,1)S(1)}, u32[]{:S(2)}, u32[]{:S(2)}) %collective-permute-start.1) | collective-permute-done | bytes 172064 | tf_op jit(solution)/shard_map/ppermute | solution.py:364
  119.8 0.7 copy-done.4
  120.5 1.7 collective-permute-start.6
  122.1 20.6 %time_first.1 = (bf16[21,8,512]{2,1,0:T(8,128)(2,1)S(1)}, bf16[21,8,512]{2,1,0:T(8,128)(2,1)S(1)}, bf16[21,8,512]{2,1,0:T(8,128)(2,1)S(1)}, bf16[21,8,512]{2,1,0...) custom-call(bf16[29,8,512]{2,1,0:T(8,128)(2,1)S(1)} %get-tuple-eleme, ...), custom_call_target="tpu_custom_call" | custom-call | bytes 59040000 | tf_op jit(solution)/shard_map/time_first/pallas_call | solution.py:283
  142.8 2.3 collective-permute-start.28
  145.1 2.0 collective-permute-start.30
  147.1 0.8 collective-permute-start.31
  147.8 3.1 %collective-permute-start.32 = (bf16[21,8,512]{2,1,0:T(8,128)(2,1)S(1)}, bf16[21,8,512]{2,1,0:T(8,128)(2,1)S(1)}, u32[]{:S(2)}, u32[]{:S(2)}) collective-permute-start(bf16[21,8,512]{2,1,0:T(8,128)(2,1)S(1)} %get-tuple-element.94), channel_id=1, source_target_pairs={{0,6},{2,4},{4,2},{6,0},{8,14},{10,12},{12,10},{14,8},{1,7},{3,5},... | collective-permute-start | bytes 516104 | tf_op jit(solution)/shard_map/ppermute | solution.py:364
  151.0 11.9 %time_second.1 = (bf16[21,8,512]{2,1,0:T(8,128)(2,1)S(1)}, bf16[21,8,512]{2,1,0:T(8,128)(2,1)S(1)}, bf16[21,8,512]{2,1,0:T(8,128)(2,1)S(1)}, bf16[21,8,512]{2,1,...) custom-call(bf16[21,8,512]{2,1,0:T(8,128)(2,1)S(1)} %get-tuple-eleme, ...), custom_call_target="tpu_custom_call" | custom-call | bytes 36900000 | tf_op jit(solution)/shard_map/time_second/pallas_call | solution.py:283
  162.9 1.5 collective-permute-start.33
  164.4 2.0 collective-permute-start.34
  166.3 1.9 collective-permute-start.21
  168.3 1.9 collective-permute-start.23
  170.2 1.9 collective-permute-done.33.refs_6_
  172.1 9.9 %collective-permute-start.24 = (bf16[21,8,512]{2,1,0:T(8,128)(2,1)S(1)}, bf16[21,8,512]{2,1,0:T(8,128)(2,1)S(1)}, u32[]{:S(2)}, u32[]{:S(2)}) collective-permute-start(bf16[21,8,512]{2,1,0:T(8,128)(2,1)S(1)} %get-tuple-element.85), channel_id=1, source_target_pairs={{0,10},{2,8},{4,14},{6,12},{8,2},{10,0},{12,6},{14,4},{1,11},{3,9}... | collective-permute-start | bytes 516104 | tf_op jit(solution)/shard_map/ppermute | solution.py:364
  182.0 4.3 %collective-permute-start.25 = (bf16[21,8,512]{2,1,0:T(8,128)(2,1)S(1)}, bf16[21,8,512]{2,1,0:T(8,128)(2,1)S(1)}, u32[]{:S(2)}, u32[]{:S(2)}) collective-permute-start(bf16[21,8,512]{2,1,0:T(8,128)(2,1)S(1)} %get-tuple-element.86), channel_id=1, source_target_pairs={{0,6},{2,4},{4,2},{6,0},{8,14},{10,12},{12,10},{14,8},{1,7},{3,5},... | collective-permute-start | bytes 516104 | tf_op jit(solution)/shard_map/ppermute | solution.py:364
  186.3 1.0 collective-permute-start.26
  187.3 8.2 %collective-permute-done.22.refs_2_ = bf16[21,8,512]{2,1,0:T(8,128)(2,1)S(1)} collective-permute-done((bf16[21,8,512]{2,1,0:T(8,128)(2,1)S(1)}, bf16[21,8,512]{2,1,0:T(8,128)(2,1)S(1)}, u32[]{:S(2)}, u32[]{:S(2)}) %collective-permute-start.22) | collective-permute-done | bytes 172064 | tf_op jit(solution)/shard_map/ppermute | solution.py:364
  195.5 2.1 collective-permute-start.27
  197.6 0.9 copy-done.1
  198.5 1.6 place_first.1
  200.2 24.1 %space_attention.1 = (bf16[7,64,1024]{2,1,0:T(8,128)(2,1)}, bf16[7,64,1024]{2,1,0:T(8,128)(2,1)}, bf16[7,64,1024]{2,1,0:T(8,128)(2,1)}) custom-call(s32[1]{0:T(128)} %bitcast.8.core_ref, bf16[7,64,1024]{2,1,0:T(8,128)(2,1)} %refs_0_.1, bf16[7,64,1024]{2,1,0:T(8,128)(2,1)} %refs_1_.1, bf16[7,64,1024]{2,1,0:T(8,128)(2,1)} %refs_2_.1, ...), custom_call_target="tpu_custom_call" | custom-call | bytes 73800000 | tf_op jit(solution)/shard_map/space_attention/pallas_call | solution.py:330
  224.4 1.6 place_second.1
  (64 shorter events, 0.3 us)
Async XLA Ops:
  7.2 115.0 %all-gather.11.cloned.1.call-start = ((), (), s32[]{:S(2)}) async-start(), calls=%async_computation | async-start | bytes 2621440 | tf_op jit(solution)/shard_map/all_gather | solution.py:418
  9.4 8.8 %collective-permute-start.14 = (bf16[11,8,1024]{2,1,0:T(8,128)(2,1)S(1)}, bf16[11,8,1024]{2,1,0:T(8,128)(2,1)S(1)}, u32[]{:S(2)}, u32[]{:S(2)}) collective-permute-start(bf16[11,8,1024]{2,1,0:T(8,128)(2,1)S(1)} %get-tuple-element.73), channel_id=1, source_target_pairs={{0,2},{2,0},{4,6},{6,4},{8,10},{10,8},{12,14},{14,12},{1,3},{3,1},... | collective-permute-start | bytes 540680 | tf_op jit(solution)/shard_map/ppermute | solution.py:364
  12.4 14.5 %collective-permute-start.15 = (bf16[11,8,1024]{2,1,0:T(8,128)(2,1)S(1)}, bf16[11,8,1024]{2,1,0:T(8,128)(2,1)S(1)}, u32[]{:S(2)}, u32[]{:S(2)}) collective-permute-start(bf16[11,8,1024]{2,1,0:T(8,128)(2,1)S(1)} %get-tuple-element.74), channel_id=1, source_target_pairs={{0,8},{2,10},{4,12},{6,14},{8,0},{10,2},{12,4},{14,6},{1,9},{3,11}... | collective-permute-start | bytes 540680 | tf_op jit(solution)/shard_map/ppermute | solution.py:364
  14.9 45.3 %collective-permute-start.16 = (bf16[11,8,1024]{2,1,0:T(8,128)(2,1)S(1)}, bf16[11,8,1024]{2,1,0:T(8,128)(2,1)S(1)}, u32[]{:S(2)}, u32[]{:S(2)}) collective-permute-start(bf16[11,8,1024]{2,1,0:T(8,128)(2,1)S(1)} %get-tuple-element.75), channel_id=1, source_target_pairs={{0,4},{2,6},{4,0},{6,2},{8,12},{10,14},{12,8},{14,10},{1,5},{3,7},... | collective-permute-start | bytes 540680 | tf_op jit(solution)/shard_map/ppermute | solution.py:364
  16.5 43.7 %collective-permute-start.17 = (bf16[11,8,1024]{2,1,0:T(8,128)(2,1)S(1)}, bf16[11,8,1024]{2,1,0:T(8,128)(2,1)S(1)}, u32[]{:S(2)}, u32[]{:S(2)}) collective-permute-start(bf16[11,8,1024]{2,1,0:T(8,128)(2,1)S(1)} %get-tuple-element.76), channel_id=1, source_target_pairs={{0,10},{2,8},{4,14},{6,12},{8,2},{10,0},{12,6},{14,4},{1,11},{3,9}... | collective-permute-start | bytes 540680 | tf_op jit(solution)/shard_map/ppermute | solution.py:364
  16.8 43.5 %collective-permute-start.18 = (bf16[11,8,1024]{2,1,0:T(8,128)(2,1)S(1)}, bf16[11,8,1024]{2,1,0:T(8,128)(2,1)S(1)}, u32[]{:S(2)}, u32[]{:S(2)}) collective-permute-start(bf16[11,8,1024]{2,1,0:T(8,128)(2,1)S(1)} %get-tuple-element.77), channel_id=1, source_target_pairs={{0,6},{2,4},{4,2},{6,0},{8,14},{10,12},{12,10},{14,8},{1,7},{3,5},... | collective-permute-start | bytes 540680 | tf_op jit(solution)/shard_map/ppermute | solution.py:364
  18.2 42.1 %collective-permute-start.19 = (bf16[11,8,1024]{2,1,0:T(8,128)(2,1)S(1)}, bf16[11,8,1024]{2,1,0:T(8,128)(2,1)S(1)}, u32[]{:S(2)}, u32[]{:S(2)}) collective-permute-start(bf16[11,8,1024]{2,1,0:T(8,128)(2,1)S(1)} %get-tuple-element.78), channel_id=1, source_target_pairs={{0,12},{2,14},{4,8},{6,10},{8,4},{10,6},{12,0},{14,2},{1,13},{3,15... | collective-permute-start | bytes 540680 | tf_op jit(solution)/shard_map/ppermute | solution.py:364
  26.9 33.4 %collective-permute-start.20 = (bf16[11,8,1024]{2,1,0:T(8,128)(2,1)S(1)}, bf16[11,8,1024]{2,1,0:T(8,128)(2,1)S(1)}, u32[]{:S(2)}, u32[]{:S(2)}) collective-permute-start(bf16[11,8,1024]{2,1,0:T(8,128)(2,1)S(1)} %get-tuple-element.79), channel_id=1, source_target_pairs={{0,14},{2,12},{4,10},{6,8},{8,6},{10,4},{12,2},{14,0},{1,15},{3,13... | collective-permute-start | bytes 540680 | tf_op jit(solution)/shard_map/ppermute | solution.py:364
  59.6 0.7 copy-start.6
  61.6 138.5 %all-gather.15.cloned.1.call-start = ((), (), s32[]{:S(2)}) async-start(), calls=%async_computation.2 | async-start | bytes 2752512 | tf_op jit(solution)/shard_map/all_gather | solution.py:415
  62.4 137.7 %all-gather.17.cloned.1.call-start = ((), (), s32[]{:S(2)}) async-start(), calls=%async_computation.3 | async-start | bytes 2752512 | tf_op jit(solution)/shard_map/all_gather | solution.py:415
  63.1 137.0 %all-gather.19.cloned.1.call-start = ((), (), s32[]{:S(2)}) async-start(), calls=%async_computation.4 | async-start | bytes 2752512 | tf_op jit(solution)/shard_map/all_gather | solution.py:415
  63.7 136.4 %all-gather.21.cloned.1.call-start = ((), (), s32[]{:S(2)}) async-start(), calls=%async_computation.5 | async-start | bytes 2752512 | tf_op jit(solution)/shard_map/all_gather | solution.py:415
  64.3 135.9 %all-gather.13.cloned.1.call-start = ((), (), s32[]{:S(2)}) async-start(), calls=%async_computation.1 | async-start | bytes 2621440 | tf_op jit(solution)/shard_map/all_gather | solution.py:418
  64.3 7.4 %collective-permute-start.7 = (bf16[29,8,512]{2,1,0:T(8,128)(2,1)S(1)}, bf16[29,8,512]{2,1,0:T(8,128)(2,1)S(1)}, u32[]{:S(2)}, u32[]{:S(2)}) collective-permute-start(bf16[29,8,512]{2,1,0:T(8,128)(2,1)S(1)} %get-tuple-element.66), channel_id=1, source_target_pairs={{0,2},{2,0},{4,6},{6,4},{8,10},{10,8},{12,14},{14,12},{1,3},{3,1},... | collective-permute-start | bytes 712712 | tf_op jit(solution)/shard_map/ppermute | solution.py:364
  65.9 14.8 %collective-permute-start.8 = (bf16[29,8,512]{2,1,0:T(8,128)(2,1)S(1)}, bf16[29,8,512]{2,1,0:T(8,128)(2,1)S(1)}, u32[]{:S(2)}, u32[]{:S(2)}) collective-permute-start(bf16[29,8,512]{2,1,0:T(8,128)(2,1)S(1)} %get-tuple-element.67), channel_id=1, source_target_pairs={{0,8},{2,10},{4,12},{6,14},{8,0},{10,2},{12,4},{14,6},{1,9},{3,11}... | collective-permute-start | bytes 712712 | tf_op jit(solution)/shard_map/ppermute | solution.py:364
  65.9 20.5 %collective-permute-start.9 = (bf16[29,8,512]{2,1,0:T(8,128)(2,1)}, bf16[29,8,512]{2,1,0:T(8,128)(2,1)S(1)}, u32[]{:S(2)}, u32[]{:S(2)}) collective-permute-start(bf16[29,8,512]{2,1,0:T(8,128)(2,1)} %get-tuple-element.68), channel_id=1, source_target_pairs={{0,4},{2,6},{4,0},{6,2},{8,12},{10,14},{12,8},{14,10},{1,5},{3,7},... | collective-permute-start | bytes 712712 | tf_op jit(solution)/shard_map/ppermute | solution.py:364
  68.0 29.3 %collective-permute-start.10 = (bf16[29,8,512]{2,1,0:T(8,128)(2,1)}, bf16[29,8,512]{2,1,0:T(8,128)(2,1)S(1)}, u32[]{:S(2)}, u32[]{:S(2)}) collective-permute-start(bf16[29,8,512]{2,1,0:T(8,128)(2,1)} %get-tuple-element.69), channel_id=1, source_target_pairs={{0,10},{2,8},{4,14},{6,12},{8,2},{10,0},{12,6},{14,4},{1,11},{3,9}... | collective-permute-start | bytes 712712 | tf_op jit(solution)/shard_map/ppermute | solution.py:364
  68.8 28.7 %collective-permute-start.11 = (bf16[29,8,512]{2,1,0:T(8,128)(2,1)}, bf16[29,8,512]{2,1,0:T(8,128)(2,1)S(1)}, u32[]{:S(2)}, u32[]{:S(2)}) collective-permute-start(bf16[29,8,512]{2,1,0:T(8,128)(2,1)} %get-tuple-element.70), channel_id=1, source_target_pairs={{0,6},{2,4},{4,2},{6,0},{8,14},{10,12},{12,10},{14,8},{1,7},{3,5},... | collective-permute-start | bytes 712712 | tf_op jit(solution)/shard_map/ppermute | solution.py:364
  71.8 25.7 %collective-permute-start.12 = (bf16[29,8,512]{2,1,0:T(8,128)(2,1)}, bf16[29,8,512]{2,1,0:T(8,128)(2,1)S(1)}, u32[]{:S(2)}, u32[]{:S(2)}) collective-permute-start(bf16[29,8,512]{2,1,0:T(8,128)(2,1)} %get-tuple-element.71), channel_id=1, source_target_pairs={{0,12},{2,14},{4,8},{6,10},{8,4},{10,6},{12,0},{14,2},{1,13},{3,15... | collective-permute-start | bytes 712712 | tf_op jit(solution)/shard_map/ppermute | solution.py:364
  80.7 16.8 %collective-permute-start.13 = (bf16[29,8,512]{2,1,0:T(8,128)(2,1)}, bf16[29,8,512]{2,1,0:T(8,128)(2,1)S(1)}, u32[]{:S(2)}, u32[]{:S(2)}) collective-permute-start(bf16[29,8,512]{2,1,0:T(8,128)(2,1)} %copy-done.6), channel_id=1, source_target_pairs={{0,14},{2,12},{4,10},{6,8},{8,6},{10,4},{12,2},{14,0},{1,15},{3,13... | collective-permute-start | bytes 712712 | tf_op jit(solution)/shard_map/ppermute | solution.py:364
  83.8 0.7 copy-start.10
  84.4 0.7 copy-start.11
  85.1 0.7 copy-start.12
  85.7 0.7 copy-start.13
  86.4 11.1 %copy-start.7 = (bf16[21,8,512]{2,1,0:T(8,128)(2,1)}, bf16[21,8,512]{2,1,0:T(8,128)(2,1)S(1)}, u32[]{:S(2)}) copy-start(bf16[21,8,512]{2,1,0:T(8,128)(2,1)S(1)} %get-tuple-element.65) | copy-start | bytes 516100
  86.4 11.1 %copy-start.8 = (bf16[21,8,512]{2,1,0:T(8,128)(2,1)}, bf16[21,8,512]{2,1,0:T(8,128)(2,1)S(1)}, u32[]{:S(2)}) copy-start(bf16[21,8,512]{2,1,0:T(8,128)(2,1)S(1)} %get-tuple-element.64) | copy-start | bytes 516100
  86.4 11.1 %copy-start.9 = (bf16[21,8,512]{2,1,0:T(8,128)(2,1)}, bf16[21,8,512]{2,1,0:T(8,128)(2,1)S(1)}, u32[]{:S(2)}) copy-start(bf16[21,8,512]{2,1,0:T(8,128)(2,1)S(1)} %get-tuple-element.63) | copy-start | bytes 516100
  98.8 14.3 %collective-permute-start = (bf16[21,8,512]{2,1,0:T(8,128)(2,1)}, bf16[21,8,512]{2,1,0:T(8,128)(2,1)S(1)}, u32[]{:S(2)}, u32[]{:S(2)}) collective-permute-start(bf16[21,8,512]{2,1,0:T(8,128)(2,1)} %copy-done.13), channel_id=1, source_target_pairs={{0,2},{2,0},{4,6},{6,4},{8,10},{10,8},{12,14},{14,12},{1,3},{3,1},... | collective-permute-start | bytes 516104 | tf_op jit(solution)/shard_map/ppermute | solution.py:364
  100.7 19.1 %collective-permute-start.1 = (bf16[21,8,512]{2,1,0:T(8,128)(2,1)}, bf16[21,8,512]{2,1,0:T(8,128)(2,1)S(1)}, u32[]{:S(2)}, u32[]{:S(2)}) collective-permute-start(bf16[21,8,512]{2,1,0:T(8,128)(2,1)} %copy-done.12), channel_id=1, source_target_pairs={{0,8},{2,10},{4,12},{6,14},{8,0},{10,2},{12,4},{14,6},{1,9},{3,11}... | collective-permute-start | bytes 516104 | tf_op jit(solution)/shard_map/ppermute | solution.py:364
  109.7 33.1 %collective-permute-start.2 = (bf16[21,8,512]{2,1,0:T(8,128)(2,1)}, bf16[21,8,512]{2,1,0:T(8,128)(2,1)}, u32[]{:S(2)}, u32[]{:S(2)}) collective-permute-start(bf16[21,8,512]{2,1,0:T(8,128)(2,1)} %copy-done.11), channel_id=1, source_target_pairs={{0,4},{2,6},{4,0},{6,2},{8,12},{10,14},{12,8},{14,10},{1,5},{3,7},... | collective-permute-start | bytes 516104 | tf_op jit(solution)/shard_map/ppermute | solution.py:364
  109.7 35.4 %collective-permute-start.3 = (bf16[21,8,512]{2,1,0:T(8,128)(2,1)}, bf16[21,8,512]{2,1,0:T(8,128)(2,1)}, u32[]{:S(2)}, u32[]{:S(2)}) collective-permute-start(bf16[21,8,512]{2,1,0:T(8,128)(2,1)} %copy-done.10), channel_id=1, source_target_pairs={{0,10},{2,8},{4,14},{6,12},{8,2},{10,0},{12,6},{14,4},{1,11},{3,9}... | collective-permute-start | bytes 516104 | tf_op jit(solution)/shard_map/ppermute | solution.py:364
  112.4 32.7 %collective-permute-start.4 = (bf16[21,8,512]{2,1,0:T(8,128)(2,1)}, bf16[21,8,512]{2,1,0:T(8,128)(2,1)}, u32[]{:S(2)}, u32[]{:S(2)}) collective-permute-start(bf16[21,8,512]{2,1,0:T(8,128)(2,1)} %copy-done.9), channel_id=1, source_target_pairs={{0,6},{2,4},{4,2},{6,0},{8,14},{10,12},{12,10},{14,8},{1,7},{3,5},... | collective-permute-start | bytes 516104 | tf_op jit(solution)/shard_map/ppermute | solution.py:364
  113.2 0.7 copy-start.2
  113.8 33.2 %collective-permute-start.5 = (bf16[21,8,512]{2,1,0:T(8,128)(2,1)}, bf16[21,8,512]{2,1,0:T(8,128)(2,1)}, u32[]{:S(2)}, u32[]{:S(2)}) collective-permute-start(bf16[21,8,512]{2,1,0:T(8,128)(2,1)} %copy-done.8), channel_id=1, source_target_pairs={{0,12},{2,14},{4,8},{6,10},{8,4},{10,6},{12,0},{14,2},{1,13},{3,15... | collective-permute-start | bytes 516104 | tf_op jit(solution)/shard_map/ppermute | solution.py:364
  119.8 0.7 copy-start.4
  120.5 27.4 %collective-permute-start.6 = (bf16[21,8,512]{2,1,0:T(8,128)(2,1)}, bf16[21,8,512]{2,1,0:T(8,128)(2,1)}, u32[]{:S(2)}, u32[]{:S(2)}) collective-permute-start(bf16[21,8,512]{2,1,0:T(8,128)(2,1)} %copy-done.7), channel_id=1, source_target_pairs={{0,14},{2,12},{4,10},{6,8},{8,6},{10,4},{12,2},{14,0},{1,15},{3,13... | collective-permute-start | bytes 516104 | tf_op jit(solution)/shard_map/ppermute | solution.py:364
  122.1 28.8 %copy-start.3 = (bf16[21,8,512]{2,1,0:T(8,128)(2,1)S(1)}, bf16[21,8,512]{2,1,0:T(8,128)(2,1)}, u32[]{:S(2)}) copy-start(bf16[21,8,512]{2,1,0:T(8,128)(2,1)} %copy-done.2) | copy-start | bytes 516100
  122.1 28.8 %copy-start.5 = (bf16[21,8,512]{2,1,0:T(8,128)(2,1)S(1)}, bf16[21,8,512]{2,1,0:T(8,128)(2,1)}, u32[]{:S(2)}) copy-start(bf16[21,8,512]{2,1,0:T(8,128)(2,1)} %copy-done.4) | copy-start | bytes 516100
  142.8 52.7 %copy-start = (bf16[21,8,512]{2,1,0:T(8,128)(2,1)}, bf16[21,8,512]{2,1,0:T(8,128)(2,1)S(1)}, u32[]{:S(2)}) copy-start(bf16[21,8,512]{2,1,0:T(8,128)(2,1)S(1)} %get-tuple-element.89.refs_0_) | copy-start | bytes 516100
  142.8 20.1 %collective-permute-start.28 = (bf16[21,8,512]{2,1,0:T(8,128)(2,1)S(1)}, bf16[21,8,512]{2,1,0:T(8,128)(2,1)S(1)}, u32[]{:S(2)}, u32[]{:S(2)}) collective-permute-start(bf16[21,8,512]{2,1,0:T(8,128)(2,1)S(1)} %get-tuple-element.90), channel_id=1, source_target_pairs={{0,2},{2,0},{4,6},{6,4},{8,10},{10,8},{12,14},{14,12},{1,3},{3,1},... | collective-permute-start | bytes 516104 | tf_op jit(solution)/shard_map/ppermute | solution.py:364
  145.1 19.3 %collective-permute-start.29 = (bf16[21,8,512]{2,1,0:T(8,128)(2,1)S(1)}, bf16[21,8,512]{2,1,0:T(8,128)(2,1)S(1)}, u32[]{:S(2)}, u32[]{:S(2)}) collective-permute-start(bf16[21,8,512]{2,1,0:T(8,128)(2,1)S(1)} %get-tuple-element.91), channel_id=1, source_target_pairs={{0,8},{2,10},{4,12},{6,14},{8,0},{10,2},{12,4},{14,6},{1,9},{3,11}... | collective-permute-start | bytes 516104 | tf_op jit(solution)/shard_map/ppermute | solution.py:364
  145.1 21.2 %collective-permute-start.30 = (bf16[21,8,512]{2,1,0:T(8,128)(2,1)S(1)}, bf16[21,8,512]{2,1,0:T(8,128)(2,1)S(1)}, u32[]{:S(2)}, u32[]{:S(2)}) collective-permute-start(bf16[21,8,512]{2,1,0:T(8,128)(2,1)S(1)} %get-tuple-element.92), channel_id=1, source_target_pairs={{0,4},{2,6},{4,0},{6,2},{8,12},{10,14},{12,8},{14,10},{1,5},{3,7},... | collective-permute-start | bytes 516104 | tf_op jit(solution)/shard_map/ppermute | solution.py:364
  147.1 21.2 %collective-permute-start.31 = (bf16[21,8,512]{2,1,0:T(8,128)(2,1)S(1)}, bf16[21,8,512]{2,1,0:T(8,128)(2,1)S(1)}, u32[]{:S(2)}, u32[]{:S(2)}) collective-permute-start(bf16[21,8,512]{2,1,0:T(8,128)(2,1)S(1)} %get-tuple-element.93), channel_id=1, source_target_pairs={{0,10},{2,8},{4,14},{6,12},{8,2},{10,0},{12,6},{14,4},{1,11},{3,9}... | collective-permute-start | bytes 516104 | tf_op jit(solution)/shard_map/ppermute | solution.py:364
  147.8 20.4 %collective-permute-start.32 = (bf16[21,8,512]{2,1,0:T(8,128)(2,1)S(1)}, bf16[21,8,512]{2,1,0:T(8,128)(2,1)S(1)}, u32[]{:S(2)}, u32[]{:S(2)}) collective-permute-start(bf16[21,8,512]{2,1,0:T(8,128)(2,1)S(1)} %get-tuple-element.94), channel_id=1, source_target_pairs={{0,6},{2,4},{4,2},{6,0},{8,14},{10,12},{12,10},{14,8},{1,7},{3,5},... | collective-permute-start | bytes 516104 | tf_op jit(solution)/shard_map/ppermute | solution.py:364
  162.9 9.2 %collective-permute-start.33 = (bf16[21,8,512]{2,1,0:T(8,128)(2,1)S(1)}, bf16[21,8,512]{2,1,0:T(8,128)(2,1)S(1)}, u32[]{:S(2)}, u32[]{:S(2)}) collective-permute-start(bf16[21,8,512]{2,1,0:T(8,128)(2,1)S(1)} %get-tuple-element.95), channel_id=1, source_target_pairs={{0,12},{2,14},{4,8},{6,10},{8,4},{10,6},{12,0},{14,2},{1,13},{3,15... | collective-permute-start | bytes 516104 | tf_op jit(solution)/shard_map/ppermute | solution.py:364
  164.4 17.6 %collective-permute-start.34 = (bf16[21,8,512]{2,1,0:T(8,128)(2,1)S(1)}, bf16[21,8,512]{2,1,0:T(8,128)(2,1)S(1)}, u32[]{:S(2)}, u32[]{:S(2)}) collective-permute-start(bf16[21,8,512]{2,1,0:T(8,128)(2,1)S(1)} %get-tuple-element.96), channel_id=1, source_target_pairs={{0,14},{2,12},{4,10},{6,8},{8,6},{10,4},{12,2},{14,0},{1,15},{3,13... | collective-permute-start | bytes 516104 | tf_op jit(solution)/shard_map/ppermute | solution.py:364
  166.3 20.0 %collective-permute-start.21 = (bf16[21,8,512]{2,1,0:T(8,128)(2,1)S(1)}, bf16[21,8,512]{2,1,0:T(8,128)(2,1)S(1)}, u32[]{:S(2)}, u32[]{:S(2)}) collective-permute-start(bf16[21,8,512]{2,1,0:T(8,128)(2,1)S(1)} %get-tuple-element.82), channel_id=1, source_target_pairs={{0,2},{2,0},{4,6},{6,4},{8,10},{10,8},{12,14},{14,12},{1,3},{3,1},... | collective-permute-start | bytes 516104 | tf_op jit(solution)/shard_map/ppermute | solution.py:364
  168.3 27.2 %collective-permute-start.22 = (bf16[21,8,512]{2,1,0:T(8,128)(2,1)S(1)}, bf16[21,8,512]{2,1,0:T(8,128)(2,1)S(1)}, u32[]{:S(2)}, u32[]{:S(2)}) collective-permute-start(bf16[21,8,512]{2,1,0:T(8,128)(2,1)S(1)} %get-tuple-element.83), channel_id=1, source_target_pairs={{0,8},{2,10},{4,12},{6,14},{8,0},{10,2},{12,4},{14,6},{1,9},{3,11}... | collective-permute-start | bytes 516104 | tf_op jit(solution)/shard_map/ppermute | solution.py:364
  168.3 56.0 %collective-permute-start.23 = (bf16[21,8,512]{2,1,0:T(8,128)(2,1)}, bf16[21,8,512]{2,1,0:T(8,128)(2,1)S(1)}, u32[]{:S(2)}, u32[]{:S(2)}) collective-permute-start(bf16[21,8,512]{2,1,0:T(8,128)(2,1)} %get-tuple-element.84), channel_id=1, source_target_pairs={{0,4},{2,6},{4,0},{6,2},{8,12},{10,14},{12,8},{14,10},{1,5},{3,7},... | collective-permute-start | bytes 516104 | tf_op jit(solution)/shard_map/ppermute | solution.py:364
  172.1 52.2 %collective-permute-start.24 = (bf16[21,8,512]{2,1,0:T(8,128)(2,1)S(1)}, bf16[21,8,512]{2,1,0:T(8,128)(2,1)S(1)}, u32[]{:S(2)}, u32[]{:S(2)}) collective-permute-start(bf16[21,8,512]{2,1,0:T(8,128)(2,1)S(1)} %get-tuple-element.85), channel_id=1, source_target_pairs={{0,10},{2,8},{4,14},{6,12},{8,2},{10,0},{12,6},{14,4},{1,11},{3,9}... | collective-permute-start | bytes 516104 | tf_op jit(solution)/shard_map/ppermute | solution.py:364
  182.0 42.3 %collective-permute-start.25 = (bf16[21,8,512]{2,1,0:T(8,128)(2,1)S(1)}, bf16[21,8,512]{2,1,0:T(8,128)(2,1)S(1)}, u32[]{:S(2)}, u32[]{:S(2)}) collective-permute-start(bf16[21,8,512]{2,1,0:T(8,128)(2,1)S(1)} %get-tuple-element.86), channel_id=1, source_target_pairs={{0,6},{2,4},{4,2},{6,0},{8,14},{10,12},{12,10},{14,8},{1,7},{3,5},... | collective-permute-start | bytes 516104 | tf_op jit(solution)/shard_map/ppermute | solution.py:364
  186.3 38.0 %collective-permute-start.26 = (bf16[21,8,512]{2,1,0:T(8,128)(2,1)S(1)}, bf16[21,8,512]{2,1,0:T(8,128)(2,1)S(1)}, u32[]{:S(2)}, u32[]{:S(2)}) collective-permute-start(bf16[21,8,512]{2,1,0:T(8,128)(2,1)S(1)} %get-tuple-element.87), channel_id=1, source_target_pairs={{0,12},{2,14},{4,8},{6,10},{8,4},{10,6},{12,0},{14,2},{1,13},{3,15... | collective-permute-start | bytes 516104 | tf_op jit(solution)/shard_map/ppermute | solution.py:364
  195.5 28.8 %collective-permute-start.27 = (bf16[21,8,512]{2,1,0:T(8,128)(2,1)S(1)}, bf16[21,8,512]{2,1,0:T(8,128)(2,1)S(1)}, u32[]{:S(2)}, u32[]{:S(2)}) collective-permute-start(bf16[21,8,512]{2,1,0:T(8,128)(2,1)S(1)} %get-tuple-element.88), channel_id=1, source_target_pairs={{0,14},{2,12},{4,10},{6,8},{8,6},{10,4},{12,2},{14,0},{1,15},{3,13... | collective-permute-start | bytes 516104 | tf_op jit(solution)/shard_map/ppermute | solution.py:364
  197.6 0.9 copy-start.1
Sparse Core Ops, SparseCore 0:
  61.8 21.6 all-gather.10
  85.0 10.1 all-gather.14
  96.8 11.3 all-gather.16
  109.6 11.3 all-gather.18
  122.4 11.3 all-gather.20
  135.8 23.7 all-gather.12
